TPU v7x, 32 devices: a whole 2x2x4 slice. The times are simulated.
32 devices in a mesh: dp: 2 (over x), expert: 16 (over z, y, core).
Axes of the slice: x: 2, y: 2, z: 4, core: 2. Of those that a mesh axis runs over, the one named last changes fastest.
Arguments:
- hidden_in: bfloat16 [4096, 1536], P(('dp', 'expert')), may hold values from -6 to 6
- cotangent: bfloat16 [4096, 1536], P(('dp', 'expert')), may hold values from -6 to 6
- routes: int32 [4096, 6], P(('dp', 'expert')), may hold values from 0 to 63, all different within a row; in each aligned block of 128 rows (0 to 127, 128 to 255, ...) at most 24 rows name the same one
- route_gates: float32 [4096, 6], P(('dp', 'expert')), may hold values from 0.1 to 0.3
- lengths: int32 [32, 3], P(('dp', 'expert')), may hold values from 1 to 64, 128 in all within a row
- in_proj: bfloat16 [1536, 6448], P(('dp', 'expert')), may hold values from -0.15625 to 0.15625
- out_proj: bfloat16 [3072, 1536], P(('dp', 'expert')), may hold values from -0.109375 to 0.109375
- conv_weight: bfloat16 [3328, 4], P(('dp', 'expert')), may hold values from -3 to 3
- conv_bias: bfloat16 [3328], P(('dp', 'expert')), may hold values from -0.5 to 0.5
- norm_gain: bfloat16 [1536], P(('dp', 'expert')), may hold values from 0.5 to 1.5
- mix_gain: bfloat16 [3072], P(('dp', 'expert')), may hold values from 0.5 to 1.5
- ffn_gain: bfloat16 [1536], P(('dp', 'expert')), may hold values from 0.5 to 1.5
- shared_gate: bfloat16 [1536, 1024], P(('dp', 'expert')), may hold values from -0.15625 to 0.15625
- shared_up: bfloat16 [1536, 1024], P(('dp', 'expert')), may hold values from -0.15625 to 0.15625
- shared_down: bfloat16 [1024, 1536], P(('dp', 'expert')), may hold values from -0.1875 to 0.1875
- expert_gate: bfloat16 [64, 1536, 512], P('expert', 'dp'), may hold values from -0.15625 to 0.15625
- expert_up: bfloat16 [64, 1536, 512], P('expert', 'dp'), may hold values from -0.15625 to 0.15625
- expert_down: bfloat16 [64, 512, 1536], P('expert', 'dp'), may hold values from -0.25 to 0.25
- decay_log: float32 [48], replicated, may hold values from 0 to 2.77
- step_bias: float32 [48], replicated, may hold values from -5 to -1
- skip_gain: float32 [48], replicated, may hold values from 0.5 to 1.5
Outputs:
- output: bfloat16 [4096, 1536], P(('dp', 'expert'))
- grad_input: float32 [4096, 1536], P(('dp', 'expert'))
- grad_in_proj: float32 [1536, 6448], P(('dp', 'expert'))
- grad_out_proj: float32 [3072, 1536], P(('dp', 'expert'))
- grad_conv_weight: float32 [3328, 4], P(('dp', 'expert'))
- grad_conv_bias: float32 [3328], P(('dp', 'expert'))
- grad_norm_gain: float32 [1536], P(('dp', 'expert'))
- grad_mix_gain: float32 [3072], P(('dp', 'expert'))
- grad_ffn_gain: float32 [1536], P(('dp', 'expert'))
- grad_shared_gate: float32 [1536, 1024], P(('dp', 'expert'))
- grad_shared_up: float32 [1536, 1024], P(('dp', 'expert'))
- grad_shared_down: float32 [1024, 1536], P(('dp', 'expert'))
- grad_expert_gate: float32 [64, 1536, 512], P('expert', 'dp')
- grad_expert_up: float32 [64, 1536, 512], P('expert', 'dp')
- grad_expert_down: float32 [64, 512, 1536], P('expert', 'dp')
- grad_decay_log: float32 [48], replicated
- grad_step_bias: float32 [48], replicated
- grad_skip_gain: float32 [48], replicated
Inputs may be any that keep to these rules, and one draw needn't show every extreme that they name: `routes`: within the rows of one device (128 tokens), no expert is named more than 24 times, a bound that some block reaches; a token's 6 experts differ. `lengths`: each device's row sums to 128; the last entry is the unused tail.
All inputs are finite; a program needn't handle non-finite values.
Results may differ from a plain program's by a relative error of at most 0.0091.
Values may be sent and summed in bfloat16 or wider, within the bound.
No kernel may reach another device: no remote copies, remote signals or barrier semaphores. Data moves between devices by JAX's collectives and lax.ppermute only.
A program may use at most 448 MiB of HBM per device.

v0:
```python
import jax
import jax.numpy as jnp
from jax import lax
from jax.sharding import PartitionSpec as P

HEADS = 48
HEAD_DIM = 64
STATE = 128
KERNEL = 4
SEQ_SLOTS = 3
INNER = 3072
CONV_CH = 3328


epsilon = 1e-05


def matmul(left, right):
    return jnp.dot(left, right, precision=lax.Precision.HIGHEST, preferred_element_type=jnp.float32)


def rms_norm(value_entries, gain):
    return (
        value_entries
        * lax.rsqrt(jnp.mean(value_entries * value_entries, axis=-1, keepdims=True) + epsilon)
        * gain
    )


def swiglu(gate_part, up_part):
    return jax.nn.silu(gate_part) * up_part


def flatten_rows(value, pieces):
    return value.reshape(pieces, -1)


def restore_rows(value, template, pieces):
    return value.reshape((template.shape[0] // pieces,) + tuple(template.shape[1:]))


def segment_ids(lengths_row, count):
    bounds = jnp.cumsum(lengths_row)
    position = jnp.arange(count, dtype=jnp.int32)
    return jnp.sum((position[:, None] >= bounds[None, : SEQ_SLOTS - 1]).astype(jnp.int32), axis=1)


def mixer_core(
    projected, segment, conv_weight, conv_bias, step_bias, decay_log, skip_gain, mix_gain
):
    count = projected.shape[0]
    gate_z = projected[:, :INNER]
    conv_in = projected[:, INNER : INNER + CONV_CH]
    step_raw = projected[:, INNER + CONV_CH :]
    total = conv_bias[None, :] + conv_weight[:, KERNEL - 1][None, :] * conv_in
    for offset in range(1, KERNEL):
        shifted = jnp.concatenate(
            [jnp.zeros((offset, CONV_CH), conv_in.dtype), conv_in[: count - offset]], axis=0
        )
        earlier = jnp.concatenate(
            [jnp.full((offset,), -1, jnp.int32), segment[: count - offset]], axis=0
        )
        same_run = (earlier == segment).astype(conv_in.dtype)
        total = total + conv_weight[:, KERNEL - 1 - offset][None, :] * shifted * same_run[:, None]
    conv_out = jax.nn.silu(total)
    value_entries = conv_out[:, :INNER].reshape(count, HEADS, HEAD_DIM)
    state_in = conv_out[:, INNER : INNER + STATE]
    state_out = conv_out[:, INNER + STATE :]
    step_size = jax.nn.softplus(step_raw + step_bias[None, :])
    decay_rate = -jnp.exp(decay_log)
    cumul = jnp.cumsum(step_size * decay_rate[None, :], axis=0)
    position = jnp.arange(count, dtype=jnp.int32)
    causal = (position[:, None] >= position[None, :]) & (segment[:, None] == segment[None, :])
    spread = cumul.T[:, :, None] - cumul.T[:, None, :]
    decay = jnp.exp(jnp.where(causal[None, :, :], spread, -jnp.inf))
    scores = matmul(state_out, state_in.T)
    mixing = decay * scores[None, :, :] * step_size.T[:, None, :]
    scan_out = jnp.einsum("hij,jhp->ihp", mixing, value_entries, precision=lax.Precision.HIGHEST)
    scan_out = scan_out + skip_gain[None, :, None] * value_entries
    gated = scan_out.reshape(count, INNER) * jax.nn.silu(gate_z)
    return rms_norm(gated, mix_gain)


def local(
    hidden_in,
    cotangent,
    routes,
    route_gates,
    lengths,
    in_proj,
    out_proj,
    conv_weight,
    conv_bias,
    norm_gain,
    mix_gain,
    ffn_gain,
    shared_gate,
    shared_up,
    shared_down,
    expert_gate,
    expert_up,
    expert_down,
    decay_log,
    step_bias,
    skip_gain,
):
    mixer_set = (
        lax.all_gather(in_proj, ("dp", "expert"), axis=0, tiled=True),
        lax.all_gather(out_proj, ("dp", "expert"), axis=0, tiled=True),
        lax.all_gather(conv_weight, ("dp", "expert"), axis=0, tiled=True),
        lax.all_gather(conv_bias, ("dp", "expert"), axis=0, tiled=True),
        lax.all_gather(norm_gain, ("dp", "expert"), axis=0, tiled=True),
        lax.all_gather(mix_gain, ("dp", "expert"), axis=0, tiled=True),
        lax.all_gather(ffn_gain, ("dp", "expert"), axis=0, tiled=True),
        lax.all_gather(shared_gate, ("dp", "expert"), axis=0, tiled=True),
        lax.all_gather(shared_up, ("dp", "expert"), axis=0, tiled=True),
        lax.all_gather(shared_down, ("dp", "expert"), axis=0, tiled=True),
    )
    expert_set = (
        lax.all_gather(expert_gate, "dp", axis=1, tiled=True),
        lax.all_gather(expert_up, "dp", axis=1, tiled=True),
        lax.all_gather(expert_down, "dp", axis=1, tiled=True),
    )
    token_count = hidden_in.shape[0]
    width = hidden_in.shape[1]
    top_count = routes.shape[1]
    local_experts = expert_gate.shape[0]
    groups = lax.axis_size("expert")
    replicas = lax.axis_size("dp")
    all_devices = replicas * groups
    capacity = 2 * token_count * top_count // (local_experts * groups)
    lanes = groups * capacity
    slot_total = local_experts * lanes
    segment = segment_ids(lengths[0], token_count)
    live = (segment < SEQ_SLOTS - 1).astype(jnp.float32)[:, None]
    flat_routes = routes.reshape(-1)
    onehot = (
        flat_routes[:, None] == jnp.arange(local_experts * groups, dtype=jnp.int32)[None, :]
    ).astype(jnp.int32)
    ranks = jnp.sum((jnp.cumsum(onehot, axis=0) - 1) * onehot, axis=1)
    slots = flat_routes % local_experts * lanes + flat_routes // local_experts * capacity + ranks
    slot_source = (
        jnp.zeros((slot_total,), jnp.int32)
        .at[slots]
        .set(jnp.arange(token_count * top_count, dtype=jnp.int32))
    )
    filled = jnp.zeros((slot_total,), jnp.bool_).at[slots].set(True)[:, None]
    zero_low = jnp.zeros((), jnp.bfloat16)
    input_rows = hidden_in.astype(jnp.float32)
    normed, norm_back = jax.vjp(rms_norm, input_rows, mixer_set[4].astype(jnp.float32))
    normed_low = normed.astype(jnp.bfloat16)
    projected = jnp.dot(normed_low, mixer_set[0], preferred_element_type=jnp.float32)

    def core_piece(proj_in, conv_w, conv_b, bias_in, decay_in, skip_in, gain_in):
        return mixer_core(proj_in, segment, conv_w, conv_b, bias_in, decay_in, skip_in, gain_in)

    mixed, core_back = jax.vjp(
        jax.checkpoint(core_piece),
        projected,
        mixer_set[2].astype(jnp.float32),
        mixer_set[3].astype(jnp.float32),
        step_bias,
        decay_log,
        skip_gain,
        mixer_set[5].astype(jnp.float32),
    )
    mixed_low = mixed.astype(jnp.bfloat16)
    mixer_out = jnp.dot(mixed_low, mixer_set[1], preferred_element_type=jnp.float32)
    resid = input_rows + live * mixer_out
    ffn_normed, ffn_back = jax.vjp(rms_norm, resid, mixer_set[6].astype(jnp.float32))
    ffn_low = ffn_normed.astype(jnp.bfloat16)
    shared_g = jnp.dot(ffn_low, mixer_set[7], preferred_element_type=jnp.float32)
    shared_u = jnp.dot(ffn_low, mixer_set[8], preferred_element_type=jnp.float32)
    shared_act, shared_back = jax.vjp(swiglu, shared_g, shared_u)
    shared_low = shared_act.astype(jnp.bfloat16)
    shared_out = jnp.dot(shared_low, mixer_set[9], preferred_element_type=jnp.float32)
    send_rows = jnp.where(filled, ffn_low[slot_source // top_count], zero_low).reshape(
        local_experts, lanes, width
    )
    incoming_rows = lax.all_to_all(send_rows, "expert", split_axis=1, concat_axis=1, tiled=True)
    hidden_g = jnp.einsum(
        "erd,edf->erf", incoming_rows, expert_set[0], preferred_element_type=jnp.float32
    )
    hidden_u = jnp.einsum(
        "erd,edf->erf", incoming_rows, expert_set[1], preferred_element_type=jnp.float32
    )
    expert_act, expert_back = jax.vjp(swiglu, hidden_g, hidden_u)
    act_low = expert_act.astype(jnp.bfloat16)
    produced_rows = jnp.einsum(
        "erf,efd->erd", act_low, expert_set[2], preferred_element_type=jnp.float32
    ).astype(jnp.bfloat16)
    returned = lax.all_to_all(produced_rows, "expert", split_axis=1, concat_axis=1, tiled=True)
    picked = returned.reshape(slot_total, width)[slots].reshape(token_count, top_count, width)
    routed = jnp.sum(picked.astype(jnp.float32) * route_gates[:, :, None], axis=1)
    output = (resid + live * (shared_out + routed)).astype(jnp.bfloat16)
    mixer_back = (
        lax.all_gather(in_proj, ("dp", "expert"), axis=0, tiled=True),
        lax.all_gather(out_proj, ("dp", "expert"), axis=0, tiled=True),
        lax.all_gather(conv_weight, ("dp", "expert"), axis=0, tiled=True),
        lax.all_gather(conv_bias, ("dp", "expert"), axis=0, tiled=True),
        lax.all_gather(norm_gain, ("dp", "expert"), axis=0, tiled=True),
        lax.all_gather(mix_gain, ("dp", "expert"), axis=0, tiled=True),
        lax.all_gather(ffn_gain, ("dp", "expert"), axis=0, tiled=True),
        lax.all_gather(shared_gate, ("dp", "expert"), axis=0, tiled=True),
        lax.all_gather(shared_up, ("dp", "expert"), axis=0, tiled=True),
        lax.all_gather(shared_down, ("dp", "expert"), axis=0, tiled=True),
    )
    expert_back_set = (
        lax.all_gather(expert_gate, "dp", axis=1, tiled=True),
        lax.all_gather(expert_up, "dp", axis=1, tiled=True),
        lax.all_gather(expert_down, "dp", axis=1, tiled=True),
    )
    grad_out = cotangent.astype(jnp.float32)
    grad_branch = grad_out * live
    branch_low = grad_branch.astype(jnp.bfloat16)
    grad_shared_down = jnp.dot(shared_low.T, branch_low, preferred_element_type=jnp.float32)
    grad_shared_act = jnp.dot(branch_low, mixer_back[9].T, preferred_element_type=jnp.float32)
    grad_sg, grad_su = shared_back(grad_shared_act)
    sg_low = grad_sg.astype(jnp.bfloat16)
    su_low = grad_su.astype(jnp.bfloat16)
    grad_shared_gate = jnp.dot(ffn_low.T, sg_low, preferred_element_type=jnp.float32)
    grad_shared_up = jnp.dot(ffn_low.T, su_low, preferred_element_type=jnp.float32)
    grad_ffn = jnp.dot(sg_low, mixer_back[7].T, preferred_element_type=jnp.float32)
    grad_ffn = grad_ffn + jnp.dot(su_low, mixer_back[8].T, preferred_element_type=jnp.float32)
    per_route = (
        (grad_branch[:, None, :] * route_gates[:, :, None])
        .astype(jnp.bfloat16)
        .reshape(token_count * top_count, width)
    )
    grad_send = jnp.where(filled, per_route[slot_source], zero_low).reshape(
        local_experts, lanes, width
    )
    grad_recv = lax.all_to_all(grad_send, "expert", split_axis=1, concat_axis=1, tiled=True)
    grad_act = jnp.einsum(
        "erd,efd->erf", grad_recv, expert_back_set[2], preferred_element_type=jnp.float32
    )
    gradient_expert_lower = jnp.einsum(
        "erf,erd->fed", act_low, grad_recv, preferred_element_type=jnp.float32
    )
    grad_hg, grad_hu = expert_back(grad_act)
    hg_low = grad_hg.astype(jnp.bfloat16)
    hidden_raise_reduced = grad_hu.astype(jnp.bfloat16)
    gradient_expert_gating = jnp.einsum(
        "bgf,bgc->fbc", incoming_rows, hg_low, preferred_element_type=jnp.float32
    )
    gradient_expert_raise = jnp.einsum(
        "bgf,bgc->fbc", incoming_rows, hidden_raise_reduced, preferred_element_type=jnp.float32
    )
    grad_rows = jnp.einsum(
        "erf,edf->erd", hg_low, expert_back_set[0], preferred_element_type=jnp.float32
    )
    grad_rows = (
        grad_rows
        + jnp.einsum(
            "erf,edf->erd",
            hidden_raise_reduced,
            expert_back_set[1],
            preferred_element_type=jnp.float32,
        )
    ).astype(jnp.bfloat16)
    grad_home = lax.all_to_all(grad_rows, "expert", split_axis=1, concat_axis=1, tiled=True)
    grad_picked = grad_home.reshape(slot_total, width)[slots].reshape(token_count, top_count, width)
    grad_ffn = grad_ffn + jnp.sum(grad_picked.astype(jnp.float32), axis=1)
    grad_resid_norm, grad_gain_ffn = ffn_back(grad_ffn)
    grad_resid = grad_out + grad_resid_norm
    mixer_low = (grad_resid * live).astype(jnp.bfloat16)
    grad_outproj = jnp.dot(mixed_low.T, mixer_low, preferred_element_type=jnp.float32)
    grad_mixed = jnp.dot(mixer_low, mixer_back[1].T, preferred_element_type=jnp.float32)
    grad_proj, grad_convw, grad_convb, grad_stepb, grad_decay, grad_skip, grad_gain_mix = core_back(
        grad_mixed
    )
    proj_low = grad_proj.astype(jnp.bfloat16)
    grad_inproj = jnp.dot(normed_low.T, proj_low, preferred_element_type=jnp.float32)
    grad_normed = jnp.dot(proj_low, mixer_back[0].T, preferred_element_type=jnp.float32)
    grad_from_norm, grad_gain_norm = norm_back(grad_normed)
    grad_input = grad_resid + grad_from_norm
    mixer_terms = (
        grad_inproj,
        grad_outproj,
        grad_convw,
        grad_convb,
        grad_gain_norm,
        grad_gain_mix,
        grad_gain_ffn,
        grad_shared_gate,
        grad_shared_up,
        grad_shared_down,
    )
    flat_terms = tuple((flatten_rows(term, all_devices) for term in mixer_terms))
    mixer_sums = (
        lax.psum_scatter(flat_terms[0], ("dp", "expert"), scatter_dimension=0, tiled=True),
        lax.psum_scatter(flat_terms[1], ("dp", "expert"), scatter_dimension=0, tiled=True),
        lax.psum_scatter(flat_terms[2], ("dp", "expert"), scatter_dimension=0, tiled=True),
        lax.psum_scatter(flat_terms[3], ("dp", "expert"), scatter_dimension=0, tiled=True),
        lax.psum_scatter(flat_terms[4], ("dp", "expert"), scatter_dimension=0, tiled=True),
        lax.psum_scatter(flat_terms[5], ("dp", "expert"), scatter_dimension=0, tiled=True),
        lax.psum_scatter(flat_terms[6], ("dp", "expert"), scatter_dimension=0, tiled=True),
        lax.psum_scatter(flat_terms[7], ("dp", "expert"), scatter_dimension=0, tiled=True),
        lax.psum_scatter(flat_terms[8], ("dp", "expert"), scatter_dimension=0, tiled=True),
        lax.psum_scatter(flat_terms[9], ("dp", "expert"), scatter_dimension=0, tiled=True),
    )
    mixer_grads = tuple(
        (restore_rows(summed, term, all_devices) for summed, term in zip(mixer_sums, mixer_terms))
    )
    expert_partials = (gradient_expert_gating, gradient_expert_raise, gradient_expert_lower)
    expert_flat = tuple((flatten_rows(term, replicas) for term in expert_partials))
    expert_sums = (
        lax.psum_scatter(
            expert_flat[0].astype(jnp.bfloat16), "dp", scatter_dimension=0, tiled=True
        ).astype(jnp.float32),
        lax.psum_scatter(
            expert_flat[1].astype(jnp.bfloat16), "dp", scatter_dimension=0, tiled=True
        ).astype(jnp.float32),
        lax.psum_scatter(
            expert_flat[2].astype(jnp.bfloat16), "dp", scatter_dimension=0, tiled=True
        ).astype(jnp.float32),
    )
    expert_grads = tuple(
        (
            jnp.transpose(restore_rows(summed, term, replicas), (1, 0, 2))
            for summed, term in zip(expert_sums, expert_partials)
        )
    )
    head_grads = lax.psum((grad_decay, grad_stepb, grad_skip), ("dp", "expert"))
    return (
        output,
        grad_input,
        mixer_grads[0],
        mixer_grads[1],
        mixer_grads[2],
        mixer_grads[3],
        mixer_grads[4],
        mixer_grads[5],
        mixer_grads[6],
        mixer_grads[7],
        mixer_grads[8],
        mixer_grads[9],
        expert_grads[0],
        expert_grads[1],
        expert_grads[2],
        head_grads[0],
        head_grads[1],
        head_grads[2],
    )


def solution(mesh):
    placed = (
        P(("dp", "expert"), None),
        P(("dp", "expert"), None),
        P(("dp", "expert"), None),
        P(("dp", "expert"), None),
        P(("dp", "expert"), None),
        P(("dp", "expert"), None),
        P(("dp", "expert"), None),
        P(("dp", "expert"), None),
        P(("dp", "expert")),
        P(("dp", "expert")),
        P(("dp", "expert")),
        P(("dp", "expert")),
        P(("dp", "expert"), None),
        P(("dp", "expert"), None),
        P(("dp", "expert"), None),
        P("expert", "dp", None),
        P("expert", "dp", None),
        P("expert", "dp", None),
        P(),
        P(),
        P(),
    )
    return jax.shard_map(
        local,
        mesh=mesh,
        in_specs=placed,
        out_specs=(
            P(("dp", "expert"), None),
            P(("dp", "expert"), None),
            P(("dp", "expert"), None),
            P(("dp", "expert"), None),
            P(("dp", "expert"), None),
            P(("dp", "expert")),
            P(("dp", "expert")),
            P(("dp", "expert")),
            P(("dp", "expert")),
            P(("dp", "expert"), None),
            P(("dp", "expert"), None),
            P(("dp", "expert"), None),
            P("expert", "dp", None),
            P("expert", "dp", None),
            P("expert", "dp", None),
            P(),
            P(),
            P(),
        ),
        check_vma=False,
    )
```

profile of v0, /device:TPU:13, one launch (start us, length us, event | category | flops | bytes accessed | tf_op | source)
XLA Modules:
  0.0 2561.8 jit_solution(2485319221737369442)
XLA Ops:
  11.7 41.0 %all-reduce.42 = (bf16[1536]{0:T(1024)(128)(2,1)S(1)}, bf16[3328]{0:T(1024)(128)(2,1)S(1)}, bf16[3072]{0:T(1024)(128)(2,1)S(1)}, bf16[1536]{0:T(1024)(128)(2,1)S(1)}) all-reduce(bf16[1536]{0:T(1024)(128)(2,1)S(1)} %dynamic-update-slice.1, bf16[3328]{0:T(1024)(128)(2,1)S(1)} %dynamic-update-slice, ...), channel_id=1, replica_groups=mesh['dp'=2,'expert'=16] {'dp','expert'}, use_global_device_ids=true, to_apply=%add.24 | all-reduce | flops 9472 | bytes 37888
  53.6 34.5 %all-gather = bf16[32,104,4]{1,2,0:T(4,128)(2,1)S(1)} all-gather(bf16[1,104,4]{1,2,0:T(4,128)(2,1)S(1)} %bitcast.148), channel_id=1, replica_groups=mesh['dp'=2,'expert'=16] {'dp','expert'}, dimensions={0}, use_global_device_ids=true | all-gather | bytes 27456 | tf_op jit(solution)/shard_map/all_gather | solution.py:110
  93.9 6.5 mul.730
  113.1 6.2 gather_fusion.2
  119.3 23.3 all-gather.10.cloned.1.call-done
  142.6 12.4 fusion.87
  164.0 8.2 bitcast_add_fusion.2
  173.9 53.3 %all-gather.12.cloned.1.call-done = bf16[3072,1536]{1,0:T(8,128)(2,1)} async-done(((bf16[96,1536]{1,0:T(8,128)(2,1)}), bf16[3072,1536]{1,0:T(8,128)(2,1)}) %all-gather.12.cloned.1.call-update) | async-done | bytes 9437200 | tf_op jit(solution)/shard_map/all_gather | solution.py:109
  227.2 5.8 multiply_reduce_fusion.14
  233.2 6.2 gather_fusion
  239.4 20.5 copy_select_fusion
  265.6 103.3 %all-to-all-done.2 = bf16[4,384,1536]{2,0,1:T(4,128)(2,1)} async-done(((bf16[4,384,1536]{2,0,1:T(4,128)(2,1)}), bf16[4,384,1536]{2,0,1:T(4,128)(2,1)}, u32[]{:S(2)}, u32[]{:S(2)}) %all-to-all-start.2) | async-done | bytes 4718624 | tf_op jit(solution)/shard_map/all_to_all | solution.py:233
  374.8 8.9 copy.242
  383.7 93.5 %all-to-all-done = bf16[4,384,1536]{2,0,1:T(4,128)(2,1)} async-done(((bf16[4,384,1536]{2,0,1:T(4,128)(2,1)}), bf16[4,384,1536]{2,0,1:T(4,128)(2,1)}, u32[]{:S(2)}, u32[]{:S(2)}) %all-to-all-start) | async-done | bytes 4718624 | tf_op jit(solution)/shard_map/all_to_all | solution.py:180
  477.2 8.5 fusion.23
  485.7 8.5 fusion.21
  494.2 11.1 multiply_convert_fusion.1
  505.2 9.9 fusion.138
  515.2 9.5 add_convert_fusion
  524.6 5.8 copy.225
  540.1 107.1 %all-gather.16.cloned.1.call-done = bf16[1536,1024]{1,0:T(8,128)(2,1)} async-done(((bf16[48,1024]{1,0:T(8,128)(2,1)}), bf16[1536,1024]{1,0:T(8,128)(2,1)}) %all-gather.16.cloned.1.call-update) | async-done | bytes 3145744 | tf_op jit(solution)/shard_map/all_gather | solution.py:116
  650.5 57.6 %all-gather.18.cloned.1.call-done = bf16[1024,1536]{1,0:T(8,128)(2,1)} async-done(((bf16[32,1536]{1,0:T(8,128)(2,1)}), bf16[1024,1536]{1,0:T(8,128)(2,1)}) %all-gather.18.cloned.1.call-update) | async-done | bytes 3145744 | tf_op jit(solution)/shard_map/all_gather | solution.py:117
  714.5 7.9 convert_bitcast_fusion
  722.4 8.2 convert_bitcast_fusion.2
  736.0 8.2 gather_fusion.3
  757.2 8.3 fusion.127
  767.4 5.5 fusion.38
  775.0 8.2 bitcast_add_fusion.1
  799.3 7.9 fusion.31
  823.5 6.2 fusion.130
  836.5 11.7 fusion.69
  851.5 9.2 convert_bitcast_fusion.1
  860.7 11.3 copy.238
  872.0 7.9 convert_element_type.187
  879.9 11.2 copy.241
  891.1 7.9 convert_element_type.190
  899.0 11.4 copy.243
  910.3 7.7 convert_element_type.193
  922.7 6.4 reshape.579
  932.8 6.3 reshape.581
  942.9 6.2 reshape.583
  949.1 17.1 fusion.85
  966.3 52.2 %reshape.565 = f32[32,309504]{1,0:T(8,128)} reshape(f32[1536,6448]{1,0:T(8,128)} %fusion.85) | data formatting | bytes 79233024 | tf_op jit(solution)/shard_map/reshape | solution.py:35
  1018.4 8.6 fusion.126
  1027.0 21.5 reshape.567
  1049.9 5.8 convolution_convert_fusion
  1055.8 5.8 copy.219
  1061.6 6.5 all-to-all-start.1
  1068.7 103.3 %all-to-all-done.1 = bf16[4,384,1536]{2,0,1:T(4,128)(2,1)} async-done(((bf16[4,384,1536]{2,0,1:T(4,128)(2,1)}), bf16[4,384,1536]{2,0,1:T(4,128)(2,1)}, u32[]{:S(2)}, u32[]{:S(2)}) %all-to-all-start.1) | async-done | bytes 4718624 | tf_op jit(solution)/shard_map/all_to_all | solution.py:192
  1177.4 8.8 gather_fusion.1
  1191.3 5.5 multiply_reduce_fusion
  1205.7 199.2 %all-reduce.52.cloned.1.call-done = (bf16[2,1572864]{1,0:T(2,128)(2,1)}, bf16[2,1572864]{1,0:T(2,128)(2,1)}, bf16[2,1572864]{1,0:T(2,128)(2,1)}) async-done(((bf16[2,1572864]{1,0:T(2,128)(2,1)}, bf16[2,1572864]{1,0:T(2,128)(2,1)}, bf16[2,1572864]{1,0:T(2,128)(2,1)}), (bf16[2,1572864]{1,0:T(2,128)(2,1)}, bf16[2,1572864]{1,0:T(2,128)(2,1)}, bf16[2,1572864]{1,0:T(2,128)(2,1)})) %all-reduce.52.cloned.1.call-update) | async-done | bytes 18874384
  1404.9 50.1 %fusion.2 = f32[1572864]{0:T(1024)} fusion(bf16[2,1572864]{1,0:T(2,128)(2,1)} %get-tuple-element.163, u32[]{:T(128)} %bitcast.35), kind=kLoop, calls=%fused_computation.12 | loop fusion | flops 1572864 | bytes 9437188 | tf_op jit(solution)/shard_map/transpose | solution.py:320
  1455.0 7.8 reshape.590
  1462.9 8.2 copy.246
  1471.0 50.2 %fusion.1 = f32[1572864]{0:T(1024)} fusion(bf16[2,1572864]{1,0:T(2,128)(2,1)} %get-tuple-element.164, u32[]{:T(128)} %bitcast.35), kind=kLoop, calls=%fused_computation.10 | loop fusion | flops 1572864 | bytes 9437188 | tf_op jit(solution)/shard_map/transpose | solution.py:320
  1521.2 7.7 reshape.591
  1528.9 7.7 copy.247
  1536.6 50.4 %fusion = f32[1572864]{0:T(1024)} fusion(bf16[2,1572864]{1,0:T(2,128)(2,1)} %get-tuple-element.165, u32[]{:T(128)} %bitcast.35), kind=kLoop, calls=%fused_computation.8 | loop fusion | flops 1572864 | bytes 9437188 | tf_op jit(solution)/shard_map/transpose | solution.py:320
  1587.0 7.7 reshape.592
  1594.7 7.9 copy.248
  1602.5 917.4 %all-reduce.50.cloned.1.call-done = (f32[32,309504]{1,0:T(8,128)}, f32[32,147456]{1,0:T(8,128)}, f32[32,49152]{1,0:T(8,128)}, f32[32,49152]{1,0:T(8,128)}, f32[32,49152]{1,0:T(8,128)}) async-done(((f32[32,309504]{1,0:T(8,128)}, f32[32,147456]{1,0:T(8,128)}, f32[32,49152]{1,0:T(8,128)}, f32[32,49152]{1,0:T(8,128)}, f32[32,49152]{1,0:T(8,128)}), (f32[32,309504]{1,0:T(8,128)}, f32[32,147456]{1,0:T(8,128)}, ...) | async-done | bytes 77365264
  2519.9 14.7 dynamic-slice_reduce_fusion
  2536.4 8.0 dynamic-slice_reduce_fusion.1
  (371 shorter events, 175.0 us)
Async XLA Ops:
  7.2 135.4 %all-gather.10.cloned.1.call-start = ((), (), s32[]{:S(2)}) async-start(), calls=%async_computation.4 | async-start | bytes 20680704 | tf_op jit(solution)/shard_map/all_gather | solution.py:108
  7.9 219.3 %all-gather.12.cloned.1.call-start = ((), (), s32[]{:S(2)}) async-start(), calls=%async_computation.5 | async-start | bytes 9732096 | tf_op jit(solution)/shard_map/all_gather | solution.py:109
  8.7 375.0 %all-gather.20.cloned.1.call-start = ((), (), s32[]{:S(2)}) async-start(), calls=%async_computation.9 | async-start | bytes 9437184 | tf_op jit(solution)/shard_map/all_gather | solution.py:120
  9.5 43.2 %copy-start.5 = (bf16[128,1536]{1,0:T(8,128)(2,1)S(1)}, bf16[128,1536]{1,0:T(8,128)(2,1)}, u32[]{:S(2)}) copy-start(bf16[128,1536]{1,0:T(8,128)(2,1)} %param.21) | copy-start | bytes 1179652
  9.5 43.9 %copy-start.86 = (s32[1,3]{1,0:T(1,128)S(1)}, s32[1,3]{1,0:T(1,128)}, u32[]{:S(2)}) copy-start(s32[1,3]{1,0:T(1,128)} %param.25) | copy-start | bytes 40
  9.5 44.2 %copy-start.75 = (bf16[104,4]{0,1:T(4,128)(2,1)S(1)}, bf16[104,4]{0,1:T(4,128)(2,1)}, u32[]{:S(2)}) copy-start(bf16[104,4]{0,1:T(4,128)(2,1)} %param.28) | copy-start | bytes 2500
  9.5 78.9 %copy-start.89 = (f32[48]{0:T(128)S(1)}, f32[48]{0:T(128)}, u32[]{:S(2)}) copy-start(f32[48]{0:T(128)} %param.39) | copy-start | bytes 580
  9.5 80.8 %copy-start.21 = (bf16[128,1536]{1,0:T(8,128)(2,1)S(1)}, bf16[128,1536]{1,0:T(8,128)(2,1)}, u32[]{:S(2)}) copy-start(bf16[128,1536]{1,0:T(8,128)(2,1)} %param.22) | copy-start | bytes 1179652
  9.5 476.1 %all-gather.22.cloned.1.call-start = ((), (), s32[]{:S(2)}) async-start(), calls=%async_computation.10 | async-start | bytes 9437184 | tf_op jit(solution)/shard_map/all_gather | solution.py:121
  52.7 89.9 %copy-start.36 = (f32[1536]{0:T(1024)}, f32[1536]{0:T(1024)S(1)}, u32[]{:S(2)}) copy-start(f32[1536]{0:T(1024)S(1)} %convert_element_type.154) | copy-start | bytes 18436
  52.8 41.0 %copy-start.76 = (f32[128]{0:T(128)}, f32[128]{0:T(128)S(1)}, u32[]{:S(2)}) copy-start(f32[128]{0:T(128)S(1)} %fusion.71) | copy-start | bytes 1540
  88.3 5.6 copy-start.41
  88.4 66.9 %copy-start.43 = (f32[3328]{0:T(1024)}, f32[3328]{0:T(1024)S(1)}, u32[]{:S(2)}) copy-start(f32[3328]{0:T(1024)S(1)} %convert_element_type.152) | copy-start | bytes 39940
  93.9 6.5 copy-start.71
  100.5 12.5 copy-start.39
  103.0 10.1 copy-start.61
  110.3 122.8 %copy-start.45 = (f32[1536]{0:T(1024)}, f32[1536]{0:T(1024)S(1)}, u32[]{:S(2)}) copy-start(f32[1536]{0:T(1024)S(1)} %convert_element_type.161) | copy-start | bytes 18436
  113.1 29.5 %copy-start.57 = (f32[128]{0:T(128)S(1)}, f32[128]{0:T(128)}, u32[]{:S(2)}) copy-start(f32[128]{0:T(128)} %fusion.120) | copy-start | bytes 1540
  155.0 17.2 copy-start
  172.2 55.0 %copy-start.54 = (f32[128]{0:T(128)S(1)}, f32[128]{0:T(128)}, u32[]{:S(2)}) copy-start(f32[128]{0:T(128)} %copy-done.53) | copy-start | bytes 1540
  173.9 59.1 %copy-start.63 = (f32[128]{0:T(128)}, f32[128]{0:T(128)S(1)}, u32[]{:S(2)}) copy-start(f32[128]{0:T(128)S(1)} %add_rsqrt_fusion) | copy-start | bytes 1540
  233.0 6.4 copy-start.78
  233.0 523.5 %copy-start.3 = (f32[128,1536]{1,0:T(8,128)}, f32[128,1536]{1,0:T(8,128)S(1)}, u32[]{:S(2)}) copy-start(f32[128,1536]{1,0:T(8,128)S(1)} %get-tuple-element.210) | copy-start | bytes 2359300
  233.1 6.4 copy-start.68
  259.9 109.0 %all-to-all-start.2 = ((bf16[4,384,1536]{2,0,1:T(4,128)(2,1)}), bf16[4,384,1536]{2,0,1:T(4,128)(2,1)}, u32[]{:S(2)}, u32[]{:S(2)}) async-start(bf16[4,384,1536]{2,0,1:T(4,128)(2,1)} %get-tuple-element.198), calls=%async_computation.2 | async-start | bytes 9437184 | tf_op jit(solution)/shard_map/all_to_all | solution.py:233
  265.0 229.1 %all-gather.24.cloned.1.call-start = ((), (), s32[]{:S(2)}) async-start(), calls=%async_computation.11 | async-start | bytes 9437184 | tf_op jit(solution)/shard_map/all_gather | solution.py:122
  368.9 108.3 %all-to-all-start = ((bf16[4,384,1536]{2,0,1:T(4,128)(2,1)}), bf16[4,384,1536]{2,0,1:T(4,128)(2,1)}, u32[]{:S(2)}, u32[]{:S(2)}) async-start(bf16[4,384,1536]{2,0,1:T(4,128)(2,1)} %get-tuple-element.199), calls=%async_computation | async-start | bytes 9437184 | tf_op jit(solution)/shard_map/all_to_all | solution.py:180
  373.5 163.4 %all-gather.14.cloned.1.call-start = ((), (), s32[]{:S(2)}) async-start(), calls=%async_computation.6 | async-start | bytes 3244032 | tf_op jit(solution)/shard_map/all_gather | solution.py:115
  374.0 273.2 %all-gather.16.cloned.1.call-start = ((), (), s32[]{:S(2)}) async-start(), calls=%async_computation.7 | async-start | bytes 3244032 | tf_op jit(solution)/shard_map/all_gather | solution.py:116
  505.2 9.9 copy-start.31
  530.5 5.8 copy-start.62
  530.5 200.1 %all-to-all-start.3 = ((bf16[4,384,1536]{2,0,1:T(4,128)(2,1)}), bf16[4,384,1536]{2,0,1:T(4,128)(2,1)}, u32[]{:S(2)}, u32[]{:S(2)}) async-start(bf16[4,384,1536]{2,0,1:T(4,128)(2,1)} %copy.225), calls=%async_computation.3 | async-start | bytes 9437184 | tf_op jit(solution)/shard_map/all_to_all | solution.py:261
  535.4 172.6 %all-gather.18.cloned.1.call-start = ((), (), s32[]{:S(2)}) async-start(), calls=%async_computation.8 | async-start | bytes 3244032 | tf_op jit(solution)/shard_map/all_gather | solution.py:117
  536.2 663.2 %all-reduce.48.cloned.1.call-start = ((), (), s32[]{:S(2)}) async-start(), calls=%async_computation.12 | async-start | bytes 265216
  540.1 168.0 %copy-start.22 = (bf16[128,1536]{1,0:T(8,128)(2,1)S(1)}, bf16[128,1536]{1,0:T(8,128)(2,1)}, u32[]{:S(2)}) copy-start(bf16[128,1536]{1,0:T(8,128)(2,1)} %param.22) | copy-start | bytes 1179652
  757.2 8.3 copy-start.16
  757.2 8.3 copy-start.1
  766.7 6.3 copy-start.9
  829.9 6.5 copy-start.6
  829.9 6.5 copy-start.13
  829.9 6.5 copy-start.37
  829.9 6.5 copy-start.58
  836.4 12.4 copy-start.49
  836.4 13.1 copy-start.52
  836.4 13.7 copy-start.91
  836.4 14.3 copy-start.50
  851.4 553.5 %all-reduce.52.cloned.1.call-start = ((), (), s32[]{:S(2)}) async-start(), calls=%async_computation.14 | async-start | bytes 37748736
  918.1 1601.8 %all-reduce.50.cloned.1.call-start = ((), (), s32[]{:S(2)}) async-start(), calls=%async_computation.13 | async-start | bytes 154730496
  922.7 6.4 copy-start.33
  932.8 6.3 copy-start.24
  932.8 6.3 copy-start.28
  932.8 6.3 copy-start.56
  966.2 52.2 %copy-start.2 = (f32[128,3072]{0,1:T(8,128)S(1)}, f32[128,3072]{0,1:T(8,128)}, u32[]{:S(2)}) copy-start(f32[128,3072]{0,1:T(8,128)} %get-tuple-element.182) | copy-start | bytes 4718596
  966.3 52.2 %copy-start.17 = (f32[128,1536]{1,0:T(8,128)S(1)}, f32[128,1536]{1,0:T(8,128)}, u32[]{:S(2)}) copy-start(f32[128,1536]{1,0:T(8,128)} %copy-done.16) | copy-start | bytes 2359300
  966.3 52.2 %copy-start.64 = (f32[128]{0:T(128)S(1)}, f32[128]{0:T(128)}, u32[]{:S(2)}) copy-start(f32[128]{0:T(128)} %copy-done.63) | copy-start | bytes 1540
  1061.6 6.5 copy-start.95
  1061.6 110.3 %all-to-all-start.1 = ((bf16[4,384,1536]{2,0,1:T(4,128)(2,1)}), bf16[4,384,1536]{2,0,1:T(4,128)(2,1)}, u32[]{:S(2)}, u32[]{:S(2)}) async-start(bf16[4,384,1536]{2,0,1:T(4,128)(2,1)} %copy.219), calls=%async_computation.1 | async-start | bytes 9437184 | tf_op jit(solution)/shard_map/all_to_all | solution.py:192
  1068.7 108.8 %copy-start.51 = (s32[1024]{0:T(1024)S(1)}, s32[1024]{0:T(1024)}, u32[]{:S(2)}) copy-start(s32[1024]{0:T(1024)} %pad_clamp_fusion.2) | copy-start | bytes 12292
  1191.3 5.5 copy-start.4
  1191.3 5.5 copy-start.26
  1191.3 5.5 copy-start.29
  2544.4 8.9 copy-start.94
  2544.4 9.4 copy-start.93
  2544.4 9.9 copy-start.92
  (49 other events, 132.6 us)
Sparse Core Ops, SparseCore 0:
  10.9 131.6 all-gather.9
  145.5 81.6 all-gather.11
  228.8 78.5 all-gather.19
  308.8 80.3 all-gather.21
  390.6 80.3 all-gather.23
  473.7 58.4 all-gather.13
  535.2 111.9 all-gather.15
  650.1 57.9 all-gather.17
  851.6 122.1 all-reduce.47
  976.9 427.9 all-reduce.51
  1412.5 1107.3 all-reduce.49
where the time goes:
time: 2580 us; the launch traced here: 2560 us
  waiting for transfers between devices  1660 us (64%)
  local copies, waits for them, and re-layouts  349 us (14%)
  other arithmetic  236 us (9%)
  matrix products  201 us (8%)
  blocking collectives  75.5 us (3%)
    unnamed x14, waiting for transfers between devices  1120 us
    transpose x3, other arithmetic, local(): jnp.transpose(restore_rows(summed, term, replicas), (1, 0, 2))  151 us
    all_gather x1, waiting for transfers between devices, local(): lax.all_gather(shared_up, ('dp', 'expert'), axis=0, tiled=True)  107 us
    all_to_all x1, waiting for transfers between devices, local(): lax.all_to_all(grad_send, 'expert', split_axis=1, concat_axis=1, tiled=True)  103 us
    all_to_all x1, waiting for transfers between devices, local(): lax.all_to_all(produced_rows, 'expert', split_axis=1, concat_axis=1, tile...  103 us
    reshape x10, local copies, waits for them, and re-layouts, flatten_rows(): return value.reshape(pieces, -1)  97.8 us
    all_to_all x1, waiting for transfers between devices, local(): lax.all_to_all(send_rows, 'expert', split_axis=1, concat_axis=1, tiled=True)  93.5 us
    unnamed x220, local copies, waits for them, and re-layouts  63.8 us
  transfers between devices with their start and end apart: 15, of which 9 were waited for; matrix products, arithmetic and copies ran while one was open for 25% of the time, Pallas kernels for 0%

commit v1 on v0

v1 whole, which is shorter than its diff:
```python
import jax
import jax.numpy as jnp
from jax import lax
from jax.sharding import Mesh, PartitionSpec as P

HEADS = 48
HEAD_DIM = 64
STATE = 128
KERNEL = 4
SEQ_SLOTS = 3
INNER = 3072
CONV_CH = 3328
EXTRA = 128

epsilon = 1e-05
bf16 = jnp.bfloat16
f32 = jnp.float32
GROUP = ("z", "y", "core")
ALL = ("dp", "z", "y", "core")


def matmul(left, right, dims=None, precision=None):
    if dims is None:
        dims = (((left.ndim - 1,), (0,)), ((), ()))
    return lax.dot_general(left, right, dims, precision=precision, preferred_element_type=f32)


def swap(value, axis):
    return lax.ppermute(value, axis, [(0, 1), (1, 0)])


def ring(value):
    size = lax.axis_size("z")
    return lax.ppermute(value, "z", [(k, (k + 1) % size) for k in range(size)])


def split_three(value):
    high = lax.reduce_precision(value, 8, 7)
    rest = value - high
    middle = lax.reduce_precision(rest, 8, 7)
    return high.astype(bf16), middle.astype(bf16), (rest - middle).astype(bf16)


def join_three(parts):
    return parts[0].astype(f32) + parts[1].astype(f32) + parts[2].astype(f32)


def group_gather(block):
    size = lax.axis_size("z")
    current = block
    out = []
    for step in range(size):
        if step < size - 1:
            following, beside = lax.optimization_barrier((ring(current), swap(current, "y")))
        else:
            following, beside = None, swap(current, "y")
        out += [current, beside, swap(current, "core"), swap(beside, "core")]
        current = following
    return jnp.concatenate(out, axis=0)


def add_low(left, right):
    return (left.astype(f32) + right.astype(f32)).astype(bf16)


def group_scatter(parts):
    size = lax.axis_size("z")
    parts = parts.reshape((size, 2, 2, parts.shape[0] // (4 * size)) + parts.shape[1:])
    summed = {}
    for step in list(range(1, size)) + [0]:
        pair = add_low(parts[step, 0], swap(parts[step, 1], "core"))
        summed[step] = (pair[0], swap(pair[1], "y"))
    total = add_low(*summed[1])
    for step in range(2, size):
        total = add_low(ring(total), add_low(*summed[step]))
    own = summed[0]
    return ring(total).astype(f32) + own[0].astype(f32) + own[1].astype(f32)


def dp_gather_rows(value, axis):
    if lax.axis_size("dp") != 2:
        return lax.all_gather(value, "dp", axis=axis, tiled=True)
    other = swap(value, "dp")
    first = lax.axis_index("dp") == 0
    return jnp.concatenate(
        [jnp.where(first, value, other), jnp.where(first, other, value)], axis=axis
    )


def dp_scatter_rows(value, axis):
    count = lax.axis_size("dp")
    if count != 2:
        return lax.psum_scatter(value.astype(bf16), "dp", scatter_dimension=axis, tiled=True).astype(f32)
    place = lax.axis_index("dp")
    extent = value.shape[axis] // count
    sent = lax.dynamic_slice_in_dim(value, (1 - place) * extent, extent, axis).astype(bf16)
    kept = lax.dynamic_slice_in_dim(value, place * extent, extent, axis)
    return kept + swap(sent, "dp").astype(f32)


def mixer_core(proj, segment, conv_w, conv_b, step_bias, decay_log, skip_gain):
    blocks, count = segment.shape
    heads = step_bias.shape[0]
    own = heads * HEAD_DIM
    gate_z = proj[:, :own]
    conv_in = proj[:, own : 2 * own + 2 * STATE].reshape(blocks, count, own + 2 * STATE)
    step_raw = proj[:, 2 * own + 2 * STATE : 2 * own + 2 * STATE + heads]
    total = conv_b + conv_w[KERNEL - 1] * conv_in
    for offset in range(1, KERNEL):
        shifted = jnp.pad(conv_in[:, : count - offset], ((0, 0), (offset, 0), (0, 0)))
        earlier = jnp.pad(segment[:, : count - offset], ((0, 0), (offset, 0)), constant_values=-1)
        same = (earlier == segment).astype(f32)[:, :, None]
        total = total + conv_w[KERNEL - 1 - offset] * (shifted * same)
    conv_out = jax.nn.silu(total)
    values = conv_out[:, :, :own].reshape(blocks, count, heads, HEAD_DIM).transpose(0, 2, 1, 3)
    state_in = conv_out[:, :, own : own + STATE]
    state_out = conv_out[:, :, own + STATE :]
    step = jax.nn.softplus(step_raw + step_bias).reshape(blocks, count, heads).transpose(0, 2, 1)
    rate = -jnp.exp(decay_log)
    cumul = jnp.cumsum(step * rate[None, :, None], axis=2)
    position = jnp.arange(count, dtype=jnp.int32)
    causal = (position[:, None] >= position[None, :]) & (segment[:, :, None] == segment[:, None, :])
    spread = cumul[:, :, :, None] - cumul[:, :, None, :]
    decay = jnp.exp(jnp.where(causal[:, None], spread, -jnp.inf))
    high = lax.Precision.HIGHEST
    scores = jnp.einsum("bin,bjn->bij", state_out, state_in, precision=high)
    mixing = decay * scores[:, None] * step[:, :, None, :]
    scan = jnp.einsum("bhij,bhjp->bhip", mixing, values, precision=high)
    scan = scan + skip_gain[None, :, None, None] * values
    scan = scan.transpose(0, 2, 1, 3).reshape(blocks * count, own)
    return scan * jax.nn.silu(gate_z)


def local(
    hidden_in,
    cotangent,
    routes,
    route_gates,
    lengths,
    in_proj,
    out_proj,
    conv_weight,
    conv_bias,
    norm_gain,
    mix_gain,
    ffn_gain,
    shared_gate,
    shared_up,
    shared_down,
    expert_gate,
    expert_up,
    expert_down,
    decay_log,
    step_bias,
    skip_gain,
):
    tokens, width = hidden_in.shape
    top = routes.shape[1]
    replicas = lax.axis_size("dp")
    groups = lax.axis_size("z") * 4
    devices = replicas * groups
    core = lax.axis_index("core")
    column = lax.axis_index("z") * 2 + lax.axis_index("y")
    place = column * 2 + core
    heads = HEADS // groups
    own = heads * HEAD_DIM
    half = groups // 2
    rows_in = in_proj.shape[0]
    hidden_units = shared_gate.shape[1]
    unit = hidden_units // devices
    units = hidden_units // groups
    local_experts = expert_gate.shape[0]
    capacity = 2 * tokens * top // (local_experts * groups)
    first_head = core * (HEADS // 2) + column * heads
    first_channel = first_head * HEAD_DIM

    small = (conv_weight.reshape(-1), conv_bias, norm_gain, mix_gain, ffn_gain)
    small_sizes = [entry.shape[0] for entry in small]
    small_lanes = -(-sum(small_sizes) // rows_in)
    small_flat = jnp.concatenate(small)
    small_flat = jnp.pad(small_flat, (0, small_lanes * rows_in - small_flat.shape[0]))

    def by_place(block):
        block = block.reshape(rows_in, 2, half, own).transpose(2, 1, 0, 3)
        return block.reshape(groups, rows_in, own)

    def by_unit(block):
        block = block.reshape(rows_in, replicas, groups, unit).transpose(2, 0, 1, 3)
        return block.reshape(groups, rows_in, units)

    def to_all(block):
        return jnp.broadcast_to(block[None], (groups,) + block.shape)

    step_columns = in_proj[:, INNER + CONV_CH :].reshape(rows_in, 2, half, heads).transpose(2, 1, 0, 3)
    step_columns = step_columns.reshape(groups, rows_in, heads)
    spare = EXTRA - heads - small_lanes
    pack = jnp.concatenate(
        [
            by_place(in_proj[:, :INNER]),
            by_place(in_proj[:, INNER : 2 * INNER]),
            to_all(in_proj[:, 2 * INNER : INNER + CONV_CH]),
            step_columns,
            to_all(small_flat.reshape(rows_in, small_lanes)),
            jnp.zeros((groups, rows_in, spare), bf16),
            by_unit(shared_gate),
            by_unit(shared_up),
        ],
        axis=2,
    )
    proj_lanes = 2 * own + 2 * STATE + EXTRA
    pack = lax.all_to_all(pack, GROUP, split_axis=0, concat_axis=0, tiled=True)
    pack = dp_gather_rows(pack.reshape(1, groups * rows_in, pack.shape[2]), 0)
    pack = pack.reshape(devices * rows_in, pack.shape[2])
    small_at = 2 * own + 2 * STATE + heads
    small_all = pack[:, small_at : small_at + small_lanes].reshape(devices, rows_in * small_lanes)
    pieces = []
    start = 0
    for size in small_sizes:
        pieces.append(small_all[:, start : start + size].reshape(-1).astype(f32))
        start += size
    conv_w_all = pieces[0].reshape(CONV_CH, KERNEL).T
    conv_b_all, norm_gain_all, mix_gain_all, ffn_gain_all = pieces[1:]
    lane = jnp.arange(proj_lanes)
    w_in = jnp.where(lane < small_at, pack[:, :proj_lanes], jnp.zeros((), bf16))
    w_shared = pack[:, proj_lanes:]

    def own_channels(rows):
        return lax.dynamic_slice_in_dim(rows, first_channel, own, rows.ndim - 1)

    conv_w = jnp.concatenate([own_channels(conv_w_all), conv_w_all[:, INNER:]], axis=1)
    conv_b = jnp.concatenate([own_channels(conv_b_all), conv_b_all[INNER:]])
    own_mix_gain = own_channels(mix_gain_all)

    def own_heads(row):
        return lax.dynamic_slice_in_dim(row, first_head, heads, 0)

    if replicas == 2:
        both = swap(out_proj, "core")
        both = jnp.concatenate(
            [jnp.where(core == 0, out_proj, both), jnp.where(core == 0, both, out_proj)]
        )
        w_out = jnp.where(lax.axis_index("dp") == core, both, swap(both, "dp"))
    else:
        w_out = lax.dynamic_slice_in_dim(
            lax.all_gather(out_proj, ALL, axis=0, tiled=True), first_channel, own, 0
        )
    w_shared_down = dp_gather_rows(shared_down[None], 0).reshape(units, width)

    bounds = jnp.cumsum(lengths[0])
    slot = jnp.arange(tokens, dtype=jnp.int32)
    run = jnp.sum((slot[:, None] >= bounds[None, : SEQ_SLOTS - 1]).astype(jnp.int32), axis=1)
    live = (run < SEQ_SLOTS - 1).astype(f32)[:, None]
    beside = [run.astype(bf16)[:, None], routes.astype(bf16), *split_three(route_gates)]
    beside = jnp.concatenate(beside, axis=1)
    beside = jnp.pad(beside, ((0, 0), (0, EXTRA - beside.shape[1])))
    gathered = group_gather(jnp.concatenate([hidden_in, beside], axis=1))
    hidden_all = gathered[:, :width]
    segment = gathered[:, width].astype(jnp.int32).reshape(groups, tokens)
    at = width + 1
    routes_all = gathered[:, at : at + top].astype(jnp.int32)
    gates_all = join_three([gathered[:, at + k * top : at + (k + 1) * top] for k in (1, 2, 3)])

    w_gate = dp_gather_rows(expert_gate, 1)
    w_up = dp_gather_rows(expert_up, 1)
    w_down = dp_gather_rows(expert_down, 1)

    rows = hidden_all.astype(f32)
    normed = rows * lax.rsqrt(jnp.mean(rows * rows, axis=1, keepdims=True) + epsilon) * norm_gain_all
    normed = normed.astype(bf16)
    proj = matmul(normed, w_in)
    gated, core_back = jax.vjp(
        lambda *args: mixer_core(args[0], segment, *args[1:]),
        proj,
        conv_w,
        conv_b,
        own_heads(step_bias),
        own_heads(decay_log),
        own_heads(skip_gain),
    )
    scaled = (gated * own_mix_gain).astype(bf16)
    squares = (gated * gated).astype(bf16)
    fold = (jnp.arange(own)[:, None] % EXTRA == jnp.arange(EXTRA)[None, :]).astype(bf16)
    w_out_fold = jnp.concatenate(
        [jnp.pad(w_out, ((0, 0), (0, EXTRA))), jnp.pad(fold, ((0, 0), (width, 0)))], axis=0
    )
    mixed_part = matmul(jnp.concatenate([scaled, squares], axis=1), w_out_fold).astype(bf16)
    mixed_sum = group_scatter(mixed_part)
    mix_rms = lax.rsqrt(jnp.sum(mixed_sum[:, width:], axis=1, keepdims=True) / INNER + epsilon)
    mixer_out = mixed_sum[:, :width] * mix_rms
    input_rows = hidden_in.astype(f32)
    resid = input_rows + live * mixer_out
    ffn_rms = lax.rsqrt(jnp.mean(resid * resid, axis=1, keepdims=True) + epsilon)
    ffn_hat = resid * ffn_rms
    ffn_all = group_gather((ffn_hat * ffn_gain_all).astype(bf16))
    grad_out = cotangent.astype(f32)
    branch = (grad_out * live).astype(bf16)
    branch_all = group_gather(branch)

    shared_gu = matmul(ffn_all, w_shared)

    def swiglu(both):
        extent = both.shape[-1] // 2
        return jax.nn.silu(both[..., :extent]) * both[..., extent:]

    shared_act, shared_back = jax.vjp(swiglu, shared_gu)
    shared_low = shared_act.astype(bf16)
    grad_shared_down = matmul(shared_low, branch_all, (((0,), (0,)), ((), ())))
    (grad_shared_gu,) = shared_back(matmul(branch_all, w_shared_down, (((1,), (1,)), ((), ()))))
    shared_gu_low = grad_shared_gu.astype(bf16)
    grad_shared_w = matmul(ffn_all, shared_gu_low, (((0,), (0,)), ((), ())))

    pairs = groups // 2
    pair_tokens = 2 * tokens
    pair_slots = 2 * capacity
    lanes = pairs * pair_slots
    numbers = place * local_experts + jnp.arange(local_experts, dtype=jnp.int32)
    named = routes_all[:, None, :] == numbers[None, :, None]
    member = jnp.any(named, axis=2).T.reshape(local_experts, pairs, pair_tokens)
    weight = jnp.sum(jnp.where(named, gates_all[:, None, :], 0.0), axis=2).T
    weight = weight.reshape(local_experts, pairs, pair_tokens)
    below = jnp.triu(jnp.ones((pair_tokens, pair_tokens), bf16))
    rank = matmul(member.astype(bf16), below)
    rank = jnp.where(member, rank.astype(jnp.int32) - 1, -1)
    chosen = rank[:, :, None, :] == jnp.arange(pair_slots, dtype=jnp.int32)[None, None, :, None]
    slot_weight = jnp.sum(jnp.where(chosen, weight[:, :, None, :], 0.0), axis=3)
    slot_weight = slot_weight.reshape(local_experts, lanes, 1)
    select = chosen.astype(bf16)

    def dispatch(values):
        values = values.reshape(pairs, pair_tokens, width)
        return jnp.einsum("ebrt,btd->ebrd", select, values, preferred_element_type=f32).reshape(
            local_experts, lanes, width
        )

    def combine(values):
        values = values.reshape(local_experts, pairs, pair_slots, width)
        return jnp.einsum("ebrt,ebrd->btd", select, values, preferred_element_type=f32).reshape(
            groups * tokens, width
        )

    batch = ((0,), (0,))
    expert_in = dispatch(ffn_all).astype(bf16)
    d_row = (dispatch(branch_all) * slot_weight).astype(bf16)
    hidden_g = matmul(expert_in, w_gate, (((2,), (1,)), batch))
    hidden_u = matmul(expert_in, w_up, (((2,), (1,)), batch))
    expert_act, expert_back = jax.vjp(lambda g, u: jax.nn.silu(g) * u, hidden_g, hidden_u)
    act_low = expert_act.astype(bf16)
    grad_g, grad_u = expert_back(matmul(d_row, w_down, (((2,), (2,)), batch)))
    g_low = grad_g.astype(bf16)
    u_low = grad_u.astype(bf16)
    d_in_row = matmul(g_low, w_gate, (((2,), (2,)), batch)) + matmul(
        u_low, w_up, (((2,), (2,)), batch)
    )
    grad_ffn_part = combine(d_in_row.astype(bf16)) + matmul(
        shared_gu_low, w_shared, (((1,), (1,)), ((), ()))
    )
    grad_ffn = group_scatter(grad_ffn_part.astype(bf16))
    grad_gate = matmul(expert_in, g_low, (((1,), (1,)), batch))
    grad_up = matmul(expert_in, u_low, (((1,), (1,)), batch))
    grad_down = matmul(act_low, d_row, (((1,), (1,)), batch))
    expert_row = (matmul(act_low, w_down, (((2,), (1,)), batch)) * slot_weight).astype(bf16)
    branch_part = combine(expert_row) + matmul(shared_low, w_shared_down)
    branch_sum = group_scatter(branch_part.astype(bf16))
    output = (resid + live * branch_sum).astype(bf16)
    grad_gate = dp_scatter_rows(grad_gate, 1)
    grad_up = dp_scatter_rows(grad_up, 1)
    grad_down = dp_scatter_rows(grad_down, 1)

    grad_ffn_gain = jnp.sum(grad_ffn * ffn_hat, axis=0)
    scaled_ffn = grad_ffn * ffn_gain_all
    grad_resid = grad_out + ffn_rms * (
        scaled_ffn - ffn_hat * jnp.mean(scaled_ffn * ffn_hat, axis=1, keepdims=True)
    )
    d_mixer = (grad_resid * live).astype(bf16).astype(f32)
    inner_term = jnp.sum(d_mixer * mixer_out, axis=1, keepdims=True) * mix_rms * mix_rms / INNER
    inner_pack = jnp.pad(jnp.concatenate(split_three(inner_term), axis=1), ((0, 0), (0, EXTRA - 3)))
    d_mixer_all = group_gather(jnp.concatenate([(d_mixer * mix_rms).astype(bf16), inner_pack], axis=1))
    inner_all = join_three([d_mixer_all[:, width + k : width + k + 1] for k in range(3)])
    d_mixer_all = d_mixer_all[:, :width]
    grad_mixed = matmul(d_mixer_all, w_out, (((1,), (1,)), ((), ())))
    grad_out_rows = matmul(scaled, d_mixer_all, (((0,), (0,)), ((), ())))
    grad_proj, grad_conv_w, grad_conv_b, grad_stepb, grad_decay, grad_skip = core_back(
        grad_mixed * own_mix_gain - gated * inner_all
    )
    proj_low = grad_proj.astype(bf16)
    grad_normed_part = matmul(proj_low, w_in, (((1,), (1,)), ((), ())))
    grad_normed = group_scatter(grad_normed_part.astype(bf16))
    grad_w_in = matmul(normed, proj_low, (((0,), (0,)), ((), ())))

    grad_pack = jnp.concatenate([grad_w_in, grad_shared_w], axis=1)
    grad_pack = dp_scatter_rows(grad_pack, 0).astype(bf16).reshape(groups, rows_in, -1)
    grad_pack = lax.all_to_all(grad_pack, GROUP, split_axis=0, concat_axis=0, tiled=True).astype(f32)

    def from_place(block):
        block = block.reshape(half, 2, rows_in, block.shape[2]).transpose(2, 1, 0, 3)
        return block.reshape(rows_in, -1)

    def from_unit(block):
        block = block.reshape(groups, rows_in, replicas, unit).transpose(1, 2, 0, 3)
        return block.reshape(rows_in, hidden_units)

    both_at = 2 * own + 2 * STATE
    grad_in_proj = jnp.concatenate(
        [
            from_place(grad_pack[:, :, :own]),
            from_place(grad_pack[:, :, own : 2 * own]),
            jnp.sum(grad_pack[:, :, 2 * own : both_at], axis=0),
            from_place(grad_pack[:, :, both_at : both_at + heads]),
        ],
        axis=1,
    )
    grad_shared_gate = from_unit(grad_pack[:, :, proj_lanes : proj_lanes + units])
    grad_shared_up = from_unit(grad_pack[:, :, proj_lanes + units :])
    grad_shared_down = dp_scatter_rows(grad_shared_down.reshape(replicas, unit, width), 0)[0]
    if replicas == 2:
        mine = lax.axis_index("dp") == core
        received = swap(grad_out_rows.astype(bf16), "dp").astype(f32)
        total = (grad_out_rows + received).reshape(2, own // 2, width)
        passed = swap(lax.dynamic_index_in_dim(total, 1 - core, 0, keepdims=False), "core")
        grad_out_proj = jnp.where(mine, lax.dynamic_index_in_dim(total, core, 0, keepdims=False), passed)
    else:
        full = jnp.zeros((INNER, width), f32)
        full = lax.dynamic_update_slice_in_dim(full, grad_out_rows, first_channel, 0)
        grad_out_proj = lax.psum_scatter(full, ALL, scatter_dimension=0, tiled=True)
    grad_mix_gain = jnp.sum(grad_out_proj * out_proj.astype(f32), axis=1) / mix_gain.astype(f32)
    grad_norm_gain = jnp.sum(grad_in_proj * in_proj.astype(f32), axis=1) / norm_gain.astype(f32)

    def to_owner(part):
        rows_part = jnp.zeros((part.shape[0], CONV_CH), f32)
        rows_part = lax.dynamic_update_slice_in_dim(rows_part, part[:, :own], first_channel, 1)
        rows_part = lax.dynamic_update_slice_in_dim(rows_part, part[:, own:], INNER, 1)
        return rows_part.reshape(part.shape[0], devices, -1).transpose(1, 0, 2).reshape(devices, -1)

    def head_row(part):
        return lax.dynamic_update_slice_in_dim(jnp.zeros((HEADS,), f32), part, first_head, 0)

    head_rows = jnp.concatenate([head_row(grad_decay), head_row(grad_stepb), head_row(grad_skip)])
    sums = jnp.concatenate(
        [
            to_owner(grad_conv_w),
            to_owner(grad_conv_b[None]),
            grad_ffn_gain.reshape(devices, -1),
            jnp.broadcast_to(head_rows[None], (devices, 3 * HEADS)),
        ],
        axis=1,
    )
    sums = lax.all_to_all(sums, ALL, split_axis=0, concat_axis=0, tiled=True)
    sums = jnp.sum(sums, axis=0)
    channels = CONV_CH // devices
    grad_conv_weight = sums[: KERNEL * channels].reshape(KERNEL, channels).T
    grad_conv_bias = sums[KERNEL * channels : (KERNEL + 1) * channels]
    at = (KERNEL + 1) * channels
    grad_ffn_gain = sums[at : at + rows_in]
    at += rows_in
    grad_decay, grad_stepb, grad_skip = (sums[at + k * HEADS : at + (k + 1) * HEADS] for k in range(3))

    in_rms = lax.rsqrt(jnp.mean(input_rows * input_rows, axis=1, keepdims=True) + epsilon)
    in_hat = input_rows * in_rms
    scaled_in = grad_normed * norm_gain_all
    grad_input = grad_resid + in_rms * (
        scaled_in - in_hat * jnp.mean(scaled_in * in_hat, axis=1, keepdims=True)
    )
    return (
        output,
        grad_input,
        grad_in_proj,
        grad_out_proj,
        grad_conv_weight,
        grad_conv_bias,
        grad_norm_gain,
        grad_mix_gain,
        grad_ffn_gain,
        grad_shared_gate,
        grad_shared_up,
        grad_shared_down,
        grad_gate,
        grad_up,
        grad_down,
        grad_decay,
        grad_stepb,
        grad_skip,
    )


def solution(mesh):
    replicas, groups = mesh.shape["dp"], mesh.shape["expert"]
    inner = Mesh(mesh.devices.reshape(replicas, groups // 4, 2, 2), ALL)
    flat = P(ALL)
    expert = P(GROUP, "dp", None)
    return jax.shard_map(
        local,
        mesh=inner,
        in_specs=(flat,) * 15 + (expert,) * 3 + (P(),) * 3,
        out_specs=(flat,) * 12 + (expert,) * 3 + (P(),) * 3,
        check_vma=False,
    )
```

time: 2580 us -> 988 us (0.38)
  waiting for transfers between devices: 1660 us -> 442 us
  local copies, waits for them, and re-layouts: 349 us -> 112 us
  other arithmetic: 236 us -> 132 us
  starting transfers between devices: 21.5 us -> 112 us
  blocking collectives: 75.5 us -> 0 us
    unnamed x14 -> x0, waiting for transfers between devices: 1120 us -> none
    ppermute x0 -> x118, waiting for transfers between devices: none -> 441 us  [the longest x94 310 us: swap(): return lax.ppermute(value, axis, [(0, 1), (1, 0)])]
    all_to_all x4 -> x3, waiting for transfers between devices: 300 us -> 0.61 us  [the longest x1 0.61 us: local(): sums = lax.all_to_all(sums, ALL, split_axis=0, concat_axis=0, tiled=True)]
    all_gather x8 -> x0, waiting for transfers between devices: 241 us -> none  [the longest x1 107 us: local(): lax.all_gather(shared_up, ('dp', 'expert'), axis=0, tiled=True)]
    transpose x3 -> x0, other arithmetic: 151 us -> none  [local(): jnp.transpose(restore_rows(summed, term, replicas), (1, 0, 2))]
    ppermute x0 -> x118, starting transfers between devices: none -> 91.8 us  [the longest x94 75.9 us: swap(): return lax.ppermute(value, axis, [(0, 1), (1, 0)])]
    reshape x21 -> x24, local copies, waits for them, and re-layouts: 108 us -> 21.2 us  [the longest x2 10.6 us: mixer_core(): proj[:, own:2 * own + 2 * STATE].reshape(blocks, count, own + 2 * STATE)]
    convert_element_type x11, local copies, waits for them, and re-layouts: 77.7 us -> 21.6 us  [the longest x4 15.3 us: dp_scatter_rows(): lax.dynamic_slice_in_dim(value, (1 - place) * extent, extent, axis)]
  transfers between devices with their start and end apart: 15 -> 121, of which waited for: 9 -> 46; matrix products, arithmetic and copies ran while one was open for 25% -> 27% of each run, Pallas kernels for 0% -> 0%
where the time goes in v1:
time: 988 us; the launch traced here: 978 us
  waiting for transfers between devices  442 us (45%)
  matrix products  177 us (18%)
  other arithmetic  132 us (13%)
  local copies, waits for them, and re-layouts  112 us (11%)
  starting transfers between devices  112 us (11%)
    ppermute x94, waiting for transfers between devices, swap(): return lax.ppermute(value, axis, [(0, 1), (1, 0)])  310 us
    ppermute x24, waiting for transfers between devices, ring(): return lax.ppermute(value, 'z', [(k, (k + 1) % size) for k in range(size)])  131 us
    dot_general x22, matrix products, matmul(): lax.dot_general(left, right, dims, precision=precision, preferred_element...  121 us
    ppermute x94, starting transfers between devices, swap(): return lax.ppermute(value, axis, [(0, 1), (1, 0)])  75.9 us
    unnamed x292, local copies, waits for them, and re-layouts  29.2 us
    dot_general x3, matrix products, mixer_core(): scan = jnp.einsum('bhij,bhjp->bhip', mixing, values, precision=high)  22.4 us
    add x3, other arithmetic, dp_scatter_rows(): return kept + swap(sent, 'dp').astype(f32)  21.4 us
  transfers between devices with their start and end apart: 121, of which 46 were waited for; matrix products, arithmetic and copies ran while one was open for 27% of the time, Pallas kernels for 0%

profile of v1, /device:TPU:13, one launch (start us, length us, event | category | flops | bytes accessed | tf_op | source)
XLA Modules:
  0.0 978.5 jit_solution(12876290297532065036)
XLA Ops:
  20.1 5.0 all-to-all-start
  37.6 7.3 collective-permute-done.1
  47.6 16.5 %collective-permute-done = bf16[128,1664]{0,1:T(8,128)(2,1)S(1)} collective-permute-done((bf16[128,1664]{0,1:T(8,128)(2,1)S(1)}, bf16[128,1664]{0,1:T(8,128)(2,1)S(1)}, u32[]{:S(2)}, u32[]{:S(2)}) %collective-permute-start) | collective-permute-done | bytes 426016 | tf_op jit(solution)/shard_map/ppermute | solution.py:34
  68.5 5.6 collective-permute-done.63
  81.7 7.4 collective-permute-done.5
  92.9 23.0 %collective-permute-done.17 = bf16[192,1536]{1,0:T(8,128)(2,1)S(1)} collective-permute-done((bf16[192,1536]{1,0:T(8,128)(2,1)S(1)}, bf16[192,1536]{1,0:T(8,128)(2,1)S(1)}, u32[]{:S(2)}, u32[]{:S(2)}) %collective-permute-start.17) | collective-permute-done | bytes 589856 | tf_op jit(solution)/shard_map/ppermute | solution.py:29
  119.2 6.5 collective-permute-done.67
  143.3 7.4 collective-permute-done.71
  154.1 6.8 collective-permute-done.12
  179.9 6.4 fusion.5
  186.3 41.2 %collective-permute-done.15 = bf16[1,768,896]{2,1,0:T(8,128)(2,1)S(1)} collective-permute-done((bf16[1,768,896]{2,1,0:T(8,128)(2,1)S(1)}, bf16[1,768,896]{2,1,0:T(8,128)(2,1)S(1)}, u32[]{:S(2)}, u32[]{:S(2)}) %collective-permute-start.15) | collective-permute-done | bytes 1376288 | tf_op jit(solution)/shard_map/ppermute | solution.py:29
  233.0 8.0 fusion.48
  245.7 5.1 copy.398
  251.1 11.8 %fusion.19 = (f32[16,128,448]{2,1,0:T(8,128)}, f32[16,128,448]{2,1,0:T(8,128)}) fusion(f32[16,128]{1,0:T(8,128)S(1)} %get-tuple-element.174, f32[16,125,448]{2,1,0:T(8,128)} %bitcast.458, f32[448]{0:T(512)S(1)} %bitcast.541, f32[16,128]{1,0:T(8,128)S(1)} %get-tuple-element.173, f32[16,126,448]{2,1,0:T(8,128)} %bitcast.459, f32[448]{0:T(512)S(1)} %bitcast.543, ...), kind=kLoop, calls=%fused_computation.55 | loop fusion | flops 13762560 | bytes 21881600 | tf_op jit(solution)/shard_map/jvp(jit(silu))/mul | solution.py:114
  273.6 8.8 bitcast_add_fusion.3
  310.9 9.7 collective-permute-done.19
  321.3 8.4 collective-permute-done.22
  332.0 6.8 collective-permute-done.25
  341.2 6.0 broadcast_select_fusion.5
  352.8 23.0 %collective-permute-done.45 = bf16[4,768,512]{2,1,0:T(8,128)(2,1)} collective-permute-done((bf16[4,768,512]{2,1,0:T(8,128)(2,1)}, bf16[4,768,512]{2,1,0:T(8,128)(2,1)}, u32[]{:S(2)}, u32[]{:S(2)}) %collective-permute-start.45) | collective-permute-done | bytes 3145760 | tf_op jit(solution)/shard_map/ppermute | solution.py:29
  382.0 8.7 collective-permute-done.34
  395.3 7.8 collective-permute-done.38
  407.0 10.0 %collective-permute-done.41 = bf16[128,1536]{1,0:T(8,128)(2,1)S(1)} collective-permute-done((bf16[128,1536]{1,0:T(8,128)(2,1)S(1)}, bf16[128,1536]{1,0:T(8,128)(2,1)S(1)}, u32[]{:S(2)}, u32[]{:S(2)}) %collective-permute-start.41) | collective-permute-done | bytes 393248 | tf_op jit(solution)/shard_map/ppermute | solution.py:29
  434.2 8.1 fusion.26
  442.3 7.6 multiply_convert_fusion
  449.9 6.4 fusion.220
  456.3 5.1 fusion.21
  461.3 6.4 fusion.219
  472.0 6.8 fusion.218
  478.8 9.5 add_convert_fusion
  488.3 8.9 fusion.10
  497.2 6.6 fusion.3
  505.4 6.4 fusion.12
  511.8 6.4 fusion.4
  527.9 4.9 dynamic-slice_convert_fusion.1
  540.3 7.5 collective-permute-done.75
  548.2 16.5 %collective-permute-done.49 = bf16[128,1536]{1,0:T(8,128)(2,1)S(1)} collective-permute-done((bf16[128,1536]{1,0:T(8,128)(2,1)S(1)}, bf16[128,1536]{1,0:T(8,128)(2,1)S(1)}, u32[]{:S(2)}, u32[]{:S(2)}) %collective-permute-start.49) | collective-permute-done | bytes 393248 | tf_op jit(solution)/shard_map/ppermute | solution.py:29
  565.2 10.9 %collective-permute-done.76 = bf16[128,1536]{1,0:T(8,128)(2,1)S(1)} collective-permute-done((bf16[128,1536]{1,0:T(8,128)(2,1)S(1)}, bf16[128,1536]{1,0:T(8,128)(2,1)S(1)}, u32[]{:S(2)}, u32[]{:S(2)}) %collective-permute-start.76) | collective-permute-done | bytes 393248 | tf_op jit(solution)/shard_map/ppermute | solution.py:34
  576.6 9.6 collective-permute-done.50
  586.7 8.6 collective-permute-done.79
  595.8 7.9 collective-permute-done.53
  604.2 8.0 collective-permute-done.82
  615.0 7.2 collective-permute-done.56
  632.8 7.8 collective-permute-start.87
  649.4 22.9 %collective-permute-done.115 = bf16[4,768,512]{2,1,0:T(8,128)(2,1)} collective-permute-done((bf16[4,768,512]{2,1,0:T(8,128)(2,1)}, bf16[4,768,512]{2,1,0:T(8,128)(2,1)}, u32[]{:S(2)}, u32[]{:S(2)}) %collective-permute-start.115) | collective-permute-done | bytes 3145760 | tf_op jit(solution)/shard_map/ppermute | solution.py:29
  672.7 7.7 convert_add_fusion.2
  680.4 7.7 convert_add_fusion
  688.1 51.7 %collective-permute-done.116 = bf16[4,768,512]{2,1,0:T(8,128)(2,1)} collective-permute-done((bf16[4,768,512]{2,1,0:T(8,128)(2,1)}, bf16[4,768,512]{2,1,0:T(8,128)(2,1)}, u32[]{:S(2)}, u32[]{:S(2)}) %collective-permute-start.116) | collective-permute-done | bytes 3145760 | tf_op jit(solution)/shard_map/ppermute | solution.py:29
  739.8 6.0 convert_add_fusion.1
  748.2 10.3 %collective-permute-done.94 = bf16[128,1664]{1,0:T(8,128)(2,1)S(1)} collective-permute-done((bf16[128,1664]{1,0:T(8,128)(2,1)S(1)}, bf16[128,1664]{1,0:T(8,128)(2,1)S(1)}, u32[]{:S(2)}, u32[]{:S(2)}) %collective-permute-start.94) | collective-permute-done | bytes 426016 | tf_op jit(solution)/shard_map/ppermute | solution.py:29
  763.2 9.8 collective-permute-done.97
  778.6 5.3 multiply_bitcast_fusion
  785.9 8.2 fusion.47
  794.2 5.4 bitcast_add_fusion.2
  811.9 12.8 %multiply_reduce_fusion.3 = (f32[448]{0:T(512)S(1)}, f32[448]{0:T(512)S(1)}, f32[448]{0:T(512)S(1)}, f32[448]{0:T(512)S(1)}, f32[448]{0:T(512)S(1)}, /*index=5*/f32[16,128,448]{2,1,0:T(8,128)S(1)}) fusion(f32[16,125,448]{2,1,0:T(8,128)} %bitcast.461, f32[16,128]{1,0:T(8,128)S(1)} %copy-done.55, f32[2048,448]{1,0:T(8,128)} %copy.398, ...), kind=kLoop, calls=%fused_computation.52 | loop fusion | flops 21100352 | bytes 25551616 | tf_op jit(solution)/shard_map/transpose(jvp())/reduce_sum | solution.py:113
  828.7 6.3 multiply_add_fusion
  835.0 5.4 copy.397
  840.5 11.2 %fusion.104 = f32[1536,768]{0,1:T(8,128)} fusion(f32[1536]{0:T(1024)S(1)} %copy-done.60, f32[2048]{0:T(1024)S(1)} %copy-done.78, bf16[2048,1664]{0,1:T(8,128)(2,1)} %copy-done.4, f32[2048,192]{0,1:T(8,128)S(1)} %copy-done.98, f32[2048,448]{0,1:T(8,128)} %copy.397, f32[2048,3]{0,1:T(4,128)S(1)} %get-tuple-element.82), kind=kOutput, calls=%fused_computation.185 | convolution fusion | flops 4849139712 | bytes 16291840 | tf_op jit(solution)/shard_map/dot_general | solution.py:25
  851.8 7.3 convolution_convert_fusion
  863.3 6.8 all-to-all-start.2
  882.9 5.0 fusion.59
  890.3 8.5 collective-permute-done.101
  908.2 8.6 all-to-all-start.1
  920.0 35.1 %collective-permute-done.105 = bf16[128,1536]{1,0:T(8,128)(2,1)S(1)} collective-permute-done((bf16[128,1536]{1,0:T(8,128)(2,1)S(1)}, bf16[128,1536]{1,0:T(8,128)(2,1)S(1)}, u32[]{:S(2)}, u32[]{:S(2)}) %collective-permute-start.105) | collective-permute-done | bytes 393248 | tf_op jit(solution)/shard_map/ppermute | solution.py:34
  (755 shorter events, 318.7 us)
Async XLA Ops:
  3.6 31.8 %collective-permute-start.61 = (bf16[128,1536]{1,0:T(8,128)(2,1)}, bf16[128,1536]{1,0:T(8,128)(2,1)}, u32[]{:S(2)}, u32[]{:S(2)}) collective-permute-start(bf16[128,1536]{1,0:T(8,128)(2,1)} %get-tuple-element.89), channel_id=1, source_target_pairs={{0,1},{1,0},{2,3},{3,2},{4,5},{5,4},{6,7},{7,6},{8,9},{9,8},{10,11... | collective-permute-start | bytes 1179656 | tf_op jit(solution)/shard_map/ppermute | solution.py:29
  4.3 28.1 %collective-permute-start.60 = (bf16[128,1536]{1,0:T(8,128)(2,1)}, bf16[128,1536]{1,0:T(8,128)(2,1)}, u32[]{:S(2)}, u32[]{:S(2)}) collective-permute-start(bf16[128,1536]{1,0:T(8,128)(2,1)} %get-tuple-element.89), channel_id=1, source_target_pairs={{0,2},{2,0},{1,3},{3,1},{4,6},{6,4},{5,7},{7,5},{8,10},{10,8},{9,1... | collective-permute-start | bytes 1179656 | tf_op jit(solution)/shard_map/ppermute | solution.py:29
  4.5 28.9 %collective-permute-start.59 = (bf16[128,1536]{1,0:T(8,128)(2,1)}, bf16[128,1536]{1,0:T(8,128)(2,1)S(1)}, u32[]{:S(2)}, u32[]{:S(2)}) collective-permute-start(bf16[128,1536]{1,0:T(8,128)(2,1)} %get-tuple-element.89), channel_id=1, source_target_pairs={{0,4},{4,8},{8,12},{12,0},{1,5},{5,9},{9,13},{13,1},{2,6},{6,10},{... | collective-permute-start | bytes 1179656 | tf_op jit(solution)/shard_map/ppermute | solution.py:34
  5.8 22.4 %collective-permute-start.47 = (bf16[1,32,1536]{2,1,0:T(8,128)(2,1)}, bf16[1,32,1536]{2,1,0:T(8,128)(2,1)}, u32[]{:S(2)}, u32[]{:S(2)}) collective-permute-start(bf16[1,32,1536]{2,1,0:T(8,128)(2,1)} %bitcast.538), channel_id=1, source_target_pairs={{0,16},{16,0},{1,17},{17,1},{2,18},{18,2},{3,19},{19,3},{4,20},{20... | collective-permute-start | bytes 294920 | tf_op jit(solution)/shard_map/ppermute | solution.py:29
  7.0 23.1 %collective-permute-start.16 = (bf16[96,1536]{1,0:T(8,128)(2,1)}, bf16[96,1536]{1,0:T(8,128)(2,1)}, u32[]{:S(2)}, u32[]{:S(2)}) collective-permute-start(bf16[96,1536]{1,0:T(8,128)(2,1)} %param.27), channel_id=1, source_target_pairs={{0,1},{1,0},{2,3},{3,2},{4,5},{5,4},{6,7},{7,6},{8,9},{9,8},{10,11... | collective-permute-start | bytes 884744 | tf_op jit(solution)/shard_map/ppermute | solution.py:29
  20.1 158.4 %all-to-all-start = ((bf16[16,48,896]{2,1,0:T(8,128)(2,1)}), bf16[16,48,896]{2,1,0:T(8,128)(2,1)S(1)}, u32[]{:S(2)}, u32[]{:S(2)}) async-start(bf16[16,48,896]{2,1,0:T(8,128)(2,1)} %concatenate.76), calls=%async_computation | async-start | bytes 2752512 | tf_op jit(solution)/shard_map/all_to_all | solution.py:211
  28.2 16.6 %collective-permute-start.1 = (bf16[128,1664]{0,1:T(8,128)(2,1)S(1)}, bf16[128,1664]{0,1:T(8,128)(2,1)S(1)}, u32[]{:S(2)}, u32[]{:S(2)}) collective-permute-start(bf16[128,1664]{0,1:T(8,128)(2,1)S(1)} %get-tuple-element.159), channel_id=1, source_target_pairs={{0,2},{2,0},{1,3},{3,1},{4,6},{6,4},{5,7},{7,5},{8,10},{10,8},{9,1... | collective-permute-start | bytes 1277960 | tf_op jit(solution)/shard_map/ppermute | solution.py:29
  30.2 34.0 %collective-permute-start = (bf16[128,1664]{0,1:T(8,128)(2,1)S(1)}, bf16[128,1664]{0,1:T(8,128)(2,1)S(1)}, u32[]{:S(2)}, u32[]{:S(2)}) collective-permute-start(bf16[128,1664]{0,1:T(8,128)(2,1)S(1)} %get-tuple-element.159), channel_id=1, source_target_pairs={{0,4},{4,8},{8,12},{12,0},{1,5},{5,9},{9,13},{13,1},{2,6},{6,10},{... | collective-permute-start | bytes 1277960 | tf_op jit(solution)/shard_map/ppermute | solution.py:34
  32.4 34.2 %collective-permute-start.2 = (bf16[128,1664]{0,1:T(8,128)(2,1)S(1)}, bf16[128,1664]{0,1:T(8,128)(2,1)S(1)}, u32[]{:S(2)}, u32[]{:S(2)}) collective-permute-start(bf16[128,1664]{0,1:T(8,128)(2,1)S(1)} %get-tuple-element.159), channel_id=1, source_target_pairs={{0,1},{1,0},{2,3},{3,2},{4,5},{5,4},{6,7},{7,6},{8,9},{9,8},{10,11... | collective-permute-start | bytes 1277960 | tf_op jit(solution)/shard_map/ppermute | solution.py:29
  33.4 307.7 %collective-permute-start.44 = (bf16[4,768,512]{2,1,0:T(8,128)(2,1)}, bf16[4,768,512]{2,1,0:T(8,128)(2,1)}, u32[]{:S(2)}, u32[]{:S(2)}) collective-permute-start(bf16[4,768,512]{2,1,0:T(8,128)(2,1)} %param.36), channel_id=1, source_target_pairs={{0,16},{16,0},{1,17},{17,1},{2,18},{18,2},{3,19},{19,3},{4,20},{20... | collective-permute-start | bytes 9437192 | tf_op jit(solution)/shard_map/ppermute | solution.py:29
  35.4 40.3 %collective-permute-start.62 = (bf16[128,1536]{1,0:T(8,128)(2,1)}, bf16[128,1536]{1,0:T(8,128)(2,1)S(1)}, u32[]{:S(2)}, u32[]{:S(2)}) collective-permute-start(bf16[128,1536]{1,0:T(8,128)(2,1)} %collective-permute-done.60), channel_id=1, source_target_pairs={{0,1},{1,0},{2,3},{3,2},{4,5},{5,4},{6,7},{7,6},{8,9},{9,8},{10,11... | collective-permute-start | bytes 1179656 | tf_op jit(solution)/shard_map/ppermute | solution.py:29
  44.9 22.2 %collective-permute-start.64 = (bf16[128,1536]{1,0:T(8,128)(2,1)S(1)}, bf16[128,1536]{1,0:T(8,128)(2,1)S(1)}, u32[]{:S(2)}, u32[]{:S(2)}) collective-permute-start(bf16[128,1536]{1,0:T(8,128)(2,1)S(1)} %collective-permute-done.59), channel_id=1, source_target_pairs={{0,2},{2,0},{1,3},{3,1},{4,6},{6,4},{5,7},{7,5},{8,10},{10,8},{9,1... | collective-permute-start | bytes 1179656 | tf_op jit(solution)/shard_map/ppermute | solution.py:29
  66.6 49.3 %collective-permute-start.17 = (bf16[192,1536]{1,0:T(8,128)(2,1)S(1)}, bf16[192,1536]{1,0:T(8,128)(2,1)S(1)}, u32[]{:S(2)}, u32[]{:S(2)}) collective-permute-start(bf16[192,1536]{1,0:T(8,128)(2,1)S(1)} %pad_maximum_fusion.11), channel_id=1, source_target_pairs={{0,16},{16,0},{1,17},{17,1},{2,18},{18,2},{3,19},{19,3},{4,20},{20... | collective-permute-start | bytes 1769480 | tf_op jit(solution)/shard_map/ppermute | solution.py:29
  75.8 15.8 %collective-permute-start.6 = (bf16[128,1664]{0,1:T(8,128)(2,1)S(1)}, bf16[128,1664]{0,1:T(8,128)(2,1)S(1)}, u32[]{:S(2)}, u32[]{:S(2)}) collective-permute-start(bf16[128,1664]{0,1:T(8,128)(2,1)S(1)} %collective-permute-done), channel_id=1, source_target_pairs={{0,1},{1,0},{2,3},{3,2},{4,5},{5,4},{6,7},{7,6},{8,9},{9,8},{10,11... | collective-permute-start | bytes 1277960 | tf_op jit(solution)/shard_map/ppermute | solution.py:29
  89.1 37.8 %collective-permute-start.66 = (bf16[128,1536]{1,0:T(8,128)(2,1)S(1)}, bf16[128,1536]{1,0:T(8,128)(2,1)S(1)}, u32[]{:S(2)}, u32[]{:S(2)}) collective-permute-start(bf16[128,1536]{1,0:T(8,128)(2,1)S(1)} %collective-permute-done.64), channel_id=1, source_target_pairs={{0,1},{1,0},{2,3},{3,2},{4,5},{5,4},{6,7},{7,6},{8,9},{9,8},{10,11... | collective-permute-start | bytes 1179656 | tf_op jit(solution)/shard_map/ppermute | solution.py:29
  90.3 40.2 %collective-permute-start.69 = (bf16[128,1536]{1,0:T(8,128)(2,1)S(1)}, bf16[128,1536]{1,0:T(8,128)(2,1)S(1)}, u32[]{:S(2)}, u32[]{:S(2)}) collective-permute-start(bf16[128,1536]{1,0:T(8,128)(2,1)S(1)} %collective-permute-done.63), channel_id=1, source_target_pairs={{0,1},{1,0},{2,3},{3,2},{4,5},{5,4},{6,7},{7,6},{8,9},{9,8},{10,11... | collective-permute-start | bytes 1179656 | tf_op jit(solution)/shard_map/ppermute | solution.py:29
  91.6 26.5 %collective-permute-start.68 = (bf16[128,1536]{1,0:T(8,128)(2,1)S(1)}, bf16[128,1536]{1,0:T(8,128)(2,1)S(1)}, u32[]{:S(2)}, u32[]{:S(2)}) collective-permute-start(bf16[128,1536]{1,0:T(8,128)(2,1)S(1)} %collective-permute-done.63), channel_id=1, source_target_pairs={{0,2},{2,0},{1,3},{3,1},{4,6},{6,4},{5,7},{7,5},{8,10},{10,8},{9,1... | collective-permute-start | bytes 1179656 | tf_op jit(solution)/shard_map/ppermute | solution.py:29
  118.1 21.8 %collective-permute-start.7 = (bf16[128,1664]{0,1:T(8,128)(2,1)S(1)}, bf16[128,1664]{0,1:T(8,128)(2,1)S(1)}, u32[]{:S(2)}, u32[]{:S(2)}) collective-permute-start(bf16[128,1664]{0,1:T(8,128)(2,1)S(1)} %collective-permute-done.5), channel_id=1, source_target_pairs={{0,1},{1,0},{2,3},{3,2},{4,5},{5,4},{6,7},{7,6},{8,9},{9,8},{10,11... | collective-permute-start | bytes 1277960 | tf_op jit(solution)/shard_map/ppermute | solution.py:29
  130.5 166.8 %collective-permute-start.46 = (bf16[4,256,1536]{2,1,0:T(8,128)(2,1)}, bf16[4,256,1536]{2,1,0:T(8,128)(2,1)}, u32[]{:S(2)}, u32[]{:S(2)}) collective-permute-start(bf16[4,256,1536]{2,1,0:T(8,128)(2,1)} %param.38), channel_id=1, source_target_pairs={{0,16},{16,0},{1,17},{17,1},{2,18},{18,2},{3,19},{19,3},{4,20},{20... | collective-permute-start | bytes 9437192 | tf_op jit(solution)/shard_map/ppermute | solution.py:29
  141.2 12.8 %collective-permute-start.11 = (bf16[128,1664]{0,1:T(8,128)(2,1)S(1)}, bf16[128,1664]{0,1:T(8,128)(2,1)S(1)}, u32[]{:S(2)}, u32[]{:S(2)}) collective-permute-start(bf16[128,1664]{0,1:T(8,128)(2,1)S(1)} %collective-permute-done.9), channel_id=1, source_target_pairs={{0,1},{1,0},{2,3},{3,2},{4,5},{5,4},{6,7},{7,6},{8,9},{9,8},{10,11... | collective-permute-start | bytes 1277960 | tf_op jit(solution)/shard_map/ppermute | solution.py:29
  178.5 49.0 %collective-permute-start.15 = (bf16[1,768,896]{2,1,0:T(8,128)(2,1)S(1)}, bf16[1,768,896]{2,1,0:T(8,128)(2,1)S(1)}, u32[]{:S(2)}, u32[]{:S(2)}) collective-permute-start(bf16[1,768,896]{2,1,0:T(8,128)(2,1)S(1)} %bitcast.505), channel_id=1, source_target_pairs={{0,16},{16,0},{1,17},{17,1},{2,18},{18,2},{3,19},{19,3},{4,20},{20... | collective-permute-start | bytes 4128776 | tf_op jit(solution)/shard_map/ppermute | solution.py:29
  293.6 12.1 %collective-permute-start.24 = (bf16[2,128,1664]{2,1,0:T(8,128)(2,1)}, bf16[2,128,1664]{2,1,0:T(8,128)(2,1)S(1)}, u32[]{:S(2)}, u32[]{:S(2)}) collective-permute-start(bf16[2,128,1664]{2,1,0:T(8,128)(2,1)} %get-tuple-element.106), channel_id=1, source_target_pairs={{0,1},{1,0},{2,3},{3,2},{4,5},{5,4},{6,7},{7,6},{8,9},{9,8},{10,11... | collective-permute-start | bytes 2555912 | tf_op jit(solution)/shard_map/ppermute | solution.py:29
  305.7 70.1 %collective-permute-start.45 = (bf16[4,768,512]{2,1,0:T(8,128)(2,1)}, bf16[4,768,512]{2,1,0:T(8,128)(2,1)}, u32[]{:S(2)}, u32[]{:S(2)}) collective-permute-start(bf16[4,768,512]{2,1,0:T(8,128)(2,1)} %param.37), channel_id=1, source_target_pairs={{0,16},{16,0},{1,17},{17,1},{2,18},{18,2},{3,19},{19,3},{4,20},{20... | collective-permute-start | bytes 9437192 | tf_op jit(solution)/shard_map/ppermute | solution.py:29
  309.6 20.1 %collective-permute-start.22 = (bf16[128,1664]{1,0:T(8,128)(2,1)S(1)}, bf16[128,1664]{1,0:T(8,128)(2,1)S(1)}, u32[]{:S(2)}, u32[]{:S(2)}) collective-permute-start(bf16[128,1664]{1,0:T(8,128)(2,1)S(1)} %slice_bitcast_fusion.36), channel_id=1, source_target_pairs={{0,2},{2,0},{1,3},{3,1},{4,6},{6,4},{5,7},{7,5},{8,10},{10,8},{9,1... | collective-permute-start | bytes 1277960 | tf_op jit(solution)/shard_map/ppermute | solution.py:29
  321.1 17.8 %collective-permute-start.25 = (bf16[128,1664]{1,0:T(8,128)(2,1)S(1)}, bf16[128,1664]{1,0:T(8,128)(2,1)S(1)}, u32[]{:S(2)}, u32[]{:S(2)}) collective-permute-start(bf16[128,1664]{1,0:T(8,128)(2,1)S(1)} %slice_bitcast_fusion.34), channel_id=1, source_target_pairs={{0,2},{2,0},{1,3},{3,1},{4,6},{6,4},{5,7},{7,5},{8,10},{10,8},{9,1... | collective-permute-start | bytes 1277960 | tf_op jit(solution)/shard_map/ppermute | solution.py:29
  331.7 16.3 %collective-permute-start.28 = (bf16[128,1664]{1,0:T(8,128)(2,1)S(1)}, bf16[128,1664]{1,0:T(8,128)(2,1)S(1)}, u32[]{:S(2)}, u32[]{:S(2)}) collective-permute-start(bf16[128,1664]{1,0:T(8,128)(2,1)S(1)} %slice_bitcast_fusion.32), channel_id=1, source_target_pairs={{0,2},{2,0},{1,3},{3,1},{4,6},{6,4},{5,7},{7,5},{8,10},{10,8},{9,1... | collective-permute-start | bytes 1277960 | tf_op jit(solution)/shard_map/ppermute | solution.py:29
  352.5 28.0 %collective-permute-start.30 = (bf16[128,1536]{1,0:T(8,128)(2,1)S(1)}, bf16[128,1536]{1,0:T(8,128)(2,1)S(1)}, u32[]{:S(2)}, u32[]{:S(2)}) collective-permute-start(bf16[128,1536]{1,0:T(8,128)(2,1)S(1)} %get-tuple-element.91), channel_id=1, source_target_pairs={{0,2},{2,0},{1,3},{3,1},{4,6},{6,4},{5,7},{7,5},{8,10},{10,8},{9,1... | collective-permute-start | bytes 1179656 | tf_op jit(solution)/shard_map/ppermute | solution.py:29
  352.8 27.6 %collective-permute-start.29 = (bf16[128,1536]{1,0:T(8,128)(2,1)S(1)}, bf16[128,1536]{1,0:T(8,128)(2,1)S(1)}, u32[]{:S(2)}, u32[]{:S(2)}) collective-permute-start(bf16[128,1536]{1,0:T(8,128)(2,1)S(1)} %get-tuple-element.91), channel_id=1, source_target_pairs={{0,4},{4,8},{8,12},{12,0},{1,5},{5,9},{9,13},{13,1},{2,6},{6,10},{... | collective-permute-start | bytes 1179656 | tf_op jit(solution)/shard_map/ppermute | solution.py:34
  380.4 14.8 %collective-permute-start.35 = (bf16[128,1536]{1,0:T(8,128)(2,1)S(1)}, bf16[128,1536]{1,0:T(8,128)(2,1)S(1)}, u32[]{:S(2)}, u32[]{:S(2)}) collective-permute-start(bf16[128,1536]{1,0:T(8,128)(2,1)S(1)} %collective-permute-done.29), channel_id=1, source_target_pairs={{0,1},{1,0},{2,3},{3,2},{4,5},{5,4},{6,7},{7,6},{8,9},{9,8},{10,11... | collective-permute-start | bytes 1179656 | tf_op jit(solution)/shard_map/ppermute | solution.py:29
  381.0 13.6 %collective-permute-start.32 = (bf16[128,1536]{1,0:T(8,128)(2,1)S(1)}, bf16[128,1536]{1,0:T(8,128)(2,1)S(1)}, u32[]{:S(2)}, u32[]{:S(2)}) collective-permute-start(bf16[128,1536]{1,0:T(8,128)(2,1)S(1)} %collective-permute-done.30), channel_id=1, source_target_pairs={{0,1},{1,0},{2,3},{3,2},{4,5},{5,4},{6,7},{7,6},{8,9},{9,8},{10,11... | collective-permute-start | bytes 1179656 | tf_op jit(solution)/shard_map/ppermute | solution.py:29
  390.8 16.2 %collective-permute-start.39 = (bf16[128,1536]{1,0:T(8,128)(2,1)S(1)}, bf16[128,1536]{1,0:T(8,128)(2,1)S(1)}, u32[]{:S(2)}, u32[]{:S(2)}) collective-permute-start(bf16[128,1536]{1,0:T(8,128)(2,1)S(1)} %collective-permute-done.33), channel_id=1, source_target_pairs={{0,1},{1,0},{2,3},{3,2},{4,5},{5,4},{6,7},{7,6},{8,9},{9,8},{10,11... | collective-permute-start | bytes 1179656 | tf_op jit(solution)/shard_map/ppermute | solution.py:29
  393.5 12.0 %collective-permute-start.37 = (bf16[128,1536]{1,0:T(8,128)(2,1)S(1)}, bf16[128,1536]{1,0:T(8,128)(2,1)S(1)}, u32[]{:S(2)}, u32[]{:S(2)}) collective-permute-start(bf16[128,1536]{1,0:T(8,128)(2,1)S(1)} %collective-permute-done.33), channel_id=1, source_target_pairs={{0,4},{4,8},{8,12},{12,0},{1,5},{5,9},{9,13},{13,1},{2,6},{6,10},{... | collective-permute-start | bytes 1179656 | tf_op jit(solution)/shard_map/ppermute | solution.py:34
  394.6 12.3 %collective-permute-start.36 = (bf16[128,1536]{1,0:T(8,128)(2,1)S(1)}, bf16[128,1536]{1,0:T(8,128)(2,1)S(1)}, u32[]{:S(2)}, u32[]{:S(2)}) collective-permute-start(bf16[128,1536]{1,0:T(8,128)(2,1)S(1)} %collective-permute-done.34), channel_id=1, source_target_pairs={{0,1},{1,0},{2,3},{3,2},{4,5},{5,4},{6,7},{7,6},{8,9},{9,8},{10,11... | collective-permute-start | bytes 1179656 | tf_op jit(solution)/shard_map/ppermute | solution.py:29
  405.5 12.4 %collective-permute-start.42 = (bf16[128,1536]{1,0:T(8,128)(2,1)S(1)}, bf16[128,1536]{1,0:T(8,128)(2,1)S(1)}, u32[]{:S(2)}, u32[]{:S(2)}) collective-permute-start(bf16[128,1536]{1,0:T(8,128)(2,1)S(1)} %collective-permute-done.37), channel_id=1, source_target_pairs={{0,1},{1,0},{2,3},{3,2},{4,5},{5,4},{6,7},{7,6},{8,9},{9,8},{10,11... | collective-permute-start | bytes 1179656 | tf_op jit(solution)/shard_map/ppermute | solution.py:29
  471.7 157.7 %collective-permute-start.114 = (bf16[1,32,1536]{2,1,0:T(8,128)(2,1)}, bf16[1,32,1536]{2,1,0:T(8,128)(2,1)}, u32[]{:S(2)}, u32[]{:S(2)}) collective-permute-start(bf16[1,32,1536]{2,1,0:T(8,128)(2,1)} %dynamic-slice_convert_fusion.3), channel_id=1, source_target_pairs={{0,16},{16,0},{1,17},{17,1},{2,18},{18,2},{3,19},{19,3},{4,20},{20... | collective-permute-start | bytes 294920 | tf_op jit(solution)/shard_map/ppermute | solution.py:29
  504.0 28.9 %collective-permute-start.80 = (bf16[2,128,1536]{2,1,0:T(8,128)(2,1)S(1)}, bf16[2,128,1536]{2,1,0:T(8,128)(2,1)S(1)}, u32[]{:S(2)}, u32[]{:S(2)}) collective-permute-start(bf16[2,128,1536]{2,1,0:T(8,128)(2,1)S(1)} %get-tuple-element.122), channel_id=1, source_target_pairs={{0,1},{1,0},{2,3},{3,2},{4,5},{5,4},{6,7},{7,6},{8,9},{9,8},{10,11... | collective-permute-start | bytes 2359304 | tf_op jit(solution)/shard_map/ppermute | solution.py:29
  504.8 28.7 %collective-permute-start.83 = (bf16[2,128,1536]{2,1,0:T(8,128)(2,1)S(1)}, bf16[2,128,1536]{2,1,0:T(8,128)(2,1)S(1)}, u32[]{:S(2)}, u32[]{:S(2)}) collective-permute-start(bf16[2,128,1536]{2,1,0:T(8,128)(2,1)S(1)} %get-tuple-element.123), channel_id=1, source_target_pairs={{0,1},{1,0},{2,3},{3,2},{4,5},{5,4},{6,7},{7,6},{8,9},{9,8},{10,11... | collective-permute-start | bytes 2359304 | tf_op jit(solution)/shard_map/ppermute | solution.py:29
  504.8 28.7 %collective-permute-start.77 = (bf16[2,128,1536]{2,1,0:T(8,128)(2,1)S(1)}, bf16[2,128,1536]{2,1,0:T(8,128)(2,1)S(1)}, u32[]{:S(2)}, u32[]{:S(2)}) collective-permute-start(bf16[2,128,1536]{2,1,0:T(8,128)(2,1)S(1)} %get-tuple-element.124), channel_id=1, source_target_pairs={{0,1},{1,0},{2,3},{3,2},{4,5},{5,4},{6,7},{7,6},{8,9},{9,8},{10,11... | collective-permute-start | bytes 2359304 | tf_op jit(solution)/shard_map/ppermute | solution.py:29
  505.3 28.7 %collective-permute-start.74 = (bf16[2,128,1536]{2,1,0:T(8,128)(2,1)S(1)}, bf16[2,128,1536]{2,1,0:T(8,128)(2,1)S(1)}, u32[]{:S(2)}, u32[]{:S(2)}) collective-permute-start(bf16[2,128,1536]{2,1,0:T(8,128)(2,1)S(1)} %get-tuple-element.125), channel_id=1, source_target_pairs={{0,1},{1,0},{2,3},{3,2},{4,5},{5,4},{6,7},{7,6},{8,9},{9,8},{10,11... | collective-permute-start | bytes 2359304 | tf_op jit(solution)/shard_map/ppermute | solution.py:29
  535.4 145.0 %collective-permute-start.117 = (bf16[4,256,1536]{2,1,0:T(8,128)(2,1)}, bf16[4,256,1536]{2,1,0:T(8,128)(2,1)}, u32[]{:S(2)}, u32[]{:S(2)}) collective-permute-start(bf16[4,256,1536]{2,1,0:T(8,128)(2,1)} %dynamic-slice_convert_fusion), channel_id=1, source_target_pairs={{0,16},{16,0},{1,17},{17,1},{2,18},{18,2},{3,19},{19,3},{4,20},{20... | collective-permute-start | bytes 9437192 | tf_op jit(solution)/shard_map/ppermute | solution.py:29
  536.6 135.8 %collective-permute-start.115 = (bf16[4,768,512]{2,1,0:T(8,128)(2,1)}, bf16[4,768,512]{2,1,0:T(8,128)(2,1)}, u32[]{:S(2)}, u32[]{:S(2)}) collective-permute-start(bf16[4,768,512]{2,1,0:T(8,128)(2,1)} %dynamic-slice_convert_fusion.2), channel_id=1, source_target_pairs={{0,16},{16,0},{1,17},{17,1},{2,18},{18,2},{3,19},{19,3},{4,20},{20... | collective-permute-start | bytes 9437192 | tf_op jit(solution)/shard_map/ppermute | solution.py:29
  538.7 26.1 %collective-permute-start.78 = (bf16[128,1536]{1,0:T(8,128)(2,1)S(1)}, bf16[128,1536]{1,0:T(8,128)(2,1)S(1)}, u32[]{:S(2)}, u32[]{:S(2)}) collective-permute-start(bf16[128,1536]{1,0:T(8,128)(2,1)S(1)} %slice_bitcast_fusion.52), channel_id=1, source_target_pairs={{0,2},{2,0},{1,3},{3,1},{4,6},{6,4},{5,7},{7,5},{8,10},{10,8},{9,1... | collective-permute-start | bytes 1179656 | tf_op jit(solution)/shard_map/ppermute | solution.py:29
  547.8 16.9 %collective-permute-start.49 = (bf16[128,1536]{1,0:T(8,128)(2,1)S(1)}, bf16[128,1536]{1,0:T(8,128)(2,1)S(1)}, u32[]{:S(2)}, u32[]{:S(2)}) collective-permute-start(bf16[128,1536]{1,0:T(8,128)(2,1)S(1)} %slice_bitcast_fusion.62), channel_id=1, source_target_pairs={{0,2},{2,0},{1,3},{3,1},{4,6},{6,4},{5,7},{7,5},{8,10},{10,8},{9,1... | collective-permute-start | bytes 1179656 | tf_op jit(solution)/shard_map/ppermute | solution.py:29
  612.7 127.1 %collective-permute-start.116 = (bf16[4,768,512]{2,1,0:T(8,128)(2,1)}, bf16[4,768,512]{2,1,0:T(8,128)(2,1)}, u32[]{:S(2)}, u32[]{:S(2)}) collective-permute-start(bf16[4,768,512]{2,1,0:T(8,128)(2,1)} %dynamic-slice_convert_fusion.1), channel_id=1, source_target_pairs={{0,16},{16,0},{1,17},{17,1},{2,18},{18,2},{3,19},{19,3},{4,20},{20... | collective-permute-start | bytes 9437192 | tf_op jit(solution)/shard_map/ppermute | solution.py:29
  629.5 12.8 %collective-permute-start.85 = (bf16[128,1664]{1,0:T(8,128)(2,1)S(1)}, bf16[128,1664]{1,0:T(8,128)(2,1)S(1)}, u32[]{:S(2)}, u32[]{:S(2)}) collective-permute-start(bf16[128,1664]{1,0:T(8,128)(2,1)S(1)} %get-tuple-element.157), channel_id=1, source_target_pairs={{0,4},{4,8},{8,12},{12,0},{1,5},{5,9},{9,13},{13,1},{2,6},{6,10},{... | collective-permute-start | bytes 1277960 | tf_op jit(solution)/shard_map/ppermute | solution.py:34
  632.8 15.9 %collective-permute-start.87 = (bf16[128,1664]{1,0:T(8,128)(2,1)S(1)}, bf16[128,1664]{1,0:T(8,128)(2,1)S(1)}, u32[]{:S(2)}, u32[]{:S(2)}) collective-permute-start(bf16[128,1664]{1,0:T(8,128)(2,1)S(1)} %get-tuple-element.157), channel_id=1, source_target_pairs={{0,1},{1,0},{2,3},{3,2},{4,5},{5,4},{6,7},{7,6},{8,9},{9,8},{10,11... | collective-permute-start | bytes 1277960 | tf_op jit(solution)/shard_map/ppermute | solution.py:29
  642.3 105.3 %collective-permute-start.88 = (bf16[128,1664]{1,0:T(8,128)(2,1)}, bf16[128,1664]{1,0:T(8,128)(2,1)S(1)}, u32[]{:S(2)}, u32[]{:S(2)}) collective-permute-start(bf16[128,1664]{1,0:T(8,128)(2,1)} %copy-done.45), channel_id=1, source_target_pairs={{0,1},{1,0},{2,3},{3,2},{4,5},{5,4},{6,7},{7,6},{8,9},{9,8},{10,11... | collective-permute-start | bytes 1277960 | tf_op jit(solution)/shard_map/ppermute | solution.py:29
  648.6 99.5 %collective-permute-start.91 = (bf16[128,1664]{1,0:T(8,128)(2,1)S(1)}, bf16[128,1664]{1,0:T(8,128)(2,1)S(1)}, u32[]{:S(2)}, u32[]{:S(2)}) collective-permute-start(bf16[128,1664]{1,0:T(8,128)(2,1)S(1)} %collective-permute-done.85), channel_id=1, source_target_pairs={{0,1},{1,0},{2,3},{3,2},{4,5},{5,4},{6,7},{7,6},{8,9},{9,8},{10,11... | collective-permute-start | bytes 1277960 | tf_op jit(solution)/shard_map/ppermute | solution.py:29
  672.4 73.4 %collective-permute-start.90 = (bf16[128,1664]{1,0:T(8,128)(2,1)S(1)}, bf16[128,1664]{1,0:T(8,128)(2,1)S(1)}, u32[]{:S(2)}, u32[]{:S(2)}) collective-permute-start(bf16[128,1664]{1,0:T(8,128)(2,1)S(1)} %collective-permute-done.85), channel_id=1, source_target_pairs={{0,2},{2,0},{1,3},{3,1},{4,6},{6,4},{5,7},{7,5},{8,10},{10,8},{9,1... | collective-permute-start | bytes 1277960 | tf_op jit(solution)/shard_map/ppermute | solution.py:29
  680.4 65.4 %collective-permute-start.89 = (bf16[128,1664]{1,0:T(8,128)(2,1)S(1)}, bf16[128,1664]{1,0:T(8,128)(2,1)S(1)}, u32[]{:S(2)}, u32[]{:S(2)}) collective-permute-start(bf16[128,1664]{1,0:T(8,128)(2,1)S(1)} %collective-permute-done.85), channel_id=1, source_target_pairs={{0,4},{4,8},{8,12},{12,0},{1,5},{5,9},{9,13},{13,1},{2,6},{6,10},{... | collective-permute-start | bytes 1277960 | tf_op jit(solution)/shard_map/ppermute | solution.py:34
  745.8 17.4 %collective-permute-start.95 = (bf16[128,1664]{1,0:T(8,128)(2,1)S(1)}, bf16[128,1664]{1,0:T(8,128)(2,1)S(1)}, u32[]{:S(2)}, u32[]{:S(2)}) collective-permute-start(bf16[128,1664]{1,0:T(8,128)(2,1)S(1)} %collective-permute-done.89), channel_id=1, source_target_pairs={{0,1},{1,0},{2,3},{3,2},{4,5},{5,4},{6,7},{7,6},{8,9},{9,8},{10,11... | collective-permute-start | bytes 1277960 | tf_op jit(solution)/shard_map/ppermute | solution.py:29
  747.3 13.4 %collective-permute-start.93 = (bf16[128,1664]{1,0:T(8,128)(2,1)S(1)}, bf16[128,1664]{1,0:T(8,128)(2,1)S(1)}, u32[]{:S(2)}, u32[]{:S(2)}) collective-permute-start(bf16[128,1664]{1,0:T(8,128)(2,1)S(1)} %collective-permute-done.89), channel_id=1, source_target_pairs={{0,4},{4,8},{8,12},{12,0},{1,5},{5,9},{9,13},{13,1},{2,6},{6,10},{... | collective-permute-start | bytes 1277960 | tf_op jit(solution)/shard_map/ppermute | solution.py:34
  747.6 15.5 %collective-permute-start.92 = (bf16[128,1664]{1,0:T(8,128)(2,1)S(1)}, bf16[128,1664]{1,0:T(8,128)(2,1)S(1)}, u32[]{:S(2)}, u32[]{:S(2)}) collective-permute-start(bf16[128,1664]{1,0:T(8,128)(2,1)S(1)} %collective-permute-done.90), channel_id=1, source_target_pairs={{0,1},{1,0},{2,3},{3,2},{4,5},{5,4},{6,7},{7,6},{8,9},{9,8},{10,11... | collective-permute-start | bytes 1277960 | tf_op jit(solution)/shard_map/ppermute | solution.py:29
  760.7 13.2 %collective-permute-start.98 = (bf16[128,1664]{1,0:T(8,128)(2,1)S(1)}, bf16[128,1664]{1,0:T(8,128)(2,1)S(1)}, u32[]{:S(2)}, u32[]{:S(2)}) collective-permute-start(bf16[128,1664]{1,0:T(8,128)(2,1)S(1)} %collective-permute-done.93), channel_id=1, source_target_pairs={{0,1},{1,0},{2,3},{3,2},{4,5},{5,4},{6,7},{7,6},{8,9},{9,8},{10,11... | collective-permute-start | bytes 1277960 | tf_op jit(solution)/shard_map/ppermute | solution.py:29
  859.0 19.8 %collective-permute-start.112 = (bf16[192,1536]{1,0:T(8,128)(2,1)}, bf16[192,1536]{1,0:T(8,128)(2,1)S(1)}, u32[]{:S(2)}, u32[]{:S(2)}) collective-permute-start(bf16[192,1536]{1,0:T(8,128)(2,1)} %get-tuple-element.184), channel_id=1, source_target_pairs={{0,16},{16,0},{1,17},{17,1},{2,18},{18,2},{3,19},{19,3},{4,20},{20... | collective-permute-start | bytes 1769480 | tf_op jit(solution)/shard_map/ppermute | solution.py:29
  863.3 13.6 %all-to-all-start.2 = ((f32[32,1,712]{2,1,0:T(1,128)}), f32[32,1,712]{2,1,0:T(1,128)S(1)}, u32[]{:S(2)}, u32[]{:S(2)}) async-start(f32[32,1,712]{2,1,0:T(1,128)} %copy.378), calls=%async_computation.2 | async-start | bytes 196608 | tf_op jit(solution)/shard_map/all_to_all | solution.py:447
  872.1 32.7 %collective-permute-start.111 = (bf16[768,896]{0,1:T(8,128)(2,1)S(1)}, bf16[768,896]{0,1:T(8,128)(2,1)}, u32[]{:S(2)}, u32[]{:S(2)}) collective-permute-start(bf16[768,896]{0,1:T(8,128)(2,1)S(1)} %fusion.35), channel_id=1, source_target_pairs={{0,16},{16,0},{1,17},{17,1},{2,18},{18,2},{3,19},{19,3},{4,20},{20... | collective-permute-start | bytes 4128776 | tf_op jit(solution)/shard_map/ppermute | solution.py:29
  882.9 75.6 %collective-permute-start.113 = (f32[96,1536]{1,0:T(8,128)}, f32[96,1536]{1,0:T(8,128)}, u32[]{:S(2)}, u32[]{:S(2)}) collective-permute-start(f32[96,1536]{1,0:T(8,128)} %dynamic-slice_bitcast_fusion), channel_id=1, source_target_pairs={{0,1},{1,0},{2,3},{3,2},{4,5},{5,4},{6,7},{7,6},{8,9},{9,8},{10,11... | collective-permute-start | bytes 1769480 | tf_op jit(solution)/shard_map/ppermute | solution.py:29
  889.2 27.6 %collective-permute-start.104 = (bf16[128,1536]{1,0:T(8,128)(2,1)}, bf16[128,1536]{1,0:T(8,128)(2,1)}, u32[]{:S(2)}, u32[]{:S(2)}) collective-permute-start(bf16[128,1536]{1,0:T(8,128)(2,1)} %slice_bitcast_fusion.44), channel_id=1, source_target_pairs={{0,2},{2,0},{1,3},{3,1},{4,6},{6,4},{5,7},{7,5},{8,10},{10,8},{9,1... | collective-permute-start | bytes 1179656 | tf_op jit(solution)/shard_map/ppermute | solution.py:29
  899.6 17.2 %collective-permute-start.102 = (bf16[128,1536]{1,0:T(8,128)(2,1)}, bf16[128,1536]{1,0:T(8,128)(2,1)}, u32[]{:S(2)}, u32[]{:S(2)}) collective-permute-start(bf16[128,1536]{1,0:T(8,128)(2,1)} %fusion.134), channel_id=1, source_target_pairs={{0,4},{4,8},{8,12},{12,0},{1,5},{5,9},{9,13},{13,1},{2,6},{6,10},{... | collective-permute-start | bytes 1179656 | tf_op jit(solution)/shard_map/ppermute | solution.py:34
  900.5 19.6 %collective-permute-start.107 = (bf16[128,1536]{1,0:T(8,128)(2,1)}, bf16[128,1536]{1,0:T(8,128)(2,1)}, u32[]{:S(2)}, u32[]{:S(2)}) collective-permute-start(bf16[128,1536]{1,0:T(8,128)(2,1)} %slice_bitcast_fusion.42), channel_id=1, source_target_pairs={{0,2},{2,0},{1,3},{3,1},{4,6},{6,4},{5,7},{7,5},{8,10},{10,8},{9,1... | collective-permute-start | bytes 1179656 | tf_op jit(solution)/shard_map/ppermute | solution.py:29
  908.2 59.5 %all-to-all-start.1 = ((bf16[16,48,896]{2,1,0:T(8,128)(2,1)}), bf16[16,48,896]{2,1,0:T(8,128)(2,1)S(1)}, u32[]{:S(2)}, u32[]{:S(2)}) async-start(bf16[16,48,896]{2,1,0:T(8,128)(2,1)} %bitcast.126), calls=%async_computation.1 | async-start | bytes 2752512 | tf_op jit(solution)/shard_map/all_to_all | solution.py:392
  918.4 36.7 %collective-permute-start.105 = (bf16[128,1536]{1,0:T(8,128)(2,1)S(1)}, bf16[128,1536]{1,0:T(8,128)(2,1)S(1)}, u32[]{:S(2)}, u32[]{:S(2)}) collective-permute-start(bf16[128,1536]{1,0:T(8,128)(2,1)S(1)} %add_convert_fusion.6), channel_id=1, source_target_pairs={{0,4},{4,8},{8,12},{12,0},{1,5},{5,9},{9,13},{13,1},{2,6},{6,10},{... | collective-permute-start | bytes 1179656 | tf_op jit(solution)/shard_map/ppermute | solution.py:34
  919.7 41.5 %collective-permute-start.110 = (bf16[128,1536]{1,0:T(8,128)(2,1)S(1)}, bf16[128,1536]{1,0:T(8,128)(2,1)S(1)}, u32[]{:S(2)}, u32[]{:S(2)}) collective-permute-start(bf16[128,1536]{1,0:T(8,128)(2,1)S(1)} %slice_bitcast_fusion.40), channel_id=1, source_target_pairs={{0,2},{2,0},{1,3},{3,1},{4,6},{6,4},{5,7},{7,5},{8,10},{10,8},{9,1... | collective-permute-start | bytes 1179656 | tf_op jit(solution)/shard_map/ppermute | solution.py:29
  (175 other events, 2721.6 us)

commit v2 on v1

v2 whole, which is shorter than its diff:
```python
import jax
import jax.numpy as jnp
from jax import lax
from jax.experimental import pallas as pl
from jax.experimental.pallas import tpu as pltpu
from jax.sharding import Mesh, PartitionSpec as P

HEADS = 48
HEAD_DIM = 64
STATE = 128
KERNEL = 4
SEQ_SLOTS = 3
INNER = 3072
CONV_CH = 3328
EXTRA = 128

epsilon = 1e-05
bf16 = jnp.bfloat16
f32 = jnp.float32
GROUP = ("z", "y", "core")
ALL = ("dp", "z", "y", "core")


def matmul(left, right, dims=None, precision=None):
    if dims is None:
        dims = (((left.ndim - 1,), (0,)), ((), ()))
    return lax.dot_general(left, right, dims, precision=precision, preferred_element_type=f32)


def swap(value, axis):
    return lax.ppermute(value, axis, [(0, 1), (1, 0)])


def ring(value):
    size = lax.axis_size("z")
    return lax.ppermute(value, "z", [(k, (k + 1) % size) for k in range(size)])


def after(value, *earlier):
    return lax.optimization_barrier((value, earlier))[0]


def split_three(value):
    high = lax.reduce_precision(value, 8, 7)
    rest = value - high
    middle = lax.reduce_precision(rest, 8, 7)
    return high.astype(bf16), middle.astype(bf16), (rest - middle).astype(bf16)


def join_three(parts):
    return parts[0].astype(f32) + parts[1].astype(f32) + parts[2].astype(f32)


def gather(block, *joined):
    size = lax.axis_size("z")
    blocks = []
    for step in range(size - 1):
        following, beside = ring(block), swap(block, "y")
        blocks += [block, beside]
        if step == size - 2 and joined:
            block, _, joined = lax.optimization_barrier((following, beside, joined))
        else:
            block, _ = lax.optimization_barrier((following, beside))
    blocks += [block, swap(block, "y")]
    near = jnp.concatenate(blocks, axis=0)
    everything = jnp.concatenate([near, swap(near, "core")], axis=0)
    return (everything, *joined) if joined else everything


def add_low(left, right):
    return (left.astype(f32) + right.astype(f32)).astype(bf16)


def scatter(parts):
    size = lax.axis_size("z")
    parts = parts.reshape((2, size, 2, parts.shape[0] // (4 * size)) + parts.shape[1:])
    pairs = add_low(parts[0], swap(parts[1], "core"))
    there = [swap(pairs[step, 1], "y") for step in list(range(1, size)) + [0]]
    total = add_low(pairs[1, 0], there[0])
    for step in range(2, size):
        total = add_low(ring(total), add_low(pairs[step, 0], there[step - 1]))
    return ring(total).astype(f32) + pairs[0, 0].astype(f32) + there[-1].astype(f32)


def dp_gather_rows(value, axis):
    if lax.axis_size("dp") != 2:
        return lax.all_gather(value, "dp", axis=axis, tiled=True)
    other = swap(value, "dp")
    first = lax.axis_index("dp") == 0
    return jnp.concatenate(
        [jnp.where(first, value, other), jnp.where(first, other, value)], axis=axis
    )


def dp_scatter_rows(value, axis):
    count = lax.axis_size("dp")
    if count != 2:
        return lax.psum_scatter(value.astype(bf16), "dp", scatter_dimension=axis, tiled=True).astype(f32)
    place = lax.axis_index("dp")
    extent = value.shape[axis] // count
    sent = lax.dynamic_slice_in_dim(value, (1 - place) * extent, extent, axis).astype(bf16)
    kept = lax.dynamic_slice_in_dim(value, place * extent, extent, axis)
    return kept + swap(sent, "dp").astype(f32)


def params(steps=1):
    return pltpu.CompilerParams(
        dimension_semantics=("arbitrary",) * steps, vmem_limit_bytes=56 * 1024 * 1024
    )


def whole(array):
    return pl.BlockSpec(array.shape, lambda step: (0,) * array.ndim)


def sigmoid(value):
    return 1.0 / (1.0 + jnp.exp(-value))


def exact(left, right, dims):
    return lax.dot_general(
        left, right, (dims, ((), ())), precision=lax.Precision.HIGHEST, preferred_element_type=f32
    )


def rows_of(array, index):
    return array[index : index + 1]


WIDE = 256
CONV_LANES = 2 * STATE + WIDE
PROJ_LANES = CONV_LANES + WIDE + EXTRA


def triangle(count):
    row = lax.broadcasted_iota(jnp.int32, (count, count), 0)
    column = lax.broadcasted_iota(jnp.int32, (count, count), 1)
    return row - column


def block_scan(proj, place, conv, head):
    heads = HEADS // 16
    count = proj.shape[0]
    taps = [proj[:, :CONV_LANES]]
    total = rows_of(conv, KERNEL) + rows_of(conv, KERNEL - 1) * taps[0]
    for offset in range(1, KERNEL):
        inside = (place >= offset).astype(f32)
        taps.append(pltpu.roll(taps[0], offset, 0) * inside)
        total = total + rows_of(conv, KERNEL - 1 - offset) * taps[offset]
    conv_sig = sigmoid(total)
    conv_out = total * conv_sig
    b_part, c_part = conv_out[:, :STATE], conv_out[:, STATE : 2 * STATE]
    raw = proj[:, CONV_LANES + WIDE :] + rows_of(head, 0)[:, :EXTRA]
    step = jnp.maximum(raw, 0.0) + jnp.log1p(jnp.exp(-jnp.abs(raw)))
    distance = triangle(count)
    lower = (distance >= 0).astype(f32)
    cumul = exact(lower, step * rows_of(head, 1)[:, :EXTRA], ((1,), (0,)))
    cumul_rows = cumul.T
    step_rows = step.T
    scores = exact(c_part, b_part, ((1,), (1,)))
    reach = jnp.logical_and(distance >= 0, distance.astype(f32) <= place)
    lane = lax.broadcasted_iota(jnp.int32, (1, 2 * HEAD_DIM), 1)
    decays, values, scan = [], [], [None] * (WIDE // EXTRA)
    for index in range(heads):
        tile = index // 2
        spread = cumul[:, index : index + 1] - rows_of(cumul_rows, index)
        decay = jnp.exp(jnp.where(reach, spread, -1e30))
        mine = (lane // HEAD_DIM == index % 2).astype(f32)
        at = 2 * STATE + tile * EXTRA
        value = conv_out[:, at : at + EXTRA] * mine
        mixing = decay * scores * rows_of(step_rows, index)
        part = exact(mixing, value, ((1,), (0,)))
        scan[tile] = part if scan[tile] is None else scan[tile] + part
        decays.append((decay, mixing))
        values.append((value, mine))
    scan = jnp.concatenate(scan, axis=1) + rows_of(head, 2) * conv_out[:, 2 * STATE :]
    gate = proj[:, CONV_LANES : CONV_LANES + WIDE]
    gate_sig = sigmoid(gate)
    gated = scan * (gate * gate_sig)
    return dict(
        taps=taps, total=total, conv_sig=conv_sig, conv_out=conv_out, raw=raw, step_rows=step_rows,
        scores=scores, decays=decays, values=values, scan=scan, gate=gate, gate_sig=gate_sig,
        gated=gated, lower=lower,
    )


def mixer_forward_kernel(
    count, tokens_ref, beside_ref, gain_ref, w_in_ref, w_out_ref, conv_ref, head_ref,
    normed_ref, proj_ref, part_ref, scaled_ref,
):
    rows = tokens_ref[...].astype(f32)
    normed = rows * lax.rsqrt(jnp.mean(rows * rows, axis=1, keepdims=True) + epsilon) * gain_ref[...]
    normed = normed.astype(bf16)
    normed_ref[...] = normed
    proj_ref[...] = jnp.dot(normed, w_in_ref[...], preferred_element_type=f32)
    conv, head = conv_ref[...], head_ref[...]
    width = tokens_ref.shape[1]
    for index in range(tokens_ref.shape[0] // count):
        part = pl.ds(index * count, count)
        place = beside_ref[part, :].astype(f32)[:, 1:2]
        found = block_scan(proj_ref[part, :], place, conv, head)
        gated = found["gated"]
        scaled_ref[part, :] = (gated * rows_of(head, 3)).astype(bf16)
        square = gated * gated
        square = square[:, :EXTRA] + square[:, EXTRA:]
        part_ref[part, width:] = square.astype(bf16)
    part_ref[:, :width] = jnp.dot(
        scaled_ref[...], w_out_ref[...], preferred_element_type=f32
    ).astype(bf16)


def mixer_forward(gathered, width, count, gain, w_in, w_out, conv, head):
    total = gathered.shape[0]
    rows = 4 * count
    lanes = width // EXTRA

    def rows_spec(extent, column=0):
        return pl.BlockSpec((rows, extent), lambda step: (step, column))

    return pl.pallas_call(
        lambda *refs: mixer_forward_kernel(count, *refs),
        grid=(total // rows,),
        in_specs=[rows_spec(width), rows_spec(EXTRA, lanes)]
        + [whole(entry) for entry in (gain, w_in, w_out, conv, head)],
        out_specs=[rows_spec(width), rows_spec(PROJ_LANES), rows_spec(width + EXTRA), rows_spec(WIDE)],
        out_shape=[
            jax.ShapeDtypeStruct((total, width), bf16),
            jax.ShapeDtypeStruct((total, PROJ_LANES), f32),
            jax.ShapeDtypeStruct((total, width + EXTRA), bf16),
            jax.ShapeDtypeStruct((total, WIDE), bf16),
        ],
        compiler_params=params(),
        name="mixer_forward",
    )(gathered, gathered, gain, w_in, w_out, conv, head)


def mixer_backward_kernel(
    count, grad_ref, inner_ref, beside_ref, proj_ref, w_in_ref, w_out_ref, conv_ref, head_ref, rate_ref,
    normed_ref, proj_grad_ref, conv_grad_ref, head_grad_ref,
):
    heads = HEADS // 16
    conv, head = conv_ref[...], head_ref[...]

    @pl.when(pl.program_id(0) == 0)
    def _():
        conv_grad_ref[...] = jnp.zeros_like(conv_grad_ref)
        head_grad_ref[...] = jnp.zeros_like(head_grad_ref)

    grad_mixed = lax.dot_general(
        grad_ref[...], w_out_ref[...], (((1,), (1,)), ((), ())), preferred_element_type=f32
    )
    lane = lax.broadcasted_iota(jnp.int32, (1, EXTRA), 1)
    for index in range(grad_ref.shape[0] // count):
        part = pl.ds(index * count, count)
        place = beside_ref[part, :].astype(f32)[:, 1:2]
        found = block_scan(proj_ref[part, :], place, conv, head)
        inner = inner_ref[part, :].astype(f32)
        inner = inner[:, 0:1] + inner[:, 1:2] + inner[:, 2:3]
        gate, gate_sig, scan = found["gate"], found["gate_sig"], found["scan"]
        d_gated = grad_mixed[index * count : (index + 1) * count] * rows_of(head, 3) - found["gated"] * inner
        d_scan = d_gated * (gate * gate_sig)
        d_gate = d_gated * scan * (gate_sig * (1.0 + gate * (1.0 - gate_sig)))
        conv_out = found["conv_out"]
        d_values = [None] * (WIDE // EXTRA)
        d_scores = jnp.zeros((count, count), f32)
        column_sums = jnp.zeros((count, EXTRA), f32)
        direct, taken = [], []
        for number in range(heads):
            tile = number // 2
            decay, mixing = found["decays"][number]
            value, mine = found["values"][number]
            d_part = d_scan[:, tile * EXTRA : (tile + 1) * EXTRA]
            back = exact(mixing, d_part, ((0,), (0,))) * mine
            d_values[tile] = back if d_values[tile] is None else d_values[tile] + back
            d_mixing = exact(d_part, value, ((1,), (1,)))
            d_decayed = d_mixing * decay
            d_scores = d_scores + d_decayed * rows_of(found["step_rows"], number)
            d_spread = d_mixing * mixing
            direct.append(jnp.sum(d_decayed * found["scores"], axis=0, keepdims=True))
            taken.append(jnp.sum(d_spread, axis=0, keepdims=True))
            sums = jnp.sum(d_spread, axis=1, keepdims=True)
            column_sums = column_sums + jnp.where(lane == number, sums, 0.0)
            head_grad_ref[16 + number : 17 + number, :] += jnp.sum(d_part * value, axis=0, keepdims=True)
        d_values = jnp.concatenate(d_values, axis=1) + rows_of(head, 2) * d_scan
        empty = jnp.zeros((8 - heads, count), f32)
        d_cumul = column_sums.T[:8] - jnp.concatenate(taken + [empty], axis=0)
        d_rated = exact(d_cumul, found["lower"], ((1,), (0,)))
        step_rows = found["step_rows"][:8]
        d_step = jnp.concatenate(direct + [empty], axis=0) + d_rated * rate_ref[...]
        d_raw = d_step * sigmoid(found["raw"]).T[:8]
        head_grad_ref[0:8, :] += d_rated * step_rows
        head_grad_ref[8:16, :] += d_raw
        d_raw = jnp.concatenate([d_raw, jnp.zeros((EXTRA - 8, count), f32)], axis=0).T
        d_b = exact(d_scores, conv_out[:, STATE : 2 * STATE], ((0,), (0,)))
        d_c = exact(d_scores, conv_out[:, :STATE], ((1,), (0,)))
        d_out = jnp.concatenate([d_b, d_c, d_values], axis=1)
        conv_sig = found["conv_sig"]
        d_total = d_out * (conv_sig * (1.0 + found["total"] * (1.0 - conv_sig)))
        conv_grad_ref[KERNEL : KERNEL + 1, :] += jnp.sum(d_total, axis=0, keepdims=True)
        d_conv = rows_of(conv, KERNEL - 1) * d_total
        for offset in range(KERNEL):
            row = KERNEL - 1 - offset
            conv_grad_ref[row : row + 1, :] += jnp.sum(d_total * found["taps"][offset], axis=0, keepdims=True)
            if offset:
                kept = d_total * (place >= offset).astype(f32)
                d_conv = d_conv + rows_of(conv, row) * pltpu.roll(kept, count - offset, 0)
        proj_grad_ref[part, :] = jnp.concatenate([d_conv, d_gate, d_raw], axis=1).astype(bf16)
    normed_ref[...] = lax.dot_general(
        proj_grad_ref[...], w_in_ref[...], (((1,), (1,)), ((), ())), preferred_element_type=f32
    ).astype(bf16)


def mixer_backward(grads, gathered, proj, width, count, w_in, w_out, conv, head, rate):
    total = grads.shape[0]
    rows = 4 * count
    lanes = width // EXTRA

    def rows_spec(extent, column=0):
        return pl.BlockSpec((rows, extent), lambda step: (step, column))

    conv_shape = jax.ShapeDtypeStruct(conv.shape, f32)
    head_shape = jax.ShapeDtypeStruct((24, EXTRA), f32)
    return pl.pallas_call(
        lambda *refs: mixer_backward_kernel(count, *refs),
        grid=(total // rows,),
        in_specs=[rows_spec(width), rows_spec(EXTRA, lanes), rows_spec(EXTRA, lanes), rows_spec(PROJ_LANES)]
        + [whole(entry) for entry in (w_in, w_out, conv, head, rate)],
        out_specs=[rows_spec(width), rows_spec(PROJ_LANES), whole(conv_shape), whole(head_shape)],
        out_shape=[
            jax.ShapeDtypeStruct((total, width), bf16),
            jax.ShapeDtypeStruct((total, PROJ_LANES), bf16),
            conv_shape,
            head_shape,
        ],
        compiler_params=params(),
        name="mixer_backward",
    )(grads, grads, gathered, proj, w_in, w_out, conv, head, rate)


def selection(rank_ref, experts, slots):
    number = lax.broadcasted_iota(jnp.int32, (slots, rank_ref.shape[2]), 0)
    return [rank_ref[0, k : k + 1, :] == number for k in range(experts)]


def dispatch_kernel(experts, slots, weigh, rank_ref, weight_ref, values_ref, out_ref, *weights_ref):
    chosen = selection(rank_ref, experts, slots)
    select = jnp.concatenate([entry.astype(f32) for entry in chosen], axis=0).astype(bf16)
    rows = jnp.dot(select, values_ref[...], preferred_element_type=f32)
    for k in range(experts):
        part = rows[k * slots : (k + 1) * slots]
        if weigh:
            own = jnp.where(chosen[k], weight_ref[0, k : k + 1, :], 0.0)
            own = jnp.sum(own, axis=1, keepdims=True)
            part = part * own
            weights_ref[0][k] = jnp.broadcast_to(own, (slots, EXTRA))
        out_ref[k] = part.astype(bf16)


def dispatch(values, rank, weight, experts, slots, weigh):
    pairs, _, tokens = rank.shape
    width = values.shape[1]
    rank_spec = pl.BlockSpec((1,) + rank.shape[1:], lambda step: (step, 0, 0))
    specs = [pl.BlockSpec((experts, slots, width), lambda step: (0, step, 0))]
    shapes = [jax.ShapeDtypeStruct((experts, pairs * slots, width), bf16)]
    if weigh:
        specs.append(pl.BlockSpec((experts, slots, EXTRA), lambda step: (0, step, 0)))
        shapes.append(jax.ShapeDtypeStruct((experts, pairs * slots, EXTRA), f32))
    return pl.pallas_call(
        lambda *refs: dispatch_kernel(experts, slots, weigh, *refs),
        grid=(pairs,),
        in_specs=[rank_spec, rank_spec, pl.BlockSpec((tokens, width), lambda step: (step, 0))],
        out_specs=specs,
        out_shape=shapes,
        compiler_params=params(),
        name="dispatch",
    )(rank, weight, values)


def combine_kernel(experts, slots, turned, rank_ref, rows_ref, left_ref, right_ref, out_ref):
    chosen = selection(rank_ref, experts, slots)
    select = jnp.concatenate([entry.astype(f32) for entry in chosen], axis=0).astype(bf16)
    rows = jnp.concatenate([rows_ref[k] for k in range(experts)], axis=0)
    total = lax.dot_general(select, rows, (((0,), (0,)), ((), ())), preferred_element_type=f32)
    dims = ((1,), (1,)) if turned else ((1,), (0,))
    total = total + lax.dot_general(
        left_ref[...], right_ref[...], (dims, ((), ())), preferred_element_type=f32
    )
    out_ref[...] = total.astype(bf16)


def combine(rows, rank, left, right, slots, turned):
    pairs, _, tokens = rank.shape
    experts, _, width = rows.shape
    return pl.pallas_call(
        lambda *refs: combine_kernel(experts, slots, turned, *refs),
        grid=(pairs,),
        in_specs=[
            pl.BlockSpec((1,) + rank.shape[1:], lambda step: (step, 0, 0)),
            pl.BlockSpec((experts, slots, width), lambda step: (0, step, 0)),
            pl.BlockSpec((tokens, left.shape[1]), lambda step: (step, 0)),
            whole(right),
        ],
        out_specs=pl.BlockSpec((tokens, width), lambda step: (step, 0)),
        out_shape=jax.ShapeDtypeStruct((pairs * tokens, width), bf16),
        compiler_params=params(),
        name="combine",
    )(rank, rows, left, right)


def expert_kernel(
    rows_ref, grad_ref, weight_ref, gate_ref, up_ref, down_ref, act_ref, g_ref, u_ref, back_ref, out_ref
):
    rows, gate_w, up_w, down_w = rows_ref[0], gate_ref[0], up_ref[0], down_ref[0]
    turned = (((1,), (1,)), ((), ()))
    gate = jnp.dot(rows, gate_w, preferred_element_type=f32)
    up = jnp.dot(rows, up_w, preferred_element_type=f32)
    sig = sigmoid(gate)
    silu = gate * sig
    act = (silu * up).astype(bf16)
    d_act = lax.dot_general(grad_ref[0], down_w, turned, preferred_element_type=f32)
    d_gate = (d_act * up * (sig * (1.0 + gate * (1.0 - sig)))).astype(bf16)
    d_up = (d_act * silu).astype(bf16)
    act_ref[0], g_ref[0], u_ref[0] = act, d_gate, d_up
    back = lax.dot_general(d_gate, gate_w, turned, preferred_element_type=f32)
    back = back + lax.dot_general(d_up, up_w, turned, preferred_element_type=f32)
    back_ref[0] = back.astype(bf16)
    out = jnp.dot(act, down_w, preferred_element_type=f32) * weight_ref[0][:, :1]
    out_ref[0] = out.astype(bf16)


def expert_pass(rows, grads, weights, gate, up, down):
    experts, lanes, width = rows.shape
    hidden = gate.shape[2]

    def each(entry):
        return pl.BlockSpec((1,) + entry.shape[1:], lambda step: (step, 0, 0))

    inputs = (rows, grads, weights, gate, up, down)
    small = jax.ShapeDtypeStruct((experts, lanes, hidden), bf16)
    large = jax.ShapeDtypeStruct((experts, lanes, width), bf16)
    outputs = [small] * 3 + [large] * 2
    return pl.pallas_call(
        expert_kernel,
        grid=(experts,),
        in_specs=[each(entry) for entry in inputs],
        out_specs=[each(entry) for entry in outputs],
        out_shape=outputs,
        compiler_params=params(),
        name="expert_pass",
    )(*inputs)


def local(
    hidden_in,
    cotangent,
    routes,
    route_gates,
    lengths,
    in_proj,
    out_proj,
    conv_weight,
    conv_bias,
    norm_gain,
    mix_gain,
    ffn_gain,
    shared_gate,
    shared_up,
    shared_down,
    expert_gate,
    expert_up,
    expert_down,
    decay_log,
    step_bias,
    skip_gain,
):
    tokens, width = hidden_in.shape
    top = routes.shape[1]
    replicas = lax.axis_size("dp")
    groups = lax.axis_size("z") * 4
    devices = replicas * groups
    core = lax.axis_index("core")
    column = lax.axis_index("z") * 2 + lax.axis_index("y")
    place = column * 2 + core
    heads = HEADS // groups
    own = heads * HEAD_DIM
    half = groups // 2
    rows_in = in_proj.shape[0]
    hidden_units = shared_gate.shape[1]
    unit = hidden_units // devices
    units = hidden_units // groups
    local_experts = expert_gate.shape[0]
    capacity = 2 * tokens * top // (local_experts * groups)
    first_head = core * (HEADS // 2) + column * heads
    first_channel = first_head * HEAD_DIM

    small = (conv_weight.reshape(-1), conv_bias, norm_gain, mix_gain, ffn_gain)
    small_sizes = [entry.shape[0] for entry in small]
    small_lanes = -(-sum(small_sizes) // rows_in)
    small_flat = jnp.concatenate(small)
    small_flat = jnp.pad(small_flat, (0, small_lanes * rows_in - small_flat.shape[0]))

    def by_place(block):
        block = block.reshape(rows_in, 2, half, own).transpose(2, 1, 0, 3)
        return block.reshape(groups, rows_in, own)

    def by_unit(block):
        block = block.reshape(rows_in, replicas, groups, unit).transpose(2, 0, 1, 3)
        return block.reshape(groups, rows_in, units)

    pack = jnp.concatenate(
        [
            by_place(in_proj[:, :INNER]),
            by_place(in_proj[:, INNER : 2 * INNER]),
            by_unit(shared_gate),
            by_unit(shared_up),
        ],
        axis=2,
    )
    pack = lax.all_to_all(pack, GROUP, split_axis=0, concat_axis=0, tiled=True)
    pack = dp_gather_rows(pack.reshape(1, groups * rows_in, pack.shape[2]), 0)
    pack = pack.reshape(devices * rows_in, pack.shape[2])

    spread = jnp.concatenate([in_proj[:, 2 * INNER :], small_flat.reshape(rows_in, small_lanes)], axis=1)
    spread = jnp.pad(spread, ((0, 0), (0, -spread.shape[1] % EXTRA)))
    spread = dp_gather_rows(spread[None], 0).reshape(replicas * rows_in, -1)

    if replicas == 2:
        both = swap(out_proj, "core")
        both = jnp.concatenate(
            [jnp.where(core == 0, out_proj, both), jnp.where(core == 0, both, out_proj)]
        )
        w_out = jnp.where(lax.axis_index("dp") == core, both, swap(both, "dp"))
    else:
        w_out = lax.dynamic_slice_in_dim(
            lax.all_gather(out_proj, ALL, axis=0, tiled=True), first_channel, own, 0
        )
    w_shared_down = dp_gather_rows(shared_down[None], 0).reshape(units, width)

    bounds = jnp.cumsum(lengths[0])
    slot = jnp.arange(tokens, dtype=jnp.int32)
    runs = jnp.sum((slot[:, None] >= bounds[None, : SEQ_SLOTS - 1]).astype(jnp.int32), axis=1)
    live = (runs < SEQ_SLOTS - 1).astype(f32)[:, None]
    starts = jnp.concatenate([jnp.zeros((1,), jnp.int32), bounds[: SEQ_SLOTS - 1].astype(jnp.int32)])
    place_in_run = slot - jnp.sum(jnp.where(runs[:, None] == jnp.arange(SEQ_SLOTS), starts, 0), axis=1)
    beside = [runs.astype(bf16)[:, None], place_in_run.astype(bf16)[:, None], routes.astype(bf16), *split_three(route_gates)]
    beside = jnp.concatenate(beside, axis=1)
    beside = jnp.pad(beside, ((0, 0), (0, EXTRA - beside.shape[1])))
    w_gate, w_up, w_down = (
        lax.all_gather(entry, "dp", axis=1, tiled=True)
        for entry in (expert_gate, expert_up, expert_down)
    )
    spread = jnp.pad(spread, ((0, tokens - spread.shape[0]), (0, 0)))
    gathered = gather(jnp.concatenate([hidden_in, beside, spread], axis=1))
    at = width + 2
    routes_all = gathered[:, at : at + top].astype(jnp.int32)
    gates_all = join_three([gathered[:, at + k * top : at + (k + 1) * top] for k in (1, 2, 3)])

    number = jnp.arange(groups, dtype=jnp.int32)
    back_z = (lax.axis_index("z") - number // 4) % (groups // 4)
    other_y = (number // 2) % 2 != lax.axis_index("y")
    other_core = number % 2 != core
    order = other_core * half + back_z * 2 + other_y
    spread = gathered[:, width + EXTRA :].reshape(groups, tokens, -1)[:, : replicas * rows_in]
    spread = spread[order].reshape(groups, replicas, rows_in, -1).transpose(1, 0, 2, 3)
    spread = spread.reshape(devices, rows_in, -1)
    small_at = 2 * STATE + HEADS
    small_all = spread[:, :, small_at : small_at + small_lanes].reshape(devices, -1)
    pieces = []
    start = 0
    for size in small_sizes:
        pieces.append(small_all[:, start : start + size].reshape(-1).astype(f32))
        start += size
    conv_w_all = pieces[0].reshape(CONV_CH, KERNEL).T
    conv_b_all, norm_gain_all, mix_gain_all, ffn_gain_all = pieces[1:]
    spread = spread.reshape(devices * rows_in, -1)
    w_step = lax.dynamic_slice_in_dim(spread, 2 * STATE + first_head, heads, 1)
    w_step = jnp.pad(w_step, ((0, 0), (0, EXTRA - heads)))
    widen = ((0, 0), (0, WIDE - own))
    w_in = [spread[:, : 2 * STATE], jnp.pad(pack[:, own : 2 * own], widen), jnp.pad(pack[:, :own], widen), w_step]
    w_in = jnp.concatenate(w_in, axis=1)
    w_shared = pack[:, 2 * own :]

    def own_channels(rows):
        return lax.dynamic_slice_in_dim(rows, first_channel, own, rows.ndim - 1)

    conv = jnp.concatenate([conv_w_all, conv_b_all[None]], axis=0)
    conv = jnp.concatenate([conv[:, INNER:], own_channels(conv)], axis=1)
    conv = jnp.pad(conv, ((0, 8 - conv.shape[0]), (0, CONV_LANES - conv.shape[1])))

    def own_heads(row):
        return lax.dynamic_slice_in_dim(row, first_head, heads, 0)

    def lanes_of(row):
        return jnp.pad(row, (0, WIDE - row.shape[0]))

    rate = -jnp.exp(own_heads(decay_log))
    head = [
        lanes_of(own_heads(step_bias)),
        lanes_of(rate),
        lanes_of(jnp.repeat(own_heads(skip_gain), HEAD_DIM)),
        lanes_of(own_channels(mix_gain_all)),
    ]
    head = jnp.pad(jnp.stack(head), ((0, 4), (0, 0)))
    rate_rows = jnp.broadcast_to(jnp.pad(rate, (0, 8 - heads))[:, None], (8, EXTRA))
    w_out = jnp.pad(w_out, ((0, WIDE - own), (0, 0)))

    normed, proj, mixed_part, scaled = mixer_forward(
        gathered, width, tokens, norm_gain_all[None], w_in, w_out, conv, head
    )
    grad_out = cotangent.astype(f32)
    branch = (grad_out * live).astype(bf16)
    branch_all = gather(after(branch, gathered))
    mixed_part, branch_all = lax.optimization_barrier((mixed_part, branch_all))
    mixed_sum = scatter(mixed_part)
    mix_rms = lax.rsqrt(jnp.sum(mixed_sum[:, width:], axis=1, keepdims=True) / INNER + epsilon)
    mixer_out = mixed_sum[:, :width] * mix_rms
    input_rows = hidden_in.astype(f32)
    resid = input_rows + live * mixer_out
    ffn_rms = lax.rsqrt(jnp.mean(resid * resid, axis=1, keepdims=True) + epsilon)
    ffn_hat = resid * ffn_rms
    ffn_low = (ffn_hat * ffn_gain_all).astype(bf16)

    ffn_all = gather(ffn_low)

    shared_gu = matmul(ffn_all, w_shared)

    def swiglu(both):
        extent = both.shape[-1] // 2
        return jax.nn.silu(both[..., :extent]) * both[..., extent:]

    shared_act, shared_back = jax.vjp(swiglu, shared_gu)
    shared_low = shared_act.astype(bf16)
    (grad_shared_gu,) = shared_back(matmul(branch_all, w_shared_down, (((1,), (1,)), ((), ()))))
    shared_gu_low = grad_shared_gu.astype(bf16)

    pairs = groups // 2
    pair_tokens = 2 * tokens
    pair_slots = 2 * capacity
    lanes = pairs * pair_slots
    numbers = place * local_experts + jnp.arange(local_experts, dtype=jnp.int32)
    named = routes_all[:, None, :] == numbers[None, :, None]
    member = jnp.any(named, axis=2).T.reshape(local_experts, pairs, pair_tokens)
    weight = jnp.sum(jnp.where(named, gates_all[:, None, :], 0.0), axis=2).T
    weight = weight.reshape(local_experts, pairs, pair_tokens)
    below = jnp.triu(jnp.ones((pair_tokens, pair_tokens), bf16))
    rank = matmul(member.astype(bf16), below)
    rank = jnp.where(member, rank.astype(jnp.int32) - 1, -1).transpose(1, 0, 2)
    rank = jnp.pad(rank, ((0, 0), (0, 8 - local_experts), (0, 0)), constant_values=-1)
    weight = jnp.pad(weight.transpose(1, 0, 2), ((0, 0), (0, 8 - local_experts), (0, 0)))
    d_row, slot_weight = dispatch(branch_all, rank, weight, local_experts, pair_slots, True)
    (expert_in,) = dispatch(ffn_all, rank, weight, local_experts, pair_slots, False)
    act_low, g_low, u_low, d_in_row, expert_row = expert_pass(
        expert_in, d_row, slot_weight, w_gate, w_up, w_down
    )
    half_grad = (((1,), (1,)), ((0,), (0,)))

    def expert_grad(left, right):
        total = matmul(left, right, half_grad).astype(bf16)
        return lax.psum_scatter(total, "dp", scatter_dimension=1, tiled=True).astype(f32)

    grad_ffn_part = combine(d_in_row, rank, shared_gu_low, w_shared, pair_slots, True)
    grad_ffn = scatter(grad_ffn_part)
    (expert_in, expert_row, act_low, shared_low, ffn_all) = after(
        (expert_in, expert_row, act_low, shared_low, ffn_all), grad_ffn_part
    )
    grad_down = expert_grad(act_low, d_row)
    grad_gate = expert_grad(expert_in, g_low)
    grad_up = expert_grad(expert_in, u_low)
    branch_part = combine(expert_row, rank, shared_low, w_shared_down, pair_slots, False)

    grad_ffn_gain = jnp.sum(grad_ffn * ffn_hat, axis=0)
    scaled_ffn = grad_ffn * ffn_gain_all
    grad_resid = grad_out + ffn_rms * (
        scaled_ffn - ffn_hat * jnp.mean(scaled_ffn * ffn_hat, axis=1, keepdims=True)
    )
    d_mixer = (grad_resid * live).astype(bf16).astype(f32)
    inner_term = jnp.sum(d_mixer * mixer_out, axis=1, keepdims=True) * mix_rms * mix_rms / INNER
    inner_pack = jnp.pad(jnp.concatenate(split_three(inner_term), axis=1), ((0, 0), (0, EXTRA - 3)))
    d_mixer_pack = jnp.concatenate([(d_mixer * mix_rms).astype(bf16), inner_pack], axis=1)
    d_mixer_all = gather(d_mixer_pack)
    output = (resid + live * scatter(after(branch_part, d_mixer_all))).astype(bf16)
    grad_normed_part, proj_low, conv_grads, head_grads = mixer_backward(
        d_mixer_all, gathered, proj, width, tokens, w_in, w_out, conv, head, rate_rows
    )
    grad_normed_part, output = lax.optimization_barrier((grad_normed_part, output))
    grad_normed = scatter(grad_normed_part)
    normed, scaled = after((normed, scaled), grad_normed_part)
    grad_w_in = matmul(normed, proj_low, (((0,), (0,)), ((), ())))
    grad_out_rows = matmul(scaled, d_mixer_all[:, :width], (((0,), (0,)), ((), ())))[:own]
    shared_low, ffn_all = after((shared_low, ffn_all), d_mixer_all)
    grad_shared_down = matmul(shared_low, branch_all, (((0,), (0,)), ((), ())))
    grad_shared_w = matmul(ffn_all, shared_gu_low, (((0,), (0,)), ((), ())))

    value_at, gate_at = 2 * STATE, CONV_LANES
    grad_pack = jnp.concatenate(
        [
            grad_w_in[:, gate_at : gate_at + own],
            grad_w_in[:, value_at : value_at + own],
            grad_w_in[:, : 2 * STATE],
            grad_w_in[:, CONV_LANES + WIDE :],
            grad_shared_w,
        ],
        axis=1,
    )
    proj_lanes = 2 * own + 2 * STATE + EXTRA
    grad_pack = dp_scatter_rows(grad_pack, 0).astype(bf16).reshape(groups, rows_in, -1)
    grad_pack = lax.all_to_all(grad_pack, GROUP, split_axis=0, concat_axis=0, tiled=True).astype(f32)

    def from_place(block):
        block = block.reshape(half, 2, rows_in, block.shape[2]).transpose(2, 1, 0, 3)
        return block.reshape(rows_in, -1)

    def from_unit(block):
        block = block.reshape(groups, rows_in, replicas, unit).transpose(1, 2, 0, 3)
        return block.reshape(rows_in, hidden_units)

    both_at = 2 * own + 2 * STATE
    grad_in_proj = jnp.concatenate(
        [
            from_place(grad_pack[:, :, :own]),
            from_place(grad_pack[:, :, own : 2 * own]),
            jnp.sum(grad_pack[:, :, 2 * own : both_at], axis=0),
            from_place(grad_pack[:, :, both_at : both_at + heads]),
        ],
        axis=1,
    )
    grad_shared_gate = from_unit(grad_pack[:, :, proj_lanes : proj_lanes + units])
    grad_shared_up = from_unit(grad_pack[:, :, proj_lanes + units :])
    grad_shared_down = dp_scatter_rows(grad_shared_down.reshape(replicas, unit, width), 0)[0]
    if replicas == 2:
        mine = lax.axis_index("dp") == core
        received = swap(grad_out_rows.astype(bf16), "dp").astype(f32)
        total = (grad_out_rows + received).reshape(2, own // 2, width)
        passed = swap(lax.dynamic_index_in_dim(total, 1 - core, 0, keepdims=False), "core")
        grad_out_proj = jnp.where(mine, lax.dynamic_index_in_dim(total, core, 0, keepdims=False), passed)
    else:
        full = jnp.zeros((INNER, width), f32)
        full = lax.dynamic_update_slice_in_dim(full, grad_out_rows, first_channel, 0)
        grad_out_proj = lax.psum_scatter(full, ALL, scatter_dimension=0, tiled=True)
    grad_mix_gain = jnp.sum(grad_out_proj * out_proj.astype(f32), axis=1) / mix_gain.astype(f32)
    grad_norm_gain = jnp.sum(grad_in_proj * in_proj.astype(f32), axis=1) / norm_gain.astype(f32)

    def to_owner(part):
        rows_part = jnp.zeros((part.shape[0], CONV_CH), f32)
        values = part[:, 2 * STATE : 2 * STATE + own]
        rows_part = lax.dynamic_update_slice_in_dim(rows_part, values, first_channel, 1)
        rows_part = lax.dynamic_update_slice_in_dim(rows_part, part[:, : 2 * STATE], INNER, 1)
        return rows_part.reshape(part.shape[0], devices, -1).transpose(1, 0, 2).reshape(devices, -1)

    def head_row(part):
        return lax.dynamic_update_slice_in_dim(jnp.zeros((HEADS,), f32), part, first_head, 0)

    head_grads = jnp.sum(head_grads.reshape(3, 8, EXTRA)[:, :heads], axis=2)
    head_rows = jnp.concatenate([head_row(entry) for entry in (head_grads[0] * rate, *head_grads[1:])])
    sums = jnp.concatenate(
        [
            to_owner(conv_grads[: KERNEL + 1]),
            grad_ffn_gain.reshape(devices, -1),
            jnp.broadcast_to(head_rows[None], (devices, 3 * HEADS)),
        ],
        axis=1,
    )
    sums = lax.all_to_all(sums, ALL, split_axis=0, concat_axis=0, tiled=True)
    sums = jnp.sum(sums, axis=0)
    channels = CONV_CH // devices
    grad_conv_weight = sums[: KERNEL * channels].reshape(KERNEL, channels).T
    grad_conv_bias = sums[KERNEL * channels : (KERNEL + 1) * channels]
    at = (KERNEL + 1) * channels
    grad_ffn_gain = sums[at : at + rows_in]
    at += rows_in
    grad_decay, grad_stepb, grad_skip = (sums[at + k * HEADS : at + (k + 1) * HEADS] for k in range(3))

    in_rms = lax.rsqrt(jnp.mean(input_rows * input_rows, axis=1, keepdims=True) + epsilon)
    in_hat = input_rows * in_rms
    scaled_in = grad_normed * norm_gain_all
    grad_input = grad_resid + in_rms * (
        scaled_in - in_hat * jnp.mean(scaled_in * in_hat, axis=1, keepdims=True)
    )
    return (
        output,
        grad_input,
        grad_in_proj,
        grad_out_proj,
        grad_conv_weight,
        grad_conv_bias,
        grad_norm_gain,
        grad_mix_gain,
        grad_ffn_gain,
        grad_shared_gate,
        grad_shared_up,
        grad_shared_down,
        grad_gate,
        grad_up,
        grad_down,
        grad_decay,
        grad_stepb,
        grad_skip,
    )


def solution(mesh):
    replicas, groups = mesh.shape["dp"], mesh.shape["expert"]
    inner = Mesh(mesh.devices.reshape(replicas, groups // 4, 2, 2), ALL)
    flat = P(ALL)
    expert = P(GROUP, "dp", None)
    return jax.shard_map(
        local,
        mesh=inner,
        in_specs=(flat,) * 15 + (expert,) * 3 + (P(),) * 3,
        out_specs=(flat,) * 12 + (expert,) * 3 + (P(),) * 3,
        check_vma=False,
    )
```

time: 988 us -> 805 us (0.81)
  waiting for transfers between devices: 442 us -> 297 us
  matrix products: 177 us -> 50.3 us
  Pallas kernels: 0 us -> 125 us
  other arithmetic: 132 us -> 83.5 us
  between operations: 3.43 us -> 15.5 us
    ppermute x94 -> x49, waiting for transfers between devices: 310 us -> 131 us  [swap(): return lax.ppermute(value, axis, [(0, 1), (1, 0)])]
    pallas_call x0 -> x7, Pallas kernels: none -> 125 us  [the longest x1 43.9 us: mixer_backward(): pl.pallas_call(lambda *refs: mixer_backward_kernel(count, *refs), grid=(t...]
    dot_general x22 -> x10, matrix products: 121 us -> 50.3 us  [matmul(): lax.dot_general(left, right, dims, precision=precision, preferred_element...]
    dot_general x10 -> x0, matrix products: 55.7 us -> none  [the longest x3 22.4 us: mixer_core(): scan = jnp.einsum('bhij,bhjp->bhip', mixing, values, precision=high)]
    all_to_all x1, waiting for transfers between devices: 0.61 us -> 33.7 us  [local(): sums = lax.all_to_all(sums, ALL, split_axis=0, concat_axis=0, tiled=True)]
    ppermute x24, waiting for transfers between devices: 131 us -> 105 us  [ring(): return lax.ppermute(value, 'z', [(k, (k + 1) % size) for k in range(size)])]
    add x4 -> x1, other arithmetic: 22.5 us -> 1.28 us  [scatter(): ring(total).astype(f32) + pairs[0, 0].astype(f32) + there[-1].astype(f32)]
    all_to_all x1, waiting for transfers between devices: 0.01 us -> 20.5 us  [local(): pack = lax.all_to_all(pack, GROUP, split_axis=0, concat_axis=0, tiled=True)]
  transfers between devices with their start and end apart: 121 -> 82, of which waited for: 46 -> 48; matrix products, arithmetic and copies ran while one was open for 27% -> 27% of each run, Pallas kernels for 0% -> 12%
where the time goes in v2:
time: 805 us; the launch traced here: 791 us
  waiting for transfers between devices  297 us (37%)
  Pallas kernels  125 us (16%)
  local copies, waits for them, and re-layouts  115 us (14%)
  starting transfers between devices  104 us (13%)
  other arithmetic  83.5 us (10%)
  matrix products  50.3 us (6%)
  between operations  15.5 us (2%)
    ppermute x49, waiting for transfers between devices, swap(): return lax.ppermute(value, axis, [(0, 1), (1, 0)])  131 us
    ppermute x24, waiting for transfers between devices, ring(): return lax.ppermute(value, 'z', [(k, (k + 1) % size) for k in range(size)])  105 us
    ppermute x49, starting transfers between devices, swap(): return lax.ppermute(value, axis, [(0, 1), (1, 0)])  58.6 us
    dot_general x10, matrix products, matmul(): lax.dot_general(left, right, dims, precision=precision, preferred_element...  50.3 us
    pallas_call x1, Pallas kernels, mixer_backward(): pl.pallas_call(lambda *refs: mixer_backward_kernel(count, *refs), grid=(t...  43.9 us
    unnamed x119, local copies, waits for them, and re-layouts  39.7 us
    all_to_all x1, waiting for transfers between devices, local(): sums = lax.all_to_all(sums, ALL, split_axis=0, concat_axis=0, tiled=True)  33.7 us
    pallas_call x1, Pallas kernels, mixer_forward(): pl.pallas_call(lambda *refs: mixer_forward_kernel(count, *refs), grid=(to...  25.3 us
  transfers between devices with their start and end apart: 82, of which 48 were waited for; matrix products, arithmetic and copies ran while one was open for 27% of the time, Pallas kernels for 12%

profile of v2, /device:TPU:13, one launch (start us, length us, event | category | flops | bytes accessed | tf_op | source)
XLA Modules:
  0.0 790.7 jit_solution(18103522454039828460)
XLA Ops:
  19.7 10.9 %collective-permute-done.1 = bf16[128,2048]{1,0:T(8,128)(2,1)S(1)} collective-permute-done((bf16[128,2048]{1,0:T(8,128)(2,1)S(1)}, bf16[128,2048]{1,0:T(8,128)(2,1)S(1)}, u32[]{:S(2)}, u32[]{:S(2)}) %collective-permute-start.1) | collective-permute-done | bytes 524320 | tf_op jit(solution)/shard_map/ppermute | solution.py:31
  33.1 9.7 %collective-permute-done.4 = bf16[128,2048]{1,0:T(8,128)(2,1)S(1)} collective-permute-done((bf16[128,2048]{1,0:T(8,128)(2,1)S(1)}, bf16[128,2048]{1,0:T(8,128)(2,1)S(1)}, u32[]{:S(2)}, u32[]{:S(2)}) %collective-permute-start.4) | collective-permute-done | bytes 524320 | tf_op jit(solution)/shard_map/ppermute | solution.py:36
  48.7 6.3 collective-permute-done.6
  59.6 5.8 collective-permute-done.7
  66.5 4.5 collective-permute-start.8
  75.4 7.7 all-to-all-start
  83.9 5.2 constant_dynamic-update-slice_fusion.8.refs_0_.refs_1_.refs_2_
  90.6 20.5 %all-to-all-done = bf16[16,48,512]{2,1,0:T(8,128)(2,1)S(1)} async-done(((bf16[16,48,512]{2,1,0:T(8,128)(2,1)}), bf16[16,48,512]{2,1,0:T(8,128)(2,1)S(1)}, u32[]{:S(2)}, u32[]{:S(2)}) %all-to-all-start) | async-done | bytes 786464 | tf_op jit(solution)/shard_map/all_to_all | solution.py:519
  115.2 7.8 collective-permute-done.15
  125.4 8.0 %collective-permute-done.17 = bf16[128,1536]{1,0:T(8,128)(2,1)S(1)} collective-permute-done((bf16[128,1536]{1,0:T(8,128)(2,1)S(1)}, bf16[128,1536]{1,0:T(8,128)(2,1)S(1)}, u32[]{:S(2)}, u32[]{:S(2)}) %collective-permute-start.17) | collective-permute-done | bytes 393248 | tf_op jit(solution)/shard_map/ppermute | solution.py:36
  135.6 7.2 collective-permute-done.18
  147.0 4.9 collective-permute-done.9
  164.8 25.3 %mixer_forward.1 = (bf16[2048,1536]{1,0:T(8,128)(2,1)}, f32[2048,896]{1,0:T(8,128)}, bf16[2048,1664]{1,0:T(8,128)(2,1)}, bf16[2048,256]{1,0:T(8,128)(2,1)}) custom-call(bf16[2048,2048]{1,0:T(8,128)(2,1)} %constant_dynamic-update-slice_fusion.8.refs_0_.refs_1_.refs_2_, bf16[2048,2048]{1,0:T(8,128)(2,1)} %constant_dynamic-update-slice_fusion.8.refs_0_.refs_1_.refs_2_, ...), custom_call_target="tpu_custom_call" | custom-call | tf_op jit(solution)/shard_map/mixer_forward/pallas_call | solution.py:220
  193.8 6.3 fusion.86
  201.9 5.8 collective-permute-done.20
  209.4 4.8 fusion
  216.5 9.7 %collective-permute-done.21 = bf16[128,1664]{1,0:T(8,128)(2,1)S(1)} collective-permute-done((bf16[128,1664]{1,0:T(8,128)(2,1)S(1)}, bf16[128,1664]{1,0:T(8,128)(2,1)S(1)}, u32[]{:S(2)}, u32[]{:S(2)}) %collective-permute-start.21) | collective-permute-done | bytes 426016 | tf_op jit(solution)/shard_map/ppermute | solution.py:31
  228.5 6.8 collective-permute-done.23
  238.3 6.2 collective-permute-done.25
  247.2 6.4 collective-permute-done.27
  262.5 6.7 collective-permute-done.29
  272.0 6.2 collective-permute-done.31
  282.9 5.3 collective-permute-done.33
  291.0 5.9 collective-permute-done.34
  297.9 10.6 %collective-permute-start.35 = (bf16[1024,1536]{1,0:T(8,128)(2,1)}, bf16[1024,1536]{1,0:T(8,128)(2,1)}, u32[]{:S(2)}, u32[]{:S(2)}) collective-permute-start(bf16[1024,1536]{1,0:T(8,128)(2,1)} %get-tuple-element.188), channel_id=1, source_target_pairs={{0,1},{1,0},{2,3},{3,2},{4,5},{5,4},{6,7},{7,6},{8,9},{9,8},{10,11... | collective-permute-start | bytes 9437192 | tf_op jit(solution)/shard_map/ppermute | solution.py:31
  308.5 6.8 collective-permute-done.36
  326.2 8.8 %dispatch.3 = (bf16[4,384,1536]{2,1,0:T(8,128)(2,1)}, f32[4,384,128]{2,1,0:T(8,128)}) custom-call(s32[8,8,256]{2,1,0:T(8,128)} %pad.89.refs_0_, f32[8,8,256]{2,1,0:T(8,128)} %pad.90.refs_1_, bf16[2048,1536]{1,0:T(8,128)(2,1)} %constant_dynamic-update-slice_fusion.25.refs_2_), custom_call_target="tpu_custom_call" | custom-call | tf_op jit(solution)/shard_map/dispatch/pallas_call | solution.py:368
  338.8 8.5 %dispatch.2.rows_ref = bf16[4,384,1536]{2,1,0:T(8,128)(2,1)} custom-call(s32[8,8,256]{2,1,0:T(8,128)} %pad.89.refs_0_, f32[8,8,256]{2,1,0:T(8,128)} %pad.90.refs_1_, bf16[2048,1536]{1,0:T(8,128)(2,1)} %constant_dynamic-update-slice_fusion.42.refs_2_), custom_call_target="tpu_custom_call" | custom-call | tf_op jit(solution)/shard_map/dispatch/pallas_call | solution.py:368
  347.2 4.6 fusion.83
  351.9 5.5 fusion.61
  358.5 6.4 all-gather.8.cloned.1.call-done.down_ref
  365.0 20.6 %expert_pass.1 = (bf16[4,384,512]{2,1,0:T(8,128)(2,1)}, bf16[4,384,512]{2,1,0:T(8,128)(2,1)}, bf16[4,384,512]{2,1,0:T(8,128)(2,1)}, bf16[4,384,1536]{2,1,0:T(8,128)(2,1)}, bf16[4,384,1536]{2,1,0:T(8,128)(2,1)}) custom-call(bf16[4,384,1536]{2,1,0:T(8,128)(2,1)} %dispatch.2.rows_ref, bf16[4,384,1536]{2,1,0:T(8,128)(2,1)} %get-tuple-element.73.grad_ref, ...), custom_call_target="tpu_custom_call" | custom-call | tf_op jit(solution)/shard_map/expert_pass/pallas_call | solution.py:442
  385.6 9.3 %combine.2 = bf16[2048,1536]{1,0:T(8,128)(2,1)} custom-call(s32[8,8,256]{2,1,0:T(8,128)} %pad.89.refs_0_, bf16[4,384,1536]{2,1,0:T(8,128)(2,1)} %get-tuple-element.75.refs_1_, bf16[2048,128]{1,0:T(8,128)(2,1)} %add_convert_fusion.1.refs_2_, bf16[1536,128]{1,0:T(8,128)(2,1)} %slice.394.refs_3_), custom_call_target="tpu_custom_call" | custom-call | tf_op jit(solution)/shard_map/combine/pallas_call | solution.py:394
  394.9 6.9 convolution_convert_fusion
  406.2 5.3 collective-permute-done.37
  414.1 9.0 %collective-permute-done.38 = bf16[128,1536]{1,0:T(8,128)(2,1)S(1)} collective-permute-done((bf16[128,1536]{1,0:T(8,128)(2,1)S(1)}, bf16[128,1536]{1,0:T(8,128)(2,1)S(1)}, u32[]{:S(2)}, u32[]{:S(2)}) %collective-permute-start.38) | collective-permute-done | bytes 393248 | tf_op jit(solution)/shard_map/ppermute | solution.py:31
  424.6 6.8 collective-permute-done.40
  433.7 6.2 collective-permute-done.42
  441.6 5.4 convolution_convert_fusion.1
  456.4 7.1 collective-permute-done.45
  467.8 7.0 collective-permute-done.48
  477.7 8.0 %collective-permute-done.50 = bf16[128,1664]{1,0:T(8,128)(2,1)S(1)} collective-permute-done((bf16[128,1664]{1,0:T(8,128)(2,1)S(1)}, bf16[128,1664]{1,0:T(8,128)(2,1)S(1)}, u32[]{:S(2)}, u32[]{:S(2)}) %collective-permute-start.50) | collective-permute-done | bytes 426016 | tf_op jit(solution)/shard_map/ppermute | solution.py:36
  488.6 7.9 collective-permute-done.51
  497.3 7.2 collective-permute-start.52
  504.5 9.2 %combine.3 = bf16[2048,1536]{1,0:T(8,128)(2,1)} custom-call(s32[8,8,256]{2,1,0:T(8,128)} %pad.89.refs_0_, bf16[4,384,1536]{2,1,0:T(8,128)(2,1)} %get-tuple-element.83.refs_1_, bf16[2048,64]{1,0:T(8,128)(2,1)} %get-tuple-element.97.refs_2_, bf16[64,1536]{1,0:T(8,128)(2,1)} %bitcast.299), custom_call_target="tpu_custom_call" | custom-call | tf_op jit(solution)/shard_map/combine/pallas_call | solution.py:394
  522.6 5.9 collective-permute-done.53
  528.5 3.8 fusion.4
  535.3 8.5 %convolution_convert_fusion.2 = bf16[4,1536,512]{2,1,0:T(8,128)(2,1)} fusion(bf16[4,384,1536]{2,1,0:T(8,128)(2,1)} %dispatch.2.rows_ref, bf16[4,384,512]{2,1,0:T(8,128)(2,1)S(1)} %copy-done.19), kind=kOutput, calls=%fused_computation.19 | convolution fusion | flops 2419064832 | bytes 12582912 | tf_op jit(solution)/shard_map/dot_general | solution.py:27
  544.5 43.9 %mixer_backward.1 = (bf16[2048,1536]{1,0:T(8,128)(2,1)}, bf16[2048,896]{1,0:T(8,128)(2,1)}, f32[8,512]{1,0:T(8,128)}, f32[24,128]{1,0:T(8,128)}) custom-call(bf16[2048,1664]{1,0:T(8,128)(2,1)} %copy-done, bf16[2048,1664]{1,0:T(8,128)(2,1)} %copy-done, bf16[2048,2048]{1,0:T(8,128)(2,1)} %constant_dynamic-update-slice_fusion.8.refs_0_.refs_1_.refs_2_, ...), custom_call_target="tpu_custom_call" | custom-call | tf_op jit(solution)/shard_map/mixer_backward/pallas_call | solution.py:323
  595.2 4.1 fusion.96
  601.3 4.1 collective-permute-done.55
  609.5 8.8 %collective-permute-done.57 = bf16[128,1536]{1,0:T(8,128)(2,1)S(1)} collective-permute-done((bf16[128,1536]{1,0:T(8,128)(2,1)S(1)}, bf16[128,1536]{1,0:T(8,128)(2,1)S(1)}, u32[]{:S(2)}, u32[]{:S(2)}) %collective-permute-start.57) | collective-permute-done | bytes 393248 | tf_op jit(solution)/shard_map/ppermute | solution.py:36
  620.5 9.0 %collective-permute-done.59 = bf16[128,1536]{1,0:T(8,128)(2,1)S(1)} collective-permute-done((bf16[128,1536]{1,0:T(8,128)(2,1)S(1)}, bf16[128,1536]{1,0:T(8,128)(2,1)S(1)}, u32[]{:S(2)}, u32[]{:S(2)}) %collective-permute-start.59) | collective-permute-done | bytes 393248 | tf_op jit(solution)/shard_map/ppermute | solution.py:36
  631.5 6.1 fusion.87
  640.5 8.3 %fusion.95 = f32[1536,896]{0,1:T(8,128)S(1)} fusion(bf16[2048,1536]{1,0:T(8,128)(2,1)} %get-tuple-element.90, bf16[2048,896]{1,0:T(8,128)(2,1)S(1)} %copy-done.34), kind=kOutput, calls=%fused_computation.353 | convolution fusion | flops 5637144576 | bytes 15466496 | tf_op jit(solution)/shard_map/dot_general | solution.py:27
  649.8 4.2 convolution_dynamic-update-slice_fusion
  661.6 7.2 all-to-all-start.2
  669.5 33.7 %all-to-all-done.2 = f32[32,1,712]{2,1,0:T(1,128)S(1)} async-done(((f32[32,1,712]{2,1,0:T(1,128)}), f32[32,1,712]{2,1,0:T(1,128)S(1)}, u32[]{:S(2)}, u32[]{:S(2)}) %all-to-all-start.2) | async-done | bytes 91168 | tf_op jit(solution)/shard_map/all_to_all | solution.py:763
  708.8 7.6 all-to-all-start.1
  725.8 5.5 convert_element_type.742
  731.3 5.5 convert_element_type.740
  736.8 5.5 convert_element_type.738
  750.1 4.5 collective-permute-done.64
  772.4 7.4 collective-permute-done.67
  (447 shorter events, 230.7 us)
Async XLA Ops:
  7.2 351.4 %all-gather.4.cloned.1.call-start = ((), (), s32[]{:S(2)}) async-start(), calls=%async_computation.6 | async-start | bytes 9437184 | tf_op jit(solution)/shard_map/all_gather | solution.py:549
  18.2 12.5 %collective-permute-start.1 = (bf16[128,2048]{1,0:T(8,128)(2,1)S(1)}, bf16[128,2048]{1,0:T(8,128)(2,1)S(1)}, u32[]{:S(2)}, u32[]{:S(2)}) collective-permute-start(bf16[128,2048]{1,0:T(8,128)(2,1)S(1)} %get-tuple-element.169), channel_id=1, source_target_pairs={{0,2},{2,0},{1,3},{3,1},{4,6},{6,4},{5,7},{7,5},{8,10},{10,8},{9,1... | collective-permute-start | bytes 1572872 | tf_op jit(solution)/shard_map/ppermute | solution.py:31
  18.4 12.2 %collective-permute-start.2 = (bf16[128,2048]{1,0:T(8,128)(2,1)S(1)}, bf16[128,2048]{1,0:T(8,128)(2,1)S(1)}, u32[]{:S(2)}, u32[]{:S(2)}) collective-permute-start(bf16[128,2048]{1,0:T(8,128)(2,1)S(1)} %get-tuple-element.169), channel_id=1, source_target_pairs={{0,4},{4,8},{8,12},{12,0},{1,5},{5,9},{9,13},{13,1},{2,6},{6,10},{... | collective-permute-start | bytes 1572872 | tf_op jit(solution)/shard_map/ppermute | solution.py:36
  30.7 12.2 %collective-permute-start.4 = (bf16[128,2048]{1,0:T(8,128)(2,1)S(1)}, bf16[128,2048]{1,0:T(8,128)(2,1)S(1)}, u32[]{:S(2)}, u32[]{:S(2)}) collective-permute-start(bf16[128,2048]{1,0:T(8,128)(2,1)S(1)} %collective-permute-done.2), channel_id=1, source_target_pairs={{0,4},{4,8},{8,12},{12,0},{1,5},{5,9},{9,13},{13,1},{2,6},{6,10},{... | collective-permute-start | bytes 1572872 | tf_op jit(solution)/shard_map/ppermute | solution.py:36
  32.0 11.0 %collective-permute-start.3 = (bf16[128,2048]{1,0:T(8,128)(2,1)S(1)}, bf16[128,2048]{1,0:T(8,128)(2,1)S(1)}, u32[]{:S(2)}, u32[]{:S(2)}) collective-permute-start(bf16[128,2048]{1,0:T(8,128)(2,1)S(1)} %collective-permute-done.2), channel_id=1, source_target_pairs={{0,2},{2,0},{1,3},{3,1},{4,6},{6,4},{5,7},{7,5},{8,10},{10,8},{9,1... | collective-permute-start | bytes 1572872 | tf_op jit(solution)/shard_map/ppermute | solution.py:31
  43.0 12.0 %collective-permute-start.6 = (bf16[128,2048]{1,0:T(8,128)(2,1)S(1)}, bf16[128,2048]{1,0:T(8,128)(2,1)S(1)}, u32[]{:S(2)}, u32[]{:S(2)}) collective-permute-start(bf16[128,2048]{1,0:T(8,128)(2,1)S(1)} %collective-permute-done.4), channel_id=1, source_target_pairs={{0,4},{4,8},{8,12},{12,0},{1,5},{5,9},{9,13},{13,1},{2,6},{6,10},{... | collective-permute-start | bytes 1572872 | tf_op jit(solution)/shard_map/ppermute | solution.py:36
  44.3 10.7 %collective-permute-start.5 = (bf16[128,2048]{1,0:T(8,128)(2,1)S(1)}, bf16[128,2048]{1,0:T(8,128)(2,1)S(1)}, u32[]{:S(2)}, u32[]{:S(2)}) collective-permute-start(bf16[128,2048]{1,0:T(8,128)(2,1)S(1)} %collective-permute-done.4), channel_id=1, source_target_pairs={{0,2},{2,0},{1,3},{3,1},{4,6},{6,4},{5,7},{7,5},{8,10},{10,8},{9,1... | collective-permute-start | bytes 1572872 | tf_op jit(solution)/shard_map/ppermute | solution.py:31
  55.0 10.4 %collective-permute-start.7 = (bf16[128,2048]{1,0:T(8,128)(2,1)S(1)}, bf16[128,2048]{1,0:T(8,128)(2,1)S(1)}, u32[]{:S(2)}, u32[]{:S(2)}) collective-permute-start(bf16[128,2048]{1,0:T(8,128)(2,1)S(1)} %collective-permute-done.6), channel_id=1, source_target_pairs={{0,2},{2,0},{1,3},{3,1},{4,6},{6,4},{5,7},{7,5},{8,10},{10,8},{9,1... | collective-permute-start | bytes 1572872 | tf_op jit(solution)/shard_map/ppermute | solution.py:31
  66.5 17.3 %collective-permute-start.8 = (bf16[1024,2048]{1,0:T(8,128)(2,1)}, bf16[1024,2048]{1,0:T(8,128)(2,1)}, u32[]{:S(2)}, u32[]{:S(2)}) collective-permute-start(bf16[1024,2048]{1,0:T(8,128)(2,1)} %get-tuple-element.153), channel_id=1, source_target_pairs={{0,1},{1,0},{2,3},{3,2},{4,5},{5,4},{6,7},{7,6},{8,9},{9,8},{10,11... | collective-permute-start | bytes 12582920 | tf_op jit(solution)/shard_map/ppermute | solution.py:31
  71.0 12.8 %collective-permute-start.10 = (bf16[96,1536]{1,0:T(8,128)(2,1)S(1)}, bf16[96,1536]{1,0:T(8,128)(2,1)S(1)}, u32[]{:S(2)}, u32[]{:S(2)}) collective-permute-start(bf16[96,1536]{1,0:T(8,128)(2,1)S(1)} %copy-done.22), channel_id=1, source_target_pairs={{0,1},{1,0},{2,3},{3,2},{4,5},{5,4},{6,7},{7,6},{8,9},{9,8},{10,11... | collective-permute-start | bytes 884744 | tf_op jit(solution)/shard_map/ppermute | solution.py:31
  75.4 35.8 %all-to-all-start = ((bf16[16,48,512]{2,1,0:T(8,128)(2,1)}), bf16[16,48,512]{2,1,0:T(8,128)(2,1)S(1)}, u32[]{:S(2)}, u32[]{:S(2)}) async-start(bf16[16,48,512]{2,1,0:T(8,128)(2,1)} %pad_maximum_fusion.2), calls=%async_computation | async-start | bytes 1572864 | tf_op jit(solution)/shard_map/all_to_all | solution.py:519
  83.1 275.5 %all-gather.6.cloned.1.call-start = ((), (), s32[]{:S(2)}) async-start(), calls=%async_computation.7 | async-start | bytes 9437184 | tf_op jit(solution)/shard_map/all_gather | solution.py:549
  89.0 23.1 %collective-permute-start.13 = (bf16[128,1536]{1,0:T(8,128)(2,1)S(1)}, bf16[128,1536]{1,0:T(8,128)(2,1)S(1)}, u32[]{:S(2)}, u32[]{:S(2)}) collective-permute-start(bf16[128,1536]{1,0:T(8,128)(2,1)S(1)} %fusion.33), channel_id=1, source_target_pairs={{0,4},{4,8},{8,12},{12,0},{1,5},{5,9},{9,13},{13,1},{2,6},{6,10},{... | collective-permute-start | bytes 1179656 | tf_op jit(solution)/shard_map/ppermute | solution.py:36
  90.2 21.9 %collective-permute-start.12 = (bf16[128,1536]{1,0:T(8,128)(2,1)S(1)}, bf16[128,1536]{1,0:T(8,128)(2,1)}, u32[]{:S(2)}, u32[]{:S(2)}) collective-permute-start(bf16[128,1536]{1,0:T(8,128)(2,1)S(1)} %fusion.33), channel_id=1, source_target_pairs={{0,2},{2,0},{1,3},{3,1},{4,6},{6,4},{5,7},{7,5},{8,10},{10,8},{9,1... | collective-permute-start | bytes 1179656 | tf_op jit(solution)/shard_map/ppermute | solution.py:31
  90.5 55.4 %collective-permute-start.11 = (bf16[192,1536]{1,0:T(8,128)(2,1)S(1)}, bf16[192,1536]{1,0:T(8,128)(2,1)S(1)}, u32[]{:S(2)}, u32[]{:S(2)}) collective-permute-start(bf16[192,1536]{1,0:T(8,128)(2,1)S(1)} %pad_maximum_fusion.3), channel_id=1, source_target_pairs={{0,16},{16,0},{1,17},{17,1},{2,18},{18,2},{3,19},{19,3},{4,20},{20... | collective-permute-start | bytes 1769480 | tf_op jit(solution)/shard_map/ppermute | solution.py:31
  111.2 40.7 %collective-permute-start.9 = (bf16[1,768,512]{2,1,0:T(8,128)(2,1)S(1)}, bf16[1,768,512]{2,1,0:T(8,128)(2,1)S(1)}, u32[]{:S(2)}, u32[]{:S(2)}) collective-permute-start(bf16[1,768,512]{2,1,0:T(8,128)(2,1)S(1)} %bitcast.283), channel_id=1, source_target_pairs={{0,16},{16,0},{1,17},{17,1},{2,18},{18,2},{3,19},{19,3},{4,20},{20... | collective-permute-start | bytes 2359304 | tf_op jit(solution)/shard_map/ppermute | solution.py:31
  112.1 11.0 %collective-permute-start.15 = (bf16[128,1536]{1,0:T(8,128)(2,1)S(1)}, bf16[128,1536]{1,0:T(8,128)(2,1)S(1)}, u32[]{:S(2)}, u32[]{:S(2)}) collective-permute-start(bf16[128,1536]{1,0:T(8,128)(2,1)S(1)} %collective-permute-done.13), channel_id=1, source_target_pairs={{0,4},{4,8},{8,12},{12,0},{1,5},{5,9},{9,13},{13,1},{2,6},{6,10},{... | collective-permute-start | bytes 1179656 | tf_op jit(solution)/shard_map/ppermute | solution.py:36
  112.1 11.0 %collective-permute-start.14 = (bf16[128,1536]{1,0:T(8,128)(2,1)S(1)}, bf16[128,1536]{1,0:T(8,128)(2,1)S(1)}, u32[]{:S(2)}, u32[]{:S(2)}) collective-permute-start(bf16[128,1536]{1,0:T(8,128)(2,1)S(1)} %collective-permute-done.13), channel_id=1, source_target_pairs={{0,2},{2,0},{1,3},{3,1},{4,6},{6,4},{5,7},{7,5},{8,10},{10,8},{9,1... | collective-permute-start | bytes 1179656 | tf_op jit(solution)/shard_map/ppermute | solution.py:31
  123.1 10.3 %collective-permute-start.17 = (bf16[128,1536]{1,0:T(8,128)(2,1)S(1)}, bf16[128,1536]{1,0:T(8,128)(2,1)S(1)}, u32[]{:S(2)}, u32[]{:S(2)}) collective-permute-start(bf16[128,1536]{1,0:T(8,128)(2,1)S(1)} %collective-permute-done.15), channel_id=1, source_target_pairs={{0,4},{4,8},{8,12},{12,0},{1,5},{5,9},{9,13},{13,1},{2,6},{6,10},{... | collective-permute-start | bytes 1179656 | tf_op jit(solution)/shard_map/ppermute | solution.py:36
  123.3 10.1 %collective-permute-start.16 = (bf16[128,1536]{1,0:T(8,128)(2,1)S(1)}, bf16[128,1536]{1,0:T(8,128)(2,1)S(1)}, u32[]{:S(2)}, u32[]{:S(2)}) collective-permute-start(bf16[128,1536]{1,0:T(8,128)(2,1)S(1)} %collective-permute-done.15), channel_id=1, source_target_pairs={{0,2},{2,0},{1,3},{3,1},{4,6},{6,4},{5,7},{7,5},{8,10},{10,8},{9,1... | collective-permute-start | bytes 1179656 | tf_op jit(solution)/shard_map/ppermute | solution.py:31
  143.7 46.4 %collective-permute-start.19 = (bf16[1024,1536]{1,0:T(8,128)(2,1)}, bf16[1024,1536]{1,0:T(8,128)(2,1)}, u32[]{:S(2)}, u32[]{:S(2)}) collective-permute-start(bf16[1024,1536]{1,0:T(8,128)(2,1)} %get-tuple-element.202), channel_id=1, source_target_pairs={{0,1},{1,0},{2,3},{3,2},{4,5},{5,4},{6,7},{7,6},{8,9},{9,8},{10,11... | collective-permute-start | bytes 9437192 | tf_op jit(solution)/shard_map/ppermute | solution.py:31
  201.8 163.2 %all-gather.8.cloned.1.call-start = ((), (), s32[]{:S(2)}) async-start(), calls=%async_computation.8 | async-start | bytes 9437184 | tf_op jit(solution)/shard_map/all_gather | solution.py:549
  215.1 11.1 %collective-permute-start.21 = (bf16[128,1664]{1,0:T(8,128)(2,1)S(1)}, bf16[128,1664]{1,0:T(8,128)(2,1)S(1)}, u32[]{:S(2)}, u32[]{:S(2)}) collective-permute-start(bf16[128,1664]{1,0:T(8,128)(2,1)S(1)} %get-tuple-element.127), channel_id=1, source_target_pairs={{0,2},{2,0},{1,3},{3,1},{4,6},{6,4},{5,7},{7,5},{8,10},{10,8},{9,1... | collective-permute-start | bytes 1277960 | tf_op jit(solution)/shard_map/ppermute | solution.py:31
  216.1 19.3 %collective-permute-start.23 = (bf16[128,1664]{1,0:T(8,128)(2,1)S(1)}, bf16[128,1664]{1,0:T(8,128)(2,1)S(1)}, u32[]{:S(2)}, u32[]{:S(2)}) collective-permute-start(bf16[128,1664]{1,0:T(8,128)(2,1)S(1)} %get-tuple-element.126), channel_id=1, source_target_pairs={{0,2},{2,0},{1,3},{3,1},{4,6},{6,4},{5,7},{7,5},{8,10},{10,8},{9,1... | collective-permute-start | bytes 1277960 | tf_op jit(solution)/shard_map/ppermute | solution.py:31
  226.3 9.6 %collective-permute-start.22 = (bf16[128,1664]{1,0:T(8,128)(2,1)S(1)}, bf16[128,1664]{1,0:T(8,128)(2,1)S(1)}, u32[]{:S(2)}, u32[]{:S(2)}) collective-permute-start(bf16[128,1664]{1,0:T(8,128)(2,1)S(1)} %fusion.27), channel_id=1, source_target_pairs={{0,4},{4,8},{8,12},{12,0},{1,5},{5,9},{9,13},{13,1},{2,6},{6,10},{... | collective-permute-start | bytes 1277960 | tf_op jit(solution)/shard_map/ppermute | solution.py:36
  227.6 16.9 %collective-permute-start.25 = (bf16[128,1664]{1,0:T(8,128)(2,1)S(1)}, bf16[128,1664]{1,0:T(8,128)(2,1)S(1)}, u32[]{:S(2)}, u32[]{:S(2)}) collective-permute-start(bf16[128,1664]{1,0:T(8,128)(2,1)S(1)} %get-tuple-element.124), channel_id=1, source_target_pairs={{0,2},{2,0},{1,3},{3,1},{4,6},{6,4},{5,7},{7,5},{8,10},{10,8},{9,1... | collective-permute-start | bytes 1277960 | tf_op jit(solution)/shard_map/ppermute | solution.py:31
  237.3 16.3 %collective-permute-start.27 = (bf16[128,1664]{1,0:T(8,128)(2,1)}, bf16[128,1664]{1,0:T(8,128)(2,1)}, u32[]{:S(2)}, u32[]{:S(2)}) collective-permute-start(bf16[128,1664]{1,0:T(8,128)(2,1)} %get-tuple-element.125), channel_id=1, source_target_pairs={{0,2},{2,0},{1,3},{3,1},{4,6},{6,4},{5,7},{7,5},{8,10},{10,8},{9,1... | collective-permute-start | bytes 1277960 | tf_op jit(solution)/shard_map/ppermute | solution.py:31
  246.4 9.8 %collective-permute-start.26 = (bf16[128,1664]{1,0:T(8,128)(2,1)}, bf16[128,1664]{1,0:T(8,128)(2,1)}, u32[]{:S(2)}, u32[]{:S(2)}) collective-permute-start(bf16[128,1664]{1,0:T(8,128)(2,1)} %add_convert_fusion.2), channel_id=1, source_target_pairs={{0,4},{4,8},{8,12},{12,0},{1,5},{5,9},{9,13},{13,1},{2,6},{6,10},{... | collective-permute-start | bytes 1277960 | tf_op jit(solution)/shard_map/ppermute | solution.py:36
  261.6 464.2 %reduce-scatter.8.cloned.1.call-start = ((), (), s32[]{:S(2)}) async-start(), calls=%async_computation.11 | async-start | bytes 9437184 | tf_op jit(solution)/shard_map/reduce_scatter | solution.py:659
  278.2 10.0 %collective-permute-start.33 = (bf16[128,1536]{1,0:T(8,128)(2,1)S(1)}, bf16[128,1536]{1,0:T(8,128)(2,1)S(1)}, u32[]{:S(2)}, u32[]{:S(2)}) collective-permute-start(bf16[128,1536]{1,0:T(8,128)(2,1)S(1)} %collective-permute-done.31), channel_id=1, source_target_pairs={{0,4},{4,8},{8,12},{12,0},{1,5},{5,9},{9,13},{13,1},{2,6},{6,10},{... | collective-permute-start | bytes 1179656 | tf_op jit(solution)/shard_map/ppermute | solution.py:36
  297.9 37.1 %collective-permute-start.35 = (bf16[1024,1536]{1,0:T(8,128)(2,1)}, bf16[1024,1536]{1,0:T(8,128)(2,1)}, u32[]{:S(2)}, u32[]{:S(2)}) collective-permute-start(bf16[1024,1536]{1,0:T(8,128)(2,1)} %get-tuple-element.188), channel_id=1, source_target_pairs={{0,1},{1,0},{2,3},{3,2},{4,5},{5,4},{6,7},{7,6},{8,9},{9,8},{10,11... | collective-permute-start | bytes 9437192 | tf_op jit(solution)/shard_map/ppermute | solution.py:31
  401.7 329.6 %reduce-scatter.6.cloned.1.call-start = ((), (), s32[]{:S(2)}) async-start(), calls=%async_computation.10 | async-start | bytes 9437184 | tf_op jit(solution)/shard_map/reduce_scatter | solution.py:659
  412.5 10.5 %collective-permute-start.38 = (bf16[128,1536]{1,0:T(8,128)(2,1)S(1)}, bf16[128,1536]{1,0:T(8,128)(2,1)S(1)}, u32[]{:S(2)}, u32[]{:S(2)}) collective-permute-start(bf16[128,1536]{1,0:T(8,128)(2,1)S(1)} %get-tuple-element.139), channel_id=1, source_target_pairs={{0,2},{2,0},{1,3},{3,1},{4,6},{6,4},{5,7},{7,5},{8,10},{10,8},{9,1... | collective-permute-start | bytes 1179656 | tf_op jit(solution)/shard_map/ppermute | solution.py:31
  412.9 18.6 %collective-permute-start.40 = (bf16[128,1536]{1,0:T(8,128)(2,1)S(1)}, bf16[128,1536]{1,0:T(8,128)(2,1)S(1)}, u32[]{:S(2)}, u32[]{:S(2)}) collective-permute-start(bf16[128,1536]{1,0:T(8,128)(2,1)S(1)} %get-tuple-element.138), channel_id=1, source_target_pairs={{0,2},{2,0},{1,3},{3,1},{4,6},{6,4},{5,7},{7,5},{8,10},{10,8},{9,1... | collective-permute-start | bytes 1179656 | tf_op jit(solution)/shard_map/ppermute | solution.py:31
  424.4 15.5 %collective-permute-start.42 = (bf16[128,1536]{1,0:T(8,128)(2,1)S(1)}, bf16[128,1536]{1,0:T(8,128)(2,1)S(1)}, u32[]{:S(2)}, u32[]{:S(2)}) collective-permute-start(bf16[128,1536]{1,0:T(8,128)(2,1)S(1)} %get-tuple-element.136), channel_id=1, source_target_pairs={{0,2},{2,0},{1,3},{3,1},{4,6},{6,4},{5,7},{7,5},{8,10},{10,8},{9,1... | collective-permute-start | bytes 1179656 | tf_op jit(solution)/shard_map/ppermute | solution.py:31
  433.4 14.9 %collective-permute-start.44 = (bf16[128,1536]{1,0:T(8,128)(2,1)S(1)}, bf16[128,1536]{1,0:T(8,128)(2,1)S(1)}, u32[]{:S(2)}, u32[]{:S(2)}) collective-permute-start(bf16[128,1536]{1,0:T(8,128)(2,1)S(1)} %get-tuple-element.137), channel_id=1, source_target_pairs={{0,2},{2,0},{1,3},{3,1},{4,6},{6,4},{5,7},{7,5},{8,10},{10,8},{9,1... | collective-permute-start | bytes 1179656 | tf_op jit(solution)/shard_map/ppermute | solution.py:31
  447.1 289.7 %reduce-scatter.4.cloned.1.call-start = ((), (), s32[]{:S(2)}) async-start(), calls=%async_computation.9 | async-start | bytes 9437184 | tf_op jit(solution)/shard_map/reduce_scatter | solution.py:659
  464.9 9.9 %collective-permute-start.48 = (bf16[128,1664]{1,0:T(8,128)(2,1)S(1)}, bf16[128,1664]{1,0:T(8,128)(2,1)S(1)}, u32[]{:S(2)}, u32[]{:S(2)}) collective-permute-start(bf16[128,1664]{1,0:T(8,128)(2,1)S(1)} %collective-permute-done.46), channel_id=1, source_target_pairs={{0,4},{4,8},{8,12},{12,0},{1,5},{5,9},{9,13},{13,1},{2,6},{6,10},{... | collective-permute-start | bytes 1277960 | tf_op jit(solution)/shard_map/ppermute | solution.py:36
  464.9 9.9 %collective-permute-start.47 = (bf16[128,1664]{1,0:T(8,128)(2,1)S(1)}, bf16[128,1664]{1,0:T(8,128)(2,1)S(1)}, u32[]{:S(2)}, u32[]{:S(2)}) collective-permute-start(bf16[128,1664]{1,0:T(8,128)(2,1)S(1)} %collective-permute-done.46), channel_id=1, source_target_pairs={{0,2},{2,0},{1,3},{3,1},{4,6},{6,4},{5,7},{7,5},{8,10},{10,8},{9,1... | collective-permute-start | bytes 1277960 | tf_op jit(solution)/shard_map/ppermute | solution.py:31
  474.8 10.9 %collective-permute-start.50 = (bf16[128,1664]{1,0:T(8,128)(2,1)S(1)}, bf16[128,1664]{1,0:T(8,128)(2,1)S(1)}, u32[]{:S(2)}, u32[]{:S(2)}) collective-permute-start(bf16[128,1664]{1,0:T(8,128)(2,1)S(1)} %collective-permute-done.48), channel_id=1, source_target_pairs={{0,4},{4,8},{8,12},{12,0},{1,5},{5,9},{9,13},{13,1},{2,6},{6,10},{... | collective-permute-start | bytes 1277960 | tf_op jit(solution)/shard_map/ppermute | solution.py:36
  474.8 10.9 %collective-permute-start.49 = (bf16[128,1664]{1,0:T(8,128)(2,1)S(1)}, bf16[128,1664]{1,0:T(8,128)(2,1)S(1)}, u32[]{:S(2)}, u32[]{:S(2)}) collective-permute-start(bf16[128,1664]{1,0:T(8,128)(2,1)S(1)} %collective-permute-done.48), channel_id=1, source_target_pairs={{0,2},{2,0},{1,3},{3,1},{4,6},{6,4},{5,7},{7,5},{8,10},{10,8},{9,1... | collective-permute-start | bytes 1277960 | tf_op jit(solution)/shard_map/ppermute | solution.py:31
  485.7 10.7 %collective-permute-start.51 = (bf16[128,1664]{1,0:T(8,128)(2,1)S(1)}, bf16[128,1664]{1,0:T(8,128)(2,1)S(1)}, u32[]{:S(2)}, u32[]{:S(2)}) collective-permute-start(bf16[128,1664]{1,0:T(8,128)(2,1)S(1)} %collective-permute-done.50), channel_id=1, source_target_pairs={{0,2},{2,0},{1,3},{3,1},{4,6},{6,4},{5,7},{7,5},{8,10},{10,8},{9,1... | collective-permute-start | bytes 1277960 | tf_op jit(solution)/shard_map/ppermute | solution.py:31
  497.3 16.4 %collective-permute-start.52 = (bf16[1024,1664]{1,0:T(8,128)(2,1)}, bf16[1024,1664]{1,0:T(8,128)(2,1)}, u32[]{:S(2)}, u32[]{:S(2)}) collective-permute-start(bf16[1024,1664]{1,0:T(8,128)(2,1)} %get-tuple-element.170), channel_id=1, source_target_pairs={{0,1},{1,0},{2,3},{3,2},{4,5},{5,4},{6,7},{7,6},{8,9},{9,8},{10,11... | collective-permute-start | bytes 10223624 | tf_op jit(solution)/shard_map/ppermute | solution.py:31
  534.1 57.1 %collective-permute-start.54 = (bf16[128,1536]{1,0:T(8,128)(2,1)S(1)}, bf16[128,1536]{1,0:T(8,128)(2,1)}, u32[]{:S(2)}, u32[]{:S(2)}) collective-permute-start(bf16[128,1536]{1,0:T(8,128)(2,1)S(1)} %get-tuple-element.135), channel_id=1, source_target_pairs={{0,2},{2,0},{1,3},{3,1},{4,6},{6,4},{5,7},{7,5},{8,10},{10,8},{9,1... | collective-permute-start | bytes 1179656 | tf_op jit(solution)/shard_map/ppermute | solution.py:31
  590.9 10.4 %collective-permute-start.56 = (bf16[128,1536]{1,0:T(8,128)(2,1)S(1)}, bf16[128,1536]{1,0:T(8,128)(2,1)S(1)}, u32[]{:S(2)}, u32[]{:S(2)}) collective-permute-start(bf16[128,1536]{1,0:T(8,128)(2,1)S(1)} %get-tuple-element.134), channel_id=1, source_target_pairs={{0,2},{2,0},{1,3},{3,1},{4,6},{6,4},{5,7},{7,5},{8,10},{10,8},{9,1... | collective-permute-start | bytes 1179656 | tf_op jit(solution)/shard_map/ppermute | solution.py:31
  592.5 12.9 %collective-permute-start.55 = (bf16[128,1536]{1,0:T(8,128)(2,1)S(1)}, bf16[128,1536]{1,0:T(8,128)(2,1)S(1)}, u32[]{:S(2)}, u32[]{:S(2)}) collective-permute-start(bf16[128,1536]{1,0:T(8,128)(2,1)S(1)} %fusion.48), channel_id=1, source_target_pairs={{0,4},{4,8},{8,12},{12,0},{1,5},{5,9},{9,13},{13,1},{2,6},{6,10},{... | collective-permute-start | bytes 1179656 | tf_op jit(solution)/shard_map/ppermute | solution.py:36
  599.3 10.2 %collective-permute-start.58 = (bf16[128,1536]{1,0:T(8,128)(2,1)S(1)}, bf16[128,1536]{1,0:T(8,128)(2,1)S(1)}, u32[]{:S(2)}, u32[]{:S(2)}) collective-permute-start(bf16[128,1536]{1,0:T(8,128)(2,1)S(1)} %get-tuple-element.132), channel_id=1, source_target_pairs={{0,2},{2,0},{1,3},{3,1},{4,6},{6,4},{5,7},{7,5},{8,10},{10,8},{9,1... | collective-permute-start | bytes 1179656 | tf_op jit(solution)/shard_map/ppermute | solution.py:31
  606.5 11.8 %collective-permute-start.57 = (bf16[128,1536]{1,0:T(8,128)(2,1)S(1)}, bf16[128,1536]{1,0:T(8,128)(2,1)S(1)}, u32[]{:S(2)}, u32[]{:S(2)}) collective-permute-start(bf16[128,1536]{1,0:T(8,128)(2,1)S(1)} %add_convert_fusion.7), channel_id=1, source_target_pairs={{0,4},{4,8},{8,12},{12,0},{1,5},{5,9},{9,13},{13,1},{2,6},{6,10},{... | collective-permute-start | bytes 1179656 | tf_op jit(solution)/shard_map/ppermute | solution.py:36
  608.2 12.3 %collective-permute-start.60 = (bf16[128,1536]{1,0:T(8,128)(2,1)S(1)}, bf16[128,1536]{1,0:T(8,128)(2,1)S(1)}, u32[]{:S(2)}, u32[]{:S(2)}) collective-permute-start(bf16[128,1536]{1,0:T(8,128)(2,1)S(1)} %get-tuple-element.133), channel_id=1, source_target_pairs={{0,2},{2,0},{1,3},{3,1},{4,6},{6,4},{5,7},{7,5},{8,10},{10,8},{9,1... | collective-permute-start | bytes 1179656 | tf_op jit(solution)/shard_map/ppermute | solution.py:31
  619.4 10.2 %collective-permute-start.59 = (bf16[128,1536]{1,0:T(8,128)(2,1)S(1)}, bf16[128,1536]{1,0:T(8,128)(2,1)S(1)}, u32[]{:S(2)}, u32[]{:S(2)}) collective-permute-start(bf16[128,1536]{1,0:T(8,128)(2,1)S(1)} %add_convert_fusion.6), channel_id=1, source_target_pairs={{0,4},{4,8},{8,12},{12,0},{1,5},{5,9},{9,13},{13,1},{2,6},{6,10},{... | collective-permute-start | bytes 1179656 | tf_op jit(solution)/shard_map/ppermute | solution.py:36
  619.8 48.9 %collective-permute-start.72 = (bf16[1,32,1536]{2,1,0:T(8,128)(2,1)S(1)}, bf16[1,32,1536]{2,1,0:T(8,128)(2,1)S(1)}, u32[]{:S(2)}, u32[]{:S(2)}) collective-permute-start(bf16[1,32,1536]{2,1,0:T(8,128)(2,1)S(1)} %dynamic-slice_convert_fusion.1), channel_id=1, source_target_pairs={{0,16},{16,0},{1,17},{17,1},{2,18},{18,2},{3,19},{19,3},{4,20},{20... | collective-permute-start | bytes 294920 | tf_op jit(solution)/shard_map/ppermute | solution.py:31
  637.7 78.7 %collective-permute-start.61 = (bf16[4,2,128,1536]{3,2,1,0:T(8,128)(2,1)}, bf16[4,2,128,1536]{3,2,1,0:T(8,128)(2,1)}, u32[]{:S(2)}, u32[]{:S(2)}) collective-permute-start(bf16[4,2,128,1536]{3,2,1,0:T(8,128)(2,1)} %bitcast.71), channel_id=1, source_target_pairs={{0,1},{1,0},{2,3},{3,2},{4,5},{5,4},{6,7},{7,6},{8,9},{9,8},{10,11... | collective-permute-start | bytes 9437192 | tf_op jit(solution)/shard_map/ppermute | solution.py:31
  656.6 48.1 %collective-permute-start.69 = (bf16[768,896]{0,1:T(8,128)(2,1)S(1)}, bf16[768,896]{0,1:T(8,128)(2,1)}, u32[]{:S(2)}, u32[]{:S(2)}) collective-permute-start(bf16[768,896]{0,1:T(8,128)(2,1)S(1)} %dynamic-slice_convert_fusion), channel_id=1, source_target_pairs={{0,16},{16,0},{1,17},{17,1},{2,18},{18,2},{3,19},{19,3},{4,20},{20... | collective-permute-start | bytes 4128776 | tf_op jit(solution)/shard_map/ppermute | solution.py:31
  659.5 43.8 %collective-permute-start.70 = (bf16[192,1536]{1,0:T(8,128)(2,1)}, bf16[192,1536]{1,0:T(8,128)(2,1)S(1)}, u32[]{:S(2)}, u32[]{:S(2)}) collective-permute-start(bf16[192,1536]{1,0:T(8,128)(2,1)} %get-tuple-element.233), channel_id=1, source_target_pairs={{0,16},{16,0},{1,17},{17,1},{2,18},{18,2},{3,19},{19,3},{4,20},{20... | collective-permute-start | bytes 1769480 | tf_op jit(solution)/shard_map/ppermute | solution.py:31
  661.6 41.6 %all-to-all-start.2 = ((f32[32,1,712]{2,1,0:T(1,128)}), f32[32,1,712]{2,1,0:T(1,128)S(1)}, u32[]{:S(2)}, u32[]{:S(2)}) async-start(f32[32,1,712]{2,1,0:T(1,128)} %copy.256), calls=%async_computation.2 | async-start | bytes 196608 | tf_op jit(solution)/shard_map/all_to_all | solution.py:763
  708.8 50.2 %all-to-all-start.1 = ((bf16[16,48,896]{2,1,0:T(8,128)(2,1)}), bf16[16,48,896]{2,1,0:T(8,128)(2,1)S(1)}, u32[]{:S(2)}, u32[]{:S(2)}) async-start(bf16[16,48,896]{2,1,0:T(8,128)(2,1)} %bitcast.80), calls=%async_computation.1 | async-start | bytes 2752512 | tf_op jit(solution)/shard_map/all_to_all | solution.py:707
  723.0 20.6 %collective-permute-start.62 = (bf16[128,1536]{1,0:T(8,128)(2,1)}, bf16[128,1536]{1,0:T(8,128)(2,1)}, u32[]{:S(2)}, u32[]{:S(2)}) collective-permute-start(bf16[128,1536]{1,0:T(8,128)(2,1)} %get-tuple-element.131), channel_id=1, source_target_pairs={{0,2},{2,0},{1,3},{3,1},{4,6},{6,4},{5,7},{7,5},{8,10},{10,8},{9,1... | collective-permute-start | bytes 1179656 | tf_op jit(solution)/shard_map/ppermute | solution.py:31
  723.3 22.7 %collective-permute-start.71 = (f32[96,1536]{1,0:T(8,128)S(1)}, f32[96,1536]{1,0:T(8,128)}, u32[]{:S(2)}, u32[]{:S(2)}) collective-permute-start(f32[96,1536]{1,0:T(8,128)S(1)} %dynamic-slice_bitcast_fusion), channel_id=1, source_target_pairs={{0,1},{1,0},{2,3},{3,2},{4,5},{5,4},{6,7},{7,6},{8,9},{9,8},{10,11... | collective-permute-start | bytes 1769480 | tf_op jit(solution)/shard_map/ppermute | solution.py:31
  742.3 12.3 %collective-permute-start.64 = (bf16[128,1536]{1,0:T(8,128)(2,1)S(1)}, bf16[128,1536]{1,0:T(8,128)(2,1)S(1)}, u32[]{:S(2)}, u32[]{:S(2)}) collective-permute-start(bf16[128,1536]{1,0:T(8,128)(2,1)S(1)} %copy-done.25), channel_id=1, source_target_pairs={{0,2},{2,0},{1,3},{3,1},{4,6},{6,4},{5,7},{7,5},{8,10},{10,8},{9,1... | collective-permute-start | bytes 1179656 | tf_op jit(solution)/shard_map/ppermute | solution.py:31
  744.8 10.5 %collective-permute-start.63 = (bf16[128,1536]{1,0:T(8,128)(2,1)S(1)}, bf16[128,1536]{1,0:T(8,128)(2,1)S(1)}, u32[]{:S(2)}, u32[]{:S(2)}) collective-permute-start(bf16[128,1536]{1,0:T(8,128)(2,1)S(1)} %fusion.41), channel_id=1, source_target_pairs={{0,4},{4,8},{8,12},{12,0},{1,5},{5,9},{9,13},{13,1},{2,6},{6,10},{... | collective-permute-start | bytes 1179656 | tf_op jit(solution)/shard_map/ppermute | solution.py:36
  748.6 18.2 %collective-permute-start.66 = (bf16[128,1536]{1,0:T(8,128)(2,1)}, bf16[128,1536]{1,0:T(8,128)(2,1)}, u32[]{:S(2)}, u32[]{:S(2)}) collective-permute-start(bf16[128,1536]{1,0:T(8,128)(2,1)} %get-tuple-element.128), channel_id=1, source_target_pairs={{0,2},{2,0},{1,3},{3,1},{4,6},{6,4},{5,7},{7,5},{8,10},{10,8},{9,1... | collective-permute-start | bytes 1179656 | tf_op jit(solution)/shard_map/ppermute | solution.py:31
  748.9 23.5 %collective-permute-start.68 = (bf16[128,1536]{1,0:T(8,128)(2,1)}, bf16[128,1536]{1,0:T(8,128)(2,1)}, u32[]{:S(2)}, u32[]{:S(2)}) collective-permute-start(bf16[128,1536]{1,0:T(8,128)(2,1)} %get-tuple-element.129), channel_id=1, source_target_pairs={{0,2},{2,0},{1,3},{3,1},{4,6},{6,4},{5,7},{7,5},{8,10},{10,8},{9,1... | collective-permute-start | bytes 1179656 | tf_op jit(solution)/shard_map/ppermute | solution.py:31
  757.1 10.9 %collective-permute-start.65 = (bf16[128,1536]{1,0:T(8,128)(2,1)}, bf16[128,1536]{1,0:T(8,128)(2,1)}, u32[]{:S(2)}, u32[]{:S(2)}) collective-permute-start(bf16[128,1536]{1,0:T(8,128)(2,1)} %add_convert_fusion.5), channel_id=1, source_target_pairs={{0,4},{4,8},{8,12},{12,0},{1,5},{5,9},{9,13},{13,1},{2,6},{6,10},{... | collective-permute-start | bytes 1179656 | tf_op jit(solution)/shard_map/ppermute | solution.py:36
  769.4 10.3 %collective-permute-start.67 = (bf16[128,1536]{1,0:T(8,128)(2,1)S(1)}, bf16[128,1536]{1,0:T(8,128)(2,1)S(1)}, u32[]{:S(2)}, u32[]{:S(2)}) collective-permute-start(bf16[128,1536]{1,0:T(8,128)(2,1)S(1)} %add_convert_fusion.4), channel_id=1, source_target_pairs={{0,4},{4,8},{8,12},{12,0},{1,5},{5,9},{9,13},{13,1},{2,6},{6,10},{... | collective-permute-start | bytes 1179656 | tf_op jit(solution)/shard_map/ppermute | solution.py:36
  (62 other events, 745.4 us)
Sparse Core Ops, SparseCore 0:
  71.1 110.8 all-gather.3
  201.9 78.9 all-gather.5
  282.5 82.4 all-gather.7
  401.9 77.0 reduce-scatter.7
  481.2 77.0 reduce-scatter.5
  560.4 79.1 reduce-scatter.3

commit v3 on v2

--- a/solution.py
+++ b/solution.py
@@ -51,35 +51,67 @@
     return parts[0].astype(f32) + parts[1].astype(f32) + parts[2].astype(f32)
 
 
-def gather(block, *joined):
+def tie(value, *others):
+    return lax.optimization_barrier((value, *others))
+
+
+def work_of(entry, token):
+    return entry(token) if callable(entry) else entry
+
+
+def gather(block, beside_work=()):
     size = lax.axis_size("z")
+    beside_work = (list(beside_work) + [()] * size)[:size]
     blocks = []
-    for step in range(size - 1):
-        following, beside = ring(block), swap(block, "y")
-        blocks += [block, beside]
-        if step == size - 2 and joined:
-            block, _, joined = lax.optimization_barrier((following, beside, joined))
-        else:
-            block, _ = lax.optimization_barrier((following, beside))
-    blocks += [block, swap(block, "y")]
-    near = jnp.concatenate(blocks, axis=0)
-    everything = jnp.concatenate([near, swap(near, "core")], axis=0)
-    return (everything, *joined) if joined else everything
+    for step in range(size):
+        following = ring(block) if step < size - 1 else ()
+        near = swap(block, "y")
+        work = work_of(beside_work[step], block)
+        following, near, beside_work[step] = tie(following, near, work)
+        blocks += [block, near]
+        block = following
+    own = jnp.concatenate(blocks, axis=0)
+    return own, swap(own, "core"), beside_work
 
 
 def add_low(left, right):
     return (left.astype(f32) + right.astype(f32)).astype(bf16)
 
 
-def scatter(parts):
+def scatter_first(near, mate, moved=None):
     size = lax.axis_size("z")
-    parts = parts.reshape((2, size, 2, parts.shape[0] // (4 * size)) + parts.shape[1:])
-    pairs = add_low(parts[0], swap(parts[1], "core"))
-    there = [swap(pairs[step, 1], "y") for step in list(range(1, size)) + [0]]
-    total = add_low(pairs[1, 0], there[0])
-    for step in range(2, size):
-        total = add_low(ring(total), add_low(pairs[step, 0], there[step - 1]))
-    return ring(total).astype(f32) + pairs[0, 0].astype(f32) + there[-1].astype(f32)
+    shape = (size, 2, near.shape[0] // (2 * size), near.shape[1])
+    there = (swap(mate, "core") if moved is None else moved).reshape(shape)
+    near = near.reshape(shape)
+    pairs = [add_low(near[step], there[step]) for step in range(size)]
+    return pairs
+
+
+def scatter_beside(pairs):
+    size = len(pairs)
+    order = list(range(1, size)) + [0]
+    there = {step: swap(pairs[step][1], "y") for step in order}
+    return [there[step] for step in range(size)]
+
+
+def ring_step(total, pairs, there, step):
+    at = (step + 1) % len(pairs)
+    total = ring(total).astype(f32) + (pairs[at][0].astype(f32) + there[at].astype(f32))
+    return total.astype(bf16) if at else total
+
+
+def scatter_last(pairs, beside_work=(), there=None):
+    size = len(pairs)
+    beside_work = (list(beside_work) + [()] * size)[:size]
+    there = there or scatter_beside(pairs)
+    total = add_low(pairs[1][0], there[1])
+    token = pairs
+    for step in range(1, size):
+        total, beside_work[step - 1] = tie(total, work_of(beside_work[step - 1], token))
+        token = total
+        total = ring_step(total, pairs, there, step)
+    total, beside_work[-1] = tie(total, work_of(beside_work[-1], token))
+    return total, beside_work
 
 
 def dp_gather_rows(value, axis):
@@ -92,7 +124,7 @@
     )
 
 
-def dp_scatter_rows(value, axis):
+def dp_scatter_rows(value, axis, hold=()):
     count = lax.axis_size("dp")
     if count != 2:
         return lax.psum_scatter(value.astype(bf16), "dp", scatter_dimension=axis, tiled=True).astype(f32)
@@ -100,12 +132,19 @@
     extent = value.shape[axis] // count
     sent = lax.dynamic_slice_in_dim(value, (1 - place) * extent, extent, axis).astype(bf16)
     kept = lax.dynamic_slice_in_dim(value, place * extent, extent, axis)
-    return kept + swap(sent, "dp").astype(f32)
+    received, kept, hold = tie(swap(sent, "dp"), kept, hold)
+    return kept + received.astype(f32)
 
 
 def params(steps=1):
     return pltpu.CompilerParams(
         dimension_semantics=("arbitrary",) * steps, vmem_limit_bytes=56 * 1024 * 1024
+    )
+
+
+def cost(micros):
+    return pl.CostEstimate(
+        flops=int(micros * 1.1e9), bytes_accessed=int(micros * 3.5e6), transcendentals=0
     )
 
 
@@ -230,6 +269,7 @@
             jax.ShapeDtypeStruct((total, WIDE), bf16),
         ],
         compiler_params=params(),
+        cost_estimate=cost(total / 80),
         name="mixer_forward",
     )(gathered, gathered, gain, w_in, w_out, conv, head)
 
@@ -333,6 +373,7 @@
             head_shape,
         ],
         compiler_params=params(),
+        cost_estimate=cost(total / 46),
         name="mixer_backward",
     )(grads, grads, gathered, proj, w_in, w_out, conv, head, rate)
 
@@ -342,69 +383,121 @@
     return [rank_ref[0, k : k + 1, :] == number for k in range(experts)]
 
 
-def dispatch_kernel(experts, slots, weigh, rank_ref, weight_ref, values_ref, out_ref, *weights_ref):
+def dispatch_kernel(experts, slots, grads, rank_ref, weight_ref, values_ref, *refs):
     chosen = selection(rank_ref, experts, slots)
     select = jnp.concatenate([entry.astype(f32) for entry in chosen], axis=0).astype(bf16)
-    rows = jnp.dot(select, values_ref[...], preferred_element_type=f32)
+    values = values_ref[...]
+    rows = jnp.dot(select, values, preferred_element_type=f32)
+    if grads:
+        down_ref = refs[0]
+        out_ref, weights_ref, act_grad_ref = refs[-3:]
+        act_grad_ref[...] = lax.dot_general(
+            values, down_ref[...], (((1,), (1,)), ((), ())), preferred_element_type=f32
+        )
+    else:
+        act_grad_ref, gate_ref, up_ref = refs[:3]
+        out_ref, act_ref, g_ref, u_ref = refs[-4:]
+        gate = jnp.dot(values, gate_ref[...], preferred_element_type=f32)
+        up = jnp.dot(values, up_ref[...], preferred_element_type=f32)
+        sig = sigmoid(gate)
+        silu = gate * sig
+        d_act = act_grad_ref[...]
+        act_ref[...] = (silu * up).astype(bf16)
+        g_ref[...] = (d_act * up * (sig * (1.0 + gate * (1.0 - sig)))).astype(bf16)
+        u_ref[...] = (d_act * silu).astype(bf16)
     for k in range(experts):
         part = rows[k * slots : (k + 1) * slots]
-        if weigh:
+        if grads:
             own = jnp.where(chosen[k], weight_ref[0, k : k + 1, :], 0.0)
             own = jnp.sum(own, axis=1, keepdims=True)
             part = part * own
-            weights_ref[0][k] = jnp.broadcast_to(own, (slots, EXTRA))
+            weights_ref[k] = jnp.broadcast_to(own, (slots, EXTRA))
         out_ref[k] = part.astype(bf16)
 
 
-def dispatch(values, rank, weight, experts, slots, weigh):
+def dispatch(values, rank, weight, experts, slots, first, shared, into=None):
     pairs, _, tokens = rank.shape
+    count = values.shape[0] // tokens
     width = values.shape[1]
-    rank_spec = pl.BlockSpec((1,) + rank.shape[1:], lambda step: (step, 0, 0))
-    specs = [pl.BlockSpec((experts, slots, width), lambda step: (0, step, 0))]
+    grads = len(shared) == 1
+    hidden = shared[0].shape[0] if grads else shared[0].shape[1]
+
+    def slots_spec(extent):
+        return pl.BlockSpec((experts, slots, extent), lambda step: (0, first + step, 0))
+
+    def rows_spec(extent):
+        return pl.BlockSpec((tokens, extent), lambda step: (step, 0))
+
+    rank_spec = pl.BlockSpec((1,) + rank.shape[1:], lambda step: (first + step, 0, 0))
+    in_specs = [rank_spec, rank_spec, rows_spec(width)]
+    out_specs = [slots_spec(width)]
     shapes = [jax.ShapeDtypeStruct((experts, pairs * slots, width), bf16)]
-    if weigh:
-        specs.append(pl.BlockSpec((experts, slots, EXTRA), lambda step: (0, step, 0)))
-        shapes.append(jax.ShapeDtypeStruct((experts, pairs * slots, EXTRA), f32))
+    small = (values.shape[0], hidden)
+    if grads:
+        in_specs += [whole(shared[0])]
+        out_specs += [slots_spec(EXTRA), rows_spec(hidden)]
+        shapes += [
+            jax.ShapeDtypeStruct((experts, pairs * slots, EXTRA), f32),
+            jax.ShapeDtypeStruct(small, f32),
+        ]
+    else:
+        in_specs += [rows_spec(hidden), whole(shared[1]), whole(shared[2])]
+        out_specs += [rows_spec(hidden)] * 3
+        shapes += [jax.ShapeDtypeStruct(small, bf16)] * 3
+    aliases = {}
+    into = () if into is None else tuple(into)
+    for index, entry in enumerate(into):
+        aliases[len(in_specs)] = index
+        in_specs.append(pl.BlockSpec(memory_space=pl.ANY))
     return pl.pallas_call(
-        lambda *refs: dispatch_kernel(experts, slots, weigh, *refs),
-        grid=(pairs,),
-        in_specs=[rank_spec, rank_spec, pl.BlockSpec((tokens, width), lambda step: (step, 0))],
-        out_specs=specs,
+        lambda *refs: dispatch_kernel(experts, slots, grads, *refs),
+        grid=(count,),
+        in_specs=in_specs,
+        out_specs=out_specs,
         out_shape=shapes,
+        input_output_aliases=aliases,
         compiler_params=params(),
+        cost_estimate=cost(5),
         name="dispatch",
-    )(rank, weight, values)
-
-
-def combine_kernel(experts, slots, turned, rank_ref, rows_ref, left_ref, right_ref, out_ref):
+    )(rank, weight, values, *shared, *into)
+
+
+def combine_kernel(experts, slots, terms, turned, rank_ref, rows_ref, *refs):
+    out_ref = refs[-1]
     chosen = selection(rank_ref, experts, slots)
     select = jnp.concatenate([entry.astype(f32) for entry in chosen], axis=0).astype(bf16)
     rows = jnp.concatenate([rows_ref[k] for k in range(experts)], axis=0)
     total = lax.dot_general(select, rows, (((0,), (0,)), ((), ())), preferred_element_type=f32)
     dims = ((1,), (1,)) if turned else ((1,), (0,))
-    total = total + lax.dot_general(
-        left_ref[...], right_ref[...], (dims, ((), ())), preferred_element_type=f32
-    )
+    for k in range(terms):
+        total = total + lax.dot_general(
+            refs[2 * k][...], refs[2 * k + 1][...], (dims, ((), ())), preferred_element_type=f32
+        )
     out_ref[...] = total.astype(bf16)
 
 
-def combine(rows, rank, left, right, slots, turned):
+def combine(rows, rank, terms, slots, first, turned):
     pairs, _, tokens = rank.shape
     experts, _, width = rows.shape
+    count = terms[0][0].shape[0] // tokens
+    specs, operands = [], []
+    for left, right in terms:
+        specs += [pl.BlockSpec((tokens, left.shape[1]), lambda step: (step, 0)), whole(right)]
+        operands += [left, right]
     return pl.pallas_call(
-        lambda *refs: combine_kernel(experts, slots, turned, *refs),
-        grid=(pairs,),
+        lambda *refs: combine_kernel(experts, slots, len(terms), turned, *refs),
+        grid=(count,),
         in_specs=[
-            pl.BlockSpec((1,) + rank.shape[1:], lambda step: (step, 0, 0)),
-            pl.BlockSpec((experts, slots, width), lambda step: (0, step, 0)),
-            pl.BlockSpec((tokens, left.shape[1]), lambda step: (step, 0)),
-            whole(right),
-        ],
+            pl.BlockSpec((1,) + rank.shape[1:], lambda step: (first + step, 0, 0)),
+            pl.BlockSpec((experts, slots, width), lambda step: (0, first + step, 0)),
+        ]
+        + specs,
         out_specs=pl.BlockSpec((tokens, width), lambda step: (step, 0)),
-        out_shape=jax.ShapeDtypeStruct((pairs * tokens, width), bf16),
+        out_shape=jax.ShapeDtypeStruct((count * tokens, width), bf16),
         compiler_params=params(),
+        cost_estimate=cost(5),
         name="combine",
-    )(rank, rows, left, right)
+    )(rank, rows, *operands)
 
 
 def expert_kernel(
@@ -446,6 +539,7 @@
         out_specs=[each(entry) for entry in outputs],
         out_shape=outputs,
         compiler_params=params(),
+        cost_estimate=cost(20),
         name="expert_pass",
     )(*inputs)
 
@@ -499,6 +593,21 @@
     small_flat = jnp.concatenate(small)
     small_flat = jnp.pad(small_flat, (0, small_lanes * rows_in - small_flat.shape[0]))
 
+    bounds = jnp.cumsum(lengths[0])
+    slot = jnp.arange(tokens, dtype=jnp.int32)
+    runs = jnp.sum((slot[:, None] >= bounds[None, : SEQ_SLOTS - 1]).astype(jnp.int32), axis=1)
+    live = (runs < SEQ_SLOTS - 1).astype(f32)[:, None]
+    starts = jnp.concatenate([jnp.zeros((1,), jnp.int32), bounds[: SEQ_SLOTS - 1].astype(jnp.int32)])
+    place_in_run = slot - jnp.sum(jnp.where(runs[:, None] == jnp.arange(SEQ_SLOTS), starts, 0), axis=1)
+    beside = [runs.astype(bf16)[:, None], place_in_run.astype(bf16)[:, None], routes.astype(bf16)]
+    beside = jnp.concatenate(beside + list(split_three(route_gates)), axis=1)
+    beside = jnp.pad(beside, ((0, 0), (0, EXTRA - beside.shape[1])))
+    spread = jnp.concatenate([in_proj[:, 2 * INNER :], small_flat.reshape(rows_in, small_lanes)], axis=1)
+    spread = jnp.pad(spread, ((0, 0), (0, -spread.shape[1] % EXTRA)))
+    spread = dp_gather_rows(spread[None], 0).reshape(replicas * rows_in, -1)
+    spread = jnp.pad(spread, ((0, tokens - replicas * rows_in), (0, 0)))
+    payload = jnp.concatenate([hidden_in, beside, spread], axis=1)
+
     def by_place(block):
         block = block.reshape(rows_in, 2, half, own).transpose(2, 1, 0, 3)
         return block.reshape(groups, rows_in, own)
@@ -517,51 +626,72 @@
         axis=2,
     )
     pack = lax.all_to_all(pack, GROUP, split_axis=0, concat_axis=0, tiled=True)
-    pack = dp_gather_rows(pack.reshape(1, groups * rows_in, pack.shape[2]), 0)
-    pack = pack.reshape(devices * rows_in, pack.shape[2])
-
-    spread = jnp.concatenate([in_proj[:, 2 * INNER :], small_flat.reshape(rows_in, small_lanes)], axis=1)
-    spread = jnp.pad(spread, ((0, 0), (0, -spread.shape[1] % EXTRA)))
-    spread = dp_gather_rows(spread[None], 0).reshape(replicas * rows_in, -1)
 
     if replicas == 2:
         both = swap(out_proj, "core")
         both = jnp.concatenate(
             [jnp.where(core == 0, out_proj, both), jnp.where(core == 0, both, out_proj)]
         )
+        payload, both = tie(payload, both)
         w_out = jnp.where(lax.axis_index("dp") == core, both, swap(both, "dp"))
     else:
         w_out = lax.dynamic_slice_in_dim(
             lax.all_gather(out_proj, ALL, axis=0, tiled=True), first_channel, own, 0
         )
+    def gather_tokens():
+        size = lax.axis_size("z")
+        block, blocks, pieces = payload, [], []
+        arrived = None
+        for step in range(size):
+            following = ring(block) if step < size - 1 else ()
+            near = swap(block, "y")
+            if step == 0:
+                work = (pack, w_out)
+            elif replicas == 2 and step < 4:
+                extent = arrived.shape[0] // 3
+                work = swap(after(arrived[(step - 1) * extent : step * extent], block), "dp")
+            else:
+                work = ()
+            following, near, work = tie(following, near, work)
+            if step == 0:
+                arrived = work[0].reshape(groups * rows_in, -1)
+                found = work[1]
+            elif replicas == 2 and step < 4:
+                pieces.append(work)
+            blocks += [block, near]
+            block = following
+        near = jnp.concatenate(blocks, axis=0)
+        if replicas == 2:
+            other = jnp.concatenate(pieces, axis=0)
+            mine = lax.axis_index("dp") == 0
+            everything = jnp.concatenate(
+                [jnp.where(mine, arrived, other), jnp.where(mine, other, arrived)], axis=0
+            )
+        else:
+            everything = lax.all_gather(arrived, "dp", axis=0, tiled=True)
+        return near, swap(near, "core"), everything, found
+
+    near, mate, pack, w_out = gather_tokens()
     w_shared_down = dp_gather_rows(shared_down[None], 0).reshape(units, width)
-
-    bounds = jnp.cumsum(lengths[0])
-    slot = jnp.arange(tokens, dtype=jnp.int32)
-    runs = jnp.sum((slot[:, None] >= bounds[None, : SEQ_SLOTS - 1]).astype(jnp.int32), axis=1)
-    live = (runs < SEQ_SLOTS - 1).astype(f32)[:, None]
-    starts = jnp.concatenate([jnp.zeros((1,), jnp.int32), bounds[: SEQ_SLOTS - 1].astype(jnp.int32)])
-    place_in_run = slot - jnp.sum(jnp.where(runs[:, None] == jnp.arange(SEQ_SLOTS), starts, 0), axis=1)
-    beside = [runs.astype(bf16)[:, None], place_in_run.astype(bf16)[:, None], routes.astype(bf16), *split_three(route_gates)]
-    beside = jnp.concatenate(beside, axis=1)
-    beside = jnp.pad(beside, ((0, 0), (0, EXTRA - beside.shape[1])))
     w_gate, w_up, w_down = (
         lax.all_gather(entry, "dp", axis=1, tiled=True)
         for entry in (expert_gate, expert_up, expert_down)
     )
-    spread = jnp.pad(spread, ((0, tokens - spread.shape[0]), (0, 0)))
-    gathered = gather(jnp.concatenate([hidden_in, beside, spread], axis=1))
-    at = width + 2
-    routes_all = gathered[:, at : at + top].astype(jnp.int32)
-    gates_all = join_three([gathered[:, at + k * top : at + (k + 1) * top] for k in (1, 2, 3)])
-
+
+    table = jnp.concatenate([near[:, width : width + EXTRA], mate[:, width : width + EXTRA]], axis=0)
+    routes_all = table[:, 2 : 2 + top].astype(jnp.int32)
+    gates_all = join_three([table[:, 2 + k * top : 2 + (k + 1) * top] for k in (1, 2, 3)])
     number = jnp.arange(groups, dtype=jnp.int32)
     back_z = (lax.axis_index("z") - number // 4) % (groups // 4)
     other_y = (number // 2) % 2 != lax.axis_index("y")
     other_core = number % 2 != core
     order = other_core * half + back_z * 2 + other_y
-    spread = gathered[:, width + EXTRA :].reshape(groups, tokens, -1)[:, : replicas * rows_in]
-    spread = spread[order].reshape(groups, replicas, rows_in, -1).transpose(1, 0, 2, 3)
+
+    def blocks_of(entry):
+        return entry[:, width + EXTRA :].reshape(half, tokens, -1)[:, : replicas * rows_in]
+
+    spread = jnp.concatenate([blocks_of(near), blocks_of(mate)], axis=0)[order]
+    spread = spread.reshape(groups, replicas, rows_in, -1).transpose(1, 0, 2, 3)
     spread = spread.reshape(devices, rows_in, -1)
     small_at = 2 * STATE + HEADS
     small_all = spread[:, :, small_at : small_at + small_lanes].reshape(devices, -1)
@@ -578,7 +708,8 @@
     widen = ((0, 0), (0, WIDE - own))
     w_in = [spread[:, : 2 * STATE], jnp.pad(pack[:, own : 2 * own], widen), jnp.pad(pack[:, :own], widen), w_step]
     w_in = jnp.concatenate(w_in, axis=1)
-    w_shared = pack[:, 2 * own :]
+    w_shared_gate = pack[:, 2 * own : 2 * own + units]
+    w_shared_up = pack[:, 2 * own + units :]
 
     def own_channels(rows):
         return lax.dynamic_slice_in_dim(rows, first_channel, own, rows.ndim - 1)
@@ -604,39 +735,13 @@
     rate_rows = jnp.broadcast_to(jnp.pad(rate, (0, 8 - heads))[:, None], (8, EXTRA))
     w_out = jnp.pad(w_out, ((0, WIDE - own), (0, 0)))
 
-    normed, proj, mixed_part, scaled = mixer_forward(
-        gathered, width, tokens, norm_gain_all[None], w_in, w_out, conv, head
-    )
+    input_rows = hidden_in.astype(f32)
     grad_out = cotangent.astype(f32)
-    branch = (grad_out * live).astype(bf16)
-    branch_all = gather(after(branch, gathered))
-    mixed_part, branch_all = lax.optimization_barrier((mixed_part, branch_all))
-    mixed_sum = scatter(mixed_part)
-    mix_rms = lax.rsqrt(jnp.sum(mixed_sum[:, width:], axis=1, keepdims=True) / INNER + epsilon)
-    mixer_out = mixed_sum[:, :width] * mix_rms
-    input_rows = hidden_in.astype(f32)
-    resid = input_rows + live * mixer_out
-    ffn_rms = lax.rsqrt(jnp.mean(resid * resid, axis=1, keepdims=True) + epsilon)
-    ffn_hat = resid * ffn_rms
-    ffn_low = (ffn_hat * ffn_gain_all).astype(bf16)
-
-    ffn_all = gather(ffn_low)
-
-    shared_gu = matmul(ffn_all, w_shared)
-
-    def swiglu(both):
-        extent = both.shape[-1] // 2
-        return jax.nn.silu(both[..., :extent]) * both[..., extent:]
-
-    shared_act, shared_back = jax.vjp(swiglu, shared_gu)
-    shared_low = shared_act.astype(bf16)
-    (grad_shared_gu,) = shared_back(matmul(branch_all, w_shared_down, (((1,), (1,)), ((), ()))))
-    shared_gu_low = grad_shared_gu.astype(bf16)
+    branch = after((grad_out * live).astype(bf16), near)
 
     pairs = groups // 2
     pair_tokens = 2 * tokens
     pair_slots = 2 * capacity
-    lanes = pairs * pair_slots
     numbers = place * local_experts + jnp.arange(local_experts, dtype=jnp.int32)
     named = routes_all[:, None, :] == numbers[None, :, None]
     member = jnp.any(named, axis=2).T.reshape(local_experts, pairs, pair_tokens)
@@ -647,26 +752,65 @@
     rank = jnp.where(member, rank.astype(jnp.int32) - 1, -1).transpose(1, 0, 2)
     rank = jnp.pad(rank, ((0, 0), (0, 8 - local_experts), (0, 0)), constant_values=-1)
     weight = jnp.pad(weight.transpose(1, 0, 2), ((0, 0), (0, 8 - local_experts), (0, 0)))
-    d_row, slot_weight = dispatch(branch_all, rank, weight, local_experts, pair_slots, True)
-    (expert_in,) = dispatch(ffn_all, rank, weight, local_experts, pair_slots, False)
+    half_pairs = pairs // 2
+
+    def rows_out(values, first, shared, into=None):
+        return dispatch(values, rank, weight, local_experts, pair_slots, first, shared, into)
+
+    mixer = (norm_gain_all[None], w_in, w_out, conv, head)
+
+    def forward(part):
+        return lambda token: mixer_forward(after(part, token), width, tokens, *after(mixer, token))
+
+    branch_near, branch_mate, ((mixer_set, w_gate), done_mate, done_near, _) = gather(
+        branch, [(mixer, w_gate), forward(mate), forward(near)]
+    )
+    _, w_in, w_out, conv, head = mixer_set
+    normed_mate, proj_mate, mixed_mate, scaled_mate = done_mate
+    normed_near, proj_near, mixed_near, scaled_near = done_near
+    pairs_sum = scatter_first(mixed_near, mixed_mate)
+    d_row, slot_weight, act_grad_near = rows_out(branch_near, 0, (w_shared_down,))
+    d_row, slot_weight, act_grad_mate = rows_out(
+        branch_mate, half_pairs, (w_shared_down,), (d_row, slot_weight)
+    )
+    mixed_sum, (_, d_row, w_up, *_) = scatter_last(pairs_sum, [(), d_row, w_up])
+    mix_rms = lax.rsqrt(jnp.sum(mixed_sum[:, width:], axis=1, keepdims=True) / INNER + epsilon)
+    mixer_out = mixed_sum[:, :width] * mix_rms
+    resid = input_rows + live * mixer_out
+    ffn_rms = lax.rsqrt(jnp.mean(resid * resid, axis=1, keepdims=True) + epsilon)
+    ffn_hat = resid * ffn_rms
+    ffn_near, ffn_mate, _ = gather((ffn_hat * ffn_gain_all).astype(bf16))
+
+    expert_in, shared_near, sg_near, su_near = rows_out(
+        ffn_near, 0, (act_grad_near, w_shared_gate, w_shared_up)
+    )
+    expert_in, shared_mate, sg_mate, su_mate = rows_out(
+        ffn_mate, half_pairs, (act_grad_mate, w_shared_gate, w_shared_up), (expert_in,)
+    )
     act_low, g_low, u_low, d_in_row, expert_row = expert_pass(
         expert_in, d_row, slot_weight, w_gate, w_up, w_down
     )
+
     half_grad = (((1,), (1,)), ((0,), (0,)))
-
-    def expert_grad(left, right):
-        total = matmul(left, right, half_grad).astype(bf16)
-        return lax.psum_scatter(total, "dp", scatter_dimension=1, tiled=True).astype(f32)
-
-    grad_ffn_part = combine(d_in_row, rank, shared_gu_low, w_shared, pair_slots, True)
-    grad_ffn = scatter(grad_ffn_part)
-    (expert_in, expert_row, act_low, shared_low, ffn_all) = after(
-        (expert_in, expert_row, act_low, shared_low, ffn_all), grad_ffn_part
-    )
-    grad_down = expert_grad(act_low, d_row)
-    grad_gate = expert_grad(expert_in, g_low)
-    grad_up = expert_grad(expert_in, u_low)
-    branch_part = combine(expert_row, rank, shared_low, w_shared_down, pair_slots, False)
+    grad_down = matmul(act_low, d_row, half_grad).astype(bf16)
+    d_in_row, grad_down = tie(d_in_row, grad_down)
+
+    def back_rows(sg, su, first):
+        terms = ((sg, w_shared_gate), (su, w_shared_up))
+        return combine(d_in_row, rank, terms, pair_slots, first, True)
+
+    grad_ffn_mate = back_rows(sg_mate, su_mate, half_pairs)
+    grad_ffn_near = back_rows(sg_near, su_near, 0)
+    pairs_sum = scatter_first(grad_ffn_near, grad_ffn_mate)
+
+    def leaving_of(part):
+        return lambda token: matmul(after(expert_in, token), part, half_grad).astype(bf16)
+
+    grad_ffn, leaving = scatter_last(pairs_sum, [leaving_of(g_low), leaving_of(u_low)])
+    grad_down, grad_gate, grad_up = (
+        lax.psum_scatter(entry, "dp", scatter_dimension=1, tiled=True)
+        for entry in (grad_down, *leaving[:2])
+    )
 
     grad_ffn_gain = jnp.sum(grad_ffn * ffn_hat, axis=0)
     scaled_ffn = grad_ffn * ffn_gain_all
@@ -677,33 +821,130 @@
     inner_term = jnp.sum(d_mixer * mixer_out, axis=1, keepdims=True) * mix_rms * mix_rms / INNER
     inner_pack = jnp.pad(jnp.concatenate(split_three(inner_term), axis=1), ((0, 0), (0, EXTRA - 3)))
     d_mixer_pack = jnp.concatenate([(d_mixer * mix_rms).astype(bf16), inner_pack], axis=1)
-    d_mixer_all = gather(d_mixer_pack)
-    output = (resid + live * scatter(after(branch_part, d_mixer_all))).astype(bf16)
-    grad_normed_part, proj_low, conv_grads, head_grads = mixer_backward(
-        d_mixer_all, gathered, proj, width, tokens, w_in, w_out, conv, head, rate_rows
-    )
-    grad_normed_part, output = lax.optimization_barrier((grad_normed_part, output))
-    grad_normed = scatter(grad_normed_part)
-    normed, scaled = after((normed, scaled), grad_normed_part)
-    grad_w_in = matmul(normed, proj_low, (((0,), (0,)), ((), ())))
-    grad_out_rows = matmul(scaled, d_mixer_all[:, :width], (((0,), (0,)), ((), ())))[:own]
-    shared_low, ffn_all = after((shared_low, ffn_all), d_mixer_all)
-    grad_shared_down = matmul(shared_low, branch_all, (((0,), (0,)), ((), ())))
-    grad_shared_w = matmul(ffn_all, shared_gu_low, (((0,), (0,)), ((), ())))
-
-    value_at, gate_at = 2 * STATE, CONV_LANES
-    grad_pack = jnp.concatenate(
+
+    def out_rows(shared_act, first):
+        def work(token):
+            terms = ((shared_act, w_shared_down),)
+            return combine(after(expert_row, token), rank, terms, pair_slots, first, False)
+
+        return work
+
+    turned = (((0,), (0,)), ((), ()))
+
+    def of_halves(left, right):
+        return matmul(left[0], right[0], turned) + matmul(left[1], right[1], turned)
+
+    def shared_grads_of(token):
+        halves = after(((branch_near, branch_mate), (ffn_near, ffn_mate)), token)
+        return (
+            of_halves((shared_near, shared_mate), halves[0]),
+            of_halves(halves[1], (sg_near, sg_mate)),
+            of_halves(halves[1], (su_near, su_mate)),
+        )
+
+    d_mixer_near, d_mixer_mate, (out_mate, out_near, shared_grads, grad_down) = gather(
+        d_mixer_pack,
         [
-            grad_w_in[:, gate_at : gate_at + own],
-            grad_w_in[:, value_at : value_at + own],
-            grad_w_in[:, : 2 * STATE],
-            grad_w_in[:, CONV_LANES + WIDE :],
-            grad_shared_w,
+            out_rows(shared_mate, half_pairs),
+            out_rows(shared_near, 0),
+            shared_grads_of,
+            lambda token: after(grad_down, token).astype(f32),
         ],
-        axis=1,
-    )
-    proj_lanes = 2 * own + 2 * STATE + EXTRA
-    grad_pack = dp_scatter_rows(grad_pack, 0).astype(bf16).reshape(groups, rows_in, -1)
+    )
+    grad_shared_down, grad_shared_g, grad_shared_u = shared_grads
+    grad_shared_gu = dp_scatter_rows(jnp.concatenate([grad_shared_g, grad_shared_u], axis=1), 0)
+    out_pairs = scatter_first(out_near, out_mate)
+    (d_mixer_near, d_mixer_mate), out_pairs = tie((d_mixer_near, d_mixer_mate), out_pairs)
+
+    def backward(grads, part, proj):
+        return mixer_backward(grads, part, proj, width, tokens, w_in, w_out, conv, head, rate_rows)
+
+    done_mate = backward(d_mixer_mate, mate, proj_mate)
+    out_there = {step: swap(out_pairs[step][1], "y") for step in (1, 2)}
+    d_mixer_near, out_pairs, out_there, done_mate = tie(d_mixer_near, out_pairs, out_there, done_mate)
+    done_near = backward(d_mixer_near, near, proj_near)
+    out_total = ring_step(add_low(out_pairs[1][0], out_there[1]), out_pairs, out_there, 1)
+    out_there |= {step: swap(out_pairs[step][1], "y") for step in (3, 0)}
+    moved = swap(done_mate[0], "core")
+    done_near, out_total, out_there, moved = tie(done_near, out_total, out_there, moved)
+    normed_grad_mate, proj_low_mate, conv_mate, head_mate = done_mate
+    normed_grad_near, proj_low_near, conv_near, head_near = done_near
+    pairs_sum = scatter_first(normed_grad_near, normed_grad_mate, moved)
+
+    def to_owner(part):
+        rows_part = jnp.zeros((part.shape[0], CONV_CH), f32)
+        values = part[:, 2 * STATE : 2 * STATE + own]
+        rows_part = lax.dynamic_update_slice_in_dim(rows_part, values, first_channel, 1)
+        rows_part = lax.dynamic_update_slice_in_dim(rows_part, part[:, : 2 * STATE], INNER, 1)
+        return rows_part.reshape(part.shape[0], devices, -1).transpose(1, 0, 2).reshape(devices, -1)
+
+    def head_row(part):
+        return lax.dynamic_update_slice_in_dim(jnp.zeros((HEADS,), f32), part, first_head, 0)
+
+    def small_sums(conv_grads, head_grads):
+        head_grads = jnp.sum(head_grads.reshape(3, 8, EXTRA)[:, :heads], axis=2)
+        head_rows = [head_row(entry) for entry in (head_grads[0] * rate, *head_grads[1:])]
+        return jnp.concatenate(
+            [
+                to_owner(conv_grads[: KERNEL + 1]),
+                grad_ffn_gain.reshape(devices, -1),
+                jnp.broadcast_to(jnp.concatenate(head_rows)[None], (devices, 3 * HEADS)),
+            ],
+            axis=1,
+        )
+
+    crossing = replicas == 2
+    here = lax.axis_index("dp")
+    normed_rows = width // 2 if crossing else width
+
+    def input_grad(where, token):
+        parts = after((normed_near, normed_mate), token)
+        if crossing:
+            parts = [lax.dynamic_slice_in_dim(part, where * normed_rows, normed_rows, 1) for part in parts]
+        return of_halves(parts, (proj_low_near, proj_low_mate))
+
+    def piece(array, index, token):
+        extent = array.shape[0] // 3
+        return swap(after(array[index * extent : (index + 1) * extent], token), "dp")
+
+    pieces = []
+
+    def window_one(token):
+        return input_grad(1 - here, token).astype(bf16)
+
+    def window_two(token):
+        conv_parts, head_parts = after(((conv_mate, conv_near), (head_mate, head_near)), token)
+        return small_sums(sum(conv_parts), sum(head_parts))
+
+    def window_three(token):
+        parts = after((scaled_near, scaled_mate), token)
+        return of_halves(parts, (d_mixer_near[:, :width], d_mixer_mate[:, :width]))[:own]
+
+    there = scatter_beside(pairs_sum)
+    total = add_low(pairs_sum[1][0], there[1])
+    total, leaving = tie(total, window_one(pairs_sum))
+    works = (window_two, window_three, lambda token: input_grad(here, token))
+    finished = []
+    for index, work in enumerate(works):
+        following = ring_step(total, pairs_sum, there, index + 1)
+        across = piece(leaving, index, total) if crossing else ()
+        if index < 2:
+            out_total = ring_step(after(out_total, total), out_pairs, out_there, index + 2)
+        result = work(total)
+        total, across, out_total, result = tie(following, across, out_total, result)
+        pieces.append(across)
+        finished.append(result)
+    grad_normed, branch_sum = total, out_total
+    sums, grad_out_rows, grad_w_in = finished
+    output = (resid + live * branch_sum).astype(bf16)
+    grad_gate, grad_up = grad_gate.astype(f32), grad_up.astype(f32)
+
+    if crossing:
+        grad_w_in = grad_w_in + jnp.concatenate(pieces, axis=0).astype(f32)
+    else:
+        grad_w_in = lax.psum_scatter(leaving, "dp", scatter_dimension=0, tiled=True)
+    grad_pack = jnp.concatenate([grad_w_in.astype(bf16), grad_shared_gu.astype(bf16)], axis=1)
+    grad_pack = grad_pack.reshape(groups, rows_in, -1)
     grad_pack = lax.all_to_all(grad_pack, GROUP, split_axis=0, concat_axis=0, tiled=True).astype(f32)
 
     def from_place(block):
@@ -714,18 +955,18 @@
         block = block.reshape(groups, rows_in, replicas, unit).transpose(1, 2, 0, 3)
         return block.reshape(rows_in, hidden_units)
 
-    both_at = 2 * own + 2 * STATE
+    value_at, gate_at, step_at = 2 * STATE, CONV_LANES, CONV_LANES + WIDE
     grad_in_proj = jnp.concatenate(
         [
-            from_place(grad_pack[:, :, :own]),
-            from_place(grad_pack[:, :, own : 2 * own]),
-            jnp.sum(grad_pack[:, :, 2 * own : both_at], axis=0),
-            from_place(grad_pack[:, :, both_at : both_at + heads]),
+            from_place(grad_pack[:, :, gate_at : gate_at + own]),
+            from_place(grad_pack[:, :, value_at : value_at + own]),
+            jnp.sum(grad_pack[:, :, : 2 * STATE], axis=0),
+            from_place(grad_pack[:, :, step_at : step_at + heads]),
         ],
         axis=1,
     )
-    grad_shared_gate = from_unit(grad_pack[:, :, proj_lanes : proj_lanes + units])
-    grad_shared_up = from_unit(grad_pack[:, :, proj_lanes + units :])
+    grad_shared_gate = from_unit(grad_pack[:, :, PROJ_LANES : PROJ_LANES + units])
+    grad_shared_up = from_unit(grad_pack[:, :, PROJ_LANES + units :])
     grad_shared_down = dp_scatter_rows(grad_shared_down.reshape(replicas, unit, width), 0)[0]
     if replicas == 2:
         mine = lax.axis_index("dp") == core
@@ -740,26 +981,6 @@
     grad_mix_gain = jnp.sum(grad_out_proj * out_proj.astype(f32), axis=1) / mix_gain.astype(f32)
     grad_norm_gain = jnp.sum(grad_in_proj * in_proj.astype(f32), axis=1) / norm_gain.astype(f32)
 
-    def to_owner(part):
-        rows_part = jnp.zeros((part.shape[0], CONV_CH), f32)
-        values = part[:, 2 * STATE : 2 * STATE + own]
-        rows_part = lax.dynamic_update_slice_in_dim(rows_part, values, first_channel, 1)
-        rows_part = lax.dynamic_update_slice_in_dim(rows_part, part[:, : 2 * STATE], INNER, 1)
-        return rows_part.reshape(part.shape[0], devices, -1).transpose(1, 0, 2).reshape(devices, -1)
-
-    def head_row(part):
-        return lax.dynamic_update_slice_in_dim(jnp.zeros((HEADS,), f32), part, first_head, 0)
-
-    head_grads = jnp.sum(head_grads.reshape(3, 8, EXTRA)[:, :heads], axis=2)
-    head_rows = jnp.concatenate([head_row(entry) for entry in (head_grads[0] * rate, *head_grads[1:])])
-    sums = jnp.concatenate(
-        [
-            to_owner(conv_grads[: KERNEL + 1]),
-            grad_ffn_gain.reshape(devices, -1),
-            jnp.broadcast_to(head_rows[None], (devices, 3 * HEADS)),
-        ],
-        axis=1,
-    )
     sums = lax.all_to_all(sums, ALL, split_axis=0, concat_axis=0, tiled=True)
     sums = jnp.sum(sums, axis=0)
     channels = CONV_CH // devices

time: 805 us -> 721 us (0.90)
  waiting for transfers between devices: 297 us -> 219 us
  local copies, waits for them, and re-layouts: 115 us -> 88.5 us
  Pallas kernels: 125 us -> 146 us
    ppermute x24, waiting for transfers between devices: 105 us -> 67.8 us  [ring(): return lax.ppermute(value, 'z', [(k, (k + 1) % size) for k in range(size)])]
    all_to_all x1, waiting for transfers between devices: 33.7 us -> 0.01 us  [local(): sums = lax.all_to_all(sums, ALL, split_axis=0, concat_axis=0, tiled=True)]
    all_to_all x1, waiting for transfers between devices: 20.5 us -> 2.41 us  [local(): pack = lax.all_to_all(pack, GROUP, split_axis=0, concat_axis=0, tiled=True)]
    concatenate x10 -> x8, local copies, waits for them, and re-layouts: 19.4 us -> 3.89 us  [the longest x3 2.61 us: gather(): own = jnp.concatenate(blocks, axis=0)]
    ppermute x24, starting transfers between devices: 22.1 us -> 33.3 us  [ring(): return lax.ppermute(value, 'z', [(k, (k + 1) % size) for k in range(size)])]
    unnamed x119 -> x216, local copies, waits for them, and re-layouts: 39.7 us -> 28.7 us
    pallas_call x4 -> x8, Pallas kernels: 35.7 us -> 46 us  [the longest x4 23 us: combine(): pl.pallas_call(lambda *refs: combine_kernel(experts, slots, len(terms), t...]
    slice x13 -> x23, local copies, waits for them, and re-layouts: 22.6 us -> 12.5 us  [the longest x12 4.1 us: scatter_beside(): there = {step: swap(pairs[step][1], 'y') for step in order}]
  transfers between devices with their start and end apart: 82 -> 87, of which waited for: 48 -> 40; matrix products, arithmetic and copies ran while one was open for 27% -> 26% of each run, Pallas kernels for 12% -> 18%
where the time goes in v3:
time: 721 us; the launch traced here: 711 us
  waiting for transfers between devices  219 us (30%)
  Pallas kernels  146 us (20%)
  starting transfers between devices  110 us (15%)
  local copies, waits for them, and re-layouts  88.5 us (12%)
  other arithmetic  85.4 us (12%)
  matrix products  46.6 us (6%)
  between operations  16.3 us (2%)
    ppermute x54, waiting for transfers between devices, swap(): return lax.ppermute(value, axis, [(0, 1), (1, 0)])  140 us
    ppermute x24, waiting for transfers between devices, ring(): return lax.ppermute(value, 'z', [(k, (k + 1) % size) for k in range(size)])  67.8 us
    ppermute x54, starting transfers between devices, swap(): return lax.ppermute(value, axis, [(0, 1), (1, 0)])  52.7 us
    pallas_call x2, Pallas kernels, mixer_backward(): pl.pallas_call(lambda *refs: mixer_backward_kernel(count, *refs), grid=(t...  49.2 us
    dot_general x16, matrix products, matmul(): lax.dot_general(left, right, dims, precision=precision, preferred_element...  46.6 us
    ppermute x24, starting transfers between devices, ring(): return lax.ppermute(value, 'z', [(k, (k + 1) % size) for k in range(size)])  33.3 us
    pallas_call x2, Pallas kernels, mixer_forward(): pl.pallas_call(lambda *refs: mixer_forward_kernel(count, *refs), grid=(to...  29.9 us
    unnamed x216, local copies, waits for them, and re-layouts  28.7 us
  transfers between devices with their start and end apart: 87, of which 40 were waited for; matrix products, arithmetic and copies ran while one was open for 26% of the time, Pallas kernels for 18%

profile of v3, /device:TPU:13, one launch (start us, length us, event | category | flops | bytes accessed | tf_op | source)
XLA Modules:
  0.0 711.3 jit_solution(7546128323784213074)
XLA Ops:
  19.4 6.1 all-to-all-start
  29.2 14.3 %collective-permute-done.4 = bf16[192,1536]{1,0:T(8,128)(2,1)S(1)} collective-permute-done((bf16[192,1536]{1,0:T(8,128)(2,1)S(1)}, bf16[192,1536]{1,0:T(8,128)(2,1)S(1)}, u32[]{:S(2)}, u32[]{:S(2)}) %collective-permute-start.4) | collective-permute-done | bytes 589856 | tf_op jit(solution)/shard_map/ppermute | solution.py:31
  43.6 10.4 %collective-permute-done.2 = bf16[128,2048]{1,0:T(8,128)(2,1)} collective-permute-done((bf16[128,2048]{1,0:T(8,128)(2,1)S(1)}, bf16[128,2048]{1,0:T(8,128)(2,1)}, u32[]{:S(2)}, u32[]{:S(2)}) %collective-permute-start.2) | collective-permute-done | bytes 524320 | tf_op jit(solution)/shard_map/ppermute | solution.py:36
  57.8 12.3 %collective-permute-done.7 = bf16[256,512]{1,0:T(8,128)(2,1)S(1)} collective-permute-done((bf16[256,512]{1,0:T(8,128)(2,1)S(1)}, bf16[256,512]{1,0:T(8,128)(2,1)S(1)}, u32[]{:S(2)}, u32[]{:S(2)}) %collective-permute-start.7) | collective-permute-done | bytes 262176 | tf_op jit(solution)/shard_map/ppermute | solution.py:31
  77.0 10.1 %collective-permute-done.10 = bf16[256,512]{1,0:T(8,128)(2,1)S(1)} collective-permute-done((bf16[256,512]{1,0:T(8,128)(2,1)S(1)}, bf16[256,512]{1,0:T(8,128)(2,1)S(1)}, u32[]{:S(2)}, u32[]{:S(2)}) %collective-permute-start.10) | collective-permute-done | bytes 262176 | tf_op jit(solution)/shard_map/ppermute | solution.py:31
  90.3 10.8 %collective-permute-done.12 = bf16[256,512]{1,0:T(8,128)(2,1)S(1)} collective-permute-done((bf16[256,512]{1,0:T(8,128)(2,1)S(1)}, bf16[256,512]{1,0:T(8,128)(2,1)S(1)}, u32[]{:S(2)}, u32[]{:S(2)}) %collective-permute-start.12) | collective-permute-done | bytes 262176 | tf_op jit(solution)/shard_map/ppermute | solution.py:31
  102.0 4.2 collective-permute-start.15
  131.3 2.8 fusion.9.refs_3_.refs_4_
  139.2 15.4 %mixer_forward.2 = (bf16[1024,1536]{1,0:T(8,128)(2,1)}, f32[1024,896]{1,0:T(8,128)}, bf16[1024,1664]{1,0:T(8,128)(2,1)}, bf16[1024,256]{1,0:T(8,128)(2,1)}) custom-call(bf16[1024,2048]{1,0:T(8,128)(2,1)} %collective-permute-done.15.refs_0_.refs_1_.refs_2_, bf16[1024,2048]{1,0:T(8,128)(2,1)} %collective-permute-done.15.refs_0_.refs_1_.refs_2_, ...), custom_call_target="tpu_custom_call" | custom-call | flops 14080000000 | bytes 44800000 | tf_op jit(solution)/shard_map/mixer_forward/pallas_call | solution.py:259
  161.5 14.5 %mixer_forward.3 = (bf16[1024,1536]{1,0:T(8,128)(2,1)}, f32[1024,896]{1,0:T(8,128)}, bf16[1024,1664]{1,0:T(8,128)(2,1)}, bf16[1024,256]{1,0:T(8,128)(2,1)}) custom-call(bf16[1024,2048]{1,0:T(8,128)(2,1)} %constant_dynamic-update-slice_fusion.refs_0_.refs_1_.refs_2_, bf16[1024,2048]{1,0:T(8,128)(2,1)} %constant_dynamic-update-slice_fusion.refs_0_.refs_1_.refs_2_, ...), custom_call_target="tpu_custom_call" | custom-call | flops 14080000000 | bytes 44800000 | tf_op jit(solution)/shard_map/mixer_forward/pallas_call | solution.py:259
  179.4 8.9 %collective-permute-done.24 = bf16[128,1536]{1,0:T(8,128)(2,1)S(1)} collective-permute-done((bf16[128,1536]{1,0:T(8,128)(2,1)S(1)}, bf16[128,1536]{1,0:T(8,128)(2,1)S(1)}, u32[]{:S(2)}, u32[]{:S(2)}) %collective-permute-start.24) | collective-permute-done | bytes 393248 | tf_op jit(solution)/shard_map/ppermute | solution.py:31
  198.6 3.7 add_convert_fusion.5
  202.8 5.3 dispatch.4
  209.8 4.1 collective-permute-done.21
  214.1 5.3 dispatch.5
  219.3 3.7 collective-permute-done.23
  225.8 6.4 collective-permute-done.28
  232.1 3.1 collective-permute-done.27
  236.3 4.9 collective-permute-done.30
  241.3 5.3 collective-permute-done.29
  249.4 8.1 %collective-permute-done.31 = bf16[128,1536]{1,0:T(8,128)(2,1)S(1)} collective-permute-done((bf16[128,1536]{1,0:T(8,128)(2,1)S(1)}, bf16[128,1536]{1,0:T(8,128)(2,1)S(1)}, u32[]{:S(2)}, u32[]{:S(2)}) %collective-permute-start.31) | collective-permute-done | bytes 393248 | tf_op jit(solution)/shard_map/ppermute | solution.py:36
  258.1 7.8 %collective-permute-done.33 = bf16[128,1536]{1,0:T(8,128)(2,1)S(1)} collective-permute-done((bf16[128,1536]{1,0:T(8,128)(2,1)S(1)}, bf16[128,1536]{1,0:T(8,128)(2,1)S(1)}, u32[]{:S(2)}, u32[]{:S(2)}) %collective-permute-start.33) | collective-permute-done | bytes 393248 | tf_op jit(solution)/shard_map/ppermute | solution.py:36
  265.9 10.5 %collective-permute-start.35 = (bf16[128,1536]{1,0:T(8,128)(2,1)S(1)}, bf16[128,1536]{1,0:T(8,128)(2,1)S(1)}, u32[]{:S(2)}, u32[]{:S(2)}) collective-permute-start(bf16[128,1536]{1,0:T(8,128)(2,1)S(1)} %collective-permute-done.33), channel_id=1, source_target_pairs={{0,4},{4,8},{8,12},{12,0},{1,5},{5,9},{9,13},{13,1},{2,6},{6,10},{... | collective-permute-start | bytes 1179656 | tf_op jit(solution)/shard_map/ppermute | solution.py:36
  277.0 5.7 collective-permute-done.35
  284.0 10.5 %collective-permute-done.37 = bf16[128,1536]{1,0:T(8,128)(2,1)S(1)} collective-permute-done((bf16[128,1536]{1,0:T(8,128)(2,1)S(1)}, bf16[128,1536]{1,0:T(8,128)(2,1)S(1)}, u32[]{:S(2)}, u32[]{:S(2)}) %collective-permute-start.37) | collective-permute-done | bytes 393248 | tf_op jit(solution)/shard_map/ppermute | solution.py:31
  294.5 8.3 %collective-permute-start.38 = (bf16[1024,1536]{1,0:T(8,128)(2,1)S(1)}, bf16[1024,1536]{1,0:T(8,128)(2,1)S(1)}, u32[]{:S(2)}, u32[]{:S(2)}) collective-permute-start(bf16[1024,1536]{1,0:T(8,128)(2,1)S(1)} %constant_dynamic-update-slice_fusion.19.refs_2_), channel_id=1, source_target_pairs={{0,1},{1,0},{2,3},{3,2},{4,5},{5,4},{6,7},{7,6},{8,9},{9,8},{10,11... | collective-permute-start | bytes 9437192 | tf_op jit(solution)/shard_map/ppermute | solution.py:31
  303.9 6.1 dispatch.6
  311.7 6.2 dispatch.7
  317.9 5.3 all-gather.8.cloned.1.call-done.down_ref
  323.2 20.6 %expert_pass.1 = (bf16[4,384,512]{2,1,0:T(8,128)(2,1)}, bf16[4,384,512]{2,1,0:T(8,128)(2,1)}, bf16[4,384,512]{2,1,0:T(8,128)(2,1)}, bf16[4,384,1536]{2,1,0:T(8,128)(2,1)}, bf16[4,384,1536]{2,1,0:T(8,128)(2,1)}) custom-call(bf16[4,384,1536]{2,1,0:T(8,128)(2,1)} %get-tuple-element.271.rows_ref, bf16[4,384,1536]{2,1,0:T(8,128)(2,1)} %get-tuple-element.258.grad_ref, ...), custom_call_target="tpu_custom_call" | custom-call | flops 22000001024 | bytes 70000000 | tf_op jit(solution)/shard_map/expert_pass/pallas_call | solution.py:535
  343.8 6.8 convolution_convert_fusion.2
  350.7 6.2 combine.5
  357.6 6.4 combine.4
  364.0 3.8 add_convert_fusion.17
  368.3 5.4 convolution_convert_fusion.1
  373.7 5.0 collective-permute-done.40
  384.4 9.3 %convolution_convert_fusion = bf16[4,1536,512]{2,1,0:T(8,128)(2,1)} fusion(bf16[4,384,1536]{2,1,0:T(8,128)(2,1)} %get-tuple-element.271.rows_ref, bf16[4,384,512]{2,1,0:T(8,128)(2,1)} %get-tuple-element.272), kind=kOutput, calls=%fused_computation.7 | convolution fusion | flops 2419064832 | bytes 12582912 | tf_op jit(solution)/shard_map/dot_general | solution.py:27
  396.8 3.1 collective-permute-done.44
  399.9 4.5 collective-permute-done.43
  408.4 5.3 collective-permute-done.45
  417.7 5.1 combine.6
  426.0 5.3 collective-permute-start.55
  432.9 5.3 combine.7
  438.1 4.4 collective-permute-start.51
  456.9 5.6 convert_element_type.766
  462.5 3.4 collective-permute-done.53
  473.2 4.5 collective-permute-done.77
  478.3 7.8 %collective-permute-done.74 = bf16[768,128]{0,1:T(8,128)(2,1)S(1)} collective-permute-done((bf16[768,128]{0,1:T(8,128)(2,1)S(1)}, bf16[768,128]{0,1:T(8,128)(2,1)S(1)}, u32[]{:S(2)}, u32[]{:S(2)}) %collective-permute-start.74) | collective-permute-done | bytes 196640 | tf_op jit(solution)/shard_map/ppermute | solution.py:31
  487.0 3.8 add_convert_fusion.10
  493.2 24.5 %mixer_backward.2 = (bf16[1024,1536]{1,0:T(8,128)(2,1)}, bf16[1024,896]{1,0:T(8,128)(2,1)}, f32[8,512]{1,0:T(8,128)}, f32[24,128]{1,0:T(8,128)}) custom-call(bf16[1024,1664]{1,0:T(8,128)(2,1)} %collective-permute-done.54.refs_0_.refs_1_, bf16[1024,1664]{1,0:T(8,128)(2,1)} %collective-permute-done.54.refs_0_.refs_1_, ...), custom_call_target="tpu_custom_call" | custom-call | flops 24486957056 | bytes 77913040 | tf_op jit(solution)/shard_map/mixer_backward/pallas_call | solution.py:363
  523.0 24.8 %mixer_backward.3 = (bf16[1024,1536]{1,0:T(8,128)(2,1)}, bf16[1024,896]{1,0:T(8,128)(2,1)}, f32[8,512]{1,0:T(8,128)}, f32[24,128]{1,0:T(8,128)}) custom-call(bf16[1024,1664]{1,0:T(8,128)(2,1)} %constant_dynamic-update-slice_fusion.27.refs_0_.refs_1_, bf16[1024,1664]{1,0:T(8,128)(2,1)} %constant_dynamic-update-slice_fusion.27.refs_0_.refs_1_, ...), custom_call_target="tpu_custom_call" | custom-call | flops 24486957056 | bytes 77913040 | tf_op jit(solution)/shard_map/mixer_backward/pallas_call | solution.py:363
  547.9 4.0 fusion.13
  560.1 3.1 add_convert_fusion.1
  572.6 10.6 %collective-permute-done.66 = bf16[128,1536]{1,0:T(8,128)(2,1)} collective-permute-done((bf16[128,1536]{1,0:T(8,128)(2,1)}, bf16[128,1536]{1,0:T(8,128)(2,1)}, u32[]{:S(2)}, u32[]{:S(2)}) %collective-permute-start.66) | collective-permute-done | bytes 393248 | tf_op jit(solution)/shard_map/ppermute | solution.py:36
  588.5 12.3 %collective-permute-done.65 = bf16[256,896]{1,0:T(8,128)(2,1)} collective-permute-done((bf16[256,896]{1,0:T(8,128)(2,1)}, bf16[256,896]{1,0:T(8,128)(2,1)}, u32[]{:S(2)}, u32[]{:S(2)}) %collective-permute-start.65) | collective-permute-done | bytes 458784 | tf_op jit(solution)/shard_map/ppermute | solution.py:31
  604.1 6.9 all-to-all-start.2
  611.0 3.1 fusion.5
  614.2 2.9 fusion.3
  634.7 11.0 %all-to-all-start.1 = ((bf16[16,48,1024]{2,1,0:T(8,128)(2,1)}), bf16[16,48,1024]{2,1,0:T(8,128)(2,1)}, u32[]{:S(2)}, u32[]{:S(2)}) async-start(bf16[16,48,1024]{2,1,0:T(8,128)(2,1)} %bitcast.168), calls=%async_computation.2 | async-start | bytes 3145728 | tf_op jit(solution)/shard_map/all_to_all | solution.py:948
  647.4 5.5 convert_element_type.845
  652.9 5.5 convert_element_type.846
  662.9 12.4 %collective-permute-done.75 = bf16[192,1536]{1,0:T(8,128)(2,1)S(1)} collective-permute-done((bf16[192,1536]{1,0:T(8,128)(2,1)S(1)}, bf16[192,1536]{1,0:T(8,128)(2,1)S(1)}, u32[]{:S(2)}, u32[]{:S(2)}) %collective-permute-start.75) | collective-permute-done | bytes 589856 | tf_op jit(solution)/shard_map/ppermute | solution.py:31
  682.0 4.6 copy.241
  686.7 3.2 convert_element_type.836
  (586 shorter events, 218.8 us)
Async XLA Ops:
  11.9 15.2 %collective-permute-start = (bf16[1,48,384]{2,1,0:T(8,128)(2,1)S(1)}, bf16[1,48,384]{2,1,0:T(8,128)(2,1)S(1)}, u32[]{:S(2)}, u32[]{:S(2)}) collective-permute-start(bf16[1,48,384]{2,1,0:T(8,128)(2,1)S(1)} %fusion.60), channel_id=1, source_target_pairs={{0,16},{16,0},{1,17},{17,1},{2,18},{18,2},{3,19},{19,3},{4,20},{20... | collective-permute-start | bytes 110600 | tf_op jit(solution)/shard_map/ppermute | solution.py:31
  13.1 14.2 %collective-permute-start.1 = (bf16[96,1536]{1,0:T(8,128)(2,1)}, bf16[96,1536]{1,0:T(8,128)(2,1)S(1)}, u32[]{:S(2)}, u32[]{:S(2)}) collective-permute-start(bf16[96,1536]{1,0:T(8,128)(2,1)} %param.27), channel_id=1, source_target_pairs={{0,1},{1,0},{2,3},{3,2},{4,5},{5,4},{6,7},{7,6},{8,9},{9,8},{10,11... | collective-permute-start | bytes 884744 | tf_op jit(solution)/shard_map/ppermute | solution.py:31
  19.4 37.0 %all-to-all-start = ((bf16[16,48,512]{2,1,0:T(8,128)(2,1)}), bf16[16,48,512]{2,1,0:T(8,128)(2,1)S(1)}, u32[]{:S(2)}, u32[]{:S(2)}) async-start(bf16[16,48,512]{2,1,0:T(8,128)(2,1)} %pad_maximum_fusion.3), calls=%async_computation | async-start | bytes 1572864 | tf_op jit(solution)/shard_map/all_to_all | solution.py:628
  25.5 110.8 %all-gather.4.cloned.1.call-start = ((), (), s32[]{:S(2)}) async-start(), calls=%async_computation.6 | async-start | bytes 9437184 | tf_op jit(solution)/shard_map/all_gather | solution.py:677
  26.3 209.9 %all-gather.6.cloned.1.call-start = ((), (), s32[]{:S(2)}) async-start(), calls=%async_computation.7 | async-start | bytes 9437184 | tf_op jit(solution)/shard_map/all_gather | solution.py:677
  27.5 16.1 %collective-permute-start.4 = (bf16[192,1536]{1,0:T(8,128)(2,1)S(1)}, bf16[192,1536]{1,0:T(8,128)(2,1)S(1)}, u32[]{:S(2)}, u32[]{:S(2)}) collective-permute-start(bf16[192,1536]{1,0:T(8,128)(2,1)S(1)} %pad_maximum_fusion.4), channel_id=1, source_target_pairs={{0,16},{16,0},{1,17},{17,1},{2,18},{18,2},{3,19},{19,3},{4,20},{20... | collective-permute-start | bytes 1769480 | tf_op jit(solution)/shard_map/ppermute | solution.py:31
  27.8 26.2 %collective-permute-start.2 = (bf16[128,2048]{1,0:T(8,128)(2,1)S(1)}, bf16[128,2048]{1,0:T(8,128)(2,1)}, u32[]{:S(2)}, u32[]{:S(2)}) collective-permute-start(bf16[128,2048]{1,0:T(8,128)(2,1)S(1)} %fusion.47), channel_id=1, source_target_pairs={{0,4},{4,8},{8,12},{12,0},{1,5},{5,9},{9,13},{13,1},{2,6},{6,10},{... | collective-permute-start | bytes 1572872 | tf_op jit(solution)/shard_map/ppermute | solution.py:36
  29.0 25.0 %collective-permute-start.3 = (bf16[128,2048]{1,0:T(8,128)(2,1)S(1)}, bf16[128,2048]{1,0:T(8,128)(2,1)}, u32[]{:S(2)}, u32[]{:S(2)}) collective-permute-start(bf16[128,2048]{1,0:T(8,128)(2,1)S(1)} %fusion.47), channel_id=1, source_target_pairs={{0,2},{2,0},{1,3},{3,1},{4,6},{6,4},{5,7},{7,5},{8,10},{10,8},{9,1... | collective-permute-start | bytes 1572872 | tf_op jit(solution)/shard_map/ppermute | solution.py:31
  56.4 14.0 %collective-permute-start.5 = (bf16[128,2048]{1,0:T(8,128)(2,1)}, bf16[128,2048]{1,0:T(8,128)(2,1)S(1)}, u32[]{:S(2)}, u32[]{:S(2)}) collective-permute-start(bf16[128,2048]{1,0:T(8,128)(2,1)} %collective-permute-done.2), channel_id=1, source_target_pairs={{0,4},{4,8},{8,12},{12,0},{1,5},{5,9},{9,13},{13,1},{2,6},{6,10},{... | collective-permute-start | bytes 1572872 | tf_op jit(solution)/shard_map/ppermute | solution.py:36
  56.4 14.0 %collective-permute-start.6 = (bf16[128,2048]{1,0:T(8,128)(2,1)}, bf16[128,2048]{1,0:T(8,128)(2,1)S(1)}, u32[]{:S(2)}, u32[]{:S(2)}) collective-permute-start(bf16[128,2048]{1,0:T(8,128)(2,1)} %collective-permute-done.2), channel_id=1, source_target_pairs={{0,2},{2,0},{1,3},{3,1},{4,6},{6,4},{5,7},{7,5},{8,10},{10,8},{9,1... | collective-permute-start | bytes 1572872 | tf_op jit(solution)/shard_map/ppermute | solution.py:31
  56.7 13.5 %collective-permute-start.7 = (bf16[256,512]{1,0:T(8,128)(2,1)S(1)}, bf16[256,512]{1,0:T(8,128)(2,1)S(1)}, u32[]{:S(2)}, u32[]{:S(2)}) collective-permute-start(bf16[256,512]{1,0:T(8,128)(2,1)S(1)} %get-tuple-element.202), channel_id=1, source_target_pairs={{0,16},{16,0},{1,17},{17,1},{2,18},{18,2},{3,19},{19,3},{4,20},{20... | collective-permute-start | bytes 786440 | tf_op jit(solution)/shard_map/ppermute | solution.py:31
  70.8 16.2 %collective-permute-start.8 = (bf16[128,2048]{1,0:T(8,128)(2,1)S(1)}, bf16[128,2048]{1,0:T(8,128)(2,1)S(1)}, u32[]{:S(2)}, u32[]{:S(2)}) collective-permute-start(bf16[128,2048]{1,0:T(8,128)(2,1)S(1)} %collective-permute-done.5), channel_id=1, source_target_pairs={{0,4},{4,8},{8,12},{12,0},{1,5},{5,9},{9,13},{13,1},{2,6},{6,10},{... | collective-permute-start | bytes 1572872 | tf_op jit(solution)/shard_map/ppermute | solution.py:36
  71.0 16.1 %collective-permute-start.9 = (bf16[128,2048]{1,0:T(8,128)(2,1)S(1)}, bf16[128,2048]{1,0:T(8,128)(2,1)S(1)}, u32[]{:S(2)}, u32[]{:S(2)}) collective-permute-start(bf16[128,2048]{1,0:T(8,128)(2,1)S(1)} %collective-permute-done.5), channel_id=1, source_target_pairs={{0,2},{2,0},{1,3},{3,1},{4,6},{6,4},{5,7},{7,5},{8,10},{10,8},{9,1... | collective-permute-start | bytes 1572872 | tf_op jit(solution)/shard_map/ppermute | solution.py:31
  74.1 13.0 %collective-permute-start.10 = (bf16[256,512]{1,0:T(8,128)(2,1)S(1)}, bf16[256,512]{1,0:T(8,128)(2,1)S(1)}, u32[]{:S(2)}, u32[]{:S(2)}) collective-permute-start(bf16[256,512]{1,0:T(8,128)(2,1)S(1)} %get-tuple-element.205), channel_id=1, source_target_pairs={{0,16},{16,0},{1,17},{17,1},{2,18},{18,2},{3,19},{19,3},{4,20},{20... | collective-permute-start | bytes 786440 | tf_op jit(solution)/shard_map/ppermute | solution.py:31
  87.1 14.0 %collective-permute-start.11 = (bf16[128,2048]{1,0:T(8,128)(2,1)S(1)}, bf16[128,2048]{1,0:T(8,128)(2,1)S(1)}, u32[]{:S(2)}, u32[]{:S(2)}) collective-permute-start(bf16[128,2048]{1,0:T(8,128)(2,1)S(1)} %collective-permute-done.8), channel_id=1, source_target_pairs={{0,2},{2,0},{1,3},{3,1},{4,6},{6,4},{5,7},{7,5},{8,10},{10,8},{9,1... | collective-permute-start | bytes 1572872 | tf_op jit(solution)/shard_map/ppermute | solution.py:31
  88.3 12.8 %collective-permute-start.12 = (bf16[256,512]{1,0:T(8,128)(2,1)S(1)}, bf16[256,512]{1,0:T(8,128)(2,1)S(1)}, u32[]{:S(2)}, u32[]{:S(2)}) collective-permute-start(bf16[256,512]{1,0:T(8,128)(2,1)S(1)} %get-tuple-element.208), channel_id=1, source_target_pairs={{0,16},{16,0},{1,17},{17,1},{2,18},{18,2},{3,19},{19,3},{4,20},{20... | collective-permute-start | bytes 786440 | tf_op jit(solution)/shard_map/ppermute | solution.py:31
  102.0 19.0 %collective-permute-start.15 = (bf16[1024,2048]{1,0:T(8,128)(2,1)}, bf16[1024,2048]{1,0:T(8,128)(2,1)}, u32[]{:S(2)}, u32[]{:S(2)}) collective-permute-start(bf16[1024,2048]{1,0:T(8,128)(2,1)} %constant_dynamic-update-slice_fusion.refs_0_.refs_1_.refs_2_), channel_id=1, source_target_pairs={{0,1},{1,0},{2,3},{3,2},{4,5},{5,4},{6,7},{7,6},{8,9},{9,8},{10,11... | collective-permute-start | bytes 12582920 | tf_op jit(solution)/shard_map/ppermute | solution.py:31
  106.2 83.7 %collective-permute-start.26 = (bf16[1,32,1536]{2,1,0:T(8,128)(2,1)}, bf16[1,32,1536]{2,1,0:T(8,128)(2,1)}, u32[]{:S(2)}, u32[]{:S(2)}) collective-permute-start(bf16[1,32,1536]{2,1,0:T(8,128)(2,1)} %bitcast.36), channel_id=1, source_target_pairs={{0,16},{16,0},{1,17},{17,1},{2,18},{18,2},{3,19},{19,3},{4,20},{20... | collective-permute-start | bytes 294920 | tf_op jit(solution)/shard_map/ppermute | solution.py:31
  106.5 216.7 %all-gather.8.cloned.1.call-start = ((), (), s32[]{:S(2)}) async-start(), calls=%async_computation.8 | async-start | bytes 9437184 | tf_op jit(solution)/shard_map/all_gather | solution.py:677
  113.8 22.5 %collective-permute-start.13 = (bf16[128,1536]{1,0:T(8,128)(2,1)}, bf16[128,1536]{1,0:T(8,128)(2,1)}, u32[]{:S(2)}, u32[]{:S(2)}) collective-permute-start(bf16[128,1536]{1,0:T(8,128)(2,1)} %fusion.29), channel_id=1, source_target_pairs={{0,4},{4,8},{8,12},{12,0},{1,5},{5,9},{9,13},{13,1},{2,6},{6,10},{... | collective-permute-start | bytes 1179656 | tf_op jit(solution)/shard_map/ppermute | solution.py:36
  115.3 21.1 %collective-permute-start.14 = (bf16[128,1536]{1,0:T(8,128)(2,1)}, bf16[128,1536]{1,0:T(8,128)(2,1)}, u32[]{:S(2)}, u32[]{:S(2)}) collective-permute-start(bf16[128,1536]{1,0:T(8,128)(2,1)} %fusion.29), channel_id=1, source_target_pairs={{0,2},{2,0},{1,3},{3,1},{4,6},{6,4},{5,7},{7,5},{8,10},{10,8},{9,1... | collective-permute-start | bytes 1179656 | tf_op jit(solution)/shard_map/ppermute | solution.py:31
  136.4 21.8 %collective-permute-start.16 = (bf16[128,1536]{1,0:T(8,128)(2,1)}, bf16[128,1536]{1,0:T(8,128)(2,1)S(1)}, u32[]{:S(2)}, u32[]{:S(2)}) collective-permute-start(bf16[128,1536]{1,0:T(8,128)(2,1)} %collective-permute-done.13), channel_id=1, source_target_pairs={{0,4},{4,8},{8,12},{12,0},{1,5},{5,9},{9,13},{13,1},{2,6},{6,10},{... | collective-permute-start | bytes 1179656 | tf_op jit(solution)/shard_map/ppermute | solution.py:36
  139.0 19.1 %collective-permute-start.17 = (bf16[128,1536]{1,0:T(8,128)(2,1)}, bf16[128,1536]{1,0:T(8,128)(2,1)S(1)}, u32[]{:S(2)}, u32[]{:S(2)}) collective-permute-start(bf16[128,1536]{1,0:T(8,128)(2,1)} %collective-permute-done.13), channel_id=1, source_target_pairs={{0,2},{2,0},{1,3},{3,1},{4,6},{6,4},{5,7},{7,5},{8,10},{10,8},{9,1... | collective-permute-start | bytes 1179656 | tf_op jit(solution)/shard_map/ppermute | solution.py:31
  158.1 19.4 %collective-permute-start.18 = (bf16[128,1536]{1,0:T(8,128)(2,1)S(1)}, bf16[128,1536]{1,0:T(8,128)(2,1)S(1)}, u32[]{:S(2)}, u32[]{:S(2)}) collective-permute-start(bf16[128,1536]{1,0:T(8,128)(2,1)S(1)} %collective-permute-done.16), channel_id=1, source_target_pairs={{0,4},{4,8},{8,12},{12,0},{1,5},{5,9},{9,13},{13,1},{2,6},{6,10},{... | collective-permute-start | bytes 1179656 | tf_op jit(solution)/shard_map/ppermute | solution.py:36
  158.4 19.2 %collective-permute-start.19 = (bf16[128,1536]{1,0:T(8,128)(2,1)S(1)}, bf16[128,1536]{1,0:T(8,128)(2,1)S(1)}, u32[]{:S(2)}, u32[]{:S(2)}) collective-permute-start(bf16[128,1536]{1,0:T(8,128)(2,1)S(1)} %collective-permute-done.16), channel_id=1, source_target_pairs={{0,2},{2,0},{1,3},{3,1},{4,6},{6,4},{5,7},{7,5},{8,10},{10,8},{9,1... | collective-permute-start | bytes 1179656 | tf_op jit(solution)/shard_map/ppermute | solution.py:31
  159.6 39.0 %collective-permute-start.20 = (bf16[1024,1664]{1,0:T(8,128)(2,1)}, bf16[1024,1664]{1,0:T(8,128)(2,1)}, u32[]{:S(2)}, u32[]{:S(2)}) collective-permute-start(bf16[1024,1664]{1,0:T(8,128)(2,1)} %get-tuple-element.238), channel_id=1, source_target_pairs={{0,1},{1,0},{2,3},{3,2},{4,5},{5,4},{6,7},{7,6},{8,9},{9,8},{10,11... | collective-permute-start | bytes 10223624 | tf_op jit(solution)/shard_map/ppermute | solution.py:31
  189.2 24.9 %collective-permute-start.25 = (bf16[1024,1536]{1,0:T(8,128)(2,1)}, bf16[1024,1536]{1,0:T(8,128)(2,1)}, u32[]{:S(2)}, u32[]{:S(2)}) collective-permute-start(bf16[1024,1536]{1,0:T(8,128)(2,1)} %constant_dynamic-update-slice_fusion.11.refs_2_), channel_id=1, source_target_pairs={{0,1},{1,0},{2,3},{3,2},{4,5},{5,4},{6,7},{7,6},{8,9},{9,8},{10,11... | collective-permute-start | bytes 9437192 | tf_op jit(solution)/shard_map/ppermute | solution.py:31
  202.4 11.5 %collective-permute-start.21 = (bf16[128,1664]{1,0:T(8,128)(2,1)S(1)}, bf16[128,1664]{1,0:T(8,128)(2,1)S(1)}, u32[]{:S(2)}, u32[]{:S(2)}) collective-permute-start(bf16[128,1664]{1,0:T(8,128)(2,1)S(1)} %slice.555), channel_id=1, source_target_pairs={{0,2},{2,0},{1,3},{3,1},{4,6},{6,4},{5,7},{7,5},{8,10},{10,8},{9,1... | collective-permute-start | bytes 1277960 | tf_op jit(solution)/shard_map/ppermute | solution.py:31
  208.1 14.9 %collective-permute-start.23 = (bf16[128,1664]{1,0:T(8,128)(2,1)S(1)}, bf16[128,1664]{1,0:T(8,128)(2,1)S(1)}, u32[]{:S(2)}, u32[]{:S(2)}) collective-permute-start(bf16[128,1664]{1,0:T(8,128)(2,1)S(1)} %slice.558), channel_id=1, source_target_pairs={{0,2},{2,0},{1,3},{3,1},{4,6},{6,4},{5,7},{7,5},{8,10},{10,8},{9,1... | collective-permute-start | bytes 1277960 | tf_op jit(solution)/shard_map/ppermute | solution.py:31
  209.3 22.8 %collective-permute-start.28 = (bf16[128,1664]{1,0:T(8,128)(2,1)S(1)}, bf16[128,1664]{1,0:T(8,128)(2,1)S(1)}, u32[]{:S(2)}, u32[]{:S(2)}) collective-permute-start(bf16[128,1664]{1,0:T(8,128)(2,1)S(1)} %slice.569), channel_id=1, source_target_pairs={{0,2},{2,0},{1,3},{3,1},{4,6},{6,4},{5,7},{7,5},{8,10},{10,8},{9,1... | collective-permute-start | bytes 1277960 | tf_op jit(solution)/shard_map/ppermute | solution.py:31
  225.2 16.1 %collective-permute-start.30 = (bf16[128,1664]{1,0:T(8,128)(2,1)}, bf16[128,1664]{1,0:T(8,128)(2,1)S(1)}, u32[]{:S(2)}, u32[]{:S(2)}) collective-permute-start(bf16[128,1664]{1,0:T(8,128)(2,1)} %slice.572), channel_id=1, source_target_pairs={{0,2},{2,0},{1,3},{3,1},{4,6},{6,4},{5,7},{7,5},{8,10},{10,8},{9,1... | collective-permute-start | bytes 1277960 | tf_op jit(solution)/shard_map/ppermute | solution.py:31
  236.2 220.7 %reduce-scatter.4.cloned.1.call-start = ((), (), s32[]{:S(2)}) async-start(), calls=%async_computation.9 | async-start | bytes 9437184 | tf_op jit(solution)/shard_map/reduce_scatter | solution.py:811
  265.9 16.7 %collective-permute-start.35 = (bf16[128,1536]{1,0:T(8,128)(2,1)S(1)}, bf16[128,1536]{1,0:T(8,128)(2,1)S(1)}, u32[]{:S(2)}, u32[]{:S(2)}) collective-permute-start(bf16[128,1536]{1,0:T(8,128)(2,1)S(1)} %collective-permute-done.33), channel_id=1, source_target_pairs={{0,4},{4,8},{8,12},{12,0},{1,5},{5,9},{9,13},{13,1},{2,6},{6,10},{... | collective-permute-start | bytes 1179656 | tf_op jit(solution)/shard_map/ppermute | solution.py:36
  294.5 15.5 %collective-permute-start.38 = (bf16[1024,1536]{1,0:T(8,128)(2,1)S(1)}, bf16[1024,1536]{1,0:T(8,128)(2,1)S(1)}, u32[]{:S(2)}, u32[]{:S(2)}) collective-permute-start(bf16[1024,1536]{1,0:T(8,128)(2,1)S(1)} %constant_dynamic-update-slice_fusion.19.refs_2_), channel_id=1, source_target_pairs={{0,1},{1,0},{2,3},{3,2},{4,5},{5,4},{6,7},{7,6},{8,9},{9,8},{10,11... | collective-permute-start | bytes 9437192 | tf_op jit(solution)/shard_map/ppermute | solution.py:31
  350.6 296.8 %reduce-scatter.6.cloned.1.call-start = ((), (), s32[]{:S(2)}) async-start(), calls=%async_computation.10 | async-start | bytes 9437184 | tf_op jit(solution)/shard_map/reduce_scatter | solution.py:811
  380.6 272.3 %reduce-scatter.8.cloned.1.call-start = ((), (), s32[]{:S(2)}) async-start(), calls=%async_computation.11 | async-start | bytes 9437184 | tf_op jit(solution)/shard_map/reduce_scatter | solution.py:811
  381.4 12.3 %collective-permute-start.42 = (bf16[128,1536]{1,0:T(8,128)(2,1)}, bf16[128,1536]{1,0:T(8,128)(2,1)}, u32[]{:S(2)}, u32[]{:S(2)}) collective-permute-start(bf16[128,1536]{1,0:T(8,128)(2,1)} %slice.585), channel_id=1, source_target_pairs={{0,2},{2,0},{1,3},{3,1},{4,6},{6,4},{5,7},{7,5},{8,10},{10,8},{9,1... | collective-permute-start | bytes 1179656 | tf_op jit(solution)/shard_map/ppermute | solution.py:31
  381.8 18.2 %collective-permute-start.44 = (bf16[128,1536]{1,0:T(8,128)(2,1)S(1)}, bf16[128,1536]{1,0:T(8,128)(2,1)}, u32[]{:S(2)}, u32[]{:S(2)}) collective-permute-start(bf16[128,1536]{1,0:T(8,128)(2,1)S(1)} %slice.589), channel_id=1, source_target_pairs={{0,2},{2,0},{1,3},{3,1},{4,6},{6,4},{5,7},{7,5},{8,10},{10,8},{9,1... | collective-permute-start | bytes 1179656 | tf_op jit(solution)/shard_map/ppermute | solution.py:31
  396.4 11.9 %collective-permute-start.46 = (bf16[128,1536]{1,0:T(8,128)(2,1)S(1)}, bf16[128,1536]{1,0:T(8,128)(2,1)S(1)}, u32[]{:S(2)}, u32[]{:S(2)}) collective-permute-start(bf16[128,1536]{1,0:T(8,128)(2,1)S(1)} %slice.593), channel_id=1, source_target_pairs={{0,2},{2,0},{1,3},{3,1},{4,6},{6,4},{5,7},{7,5},{8,10},{10,8},{9,1... | collective-permute-start | bytes 1179656 | tf_op jit(solution)/shard_map/ppermute | solution.py:31
  425.4 12.7 %collective-permute-start.49 = (bf16[128,1664]{1,0:T(8,128)(2,1)S(1)}, bf16[128,1664]{1,0:T(8,128)(2,1)S(1)}, u32[]{:S(2)}, u32[]{:S(2)}) collective-permute-start(bf16[128,1664]{1,0:T(8,128)(2,1)S(1)} %collective-permute-done.47), channel_id=1, source_target_pairs={{0,4},{4,8},{8,12},{12,0},{1,5},{5,9},{9,13},{13,1},{2,6},{6,10},{... | collective-permute-start | bytes 1277960 | tf_op jit(solution)/shard_map/ppermute | solution.py:36
  425.7 12.4 %collective-permute-start.50 = (bf16[128,1664]{1,0:T(8,128)(2,1)S(1)}, bf16[128,1664]{1,0:T(8,128)(2,1)S(1)}, u32[]{:S(2)}, u32[]{:S(2)}) collective-permute-start(bf16[128,1664]{1,0:T(8,128)(2,1)S(1)} %collective-permute-done.47), channel_id=1, source_target_pairs={{0,2},{2,0},{1,3},{3,1},{4,6},{6,4},{5,7},{7,5},{8,10},{10,8},{9,1... | collective-permute-start | bytes 1277960 | tf_op jit(solution)/shard_map/ppermute | solution.py:31
  426.0 61.0 %collective-permute-start.55 = (bf16[1024,1536]{1,0:T(8,128)(2,1)}, bf16[1024,1536]{1,0:T(8,128)(2,1)}, u32[]{:S(2)}, u32[]{:S(2)}) collective-permute-start(bf16[1024,1536]{1,0:T(8,128)(2,1)} %combine.6), channel_id=1, source_target_pairs={{0,1},{1,0},{2,3},{3,2},{4,5},{5,4},{6,7},{7,6},{8,9},{9,8},{10,11... | collective-permute-start | bytes 9437192 | tf_op jit(solution)/shard_map/ppermute | solution.py:31
  438.1 16.6 %collective-permute-start.51 = (bf16[128,1664]{1,0:T(8,128)(2,1)S(1)}, bf16[128,1664]{1,0:T(8,128)(2,1)S(1)}, u32[]{:S(2)}, u32[]{:S(2)}) collective-permute-start(bf16[128,1664]{1,0:T(8,128)(2,1)S(1)} %collective-permute-done.49), channel_id=1, source_target_pairs={{0,4},{4,8},{8,12},{12,0},{1,5},{5,9},{9,13},{13,1},{2,6},{6,10},{... | collective-permute-start | bytes 1277960 | tf_op jit(solution)/shard_map/ppermute | solution.py:36
  442.5 12.2 %collective-permute-start.52 = (bf16[128,1664]{1,0:T(8,128)(2,1)S(1)}, bf16[128,1664]{1,0:T(8,128)(2,1)S(1)}, u32[]{:S(2)}, u32[]{:S(2)}) collective-permute-start(bf16[128,1664]{1,0:T(8,128)(2,1)S(1)} %collective-permute-done.49), channel_id=1, source_target_pairs={{0,2},{2,0},{1,3},{3,1},{4,6},{6,4},{5,7},{7,5},{8,10},{10,8},{9,1... | collective-permute-start | bytes 1277960 | tf_op jit(solution)/shard_map/ppermute | solution.py:31
  467.7 23.1 %collective-permute-start.54 = (bf16[1024,1664]{1,0:T(8,128)(2,1)}, bf16[1024,1664]{1,0:T(8,128)(2,1)}, u32[]{:S(2)}, u32[]{:S(2)}) collective-permute-start(bf16[1024,1664]{1,0:T(8,128)(2,1)} %constant_dynamic-update-slice_fusion.27.refs_0_.refs_1_), channel_id=1, source_target_pairs={{0,1},{1,0},{2,3},{3,2},{4,5},{5,4},{6,7},{7,6},{8,9},{9,8},{10,11... | collective-permute-start | bytes 10223624 | tf_op jit(solution)/shard_map/ppermute | solution.py:31
  471.5 14.7 %collective-permute-start.74 = (bf16[768,128]{0,1:T(8,128)(2,1)S(1)}, bf16[768,128]{0,1:T(8,128)(2,1)S(1)}, u32[]{:S(2)}, u32[]{:S(2)}) collective-permute-start(bf16[768,128]{0,1:T(8,128)(2,1)S(1)} %dynamic-slice_convert_fusion), channel_id=1, source_target_pairs={{0,16},{16,0},{1,17},{17,1},{2,18},{18,2},{3,19},{19,3},{4,20},{20... | collective-permute-start | bytes 589832 | tf_op jit(solution)/shard_map/ppermute | solution.py:31
  490.9 26.8 %collective-permute-start.56 = (bf16[128,1536]{1,0:T(8,128)(2,1)S(1)}, bf16[128,1536]{1,0:T(8,128)(2,1)S(1)}, u32[]{:S(2)}, u32[]{:S(2)}) collective-permute-start(bf16[128,1536]{1,0:T(8,128)(2,1)S(1)} %slice_bitcast_fusion.3), channel_id=1, source_target_pairs={{0,2},{2,0},{1,3},{3,1},{4,6},{6,4},{5,7},{7,5},{8,10},{10,8},{9,1... | collective-permute-start | bytes 1179656 | tf_op jit(solution)/shard_map/ppermute | solution.py:31
  491.5 26.1 %collective-permute-start.57 = (bf16[128,1536]{1,0:T(8,128)(2,1)S(1)}, bf16[128,1536]{1,0:T(8,128)(2,1)S(1)}, u32[]{:S(2)}, u32[]{:S(2)}) collective-permute-start(bf16[128,1536]{1,0:T(8,128)(2,1)S(1)} %slice_bitcast_fusion.2), channel_id=1, source_target_pairs={{0,2},{2,0},{1,3},{3,1},{4,6},{6,4},{5,7},{7,5},{8,10},{10,8},{9,1... | collective-permute-start | bytes 1179656 | tf_op jit(solution)/shard_map/ppermute | solution.py:31
  518.5 33.3 %collective-permute-start.58 = (bf16[128,1536]{1,0:T(8,128)(2,1)}, bf16[128,1536]{1,0:T(8,128)(2,1)}, u32[]{:S(2)}, u32[]{:S(2)}) collective-permute-start(bf16[128,1536]{1,0:T(8,128)(2,1)} %fusion.41), channel_id=1, source_target_pairs={{0,4},{4,8},{8,12},{12,0},{1,5},{5,9},{9,13},{13,1},{2,6},{6,10},{... | collective-permute-start | bytes 1179656 | tf_op jit(solution)/shard_map/ppermute | solution.py:36
  519.8 34.0 %collective-permute-start.61 = (bf16[1024,1536]{1,0:T(8,128)(2,1)}, bf16[1024,1536]{1,0:T(8,128)(2,1)S(1)}, u32[]{:S(2)}, u32[]{:S(2)}) collective-permute-start(bf16[1024,1536]{1,0:T(8,128)(2,1)} %get-tuple-element.321), channel_id=1, source_target_pairs={{0,1},{1,0},{2,3},{3,2},{4,5},{5,4},{6,7},{7,6},{8,9},{9,8},{10,11... | collective-permute-start | bytes 9437192 | tf_op jit(solution)/shard_map/ppermute | solution.py:31
  521.4 32.3 %collective-permute-start.59 = (bf16[128,1536]{1,0:T(8,128)(2,1)S(1)}, bf16[128,1536]{1,0:T(8,128)(2,1)}, u32[]{:S(2)}, u32[]{:S(2)}) collective-permute-start(bf16[128,1536]{1,0:T(8,128)(2,1)S(1)} %slice_bitcast_fusion.1), channel_id=1, source_target_pairs={{0,2},{2,0},{1,3},{3,1},{4,6},{6,4},{5,7},{7,5},{8,10},{10,8},{9,1... | collective-permute-start | bytes 1179656 | tf_op jit(solution)/shard_map/ppermute | solution.py:31
  522.0 31.7 %collective-permute-start.60 = (bf16[128,1536]{1,0:T(8,128)(2,1)S(1)}, bf16[128,1536]{1,0:T(8,128)(2,1)S(1)}, u32[]{:S(2)}, u32[]{:S(2)}) collective-permute-start(bf16[128,1536]{1,0:T(8,128)(2,1)S(1)} %slice_bitcast_fusion), channel_id=1, source_target_pairs={{0,2},{2,0},{1,3},{3,1},{4,6},{6,4},{5,7},{7,5},{8,10},{10,8},{9,1... | collective-permute-start | bytes 1179656 | tf_op jit(solution)/shard_map/ppermute | solution.py:31
  556.1 30.3 %collective-permute-start.64 = (bf16[128,1536]{1,0:T(8,128)(2,1)}, bf16[128,1536]{1,0:T(8,128)(2,1)}, u32[]{:S(2)}, u32[]{:S(2)}) collective-permute-start(bf16[128,1536]{1,0:T(8,128)(2,1)} %slice.601), channel_id=1, source_target_pairs={{0,2},{2,0},{1,3},{3,1},{4,6},{6,4},{5,7},{7,5},{8,10},{10,8},{9,1... | collective-permute-start | bytes 1179656 | tf_op jit(solution)/shard_map/ppermute | solution.py:31
  557.9 63.1 %collective-permute-start.68 = (bf16[128,1536]{1,0:T(8,128)(2,1)}, bf16[128,1536]{1,0:T(8,128)(2,1)}, u32[]{:S(2)}, u32[]{:S(2)}) collective-permute-start(bf16[128,1536]{1,0:T(8,128)(2,1)} %slice.606), channel_id=1, source_target_pairs={{0,2},{2,0},{1,3},{3,1},{4,6},{6,4},{5,7},{7,5},{8,10},{10,8},{9,1... | collective-permute-start | bytes 1179656 | tf_op jit(solution)/shard_map/ppermute | solution.py:31
  559.1 69.0 %collective-permute-start.72 = (bf16[128,1536]{1,0:T(8,128)(2,1)}, bf16[128,1536]{1,0:T(8,128)(2,1)}, u32[]{:S(2)}, u32[]{:S(2)}) collective-permute-start(bf16[128,1536]{1,0:T(8,128)(2,1)} %slice.610), channel_id=1, source_target_pairs={{0,2},{2,0},{1,3},{3,1},{4,6},{6,4},{5,7},{7,5},{8,10},{10,8},{9,1... | collective-permute-start | bytes 1179656 | tf_op jit(solution)/shard_map/ppermute | solution.py:31
  566.0 20.3 %collective-permute-start.63 = (bf16[128,1536]{1,0:T(8,128)(2,1)}, bf16[128,1536]{1,0:T(8,128)(2,1)}, u32[]{:S(2)}, u32[]{:S(2)}) collective-permute-start(bf16[128,1536]{1,0:T(8,128)(2,1)} %add_convert_fusion.24), channel_id=1, source_target_pairs={{0,4},{4,8},{8,12},{12,0},{1,5},{5,9},{9,13},{13,1},{2,6},{6,10},{... | collective-permute-start | bytes 1179656 | tf_op jit(solution)/shard_map/ppermute | solution.py:36
  566.4 16.9 %collective-permute-start.66 = (bf16[128,1536]{1,0:T(8,128)(2,1)}, bf16[128,1536]{1,0:T(8,128)(2,1)}, u32[]{:S(2)}, u32[]{:S(2)}) collective-permute-start(bf16[128,1536]{1,0:T(8,128)(2,1)} %fusion.40), channel_id=1, source_target_pairs={{0,4},{4,8},{8,12},{12,0},{1,5},{5,9},{9,13},{13,1},{2,6},{6,10},{... | collective-permute-start | bytes 1179656 | tf_op jit(solution)/shard_map/ppermute | solution.py:36
  583.3 17.4 %collective-permute-start.65 = (bf16[256,896]{1,0:T(8,128)(2,1)}, bf16[256,896]{1,0:T(8,128)(2,1)}, u32[]{:S(2)}, u32[]{:S(2)}) collective-permute-start(bf16[256,896]{1,0:T(8,128)(2,1)} %get-tuple-element.332), channel_id=1, source_target_pairs={{0,16},{16,0},{1,17},{17,1},{2,18},{18,2},{3,19},{19,3},{4,20},{20... | collective-permute-start | bytes 1376264 | tf_op jit(solution)/shard_map/ppermute | solution.py:31
  600.7 20.3 %collective-permute-start.67 = (bf16[128,1536]{1,0:T(8,128)(2,1)}, bf16[128,1536]{1,0:T(8,128)(2,1)}, u32[]{:S(2)}, u32[]{:S(2)}) collective-permute-start(bf16[128,1536]{1,0:T(8,128)(2,1)} %add_convert_fusion.23), channel_id=1, source_target_pairs={{0,4},{4,8},{8,12},{12,0},{1,5},{5,9},{9,13},{13,1},{2,6},{6,10},{... | collective-permute-start | bytes 1179656 | tf_op jit(solution)/shard_map/ppermute | solution.py:36
  601.8 16.6 %collective-permute-start.70 = (bf16[128,1536]{1,0:T(8,128)(2,1)}, bf16[128,1536]{1,0:T(8,128)(2,1)}, u32[]{:S(2)}, u32[]{:S(2)}) collective-permute-start(bf16[128,1536]{1,0:T(8,128)(2,1)} %fusion.38), channel_id=1, source_target_pairs={{0,4},{4,8},{8,12},{12,0},{1,5},{5,9},{9,13},{13,1},{2,6},{6,10},{... | collective-permute-start | bytes 1179656 | tf_op jit(solution)/shard_map/ppermute | solution.py:36
  603.2 19.1 %collective-permute-start.69 = (bf16[256,896]{1,0:T(8,128)(2,1)}, bf16[256,896]{1,0:T(8,128)(2,1)}, u32[]{:S(2)}, u32[]{:S(2)}) collective-permute-start(bf16[256,896]{1,0:T(8,128)(2,1)} %get-tuple-element.345), channel_id=1, source_target_pairs={{0,16},{16,0},{1,17},{17,1},{2,18},{18,2},{3,19},{19,3},{4,20},{20... | collective-permute-start | bytes 1376264 | tf_op jit(solution)/shard_map/ppermute | solution.py:31
  604.1 30.6 %all-to-all-start.2 = ((f32[32,1,712]{2,1,0:T(1,128)}), f32[32,1,712]{2,1,0:T(1,128)}, u32[]{:S(2)}, u32[]{:S(2)}) async-start(f32[32,1,712]{2,1,0:T(1,128)} %copy.247), calls=%async_computation.3 | async-start | bytes 196608 | tf_op jit(solution)/shard_map/all_to_all | solution.py:984
  634.7 47.3 %all-to-all-start.1 = ((bf16[16,48,1024]{2,1,0:T(8,128)(2,1)}), bf16[16,48,1024]{2,1,0:T(8,128)(2,1)}, u32[]{:S(2)}, u32[]{:S(2)}) async-start(bf16[16,48,1024]{2,1,0:T(8,128)(2,1)} %bitcast.168), calls=%async_computation.2 | async-start | bytes 3145728 | tf_op jit(solution)/shard_map/all_to_all | solution.py:948
  660.7 14.6 %collective-permute-start.75 = (bf16[192,1536]{1,0:T(8,128)(2,1)S(1)}, bf16[192,1536]{1,0:T(8,128)(2,1)S(1)}, u32[]{:S(2)}, u32[]{:S(2)}) collective-permute-start(bf16[192,1536]{1,0:T(8,128)(2,1)S(1)} %convert_element_type.837), channel_id=1, source_target_pairs={{0,16},{16,0},{1,17},{17,1},{2,18},{18,2},{3,19},{19,3},{4,20},{20... | collective-permute-start | bytes 1769480 | tf_op jit(solution)/shard_map/ppermute | solution.py:31
  (116 other events, 1165.8 us)
Sparse Core Ops, SparseCore 0:
  27.9 101.4 all-gather.3
  131.0 80.1 all-gather.5
  236.3 86.8 all-gather.7
  350.8 77.0 reduce-scatter.3
  430.7 83.3 reduce-scatter.5
  516.2 81.4 reduce-scatter.7

commit v4 on v3

--- a/solution.py
+++ b/solution.py
@@ -156,10 +156,18 @@
     return 1.0 / (1.0 + jnp.exp(-value))
 
 
+def halves_of(value):
+    high = value.astype(bf16)
+    return high, (value - high.astype(f32)).astype(bf16)
+
+
 def exact(left, right, dims):
-    return lax.dot_general(
-        left, right, (dims, ((), ())), precision=lax.Precision.HIGHEST, preferred_element_type=f32
-    )
+    (left_high, left_low), (right_high, right_low) = halves_of(left), halves_of(right)
+
+    def dot(one, other):
+        return lax.dot_general(one, other, (dims, ((), ())), preferred_element_type=f32)
+
+    return dot(left_high, right_high) + (dot(left_high, right_low) + dot(left_low, right_high))
 
 
 def rows_of(array, index):
@@ -168,7 +176,7 @@
 
 WIDE = 256
 CONV_LANES = 2 * STATE + WIDE
-PROJ_LANES = CONV_LANES + WIDE + EXTRA
+PROJ_LANES = CONV_LANES + 2 * EXTRA
 
 
 def triangle(count):
@@ -189,7 +197,7 @@
     conv_sig = sigmoid(total)
     conv_out = total * conv_sig
     b_part, c_part = conv_out[:, :STATE], conv_out[:, STATE : 2 * STATE]
-    raw = proj[:, CONV_LANES + WIDE :] + rows_of(head, 0)[:, :EXTRA]
+    raw = proj[:, CONV_LANES + EXTRA :] + rows_of(head, 0)[:, :EXTRA]
     step = jnp.maximum(raw, 0.0) + jnp.log1p(jnp.exp(-jnp.abs(raw)))
     distance = triangle(count)
     lower = (distance >= 0).astype(f32)
@@ -213,7 +221,9 @@
         decays.append((decay, mixing))
         values.append((value, mine))
     scan = jnp.concatenate(scan, axis=1) + rows_of(head, 2) * conv_out[:, 2 * STATE :]
-    gate = proj[:, CONV_LANES : CONV_LANES + WIDE]
+    turned = pltpu.roll(proj[:, CONV_LANES - EXTRA : CONV_LANES], HEAD_DIM, 1)
+    turned = jnp.where(lane < HEAD_DIM, turned, 0.0)
+    gate = jnp.concatenate([proj[:, CONV_LANES : CONV_LANES + EXTRA], turned], axis=1)
     gate_sig = sigmoid(gate)
     gated = scan * (gate * gate_sig)
     return dict(
@@ -276,8 +286,9 @@
 
 def mixer_backward_kernel(
     count, grad_ref, inner_ref, beside_ref, proj_ref, w_in_ref, w_out_ref, conv_ref, head_ref, rate_ref,
-    normed_ref, proj_grad_ref, conv_grad_ref, head_grad_ref,
+    *refs,
 ):
+    normed_ref, proj_grad_ref, conv_grad_ref, head_grad_ref = refs[-4:]
     heads = HEADS // 16
     conv, head = conv_ref[...], head_ref[...]
 
@@ -344,27 +355,32 @@
             if offset:
                 kept = d_total * (place >= offset).astype(f32)
                 d_conv = d_conv + rows_of(conv, row) * pltpu.roll(kept, count - offset, 0)
-        proj_grad_ref[part, :] = jnp.concatenate([d_conv, d_gate, d_raw], axis=1).astype(bf16)
+        shared_tile = d_conv[:, CONV_LANES - EXTRA :] + pltpu.roll(d_gate[:, EXTRA:], HEAD_DIM, 1)
+        d_proj = [d_conv[:, : CONV_LANES - EXTRA], shared_tile, d_gate[:, :EXTRA], d_raw]
+        proj_grad_ref[part, :] = jnp.concatenate(d_proj, axis=1).astype(bf16)
     normed_ref[...] = lax.dot_general(
         proj_grad_ref[...], w_in_ref[...], (((1,), (1,)), ((), ())), preferred_element_type=f32
     ).astype(bf16)
 
 
-def mixer_backward(grads, gathered, proj, width, count, w_in, w_out, conv, head, rate):
+def mixer_backward(grads, gathered, proj, width, count, w_in, w_out, conv, head, rate, first, into=()):
     total = grads.shape[0]
     rows = 4 * count
     lanes = width // EXTRA
 
     def rows_spec(extent, column=0):
-        return pl.BlockSpec((rows, extent), lambda step: (step, column))
+        return pl.BlockSpec((rows, extent), lambda step: (first + step, column))
 
     conv_shape = jax.ShapeDtypeStruct(conv.shape, f32)
     head_shape = jax.ShapeDtypeStruct((24, EXTRA), f32)
+    in_specs = [rows_spec(width), rows_spec(EXTRA, lanes), rows_spec(EXTRA, lanes), rows_spec(PROJ_LANES)]
+    in_specs += [whole(entry) for entry in (w_in, w_out, conv, head, rate)]
+    aliases = {len(in_specs) + index: index for index in range(len(into))}
+    in_specs += [pl.BlockSpec(memory_space=pl.ANY)] * len(into)
     return pl.pallas_call(
         lambda *refs: mixer_backward_kernel(count, *refs),
-        grid=(total // rows,),
-        in_specs=[rows_spec(width), rows_spec(EXTRA, lanes), rows_spec(EXTRA, lanes), rows_spec(PROJ_LANES)]
-        + [whole(entry) for entry in (w_in, w_out, conv, head, rate)],
+        grid=(1,),
+        in_specs=in_specs,
         out_specs=[rows_spec(width), rows_spec(PROJ_LANES), whole(conv_shape), whole(head_shape)],
         out_shape=[
             jax.ShapeDtypeStruct((total, width), bf16),
@@ -372,10 +388,11 @@
             conv_shape,
             head_shape,
         ],
+        input_output_aliases=aliases,
         compiler_params=params(),
-        cost_estimate=cost(total / 46),
+        cost_estimate=cost(10),
         name="mixer_backward",
-    )(grads, grads, gathered, proj, w_in, w_out, conv, head, rate)
+    )(grads, grads, gathered, proj, w_in, w_out, conv, head, rate, *into)
 
 
 def selection(rank_ref, experts, slots):
@@ -542,6 +559,79 @@
         cost_estimate=cost(20),
         name="expert_pass",
     )(*inputs)
+
+
+def unpack_kernel(half, own, heads, unit, pack_ref, weight_ref, grad_ref, gate_ref, up_ref, sums_ref):
+    rows = weight_ref.shape[0]
+    lane = lax.broadcasted_iota(jnp.int32, (1, EXTRA), 1)
+    low = lane < HEAD_DIM
+    groups = 2 * half
+    sums = jnp.zeros((rows, EXTRA), f32)
+
+    def tile(index, number):
+        return pack_ref[index, :, number * EXTRA : (number + 1) * EXTRA].astype(f32)
+
+    def put(start, value):
+        grad_ref[:, start : start + EXTRA] = value
+        return value * weight_ref[:, start : start + EXTRA].astype(f32)
+
+    def turn(value, amount):
+        amount %= EXTRA
+        return pltpu.roll(value, amount, 1) if amount else value
+
+    steps = jnp.zeros((rows, EXTRA), f32)
+    shared_b = [jnp.zeros((rows, EXTRA), f32) for _ in range(2 * STATE // EXTRA)]
+    for core in range(2):
+        for column in range(0, half, 2):
+            one, two = 2 * column + core, 2 * column + 2 + core
+            values = (tile(one, 2), tile(one, 3), tile(two, 2), tile(two, 3))
+            gates = (tile(one, 4), turn(values[1], HEAD_DIM), tile(two, 4), turn(values[3], HEAD_DIM))
+            at = core * (INNER // 2) + column * own
+            for start, (first, rest, other, other_rest) in ((at, gates), (INNER + at, values)):
+                turned = turn(other, HEAD_DIM)
+                sums = sums + put(start, first)
+                sums = sums + put(start + EXTRA, jnp.where(low, rest, turned))
+                sums = sums + put(start + 2 * EXTRA, jnp.where(low, turned, turn(other_rest, HEAD_DIM)))
+            for index, place in ((one, column), (two, column + 1)):
+                steps = steps + turn(tile(index, 5), core * (HEADS // 2) + place * heads)
+                shared_b = [total + tile(index, k) for k, total in enumerate(shared_b)]
+    for k, total in enumerate(shared_b):
+        sums = sums + put(2 * INNER + k * EXTRA, total)
+    at = INNER + CONV_CH
+    steps = steps[:, :HEADS]
+    grad_ref[:, at : at + HEADS] = steps
+    rest = jnp.sum(steps * weight_ref[:, at : at + HEADS].astype(f32), axis=1, keepdims=True)
+    sums_ref[...] = jnp.broadcast_to(jnp.sum(sums, axis=1, keepdims=True) + rest, (rows, EXTRA))
+    per_tile = EXTRA // unit
+    for replica in range(2):
+        for start in range(0, groups, per_tile):
+            for kind, out_ref in enumerate((gate_ref, up_ref)):
+                begin = kind * 2 * unit + replica * unit
+                mine = jnp.logical_and(lane >= begin, lane < begin + unit)
+                total = jnp.zeros((rows, EXTRA), f32)
+                for index in range(start, start + per_tile):
+                    part = jnp.where(mine, tile(index, 6), 0.0)
+                    total = total + turn(part, (index - start) * unit - begin)
+                column = replica * groups * unit + start * unit
+                out_ref[:, column : column + EXTRA] = total
+
+
+def unpack(pack, weight, half, own, heads, unit, hidden_units):
+    rows = weight.shape[0]
+    shapes = [
+        jax.ShapeDtypeStruct((rows, columns), f32)
+        for columns in (weight.shape[1], hidden_units, hidden_units, EXTRA)
+    ]
+    return pl.pallas_call(
+        lambda *refs: unpack_kernel(half, own, heads, unit, *refs),
+        grid=(1,),
+        in_specs=[whole(pack), whole(weight)],
+        out_specs=[whole(shape) for shape in shapes],
+        out_shape=shapes,
+        compiler_params=params(),
+        cost_estimate=cost(4),
+        name="unpack",
+    )(pack, weight)
 
 
 def local(
@@ -646,7 +736,7 @@
             following = ring(block) if step < size - 1 else ()
             near = swap(block, "y")
             if step == 0:
-                work = (pack, w_out)
+                work = (pack, w_out, w_shared_down)
             elif replicas == 2 and step < 4:
                 extent = arrived.shape[0] // 3
                 work = swap(after(arrived[(step - 1) * extent : step * extent], block), "dp")
@@ -655,7 +745,7 @@
             following, near, work = tie(following, near, work)
             if step == 0:
                 arrived = work[0].reshape(groups * rows_in, -1)
-                found = work[1]
+                found = work[1:]
             elif replicas == 2 and step < 4:
                 pieces.append(work)
             blocks += [block, near]
@@ -671,8 +761,8 @@
             everything = lax.all_gather(arrived, "dp", axis=0, tiled=True)
         return near, swap(near, "core"), everything, found
 
-    near, mate, pack, w_out = gather_tokens()
     w_shared_down = dp_gather_rows(shared_down[None], 0).reshape(units, width)
+    near, mate, pack, (w_out, w_shared_down) = gather_tokens()
     w_gate, w_up, w_down = (
         lax.all_gather(entry, "dp", axis=1, tiled=True)
         for entry in (expert_gate, expert_up, expert_down)
@@ -705,8 +795,7 @@
     spread = spread.reshape(devices * rows_in, -1)
     w_step = lax.dynamic_slice_in_dim(spread, 2 * STATE + first_head, heads, 1)
     w_step = jnp.pad(w_step, ((0, 0), (0, EXTRA - heads)))
-    widen = ((0, 0), (0, WIDE - own))
-    w_in = [spread[:, : 2 * STATE], jnp.pad(pack[:, own : 2 * own], widen), jnp.pad(pack[:, :own], widen), w_step]
+    w_in = [spread[:, : 2 * STATE], pack[:, own : 2 * own], pack[:, EXTRA:own], pack[:, :EXTRA], w_step]
     w_in = jnp.concatenate(w_in, axis=1)
     w_shared_gate = pack[:, 2 * own : 2 * own + units]
     w_shared_up = pack[:, 2 * own + units :]
@@ -769,17 +858,32 @@
     normed_mate, proj_mate, mixed_mate, scaled_mate = done_mate
     normed_near, proj_near, mixed_near, scaled_near = done_near
     pairs_sum = scatter_first(mixed_near, mixed_mate)
-    d_row, slot_weight, act_grad_near = rows_out(branch_near, 0, (w_shared_down,))
-    d_row, slot_weight, act_grad_mate = rows_out(
-        branch_mate, half_pairs, (w_shared_down,), (d_row, slot_weight)
-    )
-    mixed_sum, (_, d_row, w_up, *_) = scatter_last(pairs_sum, [(), d_row, w_up])
+    mixed_sum, (_, _, w_up, *_) = scatter_last(pairs_sum, [(), (), w_up])
     mix_rms = lax.rsqrt(jnp.sum(mixed_sum[:, width:], axis=1, keepdims=True) / INNER + epsilon)
     mixer_out = mixed_sum[:, :width] * mix_rms
     resid = input_rows + live * mixer_out
     ffn_rms = lax.rsqrt(jnp.mean(resid * resid, axis=1, keepdims=True) + epsilon)
     ffn_hat = resid * ffn_rms
-    ffn_near, ffn_mate, _ = gather((ffn_hat * ffn_gain_all).astype(bf16))
+
+    def grads_near(token):
+        return rows_out(after(branch_near, token), 0, (w_shared_down,))
+
+    done_rows = []
+
+    def grads_mate(token):
+        return rows_out(after(branch_mate, token), half_pairs, (w_shared_down,), done_rows[0])
+
+    def keep(work):
+        def kept(token):
+            found = work(token)
+            done_rows.append(found[:2])
+            return found
+
+        return kept
+
+    ffn_near, ffn_mate, ((_, _, act_grad_near), (d_row, slot_weight, act_grad_mate), *_) = gather(
+        (ffn_hat * ffn_gain_all).astype(bf16), [keep(grads_near), grads_mate]
+    )
 
     expert_in, shared_near, sg_near, su_near = rows_out(
         ffn_near, 0, (act_grad_near, w_shared_gate, w_shared_up)
@@ -852,23 +956,53 @@
         ],
     )
     grad_shared_down, grad_shared_g, grad_shared_u = shared_grads
-    grad_shared_gu = dp_scatter_rows(jnp.concatenate([grad_shared_g, grad_shared_u], axis=1), 0)
+    grad_shared_gu = jnp.concatenate([grad_shared_g, grad_shared_u], axis=1)
+    grad_out_rows = of_halves(
+        (scaled_near, scaled_mate), (d_mixer_near[:, :width], d_mixer_mate[:, :width])
+    )[:own]
+    out_rows_low = grad_out_rows.astype(bf16)
     out_pairs = scatter_first(out_near, out_mate)
-    (d_mixer_near, d_mixer_mate), out_pairs = tie((d_mixer_near, d_mixer_mate), out_pairs)
-
-    def backward(grads, part, proj):
-        return mixer_backward(grads, part, proj, width, tokens, w_in, w_out, conv, head, rate_rows)
-
-    done_mate = backward(d_mixer_mate, mate, proj_mate)
-    out_there = {step: swap(out_pairs[step][1], "y") for step in (1, 2)}
-    d_mixer_near, out_pairs, out_there, done_mate = tie(d_mixer_near, out_pairs, out_there, done_mate)
-    done_near = backward(d_mixer_near, near, proj_near)
+    (d_mixer_near, d_mixer_mate), out_pairs, out_rows_low = tie(
+        (d_mixer_near, d_mixer_mate), out_pairs, out_rows_low
+    )
+
+    def backward(grads, part, proj, first, into=()):
+        return mixer_backward(
+            grads, part, proj, width, tokens, w_in, w_out, conv, head, rate_rows, first, into
+        )
+
+    def towards(step):
+        return swap(out_pairs[step][1], "y")
+
+    def window(work, *others):
+        return tie(work, *others)
+
+    part_one = backward(d_mixer_mate, mate, proj_mate, 0)
+    out_there = {1: towards(1), 2: towards(2)}
+    part_one, out_there, out_pairs, d_mixer_mate = window(part_one, out_there, out_pairs, d_mixer_mate)
+    done_mate = backward(d_mixer_mate, mate, proj_mate, 1, part_one[:2])
     out_total = ring_step(add_low(out_pairs[1][0], out_there[1]), out_pairs, out_there, 1)
-    out_there |= {step: swap(out_pairs[step][1], "y") for step in (3, 0)}
+    out_there[3] = towards(3)
+    done_mate, out_total, out_there, out_pairs, d_mixer_near = window(
+        done_mate, out_total, out_there, out_pairs, d_mixer_near
+    )
+    part_two = backward(d_mixer_near, near, proj_near, 0)
     moved = swap(done_mate[0], "core")
-    done_near, out_total, out_there, moved = tie(done_near, out_total, out_there, moved)
-    normed_grad_mate, proj_low_mate, conv_mate, head_mate = done_mate
-    normed_grad_near, proj_low_near, conv_near, head_near = done_near
+    out_total = ring_step(out_total, out_pairs, out_there, 2)
+    out_there[0] = towards(0)
+    part_two, moved, out_total, out_there, out_pairs, d_mixer_near = window(
+        part_two, moved, out_total, out_there, out_pairs, d_mixer_near
+    )
+    out_rows_there = swap(after(out_rows_low, part_two[0]), "dp") if replicas == 2 else ()
+    done_near = backward(d_mixer_near, near, proj_near, 1, part_two[:2])
+    branch_sum = ring_step(out_total, out_pairs, out_there, 3)
+    done_near, branch_sum = window(done_near, branch_sum)
+    grad_shared_gu = dp_scatter_rows(grad_shared_gu, 0, done_near[0])
+    grad_shared_down = dp_scatter_rows(grad_shared_down.reshape(replicas, unit, width), 0, done_near[0])[0]
+    normed_grad_mate, proj_low_mate = done_mate[:2]
+    normed_grad_near, proj_low_near = done_near[:2]
+    conv_parts = [part_one[2], done_mate[2], part_two[2], done_near[2]]
+    head_parts = [part_one[3], done_mate[3], part_two[3], done_near[3]]
     pairs_sum = scatter_first(normed_grad_near, normed_grad_mate, moved)
 
     def to_owner(part):
@@ -909,35 +1043,25 @@
 
     pieces = []
 
-    def window_one(token):
-        return input_grad(1 - here, token).astype(bf16)
-
-    def window_two(token):
-        conv_parts, head_parts = after(((conv_mate, conv_near), (head_mate, head_near)), token)
-        return small_sums(sum(conv_parts), sum(head_parts))
-
-    def window_three(token):
-        parts = after((scaled_near, scaled_mate), token)
-        return of_halves(parts, (d_mixer_near[:, :width], d_mixer_mate[:, :width]))[:own]
+    def small_work(token):
+        parts = after((conv_parts, head_parts), token)
+        return small_sums(sum(parts[0]), sum(parts[1]))
 
     there = scatter_beside(pairs_sum)
     total = add_low(pairs_sum[1][0], there[1])
-    total, leaving = tie(total, window_one(pairs_sum))
-    works = (window_two, window_three, lambda token: input_grad(here, token))
+    total, leaving, out_rows_there = tie(
+        total, input_grad(1 - here, pairs_sum).astype(bf16), out_rows_there
+    )
     finished = []
-    for index, work in enumerate(works):
+    for index, work in enumerate((lambda token: input_grad(here, token), small_work, lambda token: ())):
         following = ring_step(total, pairs_sum, there, index + 1)
         across = piece(leaving, index, total) if crossing else ()
-        if index < 2:
-            out_total = ring_step(after(out_total, total), out_pairs, out_there, index + 2)
-        result = work(total)
-        total, across, out_total, result = tie(following, across, out_total, result)
+        total, across, result = tie(following, across, work(total))
         pieces.append(across)
         finished.append(result)
-    grad_normed, branch_sum = total, out_total
-    sums, grad_out_rows, grad_w_in = finished
+    grad_w_in, sums, _ = finished
+    grad_normed = total
     output = (resid + live * branch_sum).astype(bf16)
-    grad_gate, grad_up = grad_gate.astype(f32), grad_up.astype(f32)
 
     if crossing:
         grad_w_in = grad_w_in + jnp.concatenate(pieces, axis=0).astype(f32)
@@ -945,7 +1069,8 @@
         grad_w_in = lax.psum_scatter(leaving, "dp", scatter_dimension=0, tiled=True)
     grad_pack = jnp.concatenate([grad_w_in.astype(bf16), grad_shared_gu.astype(bf16)], axis=1)
     grad_pack = grad_pack.reshape(groups, rows_in, -1)
-    grad_pack = lax.all_to_all(grad_pack, GROUP, split_axis=0, concat_axis=0, tiled=True).astype(f32)
+    grad_gate, grad_up = (entry.astype(f32) for entry in after((grad_gate, grad_up), grad_pack))
+    grad_pack = lax.all_to_all(grad_pack, GROUP, split_axis=0, concat_axis=0, tiled=True)
 
     def from_place(block):
         block = block.reshape(half, 2, rows_in, block.shape[2]).transpose(2, 1, 0, 3)
@@ -955,23 +1080,30 @@
         block = block.reshape(groups, rows_in, replicas, unit).transpose(1, 2, 0, 3)
         return block.reshape(rows_in, hidden_units)
 
-    value_at, gate_at, step_at = 2 * STATE, CONV_LANES, CONV_LANES + WIDE
-    grad_in_proj = jnp.concatenate(
-        [
-            from_place(grad_pack[:, :, gate_at : gate_at + own]),
-            from_place(grad_pack[:, :, value_at : value_at + own]),
-            jnp.sum(grad_pack[:, :, : 2 * STATE], axis=0),
-            from_place(grad_pack[:, :, step_at : step_at + heads]),
-        ],
-        axis=1,
-    )
-    grad_shared_gate = from_unit(grad_pack[:, :, PROJ_LANES : PROJ_LANES + units])
-    grad_shared_up = from_unit(grad_pack[:, :, PROJ_LANES + units :])
-    grad_shared_down = dp_scatter_rows(grad_shared_down.reshape(replicas, unit, width), 0)[0]
+    if replicas == 2:
+        grad_in_proj, grad_shared_gate, grad_shared_up, gain_sums = unpack(
+            grad_pack, in_proj, half, own, heads, unit, hidden_units
+        )
+        gain_sums = gain_sums[:, 0]
+    else:
+        grad_pack = grad_pack.astype(f32)
+        value_at, gate_at, step_at = 2 * STATE, CONV_LANES, CONV_LANES + EXTRA
+        gate_part = [grad_pack[:, :, gate_at : gate_at + EXTRA], grad_pack[:, :, value_at + own : gate_at]]
+        grad_in_proj = jnp.concatenate(
+            [
+                from_place(jnp.concatenate(gate_part, axis=2)),
+                from_place(grad_pack[:, :, value_at : value_at + own]),
+                jnp.sum(grad_pack[:, :, : 2 * STATE], axis=0),
+                from_place(grad_pack[:, :, step_at : step_at + heads]),
+            ],
+            axis=1,
+        )
+        grad_shared_gate = from_unit(grad_pack[:, :, PROJ_LANES : PROJ_LANES + units])
+        grad_shared_up = from_unit(grad_pack[:, :, PROJ_LANES + units :])
+        gain_sums = jnp.sum(grad_in_proj * in_proj.astype(f32), axis=1)
     if replicas == 2:
         mine = lax.axis_index("dp") == core
-        received = swap(grad_out_rows.astype(bf16), "dp").astype(f32)
-        total = (grad_out_rows + received).reshape(2, own // 2, width)
+        total = (grad_out_rows + out_rows_there.astype(f32)).reshape(2, own // 2, width)
         passed = swap(lax.dynamic_index_in_dim(total, 1 - core, 0, keepdims=False), "core")
         grad_out_proj = jnp.where(mine, lax.dynamic_index_in_dim(total, core, 0, keepdims=False), passed)
     else:
@@ -979,7 +1111,7 @@
         full = lax.dynamic_update_slice_in_dim(full, grad_out_rows, first_channel, 0)
         grad_out_proj = lax.psum_scatter(full, ALL, scatter_dimension=0, tiled=True)
     grad_mix_gain = jnp.sum(grad_out_proj * out_proj.astype(f32), axis=1) / mix_gain.astype(f32)
-    grad_norm_gain = jnp.sum(grad_in_proj * in_proj.astype(f32), axis=1) / norm_gain.astype(f32)
+    grad_norm_gain = gain_sums / norm_gain.astype(f32)
 
     sums = lax.all_to_all(sums, ALL, split_axis=0, concat_axis=0, tiled=True)
     sums = jnp.sum(sums, axis=0)

time: 721 us -> 672 us (0.932)
  waiting for transfers between devices: 219 us -> 198 us
  local copies, waits for them, and re-layouts: 88.5 us -> 75.2 us
  other arithmetic: 85.4 us -> 77.6 us
    ppermute x24, waiting for transfers between devices: 67.8 us -> 38.2 us  [ring(): return lax.ppermute(value, 'z', [(k, (k + 1) % size) for k in range(size)])]
    all_to_all x1, waiting for transfers between devices: 2.06 us -> 14.8 us  [local(): lax.all_to_all(grad_pack, GROUP, split_axis=0, concat_axis=0, tiled=True)]
    ppermute x54, waiting for transfers between devices: 140 us -> 128 us  [swap(): return lax.ppermute(value, axis, [(0, 1), (1, 0)])]
    ppermute x24, starting transfers between devices: 33.3 us -> 25.8 us  [ring(): return lax.ppermute(value, 'z', [(k, (k + 1) % size) for k in range(size)])]
    all_gather x3, waiting for transfers between devices: 5.29 us -> 12.6 us  [local(): lax.all_gather(entry, 'dp', axis=1, tiled=True)]
    pallas_call x2 -> x5, Pallas kernels: 49.2 us -> 51 us  [the longest x4 47.8 us: mixer_backward(): pl.pallas_call(lambda *refs: mixer_backward_kernel(count, *refs), grid=(1...]
    unnamed x216 -> x198, local copies, waits for them, and re-layouts: 28.7 us -> 28.3 us
  transfers between devices with their start and end apart: 87 -> 87, of which waited for: 40 -> 34; matrix products, arithmetic and copies ran while one was open for 26% -> 27% of each run, Pallas kernels for 18% -> 18%
where the time goes in v4:
time: 672 us; the launch traced here: 662 us
  waiting for transfers between devices  198 us (29%)
  Pallas kernels  145 us (22%)
  starting transfers between devices  105 us (16%)
  other arithmetic  77.6 us (12%)
  local copies, waits for them, and re-layouts  75.2 us (11%)
  matrix products  45.5 us (7%)
  between operations  16.2 us (2%)
    ppermute x54, waiting for transfers between devices, swap(): return lax.ppermute(value, axis, [(0, 1), (1, 0)])  128 us
    ppermute x54, starting transfers between devices, swap(): return lax.ppermute(value, axis, [(0, 1), (1, 0)])  56.2 us
    pallas_call x4, Pallas kernels, mixer_backward(): pl.pallas_call(lambda *refs: mixer_backward_kernel(count, *refs), grid=(1...  47.8 us
    dot_general x16, matrix products, matmul(): lax.dot_general(left, right, dims, precision=precision, preferred_element...  45.5 us
    ppermute x24, waiting for transfers between devices, ring(): return lax.ppermute(value, 'z', [(k, (k + 1) % size) for k in range(size)])  38.2 us
    unnamed x198, local copies, waits for them, and re-layouts  28.3 us
    pallas_call x2, Pallas kernels, mixer_forward(): pl.pallas_call(lambda *refs: mixer_forward_kernel(count, *refs), grid=(to...  26.2 us
    ppermute x24, starting transfers between devices, ring(): return lax.ppermute(value, 'z', [(k, (k + 1) % size) for k in range(size)])  25.8 us
  transfers between devices with their start and end apart: 87, of which 34 were waited for; matrix products, arithmetic and copies ran while one was open for 27% of the time, Pallas kernels for 18%

profile of v4, /device:TPU:13, one launch (start us, length us, event | category | flops | bytes accessed | tf_op | source)
XLA Modules:
  0.0 662.1 jit_solution(11283731154622422006)
XLA Ops:
  8.2 2.8 concatenate.86
  19.7 6.3 all-to-all-start
  31.4 11.6 %collective-permute-done.4 = bf16[192,1536]{1,0:T(8,128)(2,1)S(1)} collective-permute-done((bf16[192,1536]{1,0:T(8,128)(2,1)S(1)}, bf16[192,1536]{1,0:T(8,128)(2,1)S(1)}, u32[]{:S(2)}, u32[]{:S(2)}) %collective-permute-start.4) | collective-permute-done | bytes 589856 | tf_op jit(solution)/shard_map/ppermute | solution.py:31
  43.1 11.3 %collective-permute-done.2 = bf16[128,2048]{1,0:T(8,128)(2,1)S(1)} collective-permute-done((bf16[128,2048]{1,0:T(8,128)(2,1)S(1)}, bf16[128,2048]{1,0:T(8,128)(2,1)S(1)}, u32[]{:S(2)}, u32[]{:S(2)}) %collective-permute-start.2) | collective-permute-done | bytes 524320 | tf_op jit(solution)/shard_map/ppermute | solution.py:36
  59.2 11.4 %collective-permute-done.8 = bf16[256,512]{1,0:T(8,128)(2,1)S(1)} collective-permute-done((bf16[256,512]{1,0:T(8,128)(2,1)S(1)}, bf16[256,512]{1,0:T(8,128)(2,1)S(1)}, u32[]{:S(2)}, u32[]{:S(2)}) %collective-permute-start.8) | collective-permute-done | bytes 262176 | tf_op jit(solution)/shard_map/ppermute | solution.py:31
  76.7 10.2 %collective-permute-done.11 = bf16[256,512]{1,0:T(8,128)(2,1)S(1)} collective-permute-done((bf16[256,512]{1,0:T(8,128)(2,1)S(1)}, bf16[256,512]{1,0:T(8,128)(2,1)S(1)}, u32[]{:S(2)}, u32[]{:S(2)}) %collective-permute-start.11) | collective-permute-done | bytes 262176 | tf_op jit(solution)/shard_map/ppermute | solution.py:31
  91.1 9.8 %collective-permute-done.13 = bf16[256,512]{1,0:T(8,128)(2,1)S(1)} collective-permute-done((bf16[256,512]{1,0:T(8,128)(2,1)S(1)}, bf16[256,512]{1,0:T(8,128)(2,1)S(1)}, u32[]{:S(2)}, u32[]{:S(2)}) %collective-permute-start.13) | collective-permute-done | bytes 262176 | tf_op jit(solution)/shard_map/ppermute | solution.py:31
  101.8 4.1 collective-permute-start.16
  124.0 4.6 concatenate.97.refs_3_.refs_4_
  129.9 2.6 collective-permute-start.17
  132.7 13.1 %mixer_forward.2 = (bf16[1024,1536]{1,0:T(8,128)(2,1)}, f32[1024,768]{1,0:T(8,128)}, bf16[1024,1664]{1,0:T(8,128)(2,1)}, bf16[1024,256]{1,0:T(8,128)(2,1)}) custom-call(bf16[1024,2048]{1,0:T(8,128)(2,1)} %collective-permute-done.16.refs_0_.refs_1_.refs_2_, bf16[1024,2048]{1,0:T(8,128)(2,1)} %collective-permute-done.16.refs_0_.refs_1_.refs_2_, ...), custom_call_target="tpu_custom_call" | custom-call | flops 14080000000 | bytes 44800000 | tf_op jit(solution)/shard_map/mixer_forward/pallas_call | solution.py:269
  155.5 13.1 %mixer_forward.3 = (bf16[1024,1536]{1,0:T(8,128)(2,1)}, f32[1024,768]{1,0:T(8,128)}, bf16[1024,1664]{1,0:T(8,128)(2,1)}, bf16[1024,256]{1,0:T(8,128)(2,1)}) custom-call(bf16[1024,2048]{1,0:T(8,128)(2,1)} %constant_dynamic-update-slice_fusion.refs_0_.refs_1_.refs_2_, bf16[1024,2048]{1,0:T(8,128)(2,1)} %constant_dynamic-update-slice_fusion.refs_0_.refs_1_.refs_2_, ...), custom_call_target="tpu_custom_call" | custom-call | flops 14080000000 | bytes 44800000 | tf_op jit(solution)/shard_map/mixer_forward/pallas_call | solution.py:269
  168.6 3.7 add_convert_fusion.5
  176.6 6.8 %collective-permute-done.22 = bf16[128,1664]{1,0:T(8,128)(2,1)S(1)} collective-permute-done((bf16[128,1664]{1,0:T(8,128)(2,1)S(1)}, bf16[128,1664]{1,0:T(8,128)(2,1)S(1)}, u32[]{:S(2)}, u32[]{:S(2)}) %collective-permute-start.22) | collective-permute-done | bytes 426016 | tf_op jit(solution)/shard_map/ppermute | solution.py:31
  186.8 5.7 collective-permute-done.24
  194.4 6.6 collective-permute-done.31
  204.4 5.7 collective-permute-done.26
  213.4 5.8 collective-permute-done.28
  224.4 5.5 dispatch.4
  233.8 5.3 dispatch.5
  241.4 6.7 %collective-permute-done.35 = bf16[128,1536]{1,0:T(8,128)(2,1)S(1)} collective-permute-done((bf16[128,1536]{1,0:T(8,128)(2,1)S(1)}, bf16[128,1536]{1,0:T(8,128)(2,1)S(1)}, u32[]{:S(2)}, u32[]{:S(2)}) %collective-permute-start.35) | collective-permute-done | bytes 393248 | tf_op jit(solution)/shard_map/ppermute | solution.py:36
  249.3 9.5 %collective-permute-done.37 = bf16[128,1536]{1,0:T(8,128)(2,1)S(1)} collective-permute-done((bf16[128,1536]{1,0:T(8,128)(2,1)S(1)}, bf16[128,1536]{1,0:T(8,128)(2,1)S(1)}, u32[]{:S(2)}, u32[]{:S(2)}) %collective-permute-start.37) | collective-permute-done | bytes 393248 | tf_op jit(solution)/shard_map/ppermute | solution.py:31
  258.8 6.9 %collective-permute-start.38 = (bf16[1024,1536]{1,0:T(8,128)(2,1)S(1)}, bf16[1024,1536]{1,0:T(8,128)(2,1)S(1)}, u32[]{:S(2)}, u32[]{:S(2)}) collective-permute-start(bf16[1024,1536]{1,0:T(8,128)(2,1)S(1)} %constant_dynamic-update-slice_fusion.19.refs_2_), channel_id=1, source_target_pairs={{0,1},{1,0},{2,3},{3,2},{4,5},{5,4},{6,7},{7,6},{8,9},{9,8},{10,11... | collective-permute-start | bytes 9437192 | tf_op jit(solution)/shard_map/ppermute | solution.py:31
  265.7 6.2 dispatch.6
  273.5 6.3 dispatch.7
  279.8 12.5 %all-gather.8.cloned.1.call-done.down_ref = bf16[4,512,1536]{2,1,0:T(8,128)(2,1)} async-done(((bf16[4,256,1536]{2,1,0:T(8,128)(2,1)}), bf16[4,512,1536]{2,1,0:T(8,128)(2,1)}) %all-gather.8.cloned.1.call-update) | async-done | bytes 6291472 | tf_op jit(solution)/shard_map/all_gather | solution.py:767
  292.4 20.7 %expert_pass.1 = (bf16[4,384,512]{2,1,0:T(8,128)(2,1)}, bf16[4,384,512]{2,1,0:T(8,128)(2,1)}, bf16[4,384,512]{2,1,0:T(8,128)(2,1)}, bf16[4,384,1536]{2,1,0:T(8,128)(2,1)}, bf16[4,384,1536]{2,1,0:T(8,128)(2,1)}) custom-call(bf16[4,384,1536]{2,1,0:T(8,128)(2,1)} %get-tuple-element.309.rows_ref, bf16[4,384,1536]{2,1,0:T(8,128)(2,1)} %get-tuple-element.296.grad_ref, ...), custom_call_target="tpu_custom_call" | custom-call | flops 22000001024 | bytes 70000000 | tf_op jit(solution)/shard_map/expert_pass/pallas_call | solution.py:552
  313.0 6.8 %convolution_convert_fusion.2 = bf16[4,512,1536]{2,1,0:T(8,128)(2,1)} fusion(bf16[4,384,512]{2,1,0:T(8,128)(2,1)} %get-tuple-element.301, bf16[4,384,1536]{2,1,0:T(8,128)(2,1)S(1)} %bitcast.137), kind=kOutput, calls=%fused_computation.3 | convolution fusion | flops 2419064832 | bytes 12582912 | tf_op jit(solution)/shard_map/dot_general | solution.py:27
  320.1 6.2 combine.5
  327.0 6.3 combine.4
  333.3 4.7 add_convert_fusion.17
  340.0 5.4 convolution_convert_fusion.1
  353.8 8.7 %convolution_convert_fusion = bf16[4,1536,512]{2,1,0:T(8,128)(2,1)} fusion(bf16[4,384,1536]{2,1,0:T(8,128)(2,1)} %get-tuple-element.309.rows_ref, bf16[4,384,512]{2,1,0:T(8,128)(2,1)S(1)} %copy-done.17), kind=kOutput, calls=%fused_computation.1 | convolution fusion | flops 2419064832 | bytes 12582912 | tf_op jit(solution)/shard_map/dot_general | solution.py:27
  367.5 5.5 collective-permute-done.43
  376.3 8.0 %collective-permute-done.45 = bf16[128,1536]{1,0:T(8,128)(2,1)} collective-permute-done((bf16[128,1536]{1,0:T(8,128)(2,1)}, bf16[128,1536]{1,0:T(8,128)(2,1)}, u32[]{:S(2)}, u32[]{:S(2)}) %collective-permute-start.45) | collective-permute-done | bytes 393248 | tf_op jit(solution)/shard_map/ppermute | solution.py:36
  389.3 5.1 combine.6
  394.4 3.3 collective-permute-done.47
  400.0 5.2 collective-permute-start.55
  405.2 6.0 combine.7
  411.3 3.8 collective-permute-start.51
  419.1 2.7 fusion.87
  424.4 2.6 convolution_add_fusion.2
  429.4 5.5 convert_element_type.757
  434.9 3.0 collective-permute-done.53
  441.3 4.1 add_convert_fusion.10
  445.4 2.9 fusion.2
  448.4 3.4 fusion
  455.5 11.8 %mixer_backward.4 = (bf16[1024,1536]{1,0:T(8,128)(2,1)}, bf16[1024,768]{1,0:T(8,128)(2,1)}, f32[8,512]{1,0:T(8,128)}, f32[24,128]{1,0:T(8,128)}) custom-call(bf16[1024,1664]{1,0:T(8,128)(2,1)} %collective-permute-done.54.refs_0_.refs_1_, bf16[1024,1664]{1,0:T(8,128)(2,1)} %collective-permute-done.54.refs_0_.refs_1_, ...), custom_call_target="tpu_custom_call" | custom-call | flops 11000000512 | bytes 35000000 | tf_op jit(solution)/shard_map/mixer_backward/pallas_call | solution.py:380
  467.3 5.5 collective-permute-done.57
  475.0 11.6 %mixer_backward.5 = (bf16[1024,1536]{1,0:T(8,128)(2,1)}, bf16[1024,768]{1,0:T(8,128)(2,1)}, f32[8,512]{1,0:T(8,128)}, f32[24,128]{1,0:T(8,128)}) custom-call(bf16[1024,1664]{1,0:T(8,128)(2,1)} %collective-permute-done.54.refs_0_.refs_1_, bf16[1024,1664]{1,0:T(8,128)(2,1)} %collective-permute-done.54.refs_0_.refs_1_, ...), custom_call_target="tpu_custom_call", output_to_operand_aliasing={{0}: (9, {}), {1}: (10, {})} | custom-call | flops 11000000512 | bytes 35000000 | tf_op jit(solution)/shard_map/mixer_backward/pallas_call | solution.py:380
  494.0 12.6 %mixer_backward.6 = (bf16[1024,1536]{1,0:T(8,128)(2,1)}, bf16[1024,768]{1,0:T(8,128)(2,1)}, f32[8,512]{1,0:T(8,128)}, f32[24,128]{1,0:T(8,128)}) custom-call(bf16[1024,1664]{1,0:T(8,128)(2,1)} %constant_dynamic-update-slice_fusion.27.refs_0_.refs_1_, bf16[1024,1664]{1,0:T(8,128)(2,1)} %constant_dynamic-update-slice_fusion.27.refs_0_.refs_1_, ...), custom_call_target="tpu_custom_call" | custom-call | flops 11000000512 | bytes 35000000 | tf_op jit(solution)/shard_map/mixer_backward/pallas_call | solution.py:380
  508.0 11.8 %mixer_backward.7 = (bf16[1024,1536]{1,0:T(8,128)(2,1)}, bf16[1024,768]{1,0:T(8,128)(2,1)}, f32[8,512]{1,0:T(8,128)}, f32[24,128]{1,0:T(8,128)}) custom-call(bf16[1024,1664]{1,0:T(8,128)(2,1)} %constant_dynamic-update-slice_fusion.27.refs_0_.refs_1_, ...), custom_call_target="tpu_custom_call", output_to_operand_aliasing={{0}: (9, {}), {1}: (10, {})} | custom-call | flops 11000000512 | bytes 35000000 | tf_op jit(solution)/shard_map/mixer_backward/pallas_call | solution.py:380
  520.9 3.8 add_convert_fusion.9
  529.4 2.5 add_convert_fusion.1
  543.3 3.0 fusion.6
  546.4 2.9 fusion.12
  552.2 15.7 %collective-permute-done.68 = bf16[256,768]{1,0:T(8,128)(2,1)S(1)} collective-permute-done((bf16[256,768]{1,0:T(8,128)(2,1)S(1)}, bf16[256,768]{1,0:T(8,128)(2,1)S(1)}, u32[]{:S(2)}, u32[]{:S(2)}) %collective-permute-start.68) | collective-permute-done | bytes 393248 | tf_op jit(solution)/shard_map/ppermute | solution.py:31
  577.3 13.5 %collective-permute-done.71 = bf16[256,768]{1,0:T(8,128)(2,1)S(1)} collective-permute-done((bf16[256,768]{1,0:T(8,128)(2,1)}, bf16[256,768]{1,0:T(8,128)(2,1)S(1)}, u32[]{:S(2)}, u32[]{:S(2)}) %collective-permute-start.71) | collective-permute-done | bytes 393248 | tf_op jit(solution)/shard_map/ppermute | solution.py:31
  596.5 9.2 %all-to-all-start.2 = ((f32[32,1,712]{2,1,0:T(1,128)}), f32[32,1,712]{2,1,0:T(1,128)}, u32[]{:S(2)}, u32[]{:S(2)}) async-start(f32[32,1,712]{2,1,0:T(1,128)} %copy.210), calls=%async_computation.3 | async-start | bytes 196608 | tf_op jit(solution)/shard_map/all_to_all | solution.py:1116
  611.1 7.0 %all-to-all-start.1 = ((bf16[16,48,896]{2,1,0:T(8,128)(2,1)}), bf16[16,48,896]{2,1,0:T(8,128)(2,1)}, u32[]{:S(2)}, u32[]{:S(2)}) async-start(bf16[16,48,896]{2,1,0:T(8,128)(2,1)} %bitcast.57), calls=%async_computation.2 | async-start | bytes 2752512 | tf_op jit(solution)/shard_map/all_to_all | solution.py:1073
  624.6 5.6 convert_element_type.834
  630.3 3.6 convert_element_type.835
  635.4 14.8 %all-to-all-done.1.refs_0_ = bf16[16,48,896]{2,1,0:T(8,128)(2,1)} async-done(((bf16[16,48,896]{2,1,0:T(8,128)(2,1)}), bf16[16,48,896]{2,1,0:T(8,128)(2,1)}, u32[]{:S(2)}, u32[]{:S(2)}) %all-to-all-start.1) | async-done | bytes 1376288 | tf_op jit(solution)/shard_map/all_to_all | solution.py:1073
  650.2 3.2 unpack.1
  (554 shorter events, 193.8 us)
Async XLA Ops:
  11.9 15.7 %collective-permute-start = (bf16[1,48,384]{2,1,0:T(8,128)(2,1)S(1)}, bf16[1,48,384]{2,1,0:T(8,128)(2,1)S(1)}, u32[]{:S(2)}, u32[]{:S(2)}) collective-permute-start(bf16[1,48,384]{2,1,0:T(8,128)(2,1)S(1)} %fusion.62), channel_id=1, source_target_pairs={{0,16},{16,0},{1,17},{17,1},{2,18},{18,2},{3,19},{19,3},{4,20},{20... | collective-permute-start | bytes 110600 | tf_op jit(solution)/shard_map/ppermute | solution.py:31
  13.1 14.6 %collective-permute-start.1 = (bf16[96,1536]{1,0:T(8,128)(2,1)}, bf16[96,1536]{1,0:T(8,128)(2,1)S(1)}, u32[]{:S(2)}, u32[]{:S(2)}) collective-permute-start(bf16[96,1536]{1,0:T(8,128)(2,1)} %param.27), channel_id=1, source_target_pairs={{0,1},{1,0},{2,3},{3,2},{4,5},{5,4},{6,7},{7,6},{8,9},{9,8},{10,11... | collective-permute-start | bytes 884744 | tf_op jit(solution)/shard_map/ppermute | solution.py:31
  14.1 15.1 %collective-permute-start.5 = (bf16[1,32,1536]{2,1,0:T(8,128)(2,1)}, bf16[1,32,1536]{2,1,0:T(8,128)(2,1)S(1)}, u32[]{:S(2)}, u32[]{:S(2)}) collective-permute-start(bf16[1,32,1536]{2,1,0:T(8,128)(2,1)} %bitcast.174), channel_id=1, source_target_pairs={{0,16},{16,0},{1,17},{17,1},{2,18},{18,2},{3,19},{19,3},{4,20},{20... | collective-permute-start | bytes 294920 | tf_op jit(solution)/shard_map/ppermute | solution.py:31
  19.7 37.2 %all-to-all-start = ((bf16[16,48,512]{2,1,0:T(8,128)(2,1)}), bf16[16,48,512]{2,1,0:T(8,128)(2,1)S(1)}, u32[]{:S(2)}, u32[]{:S(2)}) async-start(bf16[16,48,512]{2,1,0:T(8,128)(2,1)} %pad_maximum_fusion.2), calls=%async_computation | async-start | bytes 1572864 | tf_op jit(solution)/shard_map/all_to_all | solution.py:718
  26.0 103.9 %all-gather.4.cloned.1.call-start = ((), (), s32[]{:S(2)}) async-start(), calls=%async_computation.6 | async-start | bytes 9437184 | tf_op jit(solution)/shard_map/all_gather | solution.py:767
  26.7 183.7 %all-gather.6.cloned.1.call-start = ((), (), s32[]{:S(2)}) async-start(), calls=%async_computation.7 | async-start | bytes 9437184 | tf_op jit(solution)/shard_map/all_gather | solution.py:767
  27.9 15.2 %collective-permute-start.4 = (bf16[192,1536]{1,0:T(8,128)(2,1)S(1)}, bf16[192,1536]{1,0:T(8,128)(2,1)S(1)}, u32[]{:S(2)}, u32[]{:S(2)}) collective-permute-start(bf16[192,1536]{1,0:T(8,128)(2,1)S(1)} %pad_maximum_fusion.3), channel_id=1, source_target_pairs={{0,16},{16,0},{1,17},{17,1},{2,18},{18,2},{3,19},{19,3},{4,20},{20... | collective-permute-start | bytes 1769480 | tf_op jit(solution)/shard_map/ppermute | solution.py:31
  29.2 25.2 %collective-permute-start.2 = (bf16[128,2048]{1,0:T(8,128)(2,1)S(1)}, bf16[128,2048]{1,0:T(8,128)(2,1)S(1)}, u32[]{:S(2)}, u32[]{:S(2)}) collective-permute-start(bf16[128,2048]{1,0:T(8,128)(2,1)S(1)} %fusion.46), channel_id=1, source_target_pairs={{0,4},{4,8},{8,12},{12,0},{1,5},{5,9},{9,13},{13,1},{2,6},{6,10},{... | collective-permute-start | bytes 1572872 | tf_op jit(solution)/shard_map/ppermute | solution.py:36
  30.4 24.0 %collective-permute-start.3 = (bf16[128,2048]{1,0:T(8,128)(2,1)S(1)}, bf16[128,2048]{1,0:T(8,128)(2,1)}, u32[]{:S(2)}, u32[]{:S(2)}) collective-permute-start(bf16[128,2048]{1,0:T(8,128)(2,1)S(1)} %fusion.46), channel_id=1, source_target_pairs={{0,2},{2,0},{1,3},{3,1},{4,6},{6,4},{5,7},{7,5},{8,10},{10,8},{9,1... | collective-permute-start | bytes 1572872 | tf_op jit(solution)/shard_map/ppermute | solution.py:31
  56.8 13.8 %collective-permute-start.6 = (bf16[128,2048]{1,0:T(8,128)(2,1)S(1)}, bf16[128,2048]{1,0:T(8,128)(2,1)S(1)}, u32[]{:S(2)}, u32[]{:S(2)}) collective-permute-start(bf16[128,2048]{1,0:T(8,128)(2,1)S(1)} %collective-permute-done.2), channel_id=1, source_target_pairs={{0,4},{4,8},{8,12},{12,0},{1,5},{5,9},{9,13},{13,1},{2,6},{6,10},{... | collective-permute-start | bytes 1572872 | tf_op jit(solution)/shard_map/ppermute | solution.py:36
  56.8 13.8 %collective-permute-start.7 = (bf16[128,2048]{1,0:T(8,128)(2,1)S(1)}, bf16[128,2048]{1,0:T(8,128)(2,1)S(1)}, u32[]{:S(2)}, u32[]{:S(2)}) collective-permute-start(bf16[128,2048]{1,0:T(8,128)(2,1)S(1)} %collective-permute-done.2), channel_id=1, source_target_pairs={{0,2},{2,0},{1,3},{3,1},{4,6},{6,4},{5,7},{7,5},{8,10},{10,8},{9,1... | collective-permute-start | bytes 1572872 | tf_op jit(solution)/shard_map/ppermute | solution.py:31
  57.1 13.5 %collective-permute-start.8 = (bf16[256,512]{1,0:T(8,128)(2,1)S(1)}, bf16[256,512]{1,0:T(8,128)(2,1)S(1)}, u32[]{:S(2)}, u32[]{:S(2)}) collective-permute-start(bf16[256,512]{1,0:T(8,128)(2,1)S(1)} %get-tuple-element.235), channel_id=1, source_target_pairs={{0,16},{16,0},{1,17},{17,1},{2,18},{18,2},{3,19},{19,3},{4,20},{20... | collective-permute-start | bytes 786440 | tf_op jit(solution)/shard_map/ppermute | solution.py:31
  70.6 16.3 %collective-permute-start.10 = (bf16[128,2048]{1,0:T(8,128)(2,1)S(1)}, bf16[128,2048]{1,0:T(8,128)(2,1)S(1)}, u32[]{:S(2)}, u32[]{:S(2)}) collective-permute-start(bf16[128,2048]{1,0:T(8,128)(2,1)S(1)} %collective-permute-done.6), channel_id=1, source_target_pairs={{0,2},{2,0},{1,3},{3,1},{4,6},{6,4},{5,7},{7,5},{8,10},{10,8},{9,1... | collective-permute-start | bytes 1572872 | tf_op jit(solution)/shard_map/ppermute | solution.py:31
  71.9 15.0 %collective-permute-start.9 = (bf16[128,2048]{1,0:T(8,128)(2,1)S(1)}, bf16[128,2048]{1,0:T(8,128)(2,1)S(1)}, u32[]{:S(2)}, u32[]{:S(2)}) collective-permute-start(bf16[128,2048]{1,0:T(8,128)(2,1)S(1)} %collective-permute-done.6), channel_id=1, source_target_pairs={{0,4},{4,8},{8,12},{12,0},{1,5},{5,9},{9,13},{13,1},{2,6},{6,10},{... | collective-permute-start | bytes 1572872 | tf_op jit(solution)/shard_map/ppermute | solution.py:36
  73.8 13.1 %collective-permute-start.11 = (bf16[256,512]{1,0:T(8,128)(2,1)S(1)}, bf16[256,512]{1,0:T(8,128)(2,1)S(1)}, u32[]{:S(2)}, u32[]{:S(2)}) collective-permute-start(bf16[256,512]{1,0:T(8,128)(2,1)S(1)} %get-tuple-element.238), channel_id=1, source_target_pairs={{0,16},{16,0},{1,17},{17,1},{2,18},{18,2},{3,19},{19,3},{4,20},{20... | collective-permute-start | bytes 786440 | tf_op jit(solution)/shard_map/ppermute | solution.py:31
  86.9 14.0 %collective-permute-start.12 = (bf16[128,2048]{1,0:T(8,128)(2,1)S(1)}, bf16[128,2048]{1,0:T(8,128)(2,1)S(1)}, u32[]{:S(2)}, u32[]{:S(2)}) collective-permute-start(bf16[128,2048]{1,0:T(8,128)(2,1)S(1)} %collective-permute-done.9), channel_id=1, source_target_pairs={{0,2},{2,0},{1,3},{3,1},{4,6},{6,4},{5,7},{7,5},{8,10},{10,8},{9,1... | collective-permute-start | bytes 1572872 | tf_op jit(solution)/shard_map/ppermute | solution.py:31
  88.1 12.8 %collective-permute-start.13 = (bf16[256,512]{1,0:T(8,128)(2,1)S(1)}, bf16[256,512]{1,0:T(8,128)(2,1)S(1)}, u32[]{:S(2)}, u32[]{:S(2)}) collective-permute-start(bf16[256,512]{1,0:T(8,128)(2,1)S(1)} %get-tuple-element.241), channel_id=1, source_target_pairs={{0,16},{16,0},{1,17},{17,1},{2,18},{18,2},{3,19},{19,3},{4,20},{20... | collective-permute-start | bytes 786440 | tf_op jit(solution)/shard_map/ppermute | solution.py:31
  101.8 14.8 %collective-permute-start.16 = (bf16[1024,2048]{1,0:T(8,128)(2,1)}, bf16[1024,2048]{1,0:T(8,128)(2,1)}, u32[]{:S(2)}, u32[]{:S(2)}) collective-permute-start(bf16[1024,2048]{1,0:T(8,128)(2,1)} %constant_dynamic-update-slice_fusion.refs_0_.refs_1_.refs_2_), channel_id=1, source_target_pairs={{0,1},{1,0},{2,3},{3,2},{4,5},{5,4},{6,7},{7,6},{8,9},{9,8},{10,11... | collective-permute-start | bytes 12582920 | tf_op jit(solution)/shard_map/ppermute | solution.py:31
  105.9 186.5 %all-gather.8.cloned.1.call-start = ((), (), s32[]{:S(2)}) async-start(), calls=%async_computation.8 | async-start | bytes 9437184 | tf_op jit(solution)/shard_map/all_gather | solution.py:767
  111.2 18.7 %collective-permute-start.14 = (bf16[128,1536]{1,0:T(8,128)(2,1)}, bf16[128,1536]{1,0:T(8,128)(2,1)}, u32[]{:S(2)}, u32[]{:S(2)}) collective-permute-start(bf16[128,1536]{1,0:T(8,128)(2,1)} %fusion.30), channel_id=1, source_target_pairs={{0,4},{4,8},{8,12},{12,0},{1,5},{5,9},{9,13},{13,1},{2,6},{6,10},{... | collective-permute-start | bytes 1179656 | tf_op jit(solution)/shard_map/ppermute | solution.py:36
  112.7 17.2 %collective-permute-start.15 = (bf16[128,1536]{1,0:T(8,128)(2,1)}, bf16[128,1536]{1,0:T(8,128)(2,1)}, u32[]{:S(2)}, u32[]{:S(2)}) collective-permute-start(bf16[128,1536]{1,0:T(8,128)(2,1)} %fusion.30), channel_id=1, source_target_pairs={{0,2},{2,0},{1,3},{3,1},{4,6},{6,4},{5,7},{7,5},{8,10},{10,8},{9,1... | collective-permute-start | bytes 1179656 | tf_op jit(solution)/shard_map/ppermute | solution.py:31
  129.9 15.9 %collective-permute-start.17 = (bf16[128,1536]{1,0:T(8,128)(2,1)}, bf16[128,1536]{1,0:T(8,128)(2,1)S(1)}, u32[]{:S(2)}, u32[]{:S(2)}) collective-permute-start(bf16[128,1536]{1,0:T(8,128)(2,1)} %collective-permute-done.14), channel_id=1, source_target_pairs={{0,4},{4,8},{8,12},{12,0},{1,5},{5,9},{9,13},{13,1},{2,6},{6,10},{... | collective-permute-start | bytes 1179656 | tf_op jit(solution)/shard_map/ppermute | solution.py:36
  132.5 13.3 %collective-permute-start.18 = (bf16[128,1536]{1,0:T(8,128)(2,1)}, bf16[128,1536]{1,0:T(8,128)(2,1)S(1)}, u32[]{:S(2)}, u32[]{:S(2)}) collective-permute-start(bf16[128,1536]{1,0:T(8,128)(2,1)} %collective-permute-done.14), channel_id=1, source_target_pairs={{0,2},{2,0},{1,3},{3,1},{4,6},{6,4},{5,7},{7,5},{8,10},{10,8},{9,1... | collective-permute-start | bytes 1179656 | tf_op jit(solution)/shard_map/ppermute | solution.py:31
  145.8 22.8 %collective-permute-start.21 = (bf16[1024,1664]{1,0:T(8,128)(2,1)}, bf16[1024,1664]{1,0:T(8,128)(2,1)}, u32[]{:S(2)}, u32[]{:S(2)}) collective-permute-start(bf16[1024,1664]{1,0:T(8,128)(2,1)} %get-tuple-element.271), channel_id=1, source_target_pairs={{0,1},{1,0},{2,3},{3,2},{4,5},{5,4},{6,7},{7,6},{8,9},{9,8},{10,11... | collective-permute-start | bytes 10223624 | tf_op jit(solution)/shard_map/ppermute | solution.py:31
  147.0 282.4 %reduce-scatter.4.cloned.1.call-start = ((), (), s32[]{:S(2)}) async-start(), calls=%async_computation.9 | async-start | bytes 9437184 | tf_op jit(solution)/shard_map/reduce_scatter | solution.py:915
  154.0 14.6 %collective-permute-start.19 = (bf16[128,1536]{1,0:T(8,128)(2,1)S(1)}, bf16[128,1536]{1,0:T(8,128)(2,1)S(1)}, u32[]{:S(2)}, u32[]{:S(2)}) collective-permute-start(bf16[128,1536]{1,0:T(8,128)(2,1)S(1)} %collective-permute-done.17), channel_id=1, source_target_pairs={{0,4},{4,8},{8,12},{12,0},{1,5},{5,9},{9,13},{13,1},{2,6},{6,10},{... | collective-permute-start | bytes 1179656 | tf_op jit(solution)/shard_map/ppermute | solution.py:36
  154.3 14.3 %collective-permute-start.20 = (bf16[128,1536]{1,0:T(8,128)(2,1)S(1)}, bf16[128,1536]{1,0:T(8,128)(2,1)S(1)}, u32[]{:S(2)}, u32[]{:S(2)}) collective-permute-start(bf16[128,1536]{1,0:T(8,128)(2,1)S(1)} %collective-permute-done.17), channel_id=1, source_target_pairs={{0,2},{2,0},{1,3},{3,1},{4,6},{6,4},{5,7},{7,5},{8,10},{10,8},{9,1... | collective-permute-start | bytes 1179656 | tf_op jit(solution)/shard_map/ppermute | solution.py:31
  175.3 17.3 %collective-permute-start.24 = (bf16[128,1664]{1,0:T(8,128)(2,1)S(1)}, bf16[128,1664]{1,0:T(8,128)(2,1)S(1)}, u32[]{:S(2)}, u32[]{:S(2)}) collective-permute-start(bf16[128,1664]{1,0:T(8,128)(2,1)S(1)} %slice.543), channel_id=1, source_target_pairs={{0,2},{2,0},{1,3},{3,1},{4,6},{6,4},{5,7},{7,5},{8,10},{10,8},{9,1... | collective-permute-start | bytes 1277960 | tf_op jit(solution)/shard_map/ppermute | solution.py:31
  184.5 16.5 %collective-permute-start.31 = (bf16[128,1536]{1,0:T(8,128)(2,1)S(1)}, bf16[128,1536]{1,0:T(8,128)(2,1)S(1)}, u32[]{:S(2)}, u32[]{:S(2)}) collective-permute-start(bf16[128,1536]{1,0:T(8,128)(2,1)S(1)} %collective-permute-done.19), channel_id=1, source_target_pairs={{0,2},{2,0},{1,3},{3,1},{4,6},{6,4},{5,7},{7,5},{8,10},{10,8},{9,1... | collective-permute-start | bytes 1179656 | tf_op jit(solution)/shard_map/ppermute | solution.py:31
  185.5 24.6 %collective-permute-start.26 = (bf16[128,1664]{1,0:T(8,128)(2,1)S(1)}, bf16[128,1664]{1,0:T(8,128)(2,1)S(1)}, u32[]{:S(2)}, u32[]{:S(2)}) collective-permute-start(bf16[128,1664]{1,0:T(8,128)(2,1)S(1)} %slice.546), channel_id=1, source_target_pairs={{0,2},{2,0},{1,3},{3,1},{4,6},{6,4},{5,7},{7,5},{8,10},{10,8},{9,1... | collective-permute-start | bytes 1277960 | tf_op jit(solution)/shard_map/ppermute | solution.py:31
  192.9 17.2 %collective-permute-start.25 = (bf16[128,1664]{1,0:T(8,128)(2,1)S(1)}, bf16[128,1664]{1,0:T(8,128)(2,1)S(1)}, u32[]{:S(2)}, u32[]{:S(2)}) collective-permute-start(bf16[128,1664]{1,0:T(8,128)(2,1)S(1)} %add_convert_fusion.19), channel_id=1, source_target_pairs={{0,4},{4,8},{8,12},{12,0},{1,5},{5,9},{9,13},{13,1},{2,6},{6,10},{... | collective-permute-start | bytes 1277960 | tf_op jit(solution)/shard_map/ppermute | solution.py:36
  201.8 32.0 %collective-permute-start.34 = (bf16[1024,1536]{1,0:T(8,128)(2,1)}, bf16[1024,1536]{1,0:T(8,128)(2,1)}, u32[]{:S(2)}, u32[]{:S(2)}) collective-permute-start(bf16[1024,1536]{1,0:T(8,128)(2,1)} %constant_dynamic-update-slice_fusion.11.refs_2_), channel_id=1, source_target_pairs={{0,1},{1,0},{2,3},{3,2},{4,5},{5,4},{6,7},{7,6},{8,9},{9,8},{10,11... | collective-permute-start | bytes 9437192 | tf_op jit(solution)/shard_map/ppermute | solution.py:31
  204.1 15.0 %collective-permute-start.28 = (bf16[128,1664]{1,0:T(8,128)(2,1)S(1)}, bf16[128,1664]{1,0:T(8,128)(2,1)S(1)}, u32[]{:S(2)}, u32[]{:S(2)}) collective-permute-start(bf16[128,1664]{1,0:T(8,128)(2,1)S(1)} %slice.549), channel_id=1, source_target_pairs={{0,2},{2,0},{1,3},{3,1},{4,6},{6,4},{5,7},{7,5},{8,10},{10,8},{9,1... | collective-permute-start | bytes 1277960 | tf_op jit(solution)/shard_map/ppermute | solution.py:31
  258.8 13.0 %collective-permute-start.38 = (bf16[1024,1536]{1,0:T(8,128)(2,1)S(1)}, bf16[1024,1536]{1,0:T(8,128)(2,1)S(1)}, u32[]{:S(2)}, u32[]{:S(2)}) collective-permute-start(bf16[1024,1536]{1,0:T(8,128)(2,1)S(1)} %constant_dynamic-update-slice_fusion.19.refs_2_), channel_id=1, source_target_pairs={{0,1},{1,0},{2,3},{3,2},{4,5},{5,4},{6,7},{7,6},{8,9},{9,8},{10,11... | collective-permute-start | bytes 9437192 | tf_op jit(solution)/shard_map/ppermute | solution.py:31
  319.9 304.7 %reduce-scatter.6.cloned.1.call-start = ((), (), s32[]{:S(2)}) async-start(), calls=%async_computation.10 | async-start | bytes 9437184 | tf_op jit(solution)/shard_map/reduce_scatter | solution.py:915
  346.5 16.0 %collective-permute-start.42 = (bf16[128,1536]{1,0:T(8,128)(2,1)S(1)}, bf16[128,1536]{1,0:T(8,128)(2,1)}, u32[]{:S(2)}, u32[]{:S(2)}) collective-permute-start(bf16[128,1536]{1,0:T(8,128)(2,1)S(1)} %slice.570), channel_id=1, source_target_pairs={{0,2},{2,0},{1,3},{3,1},{4,6},{6,4},{5,7},{7,5},{8,10},{10,8},{9,1... | collective-permute-start | bytes 1179656 | tf_op jit(solution)/shard_map/ppermute | solution.py:31
  347.8 19.7 %collective-permute-start.44 = (bf16[128,1536]{1,0:T(8,128)(2,1)S(1)}, bf16[128,1536]{1,0:T(8,128)(2,1)}, u32[]{:S(2)}, u32[]{:S(2)}) collective-permute-start(bf16[128,1536]{1,0:T(8,128)(2,1)S(1)} %slice.574), channel_id=1, source_target_pairs={{0,2},{2,0},{1,3},{3,1},{4,6},{6,4},{5,7},{7,5},{8,10},{10,8},{9,1... | collective-permute-start | bytes 1179656 | tf_op jit(solution)/shard_map/ppermute | solution.py:31
  376.3 248.3 %reduce-scatter.8.cloned.1.call-start = ((), (), s32[]{:S(2)}) async-start(), calls=%async_computation.11 | async-start | bytes 9437184 | tf_op jit(solution)/shard_map/reduce_scatter | solution.py:915
  397.8 13.5 %collective-permute-start.49 = (bf16[128,1664]{1,0:T(8,128)(2,1)S(1)}, bf16[128,1664]{1,0:T(8,128)(2,1)S(1)}, u32[]{:S(2)}, u32[]{:S(2)}) collective-permute-start(bf16[128,1664]{1,0:T(8,128)(2,1)S(1)} %collective-permute-done.47), channel_id=1, source_target_pairs={{0,4},{4,8},{8,12},{12,0},{1,5},{5,9},{9,13},{13,1},{2,6},{6,10},{... | collective-permute-start | bytes 1277960 | tf_op jit(solution)/shard_map/ppermute | solution.py:36
  397.8 13.5 %collective-permute-start.50 = (bf16[128,1664]{1,0:T(8,128)(2,1)S(1)}, bf16[128,1664]{1,0:T(8,128)(2,1)S(1)}, u32[]{:S(2)}, u32[]{:S(2)}) collective-permute-start(bf16[128,1664]{1,0:T(8,128)(2,1)S(1)} %collective-permute-done.47), channel_id=1, source_target_pairs={{0,2},{2,0},{1,3},{3,1},{4,6},{6,4},{5,7},{7,5},{8,10},{10,8},{9,1... | collective-permute-start | bytes 1277960 | tf_op jit(solution)/shard_map/ppermute | solution.py:31
  400.0 41.2 %collective-permute-start.55 = (bf16[1024,1536]{1,0:T(8,128)(2,1)}, bf16[1024,1536]{1,0:T(8,128)(2,1)}, u32[]{:S(2)}, u32[]{:S(2)}) collective-permute-start(bf16[1024,1536]{1,0:T(8,128)(2,1)} %combine.6), channel_id=1, source_target_pairs={{0,1},{1,0},{2,3},{3,2},{4,5},{5,4},{6,7},{7,6},{8,9},{9,8},{10,11... | collective-permute-start | bytes 9437192 | tf_op jit(solution)/shard_map/ppermute | solution.py:31
  411.3 15.7 %collective-permute-start.51 = (bf16[128,1664]{1,0:T(8,128)(2,1)S(1)}, bf16[128,1664]{1,0:T(8,128)(2,1)S(1)}, u32[]{:S(2)}, u32[]{:S(2)}) collective-permute-start(bf16[128,1664]{1,0:T(8,128)(2,1)S(1)} %collective-permute-done.49), channel_id=1, source_target_pairs={{0,4},{4,8},{8,12},{12,0},{1,5},{5,9},{9,13},{13,1},{2,6},{6,10},{... | collective-permute-start | bytes 1277960 | tf_op jit(solution)/shard_map/ppermute | solution.py:36
  415.1 11.9 %collective-permute-start.52 = (bf16[128,1664]{1,0:T(8,128)(2,1)S(1)}, bf16[128,1664]{1,0:T(8,128)(2,1)S(1)}, u32[]{:S(2)}, u32[]{:S(2)}) collective-permute-start(bf16[128,1664]{1,0:T(8,128)(2,1)S(1)} %collective-permute-done.49), channel_id=1, source_target_pairs={{0,2},{2,0},{1,3},{3,1},{4,6},{6,4},{5,7},{7,5},{8,10},{10,8},{9,1... | collective-permute-start | bytes 1277960 | tf_op jit(solution)/shard_map/ppermute | solution.py:31
  453.2 14.1 %collective-permute-start.56 = (bf16[128,1536]{1,0:T(8,128)(2,1)S(1)}, bf16[128,1536]{1,0:T(8,128)(2,1)S(1)}, u32[]{:S(2)}, u32[]{:S(2)}) collective-permute-start(bf16[128,1536]{1,0:T(8,128)(2,1)S(1)} %slice_bitcast_fusion.3), channel_id=1, source_target_pairs={{0,2},{2,0},{1,3},{3,1},{4,6},{6,4},{5,7},{7,5},{8,10},{10,8},{9,1... | collective-permute-start | bytes 1179656 | tf_op jit(solution)/shard_map/ppermute | solution.py:31
  454.1 18.6 %collective-permute-start.57 = (bf16[128,1536]{1,0:T(8,128)(2,1)S(1)}, bf16[128,1536]{1,0:T(8,128)(2,1)S(1)}, u32[]{:S(2)}, u32[]{:S(2)}) collective-permute-start(bf16[128,1536]{1,0:T(8,128)(2,1)S(1)} %slice_bitcast_fusion.2), channel_id=1, source_target_pairs={{0,2},{2,0},{1,3},{3,1},{4,6},{6,4},{5,7},{7,5},{8,10},{10,8},{9,1... | collective-permute-start | bytes 1179656 | tf_op jit(solution)/shard_map/ppermute | solution.py:31
  472.8 13.8 %collective-permute-start.58 = (bf16[128,1536]{1,0:T(8,128)(2,1)S(1)}, bf16[128,1536]{1,0:T(8,128)(2,1)S(1)}, u32[]{:S(2)}, u32[]{:S(2)}) collective-permute-start(bf16[128,1536]{1,0:T(8,128)(2,1)S(1)} %fusion.40), channel_id=1, source_target_pairs={{0,4},{4,8},{8,12},{12,0},{1,5},{5,9},{9,13},{13,1},{2,6},{6,10},{... | collective-permute-start | bytes 1179656 | tf_op jit(solution)/shard_map/ppermute | solution.py:36
  474.2 13.3 %collective-permute-start.59 = (bf16[128,1536]{1,0:T(8,128)(2,1)S(1)}, bf16[128,1536]{1,0:T(8,128)(2,1)S(1)}, u32[]{:S(2)}, u32[]{:S(2)}) collective-permute-start(bf16[128,1536]{1,0:T(8,128)(2,1)S(1)} %slice_bitcast_fusion.1), channel_id=1, source_target_pairs={{0,2},{2,0},{1,3},{3,1},{4,6},{6,4},{5,7},{7,5},{8,10},{10,8},{9,1... | collective-permute-start | bytes 1179656 | tf_op jit(solution)/shard_map/ppermute | solution.py:31
  488.2 18.5 %collective-permute-start.60 = (bf16[1024,1536]{1,0:T(8,128)(2,1)}, bf16[1024,1536]{1,0:T(8,128)(2,1)}, u32[]{:S(2)}, u32[]{:S(2)}) collective-permute-start(bf16[1024,1536]{1,0:T(8,128)(2,1)} %get-tuple-element.368), channel_id=1, source_target_pairs={{0,1},{1,0},{2,3},{3,2},{4,5},{5,4},{6,7},{7,6},{8,9},{9,8},{10,11... | collective-permute-start | bytes 9437192 | tf_op jit(solution)/shard_map/ppermute | solution.py:31
  490.9 41.8 %collective-permute-start.75 = (bf16[768,128]{0,1:T(8,128)(2,1)S(1)}, bf16[768,128]{0,1:T(8,128)(2,1)S(1)}, u32[]{:S(2)}, u32[]{:S(2)}) collective-permute-start(bf16[768,128]{0,1:T(8,128)(2,1)S(1)} %dynamic-slice_convert_fusion), channel_id=1, source_target_pairs={{0,16},{16,0},{1,17},{17,1},{2,18},{18,2},{3,19},{19,3},{4,20},{20... | collective-permute-start | bytes 589832 | tf_op jit(solution)/shard_map/ppermute | solution.py:31
  492.5 126.1 %collective-permute-start.77 = (bf16[1,32,1536]{2,1,0:T(8,128)(2,1)}, bf16[1,32,1536]{2,1,0:T(8,128)(2,1)}, u32[]{:S(2)}, u32[]{:S(2)}) collective-permute-start(bf16[1,32,1536]{2,1,0:T(8,128)(2,1)} %dynamic-slice_convert_fusion.1), channel_id=1, source_target_pairs={{0,16},{16,0},{1,17},{17,1},{2,18},{18,2},{3,19},{19,3},{4,20},{20... | collective-permute-start | bytes 294920 | tf_op jit(solution)/shard_map/ppermute | solution.py:31
  493.1 13.4 %collective-permute-start.61 = (bf16[128,1536]{1,0:T(8,128)(2,1)}, bf16[128,1536]{1,0:T(8,128)(2,1)S(1)}, u32[]{:S(2)}, u32[]{:S(2)}) collective-permute-start(bf16[128,1536]{1,0:T(8,128)(2,1)} %fusion.39), channel_id=1, source_target_pairs={{0,4},{4,8},{8,12},{12,0},{1,5},{5,9},{9,13},{13,1},{2,6},{6,10},{... | collective-permute-start | bytes 1179656 | tf_op jit(solution)/shard_map/ppermute | solution.py:36
  493.4 13.3 %collective-permute-start.62 = (bf16[128,1536]{1,0:T(8,128)(2,1)S(1)}, bf16[128,1536]{1,0:T(8,128)(2,1)S(1)}, u32[]{:S(2)}, u32[]{:S(2)}) collective-permute-start(bf16[128,1536]{1,0:T(8,128)(2,1)S(1)} %slice_bitcast_fusion), channel_id=1, source_target_pairs={{0,2},{2,0},{1,3},{3,1},{4,6},{6,4},{5,7},{7,5},{8,10},{10,8},{9,1... | collective-permute-start | bytes 1179656 | tf_op jit(solution)/shard_map/ppermute | solution.py:31
  506.7 13.2 %collective-permute-start.63 = (bf16[128,1536]{1,0:T(8,128)(2,1)S(1)}, bf16[128,1536]{1,0:T(8,128)(2,1)S(1)}, u32[]{:S(2)}, u32[]{:S(2)}) collective-permute-start(bf16[128,1536]{1,0:T(8,128)(2,1)S(1)} %fusion.37), channel_id=1, source_target_pairs={{0,4},{4,8},{8,12},{12,0},{1,5},{5,9},{9,13},{13,1},{2,6},{6,10},{... | collective-permute-start | bytes 1179656 | tf_op jit(solution)/shard_map/ppermute | solution.py:36
  507.0 31.8 %collective-permute-start.65 = (bf16[192,1536]{1,0:T(8,128)(2,1)}, bf16[192,1536]{1,0:T(8,128)(2,1)}, u32[]{:S(2)}, u32[]{:S(2)}) collective-permute-start(bf16[192,1536]{1,0:T(8,128)(2,1)} %fusion.51), channel_id=1, source_target_pairs={{0,16},{16,0},{1,17},{17,1},{2,18},{18,2},{3,19},{19,3},{4,20},{20... | collective-permute-start | bytes 1769480 | tf_op jit(solution)/shard_map/ppermute | solution.py:31
  527.0 22.3 %collective-permute-start.67 = (bf16[128,1536]{1,0:T(8,128)(2,1)}, bf16[128,1536]{1,0:T(8,128)(2,1)}, u32[]{:S(2)}, u32[]{:S(2)}) collective-permute-start(bf16[128,1536]{1,0:T(8,128)(2,1)} %slice.590), channel_id=1, source_target_pairs={{0,2},{2,0},{1,3},{3,1},{4,6},{6,4},{5,7},{7,5},{8,10},{10,8},{9,1... | collective-permute-start | bytes 1179656 | tf_op jit(solution)/shard_map/ppermute | solution.py:31
  532.7 41.8 %collective-permute-start.70 = (bf16[128,1536]{1,0:T(8,128)(2,1)}, bf16[128,1536]{1,0:T(8,128)(2,1)}, u32[]{:S(2)}, u32[]{:S(2)}) collective-permute-start(bf16[128,1536]{1,0:T(8,128)(2,1)} %slice.592), channel_id=1, source_target_pairs={{0,2},{2,0},{1,3},{3,1},{4,6},{6,4},{5,7},{7,5},{8,10},{10,8},{9,1... | collective-permute-start | bytes 1179656 | tf_op jit(solution)/shard_map/ppermute | solution.py:31
  536.7 69.0 %collective-permute-start.73 = (bf16[128,1536]{1,0:T(8,128)(2,1)}, bf16[128,1536]{1,0:T(8,128)(2,1)}, u32[]{:S(2)}, u32[]{:S(2)}) collective-permute-start(bf16[128,1536]{1,0:T(8,128)(2,1)} %slice.597), channel_id=1, source_target_pairs={{0,2},{2,0},{1,3},{3,1},{4,6},{6,4},{5,7},{7,5},{8,10},{10,8},{9,1... | collective-permute-start | bytes 1179656 | tf_op jit(solution)/shard_map/ppermute | solution.py:31
  538.8 11.4 %collective-permute-start.66 = (bf16[128,1536]{1,0:T(8,128)(2,1)S(1)}, bf16[128,1536]{1,0:T(8,128)(2,1)S(1)}, u32[]{:S(2)}, u32[]{:S(2)}) collective-permute-start(bf16[128,1536]{1,0:T(8,128)(2,1)S(1)} %add_convert_fusion.23), channel_id=1, source_target_pairs={{0,4},{4,8},{8,12},{12,0},{1,5},{5,9},{9,13},{13,1},{2,6},{6,10},{... | collective-permute-start | bytes 1179656 | tf_op jit(solution)/shard_map/ppermute | solution.py:36
  549.3 18.6 %collective-permute-start.68 = (bf16[256,768]{1,0:T(8,128)(2,1)S(1)}, bf16[256,768]{1,0:T(8,128)(2,1)S(1)}, u32[]{:S(2)}, u32[]{:S(2)}) collective-permute-start(bf16[256,768]{1,0:T(8,128)(2,1)S(1)} %get-tuple-element.396), channel_id=1, source_target_pairs={{0,16},{16,0},{1,17},{17,1},{2,18},{18,2},{3,19},{19,3},{4,20},{20... | collective-permute-start | bytes 1179656 | tf_op jit(solution)/shard_map/ppermute | solution.py:31
  572.4 18.4 %collective-permute-start.71 = (bf16[256,768]{1,0:T(8,128)(2,1)}, bf16[256,768]{1,0:T(8,128)(2,1)S(1)}, u32[]{:S(2)}, u32[]{:S(2)}) collective-permute-start(bf16[256,768]{1,0:T(8,128)(2,1)} %get-tuple-element.400), channel_id=1, source_target_pairs={{0,16},{16,0},{1,17},{17,1},{2,18},{18,2},{3,19},{19,3},{4,20},{20... | collective-permute-start | bytes 1179656 | tf_op jit(solution)/shard_map/ppermute | solution.py:31
  591.5 14.2 %collective-permute-start.72 = (bf16[128,1536]{1,0:T(8,128)(2,1)}, bf16[128,1536]{1,0:T(8,128)(2,1)}, u32[]{:S(2)}, u32[]{:S(2)}) collective-permute-start(bf16[128,1536]{1,0:T(8,128)(2,1)} %add_convert_fusion.21), channel_id=1, source_target_pairs={{0,4},{4,8},{8,12},{12,0},{1,5},{5,9},{9,13},{13,1},{2,6},{6,10},{... | collective-permute-start | bytes 1179656 | tf_op jit(solution)/shard_map/ppermute | solution.py:36
  595.4 11.6 %collective-permute-start.74 = (bf16[256,768]{1,0:T(8,128)(2,1)}, bf16[256,768]{1,0:T(8,128)(2,1)}, u32[]{:S(2)}, u32[]{:S(2)}) collective-permute-start(bf16[256,768]{1,0:T(8,128)(2,1)} %get-tuple-element.418), channel_id=1, source_target_pairs={{0,16},{16,0},{1,17},{17,1},{2,18},{18,2},{3,19},{19,3},{4,20},{20... | collective-permute-start | bytes 1179656 | tf_op jit(solution)/shard_map/ppermute | solution.py:31
  596.5 14.7 %all-to-all-start.2 = ((f32[32,1,712]{2,1,0:T(1,128)}), f32[32,1,712]{2,1,0:T(1,128)}, u32[]{:S(2)}, u32[]{:S(2)}) async-start(f32[32,1,712]{2,1,0:T(1,128)} %copy.210), calls=%async_computation.3 | async-start | bytes 196608 | tf_op jit(solution)/shard_map/all_to_all | solution.py:1116
  611.1 39.1 %all-to-all-start.1 = ((bf16[16,48,896]{2,1,0:T(8,128)(2,1)}), bf16[16,48,896]{2,1,0:T(8,128)(2,1)}, u32[]{:S(2)}, u32[]{:S(2)}) async-start(bf16[16,48,896]{2,1,0:T(8,128)(2,1)} %bitcast.57), calls=%async_computation.2 | async-start | bytes 2752512 | tf_op jit(solution)/shard_map/all_to_all | solution.py:1073
  (108 other events, 982.9 us)
Sparse Core Ops, SparseCore 0:
  28.4 99.3 all-gather.3
  129.3 81.0 all-gather.5
  211.9 80.3 all-gather.7
  320.0 77.0 reduce-scatter.3
  399.9 77.0 reduce-scatter.5
  490.1 108.3 reduce-scatter.7

commit v5 on v4

--- a/solution.py
+++ b/solution.py
@@ -72,6 +72,14 @@
         block = following
     own = jnp.concatenate(blocks, axis=0)
     return own, swap(own, "core"), beside_work
+
+
+def to_channels(value):
+    return lax.ppermute(value, ("dp", "core"), [(0, 2), (3, 1)])
+
+
+def from_channels(value):
+    return lax.ppermute(value, ("dp", "core"), [(2, 0), (1, 3)])
 
 
 def add_low(left, right):
@@ -723,7 +731,7 @@
             [jnp.where(core == 0, out_proj, both), jnp.where(core == 0, both, out_proj)]
         )
         payload, both = tie(payload, both)
-        w_out = jnp.where(lax.axis_index("dp") == core, both, swap(both, "dp"))
+        w_out = jnp.where(lax.axis_index("dp") == core, both, to_channels(both))
     else:
         w_out = lax.dynamic_slice_in_dim(
             lax.all_gather(out_proj, ALL, axis=0, tiled=True), first_channel, own, 0
@@ -781,6 +789,7 @@
         return entry[:, width + EXTRA :].reshape(half, tokens, -1)[:, : replicas * rows_in]
 
     spread = jnp.concatenate([blocks_of(near), blocks_of(mate)], axis=0)[order]
+    spread, w_gate = tie(spread, w_gate)
     spread = spread.reshape(groups, replicas, rows_in, -1).transpose(1, 0, 2, 3)
     spread = spread.reshape(devices, rows_in, -1)
     small_at = 2 * STATE + HEADS
@@ -851,8 +860,8 @@
     def forward(part):
         return lambda token: mixer_forward(after(part, token), width, tokens, *after(mixer, token))
 
-    branch_near, branch_mate, ((mixer_set, w_gate), done_mate, done_near, _) = gather(
-        branch, [(mixer, w_gate), forward(mate), forward(near)]
+    branch_near, branch_mate, (mixer_set, done_mate, done_near, _) = gather(
+        branch, [mixer, forward(mate), forward(near)]
     )
     _, w_in, w_out, conv, head = mixer_set
     normed_mate, proj_mate, mixed_mate, scaled_mate = done_mate
@@ -993,10 +1002,10 @@
     part_two, moved, out_total, out_there, out_pairs, d_mixer_near = window(
         part_two, moved, out_total, out_there, out_pairs, d_mixer_near
     )
-    out_rows_there = swap(after(out_rows_low, part_two[0]), "dp") if replicas == 2 else ()
+    out_rows_there = from_channels(after(out_rows_low, part_two[0])) if replicas == 2 else ()
     done_near = backward(d_mixer_near, near, proj_near, 1, part_two[:2])
     branch_sum = ring_step(out_total, out_pairs, out_there, 3)
-    done_near, branch_sum = window(done_near, branch_sum)
+    done_near, branch_sum, grad_gate = window(done_near, branch_sum, grad_gate)
     grad_shared_gu = dp_scatter_rows(grad_shared_gu, 0, done_near[0])
     grad_shared_down = dp_scatter_rows(grad_shared_down.reshape(replicas, unit, width), 0, done_near[0])[0]
     normed_grad_mate, proj_low_mate = done_mate[:2]
@@ -1053,13 +1062,14 @@
         total, input_grad(1 - here, pairs_sum).astype(bf16), out_rows_there
     )
     finished = []
-    for index, work in enumerate((lambda token: input_grad(here, token), small_work, lambda token: ())):
+    works = (lambda token: input_grad(here, token), small_work, lambda token: grad_up)
+    for index, work in enumerate(works):
         following = ring_step(total, pairs_sum, there, index + 1)
         across = piece(leaving, index, total) if crossing else ()
         total, across, result = tie(following, across, work(total))
         pieces.append(across)
         finished.append(result)
-    grad_w_in, sums, _ = finished
+    grad_w_in, sums, grad_up = finished
     grad_normed = total
     output = (resid + live * branch_sum).astype(bf16)
 

time: 672 us -> 663 us (0.987)
  waiting for transfers between devices: 198 us -> 189 us
    ppermute x54 -> x52, waiting for transfers between devices: 128 us -> 113 us  [swap(): return lax.ppermute(value, axis, [(0, 1), (1, 0)])]
    ppermute x0 -> x2, waiting for transfers between devices: none -> 7.47 us  [the longest x1 7.46 us: to_channels(): return lax.ppermute(value, ('dp', 'core'), [(0, 2), (3, 1)])]
    ppermute x54 -> x52, starting transfers between devices: 56.2 us -> 51.9 us  [swap(): return lax.ppermute(value, axis, [(0, 1), (1, 0)])]
    unnamed x198 -> x196, local copies, waits for them, and re-layouts: 28.3 us -> 28.8 us
  transfers between devices with their start and end apart: 87 -> 87, of which waited for: 34 -> 32; matrix products, arithmetic and copies ran while one was open for 27% -> 28% of each run, Pallas kernels for 18% -> 18%
where the time goes in v5:
time: 663 us; the launch traced here: 653 us
  waiting for transfers between devices  189 us (29%)
  Pallas kernels  144 us (22%)
  starting transfers between devices  103 us (16%)
  other arithmetic  78.5 us (12%)
  local copies, waits for them, and re-layouts  75.6 us (11%)
  matrix products  46.3 us (7%)
  between operations  16.2 us (2%)
    ppermute x52, waiting for transfers between devices, swap(): return lax.ppermute(value, axis, [(0, 1), (1, 0)])  113 us
    ppermute x52, starting transfers between devices, swap(): return lax.ppermute(value, axis, [(0, 1), (1, 0)])  51.9 us
    pallas_call x4, Pallas kernels, mixer_backward(): pl.pallas_call(lambda *refs: mixer_backward_kernel(count, *refs), grid=(1...  46.7 us
    dot_general x16, matrix products, matmul(): lax.dot_general(left, right, dims, precision=precision, preferred_element...  46.3 us
    ppermute x24, waiting for transfers between devices, ring(): return lax.ppermute(value, 'z', [(k, (k + 1) % size) for k in range(size)])  40.6 us
    unnamed x196, local copies, waits for them, and re-layouts  28.8 us
    pallas_call x2, Pallas kernels, mixer_forward(): pl.pallas_call(lambda *refs: mixer_forward_kernel(count, *refs), grid=(to...  26.6 us
    pallas_call x4, Pallas kernels, combine(): pl.pallas_call(lambda *refs: combine_kernel(experts, slots, len(terms), t...  23.8 us
  transfers between devices with their start and end apart: 87, of which 32 were waited for; matrix products, arithmetic and copies ran while one was open for 28% of the time, Pallas kernels for 18%

profile of v5, /device:TPU:13, one launch (start us, length us, event | category | flops | bytes accessed | tf_op | source)
XLA Modules:
  0.0 652.9 jit_solution(16773339112796141681)
XLA Ops:
  8.2 2.8 concatenate.86
  19.7 6.3 all-to-all-start
  31.5 7.5 %collective-permute-done.4 = bf16[192,1536]{1,0:T(8,128)(2,1)S(1)} collective-permute-done((bf16[192,1536]{1,0:T(8,128)(2,1)S(1)}, bf16[192,1536]{1,0:T(8,128)(2,1)S(1)}, u32[]{:S(2)}, u32[]{:S(2)}) %collective-permute-start.4) | collective-permute-done | bytes 589856 | tf_op jit(solution)/shard_map/ppermute | solution.py:78
  39.0 15.4 %collective-permute-done.2 = bf16[128,2048]{1,0:T(8,128)(2,1)S(1)} collective-permute-done((bf16[128,2048]{1,0:T(8,128)(2,1)S(1)}, bf16[128,2048]{1,0:T(8,128)(2,1)S(1)}, u32[]{:S(2)}, u32[]{:S(2)}) %collective-permute-start.2) | collective-permute-done | bytes 524320 | tf_op jit(solution)/shard_map/ppermute | solution.py:36
  59.2 11.4 %collective-permute-done.8 = bf16[256,512]{1,0:T(8,128)(2,1)S(1)} collective-permute-done((bf16[256,512]{1,0:T(8,128)(2,1)S(1)}, bf16[256,512]{1,0:T(8,128)(2,1)S(1)}, u32[]{:S(2)}, u32[]{:S(2)}) %collective-permute-start.8) | collective-permute-done | bytes 262176 | tf_op jit(solution)/shard_map/ppermute | solution.py:31
  76.7 10.2 %collective-permute-done.11 = bf16[256,512]{1,0:T(8,128)(2,1)S(1)} collective-permute-done((bf16[256,512]{1,0:T(8,128)(2,1)S(1)}, bf16[256,512]{1,0:T(8,128)(2,1)S(1)}, u32[]{:S(2)}, u32[]{:S(2)}) %collective-permute-start.11) | collective-permute-done | bytes 262176 | tf_op jit(solution)/shard_map/ppermute | solution.py:31
  91.1 9.8 %collective-permute-done.13 = bf16[256,512]{1,0:T(8,128)(2,1)S(1)} collective-permute-done((bf16[256,512]{1,0:T(8,128)(2,1)S(1)}, bf16[256,512]{1,0:T(8,128)(2,1)S(1)}, u32[]{:S(2)}, u32[]{:S(2)}) %collective-permute-start.13) | collective-permute-done | bytes 262176 | tf_op jit(solution)/shard_map/ppermute | solution.py:31
  101.8 4.1 collective-permute-start.16
  119.0 7.2 %all-gather.4.cloned.1.call-done.gate_ref = bf16[4,1536,512]{2,1,0:T(8,128)(2,1)} async-done(((bf16[4,768,512]{2,1,0:T(8,128)(2,1)}), bf16[4,1536,512]{2,1,0:T(8,128)(2,1)}) %all-gather.4.cloned.1.call-update) | async-done | bytes 6291472 | tf_op jit(solution)/shard_map/all_gather | solution.py:775
  131.3 4.6 concatenate.97.refs_3_.refs_4_
  138.9 13.5 %mixer_forward.2 = (bf16[1024,1536]{1,0:T(8,128)(2,1)}, f32[1024,768]{1,0:T(8,128)}, bf16[1024,1664]{1,0:T(8,128)(2,1)}, bf16[1024,256]{1,0:T(8,128)(2,1)}) custom-call(bf16[1024,2048]{1,0:T(8,128)(2,1)} %collective-permute-done.16.refs_0_.refs_1_.refs_2_, bf16[1024,2048]{1,0:T(8,128)(2,1)} %collective-permute-done.16.refs_0_.refs_1_.refs_2_, ...), custom_call_target="tpu_custom_call" | custom-call | flops 14080000000 | bytes 44800000 | tf_op jit(solution)/shard_map/mixer_forward/pallas_call | solution.py:277
  163.3 13.1 %mixer_forward.3 = (bf16[1024,1536]{1,0:T(8,128)(2,1)}, f32[1024,768]{1,0:T(8,128)}, bf16[1024,1664]{1,0:T(8,128)(2,1)}, bf16[1024,256]{1,0:T(8,128)(2,1)}) custom-call(bf16[1024,2048]{1,0:T(8,128)(2,1)} %constant_dynamic-update-slice_fusion.refs_0_.refs_1_.refs_2_, bf16[1024,2048]{1,0:T(8,128)(2,1)} %constant_dynamic-update-slice_fusion.refs_0_.refs_1_.refs_2_, ...), custom_call_target="tpu_custom_call" | custom-call | flops 14080000000 | bytes 44800000 | tf_op jit(solution)/shard_map/mixer_forward/pallas_call | solution.py:277
  176.4 3.7 add_convert_fusion.5
  184.4 6.8 %collective-permute-done.22 = bf16[128,1664]{1,0:T(8,128)(2,1)S(1)} collective-permute-done((bf16[128,1664]{1,0:T(8,128)(2,1)S(1)}, bf16[128,1664]{1,0:T(8,128)(2,1)S(1)}, u32[]{:S(2)}, u32[]{:S(2)}) %collective-permute-start.22) | collective-permute-done | bytes 426016 | tf_op jit(solution)/shard_map/ppermute | solution.py:31
  194.6 5.7 collective-permute-done.24
  201.9 6.7 %collective-permute-done.31 = bf16[128,1536]{1,0:T(8,128)(2,1)S(1)} collective-permute-done((bf16[128,1536]{1,0:T(8,128)(2,1)S(1)}, bf16[128,1536]{1,0:T(8,128)(2,1)S(1)}, u32[]{:S(2)}, u32[]{:S(2)}) %collective-permute-start.31) | collective-permute-done | bytes 393248 | tf_op jit(solution)/shard_map/ppermute | solution.py:31
  212.2 5.6 collective-permute-done.26
  219.9 7.1 %collective-permute-done.28 = bf16[128,1664]{1,0:T(8,128)(2,1)S(1)} collective-permute-done((bf16[128,1664]{1,0:T(8,128)(2,1)S(1)}, bf16[128,1664]{1,0:T(8,128)(2,1)S(1)}, u32[]{:S(2)}, u32[]{:S(2)}) %collective-permute-start.28) | collective-permute-done | bytes 426016 | tf_op jit(solution)/shard_map/ppermute | solution.py:31
  229.6 5.3 dispatch.4
  238.0 5.3 dispatch.5
  247.7 6.6 %collective-permute-done.35 = bf16[128,1536]{1,0:T(8,128)(2,1)S(1)} collective-permute-done((bf16[128,1536]{1,0:T(8,128)(2,1)S(1)}, bf16[128,1536]{1,0:T(8,128)(2,1)S(1)}, u32[]{:S(2)}, u32[]{:S(2)}) %collective-permute-start.35) | collective-permute-done | bytes 393248 | tf_op jit(solution)/shard_map/ppermute | solution.py:36
  254.7 10.6 %collective-permute-done.37 = bf16[128,1536]{1,0:T(8,128)(2,1)S(1)} collective-permute-done((bf16[128,1536]{1,0:T(8,128)(2,1)S(1)}, bf16[128,1536]{1,0:T(8,128)(2,1)S(1)}, u32[]{:S(2)}, u32[]{:S(2)}) %collective-permute-start.37) | collective-permute-done | bytes 393248 | tf_op jit(solution)/shard_map/ppermute | solution.py:31
  265.4 7.8 %collective-permute-start.38 = (bf16[1024,1536]{1,0:T(8,128)(2,1)S(1)}, bf16[1024,1536]{1,0:T(8,128)(2,1)S(1)}, u32[]{:S(2)}, u32[]{:S(2)}) collective-permute-start(bf16[1024,1536]{1,0:T(8,128)(2,1)S(1)} %constant_dynamic-update-slice_fusion.19.refs_2_), channel_id=1, source_target_pairs={{0,1},{1,0},{2,3},{3,2},{4,5},{5,4},{6,7},{7,6},{8,9},{9,8},{10,11... | collective-permute-start | bytes 9437192 | tf_op jit(solution)/shard_map/ppermute | solution.py:31
  273.2 6.2 dispatch.6
  281.0 6.3 dispatch.7
  287.3 2.9 all-gather.8.cloned.1.call-done.down_ref
  290.1 20.6 %expert_pass.1 = (bf16[4,384,512]{2,1,0:T(8,128)(2,1)}, bf16[4,384,512]{2,1,0:T(8,128)(2,1)}, bf16[4,384,512]{2,1,0:T(8,128)(2,1)}, bf16[4,384,1536]{2,1,0:T(8,128)(2,1)}, bf16[4,384,1536]{2,1,0:T(8,128)(2,1)}) custom-call(bf16[4,384,1536]{2,1,0:T(8,128)(2,1)} %get-tuple-element.313.rows_ref, bf16[4,384,1536]{2,1,0:T(8,128)(2,1)} %get-tuple-element.300.grad_ref, ...), custom_call_target="tpu_custom_call" | custom-call | flops 22000001024 | bytes 70000000 | tf_op jit(solution)/shard_map/expert_pass/pallas_call | solution.py:560
  310.8 6.8 %convolution_convert_fusion.2 = bf16[4,512,1536]{2,1,0:T(8,128)(2,1)} fusion(bf16[4,384,512]{2,1,0:T(8,128)(2,1)} %get-tuple-element.305, bf16[4,384,1536]{2,1,0:T(8,128)(2,1)S(1)} %bitcast.137), kind=kOutput, calls=%fused_computation.3 | convolution fusion | flops 2419064832 | bytes 12582912 | tf_op jit(solution)/shard_map/dot_general | solution.py:27
  317.8 6.2 combine.5
  324.7 6.4 combine.4
  331.1 4.7 add_convert_fusion.17
  337.0 5.4 convolution_convert_fusion.1
  342.4 5.1 collective-permute-done.40
  353.3 9.0 %convolution_convert_fusion = bf16[4,1536,512]{2,1,0:T(8,128)(2,1)} fusion(bf16[4,384,1536]{2,1,0:T(8,128)(2,1)} %get-tuple-element.313.rows_ref, bf16[4,384,512]{2,1,0:T(8,128)(2,1)} %get-tuple-element.314), kind=kOutput, calls=%fused_computation.1 | convolution fusion | flops 2419064832 | bytes 12582912 | tf_op jit(solution)/shard_map/dot_general | solution.py:27
  365.4 3.5 collective-permute-done.44
  368.9 3.8 collective-permute-done.43
  377.4 5.6 collective-permute-done.45
  388.3 5.1 combine.6
  396.5 5.6 collective-permute-start.55
  403.6 6.0 combine.7
  409.7 4.1 collective-permute-start.51
  422.7 2.9 convolution_add_fusion.2
  427.8 5.5 convert_element_type.757
  433.3 3.5 collective-permute-done.53
  440.0 4.1 add_convert_fusion.10
  444.1 2.9 fusion.2
  447.1 3.5 fusion
  454.3 11.7 %mixer_backward.4 = (bf16[1024,1536]{1,0:T(8,128)(2,1)}, bf16[1024,768]{1,0:T(8,128)(2,1)}, f32[8,512]{1,0:T(8,128)}, f32[24,128]{1,0:T(8,128)}) custom-call(bf16[1024,1664]{1,0:T(8,128)(2,1)} %collective-permute-done.54.refs_0_.refs_1_, bf16[1024,1664]{1,0:T(8,128)(2,1)} %collective-permute-done.54.refs_0_.refs_1_, ...), custom_call_target="tpu_custom_call" | custom-call | flops 11000000512 | bytes 35000000 | tf_op jit(solution)/shard_map/mixer_backward/pallas_call | solution.py:388
  466.0 5.4 collective-permute-done.57
  473.3 11.6 %mixer_backward.5 = (bf16[1024,1536]{1,0:T(8,128)(2,1)}, bf16[1024,768]{1,0:T(8,128)(2,1)}, f32[8,512]{1,0:T(8,128)}, f32[24,128]{1,0:T(8,128)}) custom-call(bf16[1024,1664]{1,0:T(8,128)(2,1)} %collective-permute-done.54.refs_0_.refs_1_, bf16[1024,1664]{1,0:T(8,128)(2,1)} %collective-permute-done.54.refs_0_.refs_1_, ...), custom_call_target="tpu_custom_call", output_to_operand_aliasing={{0}: (9, {}), {1}: (10, {})} | custom-call | flops 11000000512 | bytes 35000000 | tf_op jit(solution)/shard_map/mixer_backward/pallas_call | solution.py:388
  493.1 11.5 %mixer_backward.6 = (bf16[1024,1536]{1,0:T(8,128)(2,1)}, bf16[1024,768]{1,0:T(8,128)(2,1)}, f32[8,512]{1,0:T(8,128)}, f32[24,128]{1,0:T(8,128)}) custom-call(bf16[1024,1664]{1,0:T(8,128)(2,1)} %constant_dynamic-update-slice_fusion.27.refs_0_.refs_1_, bf16[1024,1664]{1,0:T(8,128)(2,1)} %constant_dynamic-update-slice_fusion.27.refs_0_.refs_1_, ...), custom_call_target="tpu_custom_call" | custom-call | flops 11000000512 | bytes 35000000 | tf_op jit(solution)/shard_map/mixer_backward/pallas_call | solution.py:388
  504.9 3.4 collective-permute-start.65
  508.3 11.9 %mixer_backward.7 = (bf16[1024,1536]{1,0:T(8,128)(2,1)}, bf16[1024,768]{1,0:T(8,128)(2,1)}, f32[8,512]{1,0:T(8,128)}, f32[24,128]{1,0:T(8,128)}) custom-call(bf16[1024,1664]{1,0:T(8,128)(2,1)} %constant_dynamic-update-slice_fusion.27.refs_0_.refs_1_, ...), custom_call_target="tpu_custom_call", output_to_operand_aliasing={{0}: (9, {}), {1}: (10, {})} | custom-call | flops 11000000512 | bytes 35000000 | tf_op jit(solution)/shard_map/mixer_backward/pallas_call | solution.py:388
  521.2 4.0 add_convert_fusion.9
  545.0 3.0 fusion.6
  548.1 2.9 fusion.12
  553.3 16.6 %collective-permute-done.68 = bf16[256,768]{1,0:T(8,128)(2,1)S(1)} collective-permute-done((bf16[256,768]{1,0:T(8,128)(2,1)S(1)}, bf16[256,768]{1,0:T(8,128)(2,1)S(1)}, u32[]{:S(2)}, u32[]{:S(2)}) %collective-permute-start.68) | collective-permute-done | bytes 393248 | tf_op jit(solution)/shard_map/ppermute | solution.py:31
  580.0 3.0 collective-permute-done.71
  586.7 9.9 %all-to-all-start.2 = ((f32[32,1,712]{2,1,0:T(1,128)}), f32[32,1,712]{2,1,0:T(1,128)}, u32[]{:S(2)}, u32[]{:S(2)}) async-start(f32[32,1,712]{2,1,0:T(1,128)} %copy.210), calls=%async_computation.5 | async-start | bytes 196608 | tf_op jit(solution)/shard_map/all_to_all | solution.py:1126
  602.3 6.7 %all-to-all-start.1 = ((bf16[16,48,896]{2,1,0:T(8,128)(2,1)}), bf16[16,48,896]{2,1,0:T(8,128)(2,1)}, u32[]{:S(2)}, u32[]{:S(2)}) async-start(bf16[16,48,896]{2,1,0:T(8,128)(2,1)} %bitcast.57), calls=%async_computation.4 | async-start | bytes 2752512 | tf_op jit(solution)/shard_map/all_to_all | solution.py:1083
  615.4 5.6 convert_element_type.834
  621.1 3.6 convert_element_type.835
  626.3 14.8 %all-to-all-done.1.refs_0_ = bf16[16,48,896]{2,1,0:T(8,128)(2,1)} async-done(((bf16[16,48,896]{2,1,0:T(8,128)(2,1)}), bf16[16,48,896]{2,1,0:T(8,128)(2,1)}, u32[]{:S(2)}, u32[]{:S(2)}) %all-to-all-start.1) | async-done | bytes 1376288 | tf_op jit(solution)/shard_map/all_to_all | solution.py:1083
  641.1 3.2 unpack.1
  (552 shorter events, 195.1 us)
Async XLA Ops:
  11.9 15.7 %collective-permute-start = (bf16[1,48,384]{2,1,0:T(8,128)(2,1)S(1)}, bf16[1,48,384]{2,1,0:T(8,128)(2,1)S(1)}, u32[]{:S(2)}, u32[]{:S(2)}) collective-permute-start(bf16[1,48,384]{2,1,0:T(8,128)(2,1)S(1)} %fusion.62), channel_id=1, source_target_pairs={{0,16},{16,0},{1,17},{17,1},{2,18},{18,2},{3,19},{19,3},{4,20},{20... | collective-permute-start | bytes 110600 | tf_op jit(solution)/shard_map/ppermute | solution.py:31
  13.1 14.6 %collective-permute-start.1 = (bf16[96,1536]{1,0:T(8,128)(2,1)}, bf16[96,1536]{1,0:T(8,128)(2,1)S(1)}, u32[]{:S(2)}, u32[]{:S(2)}) collective-permute-start(bf16[96,1536]{1,0:T(8,128)(2,1)} %param.27), channel_id=1, source_target_pairs={{0,1},{1,0},{2,3},{3,2},{4,5},{5,4},{6,7},{7,6},{8,9},{9,8},{10,11... | collective-permute-start | bytes 884744 | tf_op jit(solution)/shard_map/ppermute | solution.py:31
  14.1 15.1 %collective-permute-start.5 = (bf16[1,32,1536]{2,1,0:T(8,128)(2,1)}, bf16[1,32,1536]{2,1,0:T(8,128)(2,1)S(1)}, u32[]{:S(2)}, u32[]{:S(2)}) collective-permute-start(bf16[1,32,1536]{2,1,0:T(8,128)(2,1)} %bitcast.174), channel_id=1, source_target_pairs={{0,16},{16,0},{1,17},{17,1},{2,18},{18,2},{3,19},{19,3},{4,20},{20... | collective-permute-start | bytes 294920 | tf_op jit(solution)/shard_map/ppermute | solution.py:31
  19.7 37.2 %all-to-all-start = ((bf16[16,48,512]{2,1,0:T(8,128)(2,1)}), bf16[16,48,512]{2,1,0:T(8,128)(2,1)S(1)}, u32[]{:S(2)}, u32[]{:S(2)}) async-start(bf16[16,48,512]{2,1,0:T(8,128)(2,1)} %pad_maximum_fusion.2), calls=%async_computation | async-start | bytes 1572864 | tf_op jit(solution)/shard_map/all_to_all | solution.py:726
  26.0 100.2 %all-gather.4.cloned.1.call-start = ((), (), s32[]{:S(2)}) async-start(), calls=%async_computation.6 | async-start | bytes 9437184 | tf_op jit(solution)/shard_map/all_gather | solution.py:775
  26.7 191.2 %all-gather.6.cloned.1.call-start = ((), (), s32[]{:S(2)}) async-start(), calls=%async_computation.7 | async-start | bytes 9437184 | tf_op jit(solution)/shard_map/all_gather | solution.py:775
  29.2 25.2 %collective-permute-start.2 = (bf16[128,2048]{1,0:T(8,128)(2,1)S(1)}, bf16[128,2048]{1,0:T(8,128)(2,1)S(1)}, u32[]{:S(2)}, u32[]{:S(2)}) collective-permute-start(bf16[128,2048]{1,0:T(8,128)(2,1)S(1)} %fusion.46), channel_id=1, source_target_pairs={{0,4},{4,8},{8,12},{12,0},{1,5},{5,9},{9,13},{13,1},{2,6},{6,10},{... | collective-permute-start | bytes 1572872 | tf_op jit(solution)/shard_map/ppermute | solution.py:36
  30.5 23.9 %collective-permute-start.3 = (bf16[128,2048]{1,0:T(8,128)(2,1)S(1)}, bf16[128,2048]{1,0:T(8,128)(2,1)}, u32[]{:S(2)}, u32[]{:S(2)}) collective-permute-start(bf16[128,2048]{1,0:T(8,128)(2,1)S(1)} %fusion.46), channel_id=1, source_target_pairs={{0,2},{2,0},{1,3},{3,1},{4,6},{6,4},{5,7},{7,5},{8,10},{10,8},{9,1... | collective-permute-start | bytes 1572872 | tf_op jit(solution)/shard_map/ppermute | solution.py:31
  56.8 13.8 %collective-permute-start.6 = (bf16[128,2048]{1,0:T(8,128)(2,1)S(1)}, bf16[128,2048]{1,0:T(8,128)(2,1)S(1)}, u32[]{:S(2)}, u32[]{:S(2)}) collective-permute-start(bf16[128,2048]{1,0:T(8,128)(2,1)S(1)} %collective-permute-done.2), channel_id=1, source_target_pairs={{0,4},{4,8},{8,12},{12,0},{1,5},{5,9},{9,13},{13,1},{2,6},{6,10},{... | collective-permute-start | bytes 1572872 | tf_op jit(solution)/shard_map/ppermute | solution.py:36
  56.8 13.8 %collective-permute-start.7 = (bf16[128,2048]{1,0:T(8,128)(2,1)S(1)}, bf16[128,2048]{1,0:T(8,128)(2,1)S(1)}, u32[]{:S(2)}, u32[]{:S(2)}) collective-permute-start(bf16[128,2048]{1,0:T(8,128)(2,1)S(1)} %collective-permute-done.2), channel_id=1, source_target_pairs={{0,2},{2,0},{1,3},{3,1},{4,6},{6,4},{5,7},{7,5},{8,10},{10,8},{9,1... | collective-permute-start | bytes 1572872 | tf_op jit(solution)/shard_map/ppermute | solution.py:31
  57.1 13.5 %collective-permute-start.8 = (bf16[256,512]{1,0:T(8,128)(2,1)S(1)}, bf16[256,512]{1,0:T(8,128)(2,1)S(1)}, u32[]{:S(2)}, u32[]{:S(2)}) collective-permute-start(bf16[256,512]{1,0:T(8,128)(2,1)S(1)} %get-tuple-element.238), channel_id=1, source_target_pairs={{0,16},{16,0},{1,17},{17,1},{2,18},{18,2},{3,19},{19,3},{4,20},{20... | collective-permute-start | bytes 786440 | tf_op jit(solution)/shard_map/ppermute | solution.py:31
  70.6 16.3 %collective-permute-start.10 = (bf16[128,2048]{1,0:T(8,128)(2,1)S(1)}, bf16[128,2048]{1,0:T(8,128)(2,1)S(1)}, u32[]{:S(2)}, u32[]{:S(2)}) collective-permute-start(bf16[128,2048]{1,0:T(8,128)(2,1)S(1)} %collective-permute-done.6), channel_id=1, source_target_pairs={{0,2},{2,0},{1,3},{3,1},{4,6},{6,4},{5,7},{7,5},{8,10},{10,8},{9,1... | collective-permute-start | bytes 1572872 | tf_op jit(solution)/shard_map/ppermute | solution.py:31
  71.9 15.0 %collective-permute-start.9 = (bf16[128,2048]{1,0:T(8,128)(2,1)S(1)}, bf16[128,2048]{1,0:T(8,128)(2,1)S(1)}, u32[]{:S(2)}, u32[]{:S(2)}) collective-permute-start(bf16[128,2048]{1,0:T(8,128)(2,1)S(1)} %collective-permute-done.6), channel_id=1, source_target_pairs={{0,4},{4,8},{8,12},{12,0},{1,5},{5,9},{9,13},{13,1},{2,6},{6,10},{... | collective-permute-start | bytes 1572872 | tf_op jit(solution)/shard_map/ppermute | solution.py:36
  73.8 13.1 %collective-permute-start.11 = (bf16[256,512]{1,0:T(8,128)(2,1)S(1)}, bf16[256,512]{1,0:T(8,128)(2,1)S(1)}, u32[]{:S(2)}, u32[]{:S(2)}) collective-permute-start(bf16[256,512]{1,0:T(8,128)(2,1)S(1)} %get-tuple-element.241), channel_id=1, source_target_pairs={{0,16},{16,0},{1,17},{17,1},{2,18},{18,2},{3,19},{19,3},{4,20},{20... | collective-permute-start | bytes 786440 | tf_op jit(solution)/shard_map/ppermute | solution.py:31
  86.9 14.0 %collective-permute-start.12 = (bf16[128,2048]{1,0:T(8,128)(2,1)S(1)}, bf16[128,2048]{1,0:T(8,128)(2,1)S(1)}, u32[]{:S(2)}, u32[]{:S(2)}) collective-permute-start(bf16[128,2048]{1,0:T(8,128)(2,1)S(1)} %collective-permute-done.9), channel_id=1, source_target_pairs={{0,2},{2,0},{1,3},{3,1},{4,6},{6,4},{5,7},{7,5},{8,10},{10,8},{9,1... | collective-permute-start | bytes 1572872 | tf_op jit(solution)/shard_map/ppermute | solution.py:31
  88.1 12.8 %collective-permute-start.13 = (bf16[256,512]{1,0:T(8,128)(2,1)S(1)}, bf16[256,512]{1,0:T(8,128)(2,1)S(1)}, u32[]{:S(2)}, u32[]{:S(2)}) collective-permute-start(bf16[256,512]{1,0:T(8,128)(2,1)S(1)} %get-tuple-element.244), channel_id=1, source_target_pairs={{0,16},{16,0},{1,17},{17,1},{2,18},{18,2},{3,19},{19,3},{4,20},{20... | collective-permute-start | bytes 786440 | tf_op jit(solution)/shard_map/ppermute | solution.py:31
  101.8 14.9 %collective-permute-start.16 = (bf16[1024,2048]{1,0:T(8,128)(2,1)}, bf16[1024,2048]{1,0:T(8,128)(2,1)}, u32[]{:S(2)}, u32[]{:S(2)}) collective-permute-start(bf16[1024,2048]{1,0:T(8,128)(2,1)} %constant_dynamic-update-slice_fusion.refs_0_.refs_1_.refs_2_), channel_id=1, source_target_pairs={{0,1},{1,0},{2,3},{3,2},{4,5},{5,4},{6,7},{7,6},{8,9},{9,8},{10,11... | collective-permute-start | bytes 12582920 | tf_op jit(solution)/shard_map/ppermute | solution.py:31
  105.9 184.2 %all-gather.8.cloned.1.call-start = ((), (), s32[]{:S(2)}) async-start(), calls=%async_computation.8 | async-start | bytes 9437184 | tf_op jit(solution)/shard_map/all_gather | solution.py:775
  111.3 26.0 %collective-permute-start.14 = (bf16[128,1536]{1,0:T(8,128)(2,1)}, bf16[128,1536]{1,0:T(8,128)(2,1)}, u32[]{:S(2)}, u32[]{:S(2)}) collective-permute-start(bf16[128,1536]{1,0:T(8,128)(2,1)} %fusion.30), channel_id=1, source_target_pairs={{0,4},{4,8},{8,12},{12,0},{1,5},{5,9},{9,13},{13,1},{2,6},{6,10},{... | collective-permute-start | bytes 1179656 | tf_op jit(solution)/shard_map/ppermute | solution.py:36
  112.8 24.5 %collective-permute-start.15 = (bf16[128,1536]{1,0:T(8,128)(2,1)}, bf16[128,1536]{1,0:T(8,128)(2,1)}, u32[]{:S(2)}, u32[]{:S(2)}) collective-permute-start(bf16[128,1536]{1,0:T(8,128)(2,1)} %fusion.30), channel_id=1, source_target_pairs={{0,2},{2,0},{1,3},{3,1},{4,6},{6,4},{5,7},{7,5},{8,10},{10,8},{9,1... | collective-permute-start | bytes 1179656 | tf_op jit(solution)/shard_map/ppermute | solution.py:31
  137.3 15.2 %collective-permute-start.17 = (bf16[128,1536]{1,0:T(8,128)(2,1)}, bf16[128,1536]{1,0:T(8,128)(2,1)S(1)}, u32[]{:S(2)}, u32[]{:S(2)}) collective-permute-start(bf16[128,1536]{1,0:T(8,128)(2,1)} %collective-permute-done.14), channel_id=1, source_target_pairs={{0,4},{4,8},{8,12},{12,0},{1,5},{5,9},{9,13},{13,1},{2,6},{6,10},{... | collective-permute-start | bytes 1179656 | tf_op jit(solution)/shard_map/ppermute | solution.py:36
  138.7 13.8 %collective-permute-start.18 = (bf16[128,1536]{1,0:T(8,128)(2,1)}, bf16[128,1536]{1,0:T(8,128)(2,1)S(1)}, u32[]{:S(2)}, u32[]{:S(2)}) collective-permute-start(bf16[128,1536]{1,0:T(8,128)(2,1)} %collective-permute-done.14), channel_id=1, source_target_pairs={{0,2},{2,0},{1,3},{3,1},{4,6},{6,4},{5,7},{7,5},{8,10},{10,8},{9,1... | collective-permute-start | bytes 1179656 | tf_op jit(solution)/shard_map/ppermute | solution.py:31
  152.5 23.9 %collective-permute-start.21 = (bf16[1024,1664]{1,0:T(8,128)(2,1)}, bf16[1024,1664]{1,0:T(8,128)(2,1)}, u32[]{:S(2)}, u32[]{:S(2)}) collective-permute-start(bf16[1024,1664]{1,0:T(8,128)(2,1)} %get-tuple-element.275), channel_id=1, source_target_pairs={{0,1},{1,0},{2,3},{3,2},{4,5},{5,4},{6,7},{7,6},{8,9},{9,8},{10,11... | collective-permute-start | bytes 10223624 | tf_op jit(solution)/shard_map/ppermute | solution.py:31
  153.8 274.0 %reduce-scatter.4.cloned.1.call-start = ((), (), s32[]{:S(2)}) async-start(), calls=%async_computation.9 | async-start | bytes 9437184 | tf_op jit(solution)/shard_map/reduce_scatter | solution.py:924
  160.8 15.6 %collective-permute-start.19 = (bf16[128,1536]{1,0:T(8,128)(2,1)S(1)}, bf16[128,1536]{1,0:T(8,128)(2,1)S(1)}, u32[]{:S(2)}, u32[]{:S(2)}) collective-permute-start(bf16[128,1536]{1,0:T(8,128)(2,1)S(1)} %collective-permute-done.17), channel_id=1, source_target_pairs={{0,4},{4,8},{8,12},{12,0},{1,5},{5,9},{9,13},{13,1},{2,6},{6,10},{... | collective-permute-start | bytes 1179656 | tf_op jit(solution)/shard_map/ppermute | solution.py:36
  162.0 14.4 %collective-permute-start.20 = (bf16[128,1536]{1,0:T(8,128)(2,1)S(1)}, bf16[128,1536]{1,0:T(8,128)(2,1)S(1)}, u32[]{:S(2)}, u32[]{:S(2)}) collective-permute-start(bf16[128,1536]{1,0:T(8,128)(2,1)S(1)} %collective-permute-done.17), channel_id=1, source_target_pairs={{0,2},{2,0},{1,3},{3,1},{4,6},{6,4},{5,7},{7,5},{8,10},{10,8},{9,1... | collective-permute-start | bytes 1179656 | tf_op jit(solution)/shard_map/ppermute | solution.py:31
  183.0 17.3 %collective-permute-start.24 = (bf16[128,1664]{1,0:T(8,128)(2,1)S(1)}, bf16[128,1664]{1,0:T(8,128)(2,1)S(1)}, u32[]{:S(2)}, u32[]{:S(2)}) collective-permute-start(bf16[128,1664]{1,0:T(8,128)(2,1)S(1)} %slice.543), channel_id=1, source_target_pairs={{0,2},{2,0},{1,3},{3,1},{4,6},{6,4},{5,7},{7,5},{8,10},{10,8},{9,1... | collective-permute-start | bytes 1277960 | tf_op jit(solution)/shard_map/ppermute | solution.py:31
  192.2 16.4 %collective-permute-start.31 = (bf16[128,1536]{1,0:T(8,128)(2,1)S(1)}, bf16[128,1536]{1,0:T(8,128)(2,1)S(1)}, u32[]{:S(2)}, u32[]{:S(2)}) collective-permute-start(bf16[128,1536]{1,0:T(8,128)(2,1)S(1)} %collective-permute-done.19), channel_id=1, source_target_pairs={{0,2},{2,0},{1,3},{3,1},{4,6},{6,4},{5,7},{7,5},{8,10},{10,8},{9,1... | collective-permute-start | bytes 1179656 | tf_op jit(solution)/shard_map/ppermute | solution.py:31
  193.3 24.4 %collective-permute-start.26 = (bf16[128,1664]{1,0:T(8,128)(2,1)S(1)}, bf16[128,1664]{1,0:T(8,128)(2,1)S(1)}, u32[]{:S(2)}, u32[]{:S(2)}) collective-permute-start(bf16[128,1664]{1,0:T(8,128)(2,1)S(1)} %slice.546), channel_id=1, source_target_pairs={{0,2},{2,0},{1,3},{3,1},{4,6},{6,4},{5,7},{7,5},{8,10},{10,8},{9,1... | collective-permute-start | bytes 1277960 | tf_op jit(solution)/shard_map/ppermute | solution.py:31
  200.6 17.2 %collective-permute-start.25 = (bf16[128,1664]{1,0:T(8,128)(2,1)S(1)}, bf16[128,1664]{1,0:T(8,128)(2,1)S(1)}, u32[]{:S(2)}, u32[]{:S(2)}) collective-permute-start(bf16[128,1664]{1,0:T(8,128)(2,1)S(1)} %add_convert_fusion.19), channel_id=1, source_target_pairs={{0,4},{4,8},{8,12},{12,0},{1,5},{5,9},{9,13},{13,1},{2,6},{6,10},{... | collective-permute-start | bytes 1277960 | tf_op jit(solution)/shard_map/ppermute | solution.py:36
  209.4 28.5 %collective-permute-start.34 = (bf16[1024,1536]{1,0:T(8,128)(2,1)}, bf16[1024,1536]{1,0:T(8,128)(2,1)}, u32[]{:S(2)}, u32[]{:S(2)}) collective-permute-start(bf16[1024,1536]{1,0:T(8,128)(2,1)} %constant_dynamic-update-slice_fusion.11.refs_2_), channel_id=1, source_target_pairs={{0,1},{1,0},{2,3},{3,2},{4,5},{5,4},{6,7},{7,6},{8,9},{9,8},{10,11... | collective-permute-start | bytes 9437192 | tf_op jit(solution)/shard_map/ppermute | solution.py:31
  211.9 15.1 %collective-permute-start.28 = (bf16[128,1664]{1,0:T(8,128)(2,1)S(1)}, bf16[128,1664]{1,0:T(8,128)(2,1)S(1)}, u32[]{:S(2)}, u32[]{:S(2)}) collective-permute-start(bf16[128,1664]{1,0:T(8,128)(2,1)S(1)} %slice.549), channel_id=1, source_target_pairs={{0,2},{2,0},{1,3},{3,1},{4,6},{6,4},{5,7},{7,5},{8,10},{10,8},{9,1... | collective-permute-start | bytes 1277960 | tf_op jit(solution)/shard_map/ppermute | solution.py:31
  265.4 14.0 %collective-permute-start.38 = (bf16[1024,1536]{1,0:T(8,128)(2,1)S(1)}, bf16[1024,1536]{1,0:T(8,128)(2,1)S(1)}, u32[]{:S(2)}, u32[]{:S(2)}) collective-permute-start(bf16[1024,1536]{1,0:T(8,128)(2,1)S(1)} %constant_dynamic-update-slice_fusion.19.refs_2_), channel_id=1, source_target_pairs={{0,1},{1,0},{2,3},{3,2},{4,5},{5,4},{6,7},{7,6},{8,9},{9,8},{10,11... | collective-permute-start | bytes 9437192 | tf_op jit(solution)/shard_map/ppermute | solution.py:31
  317.6 203.6 %reduce-scatter.6.cloned.1.call-start = ((), (), s32[]{:S(2)}) async-start(), calls=%async_computation.10 | async-start | bytes 9437184 | tf_op jit(solution)/shard_map/reduce_scatter | solution.py:924
  349.4 248.5 %reduce-scatter.8.cloned.1.call-start = ((), (), s32[]{:S(2)}) async-start(), calls=%async_computation.11 | async-start | bytes 9437184 | tf_op jit(solution)/shard_map/reduce_scatter | solution.py:924
  350.4 11.9 %collective-permute-start.42 = (bf16[128,1536]{1,0:T(8,128)(2,1)S(1)}, bf16[128,1536]{1,0:T(8,128)(2,1)}, u32[]{:S(2)}, u32[]{:S(2)}) collective-permute-start(bf16[128,1536]{1,0:T(8,128)(2,1)S(1)} %slice.570), channel_id=1, source_target_pairs={{0,2},{2,0},{1,3},{3,1},{4,6},{6,4},{5,7},{7,5},{8,10},{10,8},{9,1... | collective-permute-start | bytes 1179656 | tf_op jit(solution)/shard_map/ppermute | solution.py:31
  350.8 18.1 %collective-permute-start.44 = (bf16[128,1536]{1,0:T(8,128)(2,1)S(1)}, bf16[128,1536]{1,0:T(8,128)(2,1)}, u32[]{:S(2)}, u32[]{:S(2)}) collective-permute-start(bf16[128,1536]{1,0:T(8,128)(2,1)S(1)} %slice.574), channel_id=1, source_target_pairs={{0,2},{2,0},{1,3},{3,1},{4,6},{6,4},{5,7},{7,5},{8,10},{10,8},{9,1... | collective-permute-start | bytes 1179656 | tf_op jit(solution)/shard_map/ppermute | solution.py:31
  365.1 12.3 %collective-permute-start.46 = (bf16[128,1536]{1,0:T(8,128)(2,1)S(1)}, bf16[128,1536]{1,0:T(8,128)(2,1)S(1)}, u32[]{:S(2)}, u32[]{:S(2)}) collective-permute-start(bf16[128,1536]{1,0:T(8,128)(2,1)S(1)} %slice.578), channel_id=1, source_target_pairs={{0,2},{2,0},{1,3},{3,1},{4,6},{6,4},{5,7},{7,5},{8,10},{10,8},{9,1... | collective-permute-start | bytes 1179656 | tf_op jit(solution)/shard_map/ppermute | solution.py:31
  396.1 13.6 %collective-permute-start.49 = (bf16[128,1664]{1,0:T(8,128)(2,1)S(1)}, bf16[128,1664]{1,0:T(8,128)(2,1)S(1)}, u32[]{:S(2)}, u32[]{:S(2)}) collective-permute-start(bf16[128,1664]{1,0:T(8,128)(2,1)S(1)} %collective-permute-done.47), channel_id=1, source_target_pairs={{0,4},{4,8},{8,12},{12,0},{1,5},{5,9},{9,13},{13,1},{2,6},{6,10},{... | collective-permute-start | bytes 1277960 | tf_op jit(solution)/shard_map/ppermute | solution.py:36
  396.1 13.6 %collective-permute-start.50 = (bf16[128,1664]{1,0:T(8,128)(2,1)S(1)}, bf16[128,1664]{1,0:T(8,128)(2,1)S(1)}, u32[]{:S(2)}, u32[]{:S(2)}) collective-permute-start(bf16[128,1664]{1,0:T(8,128)(2,1)S(1)} %collective-permute-done.47), channel_id=1, source_target_pairs={{0,2},{2,0},{1,3},{3,1},{4,6},{6,4},{5,7},{7,5},{8,10},{10,8},{9,1... | collective-permute-start | bytes 1277960 | tf_op jit(solution)/shard_map/ppermute | solution.py:31
  396.5 43.5 %collective-permute-start.55 = (bf16[1024,1536]{1,0:T(8,128)(2,1)}, bf16[1024,1536]{1,0:T(8,128)(2,1)}, u32[]{:S(2)}, u32[]{:S(2)}) collective-permute-start(bf16[1024,1536]{1,0:T(8,128)(2,1)} %combine.6), channel_id=1, source_target_pairs={{0,1},{1,0},{2,3},{3,2},{4,5},{5,4},{6,7},{7,6},{8,9},{9,8},{10,11... | collective-permute-start | bytes 9437192 | tf_op jit(solution)/shard_map/ppermute | solution.py:31
  409.7 15.9 %collective-permute-start.51 = (bf16[128,1664]{1,0:T(8,128)(2,1)S(1)}, bf16[128,1664]{1,0:T(8,128)(2,1)S(1)}, u32[]{:S(2)}, u32[]{:S(2)}) collective-permute-start(bf16[128,1664]{1,0:T(8,128)(2,1)S(1)} %collective-permute-done.49), channel_id=1, source_target_pairs={{0,4},{4,8},{8,12},{12,0},{1,5},{5,9},{9,13},{13,1},{2,6},{6,10},{... | collective-permute-start | bytes 1277960 | tf_op jit(solution)/shard_map/ppermute | solution.py:36
  413.8 11.9 %collective-permute-start.52 = (bf16[128,1664]{1,0:T(8,128)(2,1)S(1)}, bf16[128,1664]{1,0:T(8,128)(2,1)S(1)}, u32[]{:S(2)}, u32[]{:S(2)}) collective-permute-start(bf16[128,1664]{1,0:T(8,128)(2,1)S(1)} %collective-permute-done.49), channel_id=1, source_target_pairs={{0,2},{2,0},{1,3},{3,1},{4,6},{6,4},{5,7},{7,5},{8,10},{10,8},{9,1... | collective-permute-start | bytes 1277960 | tf_op jit(solution)/shard_map/ppermute | solution.py:31
  425.6 11.2 %collective-permute-start.53 = (bf16[128,1664]{1,0:T(8,128)(2,1)S(1)}, bf16[128,1664]{1,0:T(8,128)(2,1)S(1)}, u32[]{:S(2)}, u32[]{:S(2)}) collective-permute-start(bf16[128,1664]{1,0:T(8,128)(2,1)S(1)} %collective-permute-done.51), channel_id=1, source_target_pairs={{0,2},{2,0},{1,3},{3,1},{4,6},{6,4},{5,7},{7,5},{8,10},{10,8},{9,1... | collective-permute-start | bytes 1277960 | tf_op jit(solution)/shard_map/ppermute | solution.py:31
  452.0 14.0 %collective-permute-start.56 = (bf16[128,1536]{1,0:T(8,128)(2,1)S(1)}, bf16[128,1536]{1,0:T(8,128)(2,1)S(1)}, u32[]{:S(2)}, u32[]{:S(2)}) collective-permute-start(bf16[128,1536]{1,0:T(8,128)(2,1)S(1)} %slice_bitcast_fusion.3), channel_id=1, source_target_pairs={{0,2},{2,0},{1,3},{3,1},{4,6},{6,4},{5,7},{7,5},{8,10},{10,8},{9,1... | collective-permute-start | bytes 1179656 | tf_op jit(solution)/shard_map/ppermute | solution.py:31
  452.5 18.9 %collective-permute-start.57 = (bf16[128,1536]{1,0:T(8,128)(2,1)S(1)}, bf16[128,1536]{1,0:T(8,128)(2,1)S(1)}, u32[]{:S(2)}, u32[]{:S(2)}) collective-permute-start(bf16[128,1536]{1,0:T(8,128)(2,1)S(1)} %slice_bitcast_fusion.2), channel_id=1, source_target_pairs={{0,2},{2,0},{1,3},{3,1},{4,6},{6,4},{5,7},{7,5},{8,10},{10,8},{9,1... | collective-permute-start | bytes 1179656 | tf_op jit(solution)/shard_map/ppermute | solution.py:31
  471.5 13.4 %collective-permute-start.58 = (bf16[128,1536]{1,0:T(8,128)(2,1)S(1)}, bf16[128,1536]{1,0:T(8,128)(2,1)S(1)}, u32[]{:S(2)}, u32[]{:S(2)}) collective-permute-start(bf16[128,1536]{1,0:T(8,128)(2,1)S(1)} %fusion.40), channel_id=1, source_target_pairs={{0,4},{4,8},{8,12},{12,0},{1,5},{5,9},{9,13},{13,1},{2,6},{6,10},{... | collective-permute-start | bytes 1179656 | tf_op jit(solution)/shard_map/ppermute | solution.py:36
  472.9 12.9 %collective-permute-start.59 = (bf16[128,1536]{1,0:T(8,128)(2,1)S(1)}, bf16[128,1536]{1,0:T(8,128)(2,1)S(1)}, u32[]{:S(2)}, u32[]{:S(2)}) collective-permute-start(bf16[128,1536]{1,0:T(8,128)(2,1)S(1)} %slice_bitcast_fusion.1), channel_id=1, source_target_pairs={{0,2},{2,0},{1,3},{3,1},{4,6},{6,4},{5,7},{7,5},{8,10},{10,8},{9,1... | collective-permute-start | bytes 1179656 | tf_op jit(solution)/shard_map/ppermute | solution.py:31
  486.5 18.3 %collective-permute-start.60 = (bf16[1024,1536]{1,0:T(8,128)(2,1)}, bf16[1024,1536]{1,0:T(8,128)(2,1)}, u32[]{:S(2)}, u32[]{:S(2)}) collective-permute-start(bf16[1024,1536]{1,0:T(8,128)(2,1)} %get-tuple-element.372), channel_id=1, source_target_pairs={{0,1},{1,0},{2,3},{3,2},{4,5},{5,4},{6,7},{7,6},{8,9},{9,8},{10,11... | collective-permute-start | bytes 9437192 | tf_op jit(solution)/shard_map/ppermute | solution.py:31
  489.9 43.8 %collective-permute-start.75 = (bf16[768,128]{0,1:T(8,128)(2,1)}, bf16[768,128]{0,1:T(8,128)(2,1)}, u32[]{:S(2)}, u32[]{:S(2)}) collective-permute-start(bf16[768,128]{0,1:T(8,128)(2,1)} %dynamic-slice_convert_fusion), channel_id=1, source_target_pairs={{0,16},{16,0},{1,17},{17,1},{2,18},{18,2},{3,19},{19,3},{4,20},{20... | collective-permute-start | bytes 589832 | tf_op jit(solution)/shard_map/ppermute | solution.py:31
  490.9 118.5 %collective-permute-start.77 = (bf16[1,32,1536]{2,1,0:T(8,128)(2,1)}, bf16[1,32,1536]{2,1,0:T(8,128)(2,1)}, u32[]{:S(2)}, u32[]{:S(2)}) collective-permute-start(bf16[1,32,1536]{2,1,0:T(8,128)(2,1)} %dynamic-slice_convert_fusion.1), channel_id=1, source_target_pairs={{0,16},{16,0},{1,17},{17,1},{2,18},{18,2},{3,19},{19,3},{4,20},{20... | collective-permute-start | bytes 294920 | tf_op jit(solution)/shard_map/ppermute | solution.py:31
  492.0 12.6 %collective-permute-start.61 = (bf16[128,1536]{1,0:T(8,128)(2,1)}, bf16[128,1536]{1,0:T(8,128)(2,1)S(1)}, u32[]{:S(2)}, u32[]{:S(2)}) collective-permute-start(bf16[128,1536]{1,0:T(8,128)(2,1)} %fusion.39), channel_id=1, source_target_pairs={{0,4},{4,8},{8,12},{12,0},{1,5},{5,9},{9,13},{13,1},{2,6},{6,10},{... | collective-permute-start | bytes 1179656 | tf_op jit(solution)/shard_map/ppermute | solution.py:36
  492.4 12.4 %collective-permute-start.62 = (bf16[128,1536]{1,0:T(8,128)(2,1)S(1)}, bf16[128,1536]{1,0:T(8,128)(2,1)S(1)}, u32[]{:S(2)}, u32[]{:S(2)}) collective-permute-start(bf16[128,1536]{1,0:T(8,128)(2,1)S(1)} %slice_bitcast_fusion), channel_id=1, source_target_pairs={{0,2},{2,0},{1,3},{3,1},{4,6},{6,4},{5,7},{7,5},{8,10},{10,8},{9,1... | collective-permute-start | bytes 1179656 | tf_op jit(solution)/shard_map/ppermute | solution.py:31
  504.8 15.3 %collective-permute-start.63 = (bf16[128,1536]{1,0:T(8,128)(2,1)S(1)}, bf16[128,1536]{1,0:T(8,128)(2,1)S(1)}, u32[]{:S(2)}, u32[]{:S(2)}) collective-permute-start(bf16[128,1536]{1,0:T(8,128)(2,1)S(1)} %fusion.37), channel_id=1, source_target_pairs={{0,4},{4,8},{8,12},{12,0},{1,5},{5,9},{9,13},{13,1},{2,6},{6,10},{... | collective-permute-start | bytes 1179656 | tf_op jit(solution)/shard_map/ppermute | solution.py:36
  504.9 35.7 %collective-permute-start.65 = (bf16[192,1536]{1,0:T(8,128)(2,1)}, bf16[192,1536]{1,0:T(8,128)(2,1)}, u32[]{:S(2)}, u32[]{:S(2)}) collective-permute-start(bf16[192,1536]{1,0:T(8,128)(2,1)} %fusion.51), channel_id=1, source_target_pairs={{16,0},{1,17},{18,2},{3,19},{20,4},{5,21},{22,6},{7,23},{24,8},{9,... | collective-permute-start | bytes 1769480 | tf_op jit(solution)/shard_map/ppermute | solution.py:82
  526.0 12.4 %collective-permute-start.64 = (bf16[128,1536]{1,0:T(8,128)(2,1)}, bf16[128,1536]{1,0:T(8,128)(2,1)}, u32[]{:S(2)}, u32[]{:S(2)}) collective-permute-start(bf16[128,1536]{1,0:T(8,128)(2,1)} %slice.588), channel_id=1, source_target_pairs={{0,2},{2,0},{1,3},{3,1},{4,6},{6,4},{5,7},{7,5},{8,10},{10,8},{9,1... | collective-permute-start | bytes 1179656 | tf_op jit(solution)/shard_map/ppermute | solution.py:31
  528.0 23.1 %collective-permute-start.67 = (bf16[128,1536]{1,0:T(8,128)(2,1)}, bf16[128,1536]{1,0:T(8,128)(2,1)}, u32[]{:S(2)}, u32[]{:S(2)}) collective-permute-start(bf16[128,1536]{1,0:T(8,128)(2,1)} %slice.590), channel_id=1, source_target_pairs={{0,2},{2,0},{1,3},{3,1},{4,6},{6,4},{5,7},{7,5},{8,10},{10,8},{9,1... | collective-permute-start | bytes 1179656 | tf_op jit(solution)/shard_map/ppermute | solution.py:31
  533.7 43.1 %collective-permute-start.70 = (bf16[128,1536]{1,0:T(8,128)(2,1)}, bf16[128,1536]{1,0:T(8,128)(2,1)}, u32[]{:S(2)}, u32[]{:S(2)}) collective-permute-start(bf16[128,1536]{1,0:T(8,128)(2,1)} %slice.592), channel_id=1, source_target_pairs={{0,2},{2,0},{1,3},{3,1},{4,6},{6,4},{5,7},{7,5},{8,10},{10,8},{9,1... | collective-permute-start | bytes 1179656 | tf_op jit(solution)/shard_map/ppermute | solution.py:31
  538.5 58.1 %collective-permute-start.73 = (bf16[128,1536]{1,0:T(8,128)(2,1)}, bf16[128,1536]{1,0:T(8,128)(2,1)}, u32[]{:S(2)}, u32[]{:S(2)}) collective-permute-start(bf16[128,1536]{1,0:T(8,128)(2,1)} %slice.597), channel_id=1, source_target_pairs={{0,2},{2,0},{1,3},{3,1},{4,6},{6,4},{5,7},{7,5},{8,10},{10,8},{9,1... | collective-permute-start | bytes 1179656 | tf_op jit(solution)/shard_map/ppermute | solution.py:31
  551.0 18.8 %collective-permute-start.68 = (bf16[256,768]{1,0:T(8,128)(2,1)S(1)}, bf16[256,768]{1,0:T(8,128)(2,1)S(1)}, u32[]{:S(2)}, u32[]{:S(2)}) collective-permute-start(bf16[256,768]{1,0:T(8,128)(2,1)S(1)} %get-tuple-element.401), channel_id=1, source_target_pairs={{0,16},{16,0},{1,17},{17,1},{2,18},{18,2},{3,19},{19,3},{4,20},{20... | collective-permute-start | bytes 1179656 | tf_op jit(solution)/shard_map/ppermute | solution.py:31
  583.7 12.8 %collective-permute-start.72 = (bf16[128,1536]{1,0:T(8,128)(2,1)}, bf16[128,1536]{1,0:T(8,128)(2,1)}, u32[]{:S(2)}, u32[]{:S(2)}) collective-permute-start(bf16[128,1536]{1,0:T(8,128)(2,1)} %add_convert_fusion.21), channel_id=1, source_target_pairs={{0,4},{4,8},{8,12},{12,0},{1,5},{5,9},{9,13},{13,1},{2,6},{6,10},{... | collective-permute-start | bytes 1179656 | tf_op jit(solution)/shard_map/ppermute | solution.py:36
  585.8 12.0 %collective-permute-start.74 = (bf16[256,768]{1,0:T(8,128)(2,1)}, bf16[256,768]{1,0:T(8,128)(2,1)}, u32[]{:S(2)}, u32[]{:S(2)}) collective-permute-start(bf16[256,768]{1,0:T(8,128)(2,1)} %get-tuple-element.423), channel_id=1, source_target_pairs={{0,16},{16,0},{1,17},{17,1},{2,18},{18,2},{3,19},{19,3},{4,20},{20... | collective-permute-start | bytes 1179656 | tf_op jit(solution)/shard_map/ppermute | solution.py:31
  586.7 15.6 %all-to-all-start.2 = ((f32[32,1,712]{2,1,0:T(1,128)}), f32[32,1,712]{2,1,0:T(1,128)}, u32[]{:S(2)}, u32[]{:S(2)}) async-start(f32[32,1,712]{2,1,0:T(1,128)} %copy.210), calls=%async_computation.5 | async-start | bytes 196608 | tf_op jit(solution)/shard_map/all_to_all | solution.py:1126
  602.3 38.8 %all-to-all-start.1 = ((bf16[16,48,896]{2,1,0:T(8,128)(2,1)}), bf16[16,48,896]{2,1,0:T(8,128)(2,1)}, u32[]{:S(2)}, u32[]{:S(2)}) async-start(bf16[16,48,896]{2,1,0:T(8,128)(2,1)} %bitcast.57), calls=%async_computation.4 | async-start | bytes 2752512 | tf_op jit(solution)/shard_map/all_to_all | solution.py:1083
  (107 other events, 989.0 us)
Sparse Core Ops, SparseCore 0:
  28.4 97.7 all-gather.3
  127.7 80.3 all-gather.5
  209.7 80.3 all-gather.7
  317.7 77.0 reduce-scatter.3
  397.6 77.0 reduce-scatter.5
  477.4 98.1 reduce-scatter.7

commit v6 on v5

--- a/solution.py
+++ b/solution.py
@@ -420,16 +420,19 @@
             values, down_ref[...], (((1,), (1,)), ((), ())), preferred_element_type=f32
         )
     else:
-        act_grad_ref, gate_ref, up_ref = refs[:3]
-        out_ref, act_ref, g_ref, u_ref = refs[-4:]
-        gate = jnp.dot(values, gate_ref[...], preferred_element_type=f32)
-        up = jnp.dot(values, up_ref[...], preferred_element_type=f32)
+        act_grad_ref, weights_in_ref = refs[:2]
+        out_ref, act_ref, gu_ref = refs[-3:]
+        gate = jnp.dot(values, weights_in_ref[...], preferred_element_type=f32)
+        hidden = act_ref.shape[1]
+        up = pltpu.roll(gate, hidden, 1)
         sig = sigmoid(gate)
         silu = gate * sig
         d_act = act_grad_ref[...]
-        act_ref[...] = (silu * up).astype(bf16)
-        g_ref[...] = (d_act * up * (sig * (1.0 + gate * (1.0 - sig)))).astype(bf16)
-        u_ref[...] = (d_act * silu).astype(bf16)
+        act_ref[...] = (silu * up)[:, :hidden].astype(bf16)
+        d_gate = d_act * up * (sig * (1.0 + gate * (1.0 - sig)))
+        d_up = pltpu.roll(d_act * silu, hidden, 1)
+        lane = lax.broadcasted_iota(jnp.int32, (1, 2 * hidden), 1)
+        gu_ref[...] = jnp.where(lane < hidden, d_gate, d_up).astype(bf16)
     for k in range(experts):
         part = rows[k * slots : (k + 1) * slots]
         if grads:
@@ -445,7 +448,7 @@
     count = values.shape[0] // tokens
     width = values.shape[1]
     grads = len(shared) == 1
-    hidden = shared[0].shape[0] if grads else shared[0].shape[1]
+    hidden = shared[0].shape[0] if grads else shared[1].shape[1]
 
     def slots_spec(extent):
         return pl.BlockSpec((experts, slots, extent), lambda step: (0, first + step, 0))
@@ -466,9 +469,9 @@
             jax.ShapeDtypeStruct(small, f32),
         ]
     else:
-        in_specs += [rows_spec(hidden), whole(shared[1]), whole(shared[2])]
-        out_specs += [rows_spec(hidden)] * 3
-        shapes += [jax.ShapeDtypeStruct(small, bf16)] * 3
+        in_specs += [rows_spec(hidden), whole(shared[1])]
+        out_specs += [rows_spec(hidden // 2), rows_spec(hidden)]
+        shapes += [jax.ShapeDtypeStruct((small[0], extent), bf16) for extent in (hidden // 2, hidden)]
     aliases = {}
     into = () if into is None else tuple(into)
     for index, entry in enumerate(into):
@@ -806,8 +809,8 @@
     w_step = jnp.pad(w_step, ((0, 0), (0, EXTRA - heads)))
     w_in = [spread[:, : 2 * STATE], pack[:, own : 2 * own], pack[:, EXTRA:own], pack[:, :EXTRA], w_step]
     w_in = jnp.concatenate(w_in, axis=1)
-    w_shared_gate = pack[:, 2 * own : 2 * own + units]
-    w_shared_up = pack[:, 2 * own + units :]
+    w_shared = pack[:, 2 * own :]
+    w_shared_wide = jnp.pad(w_shared_down, ((0, units), (0, 0)))
 
     def own_channels(rows):
         return lax.dynamic_slice_in_dim(rows, first_channel, own, rows.ndim - 1)
@@ -875,12 +878,12 @@
     ffn_hat = resid * ffn_rms
 
     def grads_near(token):
-        return rows_out(after(branch_near, token), 0, (w_shared_down,))
+        return rows_out(after(branch_near, token), 0, (w_shared_wide,))
 
     done_rows = []
 
     def grads_mate(token):
-        return rows_out(after(branch_mate, token), half_pairs, (w_shared_down,), done_rows[0])
+        return rows_out(after(branch_mate, token), half_pairs, (w_shared_wide,), done_rows[0])
 
     def keep(work):
         def kept(token):
@@ -894,11 +897,9 @@
         (ffn_hat * ffn_gain_all).astype(bf16), [keep(grads_near), grads_mate]
     )
 
-    expert_in, shared_near, sg_near, su_near = rows_out(
-        ffn_near, 0, (act_grad_near, w_shared_gate, w_shared_up)
-    )
-    expert_in, shared_mate, sg_mate, su_mate = rows_out(
-        ffn_mate, half_pairs, (act_grad_mate, w_shared_gate, w_shared_up), (expert_in,)
+    expert_in, shared_near, gu_near = rows_out(ffn_near, 0, (act_grad_near, w_shared))
+    expert_in, shared_mate, gu_mate = rows_out(
+        ffn_mate, half_pairs, (act_grad_mate, w_shared), (expert_in,)
     )
     act_low, g_low, u_low, d_in_row, expert_row = expert_pass(
         expert_in, d_row, slot_weight, w_gate, w_up, w_down
@@ -908,12 +909,11 @@
     grad_down = matmul(act_low, d_row, half_grad).astype(bf16)
     d_in_row, grad_down = tie(d_in_row, grad_down)
 
-    def back_rows(sg, su, first):
-        terms = ((sg, w_shared_gate), (su, w_shared_up))
-        return combine(d_in_row, rank, terms, pair_slots, first, True)
-
-    grad_ffn_mate = back_rows(sg_mate, su_mate, half_pairs)
-    grad_ffn_near = back_rows(sg_near, su_near, 0)
+    def back_rows(gu, first):
+        return combine(d_in_row, rank, ((gu, w_shared),), pair_slots, first, True)
+
+    grad_ffn_mate = back_rows(gu_mate, half_pairs)
+    grad_ffn_near = back_rows(gu_near, 0)
     pairs_sum = scatter_first(grad_ffn_near, grad_ffn_mate)
 
     def leaving_of(part):
@@ -951,8 +951,7 @@
         halves = after(((branch_near, branch_mate), (ffn_near, ffn_mate)), token)
         return (
             of_halves((shared_near, shared_mate), halves[0]),
-            of_halves(halves[1], (sg_near, sg_mate)),
-            of_halves(halves[1], (su_near, su_mate)),
+            of_halves(halves[1], (gu_near, gu_mate)),
         )
 
     d_mixer_near, d_mixer_mate, (out_mate, out_near, shared_grads, grad_down) = gather(
@@ -964,8 +963,7 @@
             lambda token: after(grad_down, token).astype(f32),
         ],
     )
-    grad_shared_down, grad_shared_g, grad_shared_u = shared_grads
-    grad_shared_gu = jnp.concatenate([grad_shared_g, grad_shared_u], axis=1)
+    grad_shared_down, grad_shared_gu = shared_grads
     grad_out_rows = of_halves(
         (scaled_near, scaled_mate), (d_mixer_near[:, :width], d_mixer_mate[:, :width])
     )[:own]
@@ -1047,7 +1045,7 @@
         return of_halves(parts, (proj_low_near, proj_low_mate))
 
     def piece(array, index, token):
-        extent = array.shape[0] // 3
+        extent = array.shape[0] // 2
         return swap(after(array[index * extent : (index + 1) * extent], token), "dp")
 
     pieces = []
@@ -1065,11 +1063,13 @@
     works = (lambda token: input_grad(here, token), small_work, lambda token: grad_up)
     for index, work in enumerate(works):
         following = ring_step(total, pairs_sum, there, index + 1)
-        across = piece(leaving, index, total) if crossing else ()
-        total, across, result = tie(following, across, work(total))
-        pieces.append(across)
+        if crossing and index < 2:
+            pieces.append(piece(leaving, index, total))
+        last = index == len(works) - 1
+        total, arrived, result = tie(following, tuple(pieces) if last else (), work(total))
         finished.append(result)
     grad_w_in, sums, grad_up = finished
+    pieces = list(arrived)
     grad_normed = total
     output = (resid + live * branch_sum).astype(bf16)
 

time: 663 us -> 657 us (level)
  local copies, waits for them, and re-layouts: 75.6 us -> 67.9 us
  starting transfers between devices: 103 us -> 110 us
    ppermute x52 -> x51, waiting for transfers between devices: 113 us -> 95.7 us  [swap(): return lax.ppermute(value, axis, [(0, 1), (1, 0)])]
    reduce_scatter x3, waiting for transfers between devices: 0.02 us -> 10.4 us  [local(): lax.psum_scatter(entry, 'dp', scatter_dimension=1, tiled=True)]
    ppermute x24, waiting for transfers between devices: 40.6 us -> 50 us  [ring(): return lax.ppermute(value, 'z', [(k, (k + 1) % size) for k in range(size)])]
    ppermute x52 -> x51, starting transfers between devices: 51.9 us -> 58.5 us  [swap(): return lax.ppermute(value, axis, [(0, 1), (1, 0)])]
    unnamed x196 -> x165, local copies, waits for them, and re-layouts: 28.8 us -> 24.7 us
    dot_general x16 -> x14, matrix products: 46.3 us -> 47.1 us  [matmul(): lax.dot_general(left, right, dims, precision=precision, preferred_element...]
  transfers between devices with their start and end apart: 87 -> 86, of which waited for: 32 -> 34; matrix products, arithmetic and copies ran while one was open for 28% -> 26% of each run, Pallas kernels for 18% -> 18%
where the time goes in v6:
time: 657 us; the launch traced here: 648 us
  waiting for transfers between devices  193 us (29%)
  Pallas kernels  141 us (21%)
  starting transfers between devices  110 us (17%)
  other arithmetic  72.3 us (11%)
  local copies, waits for them, and re-layouts  67.9 us (10%)
  matrix products  47.1 us (7%)
  between operations  16.2 us (2%)
    ppermute x51, waiting for transfers between devices, swap(): return lax.ppermute(value, axis, [(0, 1), (1, 0)])  95.7 us
    ppermute x51, starting transfers between devices, swap(): return lax.ppermute(value, axis, [(0, 1), (1, 0)])  58.5 us
    ppermute x24, waiting for transfers between devices, ring(): return lax.ppermute(value, 'z', [(k, (k + 1) % size) for k in range(size)])  50 us
    dot_general x14, matrix products, matmul(): lax.dot_general(left, right, dims, precision=precision, preferred_element...  47.1 us
    pallas_call x4, Pallas kernels, mixer_backward(): pl.pallas_call(lambda *refs: mixer_backward_kernel(count, *refs), grid=(1...  46.5 us
    pallas_call x2, Pallas kernels, mixer_forward(): pl.pallas_call(lambda *refs: mixer_forward_kernel(count, *refs), grid=(to...  26.9 us
    unnamed x165, local copies, waits for them, and re-layouts  24.7 us
    ppermute x24, starting transfers between devices, ring(): return lax.ppermute(value, 'z', [(k, (k + 1) % size) for k in range(size)])  23.8 us
  transfers between devices with their start and end apart: 86, of which 34 were waited for; matrix products, arithmetic and copies ran while one was open for 26% of the time, Pallas kernels for 18%

profile of v6, /device:TPU:13, one launch (start us, length us, event | category | flops | bytes accessed | tf_op | source)
XLA Modules:
  0.0 647.6 jit_solution(10423702334124511459)
XLA Ops:
  19.7 6.3 all-to-all-start
  31.5 7.4 %collective-permute-done.4 = bf16[192,1536]{1,0:T(8,128)(2,1)S(1)} collective-permute-done((bf16[192,1536]{1,0:T(8,128)(2,1)S(1)}, bf16[192,1536]{1,0:T(8,128)(2,1)S(1)}, u32[]{:S(2)}, u32[]{:S(2)}) %collective-permute-start.4) | collective-permute-done | bytes 589856 | tf_op jit(solution)/shard_map/ppermute | solution.py:78
  38.9 15.5 %collective-permute-done.2 = bf16[128,2048]{1,0:T(8,128)(2,1)S(1)} collective-permute-done((bf16[128,2048]{1,0:T(8,128)(2,1)S(1)}, bf16[128,2048]{1,0:T(8,128)(2,1)S(1)}, u32[]{:S(2)}, u32[]{:S(2)}) %collective-permute-start.2) | collective-permute-done | bytes 524320 | tf_op jit(solution)/shard_map/ppermute | solution.py:36
  59.2 11.4 %collective-permute-done.8 = bf16[256,512]{1,0:T(8,128)(2,1)S(1)} collective-permute-done((bf16[256,512]{1,0:T(8,128)(2,1)S(1)}, bf16[256,512]{1,0:T(8,128)(2,1)S(1)}, u32[]{:S(2)}, u32[]{:S(2)}) %collective-permute-start.8) | collective-permute-done | bytes 262176 | tf_op jit(solution)/shard_map/ppermute | solution.py:31
  76.3 10.2 %collective-permute-done.11 = bf16[256,512]{1,0:T(8,128)(2,1)S(1)} collective-permute-done((bf16[256,512]{1,0:T(8,128)(2,1)S(1)}, bf16[256,512]{1,0:T(8,128)(2,1)S(1)}, u32[]{:S(2)}, u32[]{:S(2)}) %collective-permute-start.11) | collective-permute-done | bytes 262176 | tf_op jit(solution)/shard_map/ppermute | solution.py:31
  90.6 9.9 %collective-permute-done.13 = bf16[256,512]{1,0:T(8,128)(2,1)S(1)} collective-permute-done((bf16[256,512]{1,0:T(8,128)(2,1)S(1)}, bf16[256,512]{1,0:T(8,128)(2,1)S(1)}, u32[]{:S(2)}, u32[]{:S(2)}) %collective-permute-start.13) | collective-permute-done | bytes 262176 | tf_op jit(solution)/shard_map/ppermute | solution.py:31
  101.3 4.1 collective-permute-start.16
  118.4 7.8 %all-gather.4.cloned.1.call-done.gate_ref = bf16[4,1536,512]{2,1,0:T(8,128)(2,1)} async-done(((bf16[4,768,512]{2,1,0:T(8,128)(2,1)}), bf16[4,1536,512]{2,1,0:T(8,128)(2,1)}) %all-gather.4.cloned.1.call-update) | async-done | bytes 6291472 | tf_op jit(solution)/shard_map/all_gather | solution.py:778
  129.3 4.7 concatenate.94.refs_3_.refs_4_
  137.0 13.8 %mixer_forward.2 = (bf16[1024,1536]{1,0:T(8,128)(2,1)}, f32[1024,768]{1,0:T(8,128)}, bf16[1024,1664]{1,0:T(8,128)(2,1)}, bf16[1024,256]{1,0:T(8,128)(2,1)}) custom-call(bf16[1024,2048]{1,0:T(8,128)(2,1)} %collective-permute-done.16.refs_0_.refs_1_.refs_2_, bf16[1024,2048]{1,0:T(8,128)(2,1)} %collective-permute-done.16.refs_0_.refs_1_.refs_2_, ...), custom_call_target="tpu_custom_call" | custom-call | flops 14080000000 | bytes 44800000 | tf_op jit(solution)/shard_map/mixer_forward/pallas_call | solution.py:277
  162.2 13.1 %mixer_forward.3 = (bf16[1024,1536]{1,0:T(8,128)(2,1)}, f32[1024,768]{1,0:T(8,128)}, bf16[1024,1664]{1,0:T(8,128)(2,1)}, bf16[1024,256]{1,0:T(8,128)(2,1)}) custom-call(bf16[1024,2048]{1,0:T(8,128)(2,1)} %constant_dynamic-update-slice_fusion.refs_0_.refs_1_.refs_2_, bf16[1024,2048]{1,0:T(8,128)(2,1)} %constant_dynamic-update-slice_fusion.refs_0_.refs_1_.refs_2_, ...), custom_call_target="tpu_custom_call" | custom-call | flops 14080000000 | bytes 44800000 | tf_op jit(solution)/shard_map/mixer_forward/pallas_call | solution.py:277
  175.3 3.8 add_convert_fusion.5
  183.3 5.9 collective-permute-done.22
  192.9 5.5 collective-permute-done.24
  200.1 6.7 %collective-permute-done.31 = bf16[128,1536]{1,0:T(8,128)(2,1)S(1)} collective-permute-done((bf16[128,1536]{1,0:T(8,128)(2,1)S(1)}, bf16[128,1536]{1,0:T(8,128)(2,1)S(1)}, u32[]{:S(2)}, u32[]{:S(2)}) %collective-permute-start.31) | collective-permute-done | bytes 393248 | tf_op jit(solution)/shard_map/ppermute | solution.py:31
  207.6 4.1 collective-permute-start.34
  212.9 2.9 collective-permute-done.26
  218.9 6.2 collective-permute-done.28
  227.1 5.4 dispatch.4
  235.2 5.4 dispatch.5
  244.4 9.3 %collective-permute-done.35 = bf16[128,1536]{1,0:T(8,128)(2,1)S(1)} collective-permute-done((bf16[128,1536]{1,0:T(8,128)(2,1)S(1)}, bf16[128,1536]{1,0:T(8,128)(2,1)S(1)}, u32[]{:S(2)}, u32[]{:S(2)}) %collective-permute-start.35) | collective-permute-done | bytes 393248 | tf_op jit(solution)/shard_map/ppermute | solution.py:36
  254.2 7.9 %collective-permute-done.37 = bf16[128,1536]{1,0:T(8,128)(2,1)S(1)} collective-permute-done((bf16[128,1536]{1,0:T(8,128)(2,1)S(1)}, bf16[128,1536]{1,0:T(8,128)(2,1)S(1)}, u32[]{:S(2)}, u32[]{:S(2)}) %collective-permute-start.37) | collective-permute-done | bytes 393248 | tf_op jit(solution)/shard_map/ppermute | solution.py:31
  262.1 11.0 %collective-permute-start.38 = (bf16[1024,1536]{1,0:T(8,128)(2,1)S(1)}, bf16[1024,1536]{1,0:T(8,128)(2,1)}, u32[]{:S(2)}, u32[]{:S(2)}) collective-permute-start(bf16[1024,1536]{1,0:T(8,128)(2,1)S(1)} %constant_dynamic-update-slice_fusion.19.refs_2_), channel_id=1, source_target_pairs={{0,1},{1,0},{2,3},{3,2},{4,5},{5,4},{6,7},{7,6},{8,9},{9,8},{10,11... | collective-permute-start | bytes 9437192 | tf_op jit(solution)/shard_map/ppermute | solution.py:31
  273.1 5.6 dispatch.6
  278.8 5.7 dispatch.7
  284.4 5.7 all-gather.8.cloned.1.call-done.down_ref
  290.1 20.4 %expert_pass.1 = (bf16[4,384,512]{2,1,0:T(8,128)(2,1)}, bf16[4,384,512]{2,1,0:T(8,128)(2,1)}, bf16[4,384,512]{2,1,0:T(8,128)(2,1)}, bf16[4,384,1536]{2,1,0:T(8,128)(2,1)}, bf16[4,384,1536]{2,1,0:T(8,128)(2,1)}) custom-call(bf16[4,384,1536]{2,1,0:T(8,128)(2,1)} %get-tuple-element.306.rows_ref, bf16[4,384,1536]{2,1,0:T(8,128)(2,1)} %get-tuple-element.295.grad_ref, ...), custom_call_target="tpu_custom_call" | custom-call | flops 22000001024 | bytes 70000000 | tf_op jit(solution)/shard_map/expert_pass/pallas_call | solution.py:563
  310.5 9.0 %convolution_convert_fusion.2 = bf16[4,512,1536]{2,1,0:T(8,128)(2,1)} fusion(bf16[4,384,512]{2,1,0:T(8,128)(2,1)} %get-tuple-element.300, bf16[4,384,1536]{2,1,0:T(8,128)(2,1)} %get-tuple-element.295.grad_ref), kind=kOutput, calls=%fused_computation.3 | convolution fusion | flops 2419064832 | bytes 12582912 | tf_op jit(solution)/shard_map/dot_general | solution.py:27
  319.8 5.4 combine.5
  325.9 5.7 combine.4
  331.6 4.7 add_convert_fusion.17
  338.2 5.4 convolution_convert_fusion.1
  343.6 5.0 collective-permute-done.40
  355.8 9.0 %convolution_convert_fusion = bf16[4,1536,512]{2,1,0:T(8,128)(2,1)} fusion(bf16[4,384,1536]{2,1,0:T(8,128)(2,1)} %get-tuple-element.306.rows_ref, bf16[4,384,512]{2,1,0:T(8,128)(2,1)} %get-tuple-element.307), kind=kOutput, calls=%fused_computation.1 | convolution fusion | flops 2419064832 | bytes 12582912 | tf_op jit(solution)/shard_map/dot_general | solution.py:27
  370.6 4.4 collective-permute-done.43
  379.0 5.3 collective-permute-done.45
  388.3 5.1 combine.6
  396.1 6.2 collective-permute-start.55
  403.9 5.4 combine.7
  409.3 4.7 collective-permute-start.51
  418.8 3.0 fusion.87
  429.4 5.5 convert_element_type.759
  439.8 3.7 add_convert_fusion.10
  443.6 3.2 fusion.2
  446.8 3.4 fusion
  454.0 11.7 %mixer_backward.4 = (bf16[1024,1536]{1,0:T(8,128)(2,1)}, bf16[1024,768]{1,0:T(8,128)(2,1)}, f32[8,512]{1,0:T(8,128)}, f32[24,128]{1,0:T(8,128)}) custom-call(bf16[1024,1664]{1,0:T(8,128)(2,1)} %collective-permute-done.54.refs_0_.refs_1_, bf16[1024,1664]{1,0:T(8,128)(2,1)} %collective-permute-done.54.refs_0_.refs_1_, ...), custom_call_target="tpu_custom_call" | custom-call | flops 11000000512 | bytes 35000000 | tf_op jit(solution)/shard_map/mixer_backward/pallas_call | solution.py:388
  465.7 5.2 collective-permute-done.57
  472.8 11.6 %mixer_backward.5 = (bf16[1024,1536]{1,0:T(8,128)(2,1)}, bf16[1024,768]{1,0:T(8,128)(2,1)}, f32[8,512]{1,0:T(8,128)}, f32[24,128]{1,0:T(8,128)}) custom-call(bf16[1024,1664]{1,0:T(8,128)(2,1)} %collective-permute-done.54.refs_0_.refs_1_, bf16[1024,1664]{1,0:T(8,128)(2,1)} %collective-permute-done.54.refs_0_.refs_1_, ...), custom_call_target="tpu_custom_call", output_to_operand_aliasing={{0}: (9, {}), {1}: (10, {})} | custom-call | flops 11000000512 | bytes 35000000 | tf_op jit(solution)/shard_map/mixer_backward/pallas_call | solution.py:388
  494.3 11.5 %mixer_backward.6 = (bf16[1024,1536]{1,0:T(8,128)(2,1)}, bf16[1024,768]{1,0:T(8,128)(2,1)}, f32[8,512]{1,0:T(8,128)}, f32[24,128]{1,0:T(8,128)}) custom-call(bf16[1024,1664]{1,0:T(8,128)(2,1)} %constant_dynamic-update-slice_fusion.27.refs_0_.refs_1_, bf16[1024,1664]{1,0:T(8,128)(2,1)} %constant_dynamic-update-slice_fusion.27.refs_0_.refs_1_, ...), custom_call_target="tpu_custom_call" | custom-call | flops 11000000512 | bytes 35000000 | tf_op jit(solution)/shard_map/mixer_backward/pallas_call | solution.py:388
  506.1 3.4 collective-permute-start.65
  509.5 11.7 %mixer_backward.7 = (bf16[1024,1536]{1,0:T(8,128)(2,1)}, bf16[1024,768]{1,0:T(8,128)(2,1)}, f32[8,512]{1,0:T(8,128)}, f32[24,128]{1,0:T(8,128)}) custom-call(bf16[1024,1664]{1,0:T(8,128)(2,1)} %constant_dynamic-update-slice_fusion.27.refs_0_.refs_1_, ...), custom_call_target="tpu_custom_call", output_to_operand_aliasing={{0}: (9, {}), {1}: (10, {})} | custom-call | flops 11000000512 | bytes 35000000 | tf_op jit(solution)/shard_map/mixer_backward/pallas_call | solution.py:388
  522.2 4.2 add_convert_fusion.9
  534.4 3.3 collective-permute-done.64
  543.4 2.9 fusion.12
  546.3 3.7 collective-permute-done.66
  554.5 6.7 %collective-permute-done.68 = bf16[128,1536]{1,0:T(8,128)(2,1)} collective-permute-done((bf16[128,1536]{1,0:T(8,128)(2,1)S(1)}, bf16[128,1536]{1,0:T(8,128)(2,1)}, u32[]{:S(2)}, u32[]{:S(2)}) %collective-permute-start.68) | collective-permute-done | bytes 393248 | tf_op jit(solution)/shard_map/ppermute | solution.py:36
  566.1 9.5 %all-to-all-start.2 = ((f32[32,1,712]{2,1,0:T(1,128)}), f32[32,1,712]{2,1,0:T(1,128)}, u32[]{:S(2)}, u32[]{:S(2)}) async-start(f32[32,1,712]{2,1,0:T(1,128)} %copy.204), calls=%async_computation.5 | async-start | bytes 196608 | tf_op jit(solution)/shard_map/all_to_all | solution.py:1126
  577.0 10.4 %reduce-scatter.8.cloned.1.call-done = bf16[4,768,512]{2,1,0:T(8,128)(2,1)} async-done(((bf16[4,1536,512]{2,1,0:T(8,128)(2,1)}), bf16[4,768,512]{2,1,0:T(8,128)(2,1)}) %reduce-scatter.8.cloned.1.call-update) | async-done | bytes 3145744 | tf_op jit(solution)/shard_map/reduce_scatter | solution.py:924
  587.3 5.7 collective-permute-done.73
  596.5 7.2 %all-to-all-start.1 = ((bf16[16,48,896]{2,1,0:T(8,128)(2,1)}), bf16[16,48,896]{2,1,0:T(8,128)(2,1)}, u32[]{:S(2)}, u32[]{:S(2)}) async-start(bf16[16,48,896]{2,1,0:T(8,128)(2,1)} %bitcast.136), calls=%async_computation.4 | async-start | bytes 2752512 | tf_op jit(solution)/shard_map/all_to_all | solution.py:1083
  612.0 5.6 convert_element_type.836
  617.7 3.6 convert_element_type.837
  622.8 12.9 %all-to-all-done.1.refs_0_ = bf16[16,48,896]{2,1,0:T(8,128)(2,1)} async-done(((bf16[16,48,896]{2,1,0:T(8,128)(2,1)}), bf16[16,48,896]{2,1,0:T(8,128)(2,1)}, u32[]{:S(2)}, u32[]{:S(2)}) %all-to-all-start.1) | async-done | bytes 1376288 | tf_op jit(solution)/shard_map/all_to_all | solution.py:1083
  635.8 3.2 unpack.1
  (514 shorter events, 187.8 us)
Async XLA Ops:
  11.9 15.7 %collective-permute-start = (bf16[1,48,384]{2,1,0:T(8,128)(2,1)S(1)}, bf16[1,48,384]{2,1,0:T(8,128)(2,1)S(1)}, u32[]{:S(2)}, u32[]{:S(2)}) collective-permute-start(bf16[1,48,384]{2,1,0:T(8,128)(2,1)S(1)} %fusion.61), channel_id=1, source_target_pairs={{0,16},{16,0},{1,17},{17,1},{2,18},{18,2},{3,19},{19,3},{4,20},{20... | collective-permute-start | bytes 110600 | tf_op jit(solution)/shard_map/ppermute | solution.py:31
  13.1 14.6 %collective-permute-start.1 = (bf16[96,1536]{1,0:T(8,128)(2,1)}, bf16[96,1536]{1,0:T(8,128)(2,1)S(1)}, u32[]{:S(2)}, u32[]{:S(2)}) collective-permute-start(bf16[96,1536]{1,0:T(8,128)(2,1)} %param.27), channel_id=1, source_target_pairs={{0,1},{1,0},{2,3},{3,2},{4,5},{5,4},{6,7},{7,6},{8,9},{9,8},{10,11... | collective-permute-start | bytes 884744 | tf_op jit(solution)/shard_map/ppermute | solution.py:31
  14.1 15.1 %collective-permute-start.5 = (bf16[1,32,1536]{2,1,0:T(8,128)(2,1)}, bf16[1,32,1536]{2,1,0:T(8,128)(2,1)S(1)}, u32[]{:S(2)}, u32[]{:S(2)}) collective-permute-start(bf16[1,32,1536]{2,1,0:T(8,128)(2,1)} %bitcast.168), channel_id=1, source_target_pairs={{0,16},{16,0},{1,17},{17,1},{2,18},{18,2},{3,19},{19,3},{4,20},{20... | collective-permute-start | bytes 294920 | tf_op jit(solution)/shard_map/ppermute | solution.py:31
  19.7 37.2 %all-to-all-start = ((bf16[16,48,512]{2,1,0:T(8,128)(2,1)}), bf16[16,48,512]{2,1,0:T(8,128)(2,1)S(1)}, u32[]{:S(2)}, u32[]{:S(2)}) async-start(bf16[16,48,512]{2,1,0:T(8,128)(2,1)} %pad_maximum_fusion.2), calls=%async_computation | async-start | bytes 1572864 | tf_op jit(solution)/shard_map/all_to_all | solution.py:729
  26.0 100.2 %all-gather.4.cloned.1.call-start = ((), (), s32[]{:S(2)}) async-start(), calls=%async_computation.6 | async-start | bytes 9437184 | tf_op jit(solution)/shard_map/all_gather | solution.py:778
  26.7 190.0 %all-gather.6.cloned.1.call-start = ((), (), s32[]{:S(2)}) async-start(), calls=%async_computation.7 | async-start | bytes 9437184 | tf_op jit(solution)/shard_map/all_gather | solution.py:778
  29.2 25.2 %collective-permute-start.2 = (bf16[128,2048]{1,0:T(8,128)(2,1)S(1)}, bf16[128,2048]{1,0:T(8,128)(2,1)S(1)}, u32[]{:S(2)}, u32[]{:S(2)}) collective-permute-start(bf16[128,2048]{1,0:T(8,128)(2,1)S(1)} %fusion.46), channel_id=1, source_target_pairs={{0,4},{4,8},{8,12},{12,0},{1,5},{5,9},{9,13},{13,1},{2,6},{6,10},{... | collective-permute-start | bytes 1572872 | tf_op jit(solution)/shard_map/ppermute | solution.py:36
  30.5 23.9 %collective-permute-start.3 = (bf16[128,2048]{1,0:T(8,128)(2,1)S(1)}, bf16[128,2048]{1,0:T(8,128)(2,1)S(1)}, u32[]{:S(2)}, u32[]{:S(2)}) collective-permute-start(bf16[128,2048]{1,0:T(8,128)(2,1)S(1)} %fusion.46), channel_id=1, source_target_pairs={{0,2},{2,0},{1,3},{3,1},{4,6},{6,4},{5,7},{7,5},{8,10},{10,8},{9,1... | collective-permute-start | bytes 1572872 | tf_op jit(solution)/shard_map/ppermute | solution.py:31
  56.8 13.8 %collective-permute-start.6 = (bf16[128,2048]{1,0:T(8,128)(2,1)S(1)}, bf16[128,2048]{1,0:T(8,128)(2,1)S(1)}, u32[]{:S(2)}, u32[]{:S(2)}) collective-permute-start(bf16[128,2048]{1,0:T(8,128)(2,1)S(1)} %collective-permute-done.2), channel_id=1, source_target_pairs={{0,4},{4,8},{8,12},{12,0},{1,5},{5,9},{9,13},{13,1},{2,6},{6,10},{... | collective-permute-start | bytes 1572872 | tf_op jit(solution)/shard_map/ppermute | solution.py:36
  56.8 13.8 %collective-permute-start.7 = (bf16[128,2048]{1,0:T(8,128)(2,1)S(1)}, bf16[128,2048]{1,0:T(8,128)(2,1)S(1)}, u32[]{:S(2)}, u32[]{:S(2)}) collective-permute-start(bf16[128,2048]{1,0:T(8,128)(2,1)S(1)} %collective-permute-done.2), channel_id=1, source_target_pairs={{0,2},{2,0},{1,3},{3,1},{4,6},{6,4},{5,7},{7,5},{8,10},{10,8},{9,1... | collective-permute-start | bytes 1572872 | tf_op jit(solution)/shard_map/ppermute | solution.py:31
  57.1 13.5 %collective-permute-start.8 = (bf16[256,512]{1,0:T(8,128)(2,1)S(1)}, bf16[256,512]{1,0:T(8,128)(2,1)S(1)}, u32[]{:S(2)}, u32[]{:S(2)}) collective-permute-start(bf16[256,512]{1,0:T(8,128)(2,1)S(1)} %get-tuple-element.233), channel_id=1, source_target_pairs={{0,16},{16,0},{1,17},{17,1},{2,18},{18,2},{3,19},{19,3},{4,20},{20... | collective-permute-start | bytes 786440 | tf_op jit(solution)/shard_map/ppermute | solution.py:31
  71.3 15.2 %collective-permute-start.10 = (bf16[128,2048]{1,0:T(8,128)(2,1)S(1)}, bf16[128,2048]{1,0:T(8,128)(2,1)S(1)}, u32[]{:S(2)}, u32[]{:S(2)}) collective-permute-start(bf16[128,2048]{1,0:T(8,128)(2,1)S(1)} %collective-permute-done.6), channel_id=1, source_target_pairs={{0,2},{2,0},{1,3},{3,1},{4,6},{6,4},{5,7},{7,5},{8,10},{10,8},{9,1... | collective-permute-start | bytes 1572872 | tf_op jit(solution)/shard_map/ppermute | solution.py:31
  72.6 13.9 %collective-permute-start.9 = (bf16[128,2048]{1,0:T(8,128)(2,1)S(1)}, bf16[128,2048]{1,0:T(8,128)(2,1)S(1)}, u32[]{:S(2)}, u32[]{:S(2)}) collective-permute-start(bf16[128,2048]{1,0:T(8,128)(2,1)S(1)} %collective-permute-done.6), channel_id=1, source_target_pairs={{0,4},{4,8},{8,12},{12,0},{1,5},{5,9},{9,13},{13,1},{2,6},{6,10},{... | collective-permute-start | bytes 1572872 | tf_op jit(solution)/shard_map/ppermute | solution.py:36
  73.4 13.1 %collective-permute-start.11 = (bf16[256,512]{1,0:T(8,128)(2,1)S(1)}, bf16[256,512]{1,0:T(8,128)(2,1)S(1)}, u32[]{:S(2)}, u32[]{:S(2)}) collective-permute-start(bf16[256,512]{1,0:T(8,128)(2,1)S(1)} %get-tuple-element.236), channel_id=1, source_target_pairs={{0,16},{16,0},{1,17},{17,1},{2,18},{18,2},{3,19},{19,3},{4,20},{20... | collective-permute-start | bytes 786440 | tf_op jit(solution)/shard_map/ppermute | solution.py:31
  86.5 13.9 %collective-permute-start.12 = (bf16[128,2048]{1,0:T(8,128)(2,1)S(1)}, bf16[128,2048]{1,0:T(8,128)(2,1)S(1)}, u32[]{:S(2)}, u32[]{:S(2)}) collective-permute-start(bf16[128,2048]{1,0:T(8,128)(2,1)S(1)} %collective-permute-done.9), channel_id=1, source_target_pairs={{0,2},{2,0},{1,3},{3,1},{4,6},{6,4},{5,7},{7,5},{8,10},{10,8},{9,1... | collective-permute-start | bytes 1572872 | tf_op jit(solution)/shard_map/ppermute | solution.py:31
  87.7 12.8 %collective-permute-start.13 = (bf16[256,512]{1,0:T(8,128)(2,1)S(1)}, bf16[256,512]{1,0:T(8,128)(2,1)S(1)}, u32[]{:S(2)}, u32[]{:S(2)}) collective-permute-start(bf16[256,512]{1,0:T(8,128)(2,1)S(1)} %get-tuple-element.239), channel_id=1, source_target_pairs={{0,16},{16,0},{1,17},{17,1},{2,18},{18,2},{3,19},{19,3},{4,20},{20... | collective-permute-start | bytes 786440 | tf_op jit(solution)/shard_map/ppermute | solution.py:31
  101.3 14.8 %collective-permute-start.16 = (bf16[1024,2048]{1,0:T(8,128)(2,1)}, bf16[1024,2048]{1,0:T(8,128)(2,1)}, u32[]{:S(2)}, u32[]{:S(2)}) collective-permute-start(bf16[1024,2048]{1,0:T(8,128)(2,1)} %constant_dynamic-update-slice_fusion.refs_0_.refs_1_.refs_2_), channel_id=1, source_target_pairs={{0,1},{1,0},{2,3},{3,2},{4,5},{5,4},{6,7},{7,6},{8,9},{9,8},{10,11... | collective-permute-start | bytes 12582920 | tf_op jit(solution)/shard_map/ppermute | solution.py:31
  105.5 184.6 %all-gather.8.cloned.1.call-start = ((), (), s32[]{:S(2)}) async-start(), calls=%async_computation.8 | async-start | bytes 9437184 | tf_op jit(solution)/shard_map/all_gather | solution.py:778
  110.2 25.2 %collective-permute-start.14 = (bf16[128,1536]{1,0:T(8,128)(2,1)}, bf16[128,1536]{1,0:T(8,128)(2,1)}, u32[]{:S(2)}, u32[]{:S(2)}) collective-permute-start(bf16[128,1536]{1,0:T(8,128)(2,1)} %fusion.30), channel_id=1, source_target_pairs={{0,4},{4,8},{8,12},{12,0},{1,5},{5,9},{9,13},{13,1},{2,6},{6,10},{... | collective-permute-start | bytes 1179656 | tf_op jit(solution)/shard_map/ppermute | solution.py:36
  111.6 23.8 %collective-permute-start.15 = (bf16[128,1536]{1,0:T(8,128)(2,1)}, bf16[128,1536]{1,0:T(8,128)(2,1)}, u32[]{:S(2)}, u32[]{:S(2)}) collective-permute-start(bf16[128,1536]{1,0:T(8,128)(2,1)} %fusion.30), channel_id=1, source_target_pairs={{0,2},{2,0},{1,3},{3,1},{4,6},{6,4},{5,7},{7,5},{8,10},{10,8},{9,1... | collective-permute-start | bytes 1179656 | tf_op jit(solution)/shard_map/ppermute | solution.py:31
  135.4 15.5 %collective-permute-start.17 = (bf16[128,1536]{1,0:T(8,128)(2,1)}, bf16[128,1536]{1,0:T(8,128)(2,1)S(1)}, u32[]{:S(2)}, u32[]{:S(2)}) collective-permute-start(bf16[128,1536]{1,0:T(8,128)(2,1)} %collective-permute-done.14), channel_id=1, source_target_pairs={{0,4},{4,8},{8,12},{12,0},{1,5},{5,9},{9,13},{13,1},{2,6},{6,10},{... | collective-permute-start | bytes 1179656 | tf_op jit(solution)/shard_map/ppermute | solution.py:36
  136.8 14.1 %collective-permute-start.18 = (bf16[128,1536]{1,0:T(8,128)(2,1)}, bf16[128,1536]{1,0:T(8,128)(2,1)S(1)}, u32[]{:S(2)}, u32[]{:S(2)}) collective-permute-start(bf16[128,1536]{1,0:T(8,128)(2,1)} %collective-permute-done.14), channel_id=1, source_target_pairs={{0,2},{2,0},{1,3},{3,1},{4,6},{6,4},{5,7},{7,5},{8,10},{10,8},{9,1... | collective-permute-start | bytes 1179656 | tf_op jit(solution)/shard_map/ppermute | solution.py:31
  150.9 24.4 %collective-permute-start.21 = (bf16[1024,1664]{1,0:T(8,128)(2,1)}, bf16[1024,1664]{1,0:T(8,128)(2,1)}, u32[]{:S(2)}, u32[]{:S(2)}) collective-permute-start(bf16[1024,1664]{1,0:T(8,128)(2,1)} %get-tuple-element.270), channel_id=1, source_target_pairs={{0,1},{1,0},{2,3},{3,2},{4,5},{5,4},{6,7},{7,6},{8,9},{9,8},{10,11... | collective-permute-start | bytes 10223624 | tf_op jit(solution)/shard_map/ppermute | solution.py:31
  152.0 277.4 %reduce-scatter.4.cloned.1.call-start = ((), (), s32[]{:S(2)}) async-start(), calls=%async_computation.9 | async-start | bytes 9437184 | tf_op jit(solution)/shard_map/reduce_scatter | solution.py:924
  159.9 15.4 %collective-permute-start.19 = (bf16[128,1536]{1,0:T(8,128)(2,1)S(1)}, bf16[128,1536]{1,0:T(8,128)(2,1)S(1)}, u32[]{:S(2)}, u32[]{:S(2)}) collective-permute-start(bf16[128,1536]{1,0:T(8,128)(2,1)S(1)} %collective-permute-done.17), channel_id=1, source_target_pairs={{0,4},{4,8},{8,12},{12,0},{1,5},{5,9},{9,13},{13,1},{2,6},{6,10},{... | collective-permute-start | bytes 1179656 | tf_op jit(solution)/shard_map/ppermute | solution.py:36
  161.1 14.2 %collective-permute-start.20 = (bf16[128,1536]{1,0:T(8,128)(2,1)S(1)}, bf16[128,1536]{1,0:T(8,128)(2,1)S(1)}, u32[]{:S(2)}, u32[]{:S(2)}) collective-permute-start(bf16[128,1536]{1,0:T(8,128)(2,1)S(1)} %collective-permute-done.17), channel_id=1, source_target_pairs={{0,2},{2,0},{1,3},{3,1},{4,6},{6,4},{5,7},{7,5},{8,10},{10,8},{9,1... | collective-permute-start | bytes 1179656 | tf_op jit(solution)/shard_map/ppermute | solution.py:31
  182.2 16.2 %collective-permute-start.24 = (bf16[128,1664]{1,0:T(8,128)(2,1)S(1)}, bf16[128,1664]{1,0:T(8,128)(2,1)S(1)}, u32[]{:S(2)}, u32[]{:S(2)}) collective-permute-start(bf16[128,1664]{1,0:T(8,128)(2,1)S(1)} %slice.535), channel_id=1, source_target_pairs={{0,2},{2,0},{1,3},{3,1},{4,6},{6,4},{5,7},{7,5},{8,10},{10,8},{9,1... | collective-permute-start | bytes 1277960 | tf_op jit(solution)/shard_map/ppermute | solution.py:31
  190.5 16.2 %collective-permute-start.31 = (bf16[128,1536]{1,0:T(8,128)(2,1)S(1)}, bf16[128,1536]{1,0:T(8,128)(2,1)S(1)}, u32[]{:S(2)}, u32[]{:S(2)}) collective-permute-start(bf16[128,1536]{1,0:T(8,128)(2,1)S(1)} %collective-permute-done.19), channel_id=1, source_target_pairs={{0,2},{2,0},{1,3},{3,1},{4,6},{6,4},{5,7},{7,5},{8,10},{10,8},{9,1... | collective-permute-start | bytes 1179656 | tf_op jit(solution)/shard_map/ppermute | solution.py:31
  191.8 24.0 %collective-permute-start.26 = (bf16[128,1664]{1,0:T(8,128)(2,1)S(1)}, bf16[128,1664]{1,0:T(8,128)(2,1)S(1)}, u32[]{:S(2)}, u32[]{:S(2)}) collective-permute-start(bf16[128,1664]{1,0:T(8,128)(2,1)S(1)} %slice.538), channel_id=1, source_target_pairs={{0,2},{2,0},{1,3},{3,1},{4,6},{6,4},{5,7},{7,5},{8,10},{10,8},{9,1... | collective-permute-start | bytes 1277960 | tf_op jit(solution)/shard_map/ppermute | solution.py:31
  198.5 17.3 %collective-permute-start.25 = (bf16[128,1664]{1,0:T(8,128)(2,1)S(1)}, bf16[128,1664]{1,0:T(8,128)(2,1)S(1)}, u32[]{:S(2)}, u32[]{:S(2)}) collective-permute-start(bf16[128,1664]{1,0:T(8,128)(2,1)S(1)} %add_convert_fusion.19), channel_id=1, source_target_pairs={{0,4},{4,8},{8,12},{12,0},{1,5},{5,9},{9,13},{13,1},{2,6},{6,10},{... | collective-permute-start | bytes 1277960 | tf_op jit(solution)/shard_map/ppermute | solution.py:36
  207.6 27.6 %collective-permute-start.34 = (bf16[1024,1536]{1,0:T(8,128)(2,1)}, bf16[1024,1536]{1,0:T(8,128)(2,1)}, u32[]{:S(2)}, u32[]{:S(2)}) collective-permute-start(bf16[1024,1536]{1,0:T(8,128)(2,1)} %constant_dynamic-update-slice_fusion.11.refs_2_), channel_id=1, source_target_pairs={{0,1},{1,0},{2,3},{3,2},{4,5},{5,4},{6,7},{7,6},{8,9},{9,8},{10,11... | collective-permute-start | bytes 9437192 | tf_op jit(solution)/shard_map/ppermute | solution.py:31
  212.5 12.6 %collective-permute-start.28 = (bf16[128,1664]{1,0:T(8,128)(2,1)}, bf16[128,1664]{1,0:T(8,128)(2,1)S(1)}, u32[]{:S(2)}, u32[]{:S(2)}) collective-permute-start(bf16[128,1664]{1,0:T(8,128)(2,1)} %slice.541), channel_id=1, source_target_pairs={{0,2},{2,0},{1,3},{3,1},{4,6},{6,4},{5,7},{7,5},{8,10},{10,8},{9,1... | collective-permute-start | bytes 1277960 | tf_op jit(solution)/shard_map/ppermute | solution.py:31
  262.1 16.6 %collective-permute-start.38 = (bf16[1024,1536]{1,0:T(8,128)(2,1)S(1)}, bf16[1024,1536]{1,0:T(8,128)(2,1)}, u32[]{:S(2)}, u32[]{:S(2)}) collective-permute-start(bf16[1024,1536]{1,0:T(8,128)(2,1)S(1)} %constant_dynamic-update-slice_fusion.19.refs_2_), channel_id=1, source_target_pairs={{0,1},{1,0},{2,3},{3,2},{4,5},{5,4},{6,7},{7,6},{8,9},{9,8},{10,11... | collective-permute-start | bytes 9437192 | tf_op jit(solution)/shard_map/ppermute | solution.py:31
  319.5 202.6 %reduce-scatter.6.cloned.1.call-start = ((), (), s32[]{:S(2)}) async-start(), calls=%async_computation.10 | async-start | bytes 9437184 | tf_op jit(solution)/shard_map/reduce_scatter | solution.py:924
  350.6 236.8 %reduce-scatter.8.cloned.1.call-start = ((), (), s32[]{:S(2)}) async-start(), calls=%async_computation.11 | async-start | bytes 9437184 | tf_op jit(solution)/shard_map/reduce_scatter | solution.py:924
  352.4 12.5 %collective-permute-start.42 = (bf16[128,1536]{1,0:T(8,128)(2,1)}, bf16[128,1536]{1,0:T(8,128)(2,1)}, u32[]{:S(2)}, u32[]{:S(2)}) collective-permute-start(bf16[128,1536]{1,0:T(8,128)(2,1)} %slice.560), channel_id=1, source_target_pairs={{0,2},{2,0},{1,3},{3,1},{4,6},{6,4},{5,7},{7,5},{8,10},{10,8},{9,1... | collective-permute-start | bytes 1179656 | tf_op jit(solution)/shard_map/ppermute | solution.py:31
  353.4 17.1 %collective-permute-start.44 = (bf16[128,1536]{1,0:T(8,128)(2,1)}, bf16[128,1536]{1,0:T(8,128)(2,1)}, u32[]{:S(2)}, u32[]{:S(2)}) collective-permute-start(bf16[128,1536]{1,0:T(8,128)(2,1)} %slice.564), channel_id=1, source_target_pairs={{0,2},{2,0},{1,3},{3,1},{4,6},{6,4},{5,7},{7,5},{8,10},{10,8},{9,1... | collective-permute-start | bytes 1179656 | tf_op jit(solution)/shard_map/ppermute | solution.py:31
  367.5 11.5 %collective-permute-start.46 = (bf16[128,1536]{1,0:T(8,128)(2,1)S(1)}, bf16[128,1536]{1,0:T(8,128)(2,1)S(1)}, u32[]{:S(2)}, u32[]{:S(2)}) collective-permute-start(bf16[128,1536]{1,0:T(8,128)(2,1)S(1)} %slice.568), channel_id=1, source_target_pairs={{0,2},{2,0},{1,3},{3,1},{4,6},{6,4},{5,7},{7,5},{8,10},{10,8},{9,1... | collective-permute-start | bytes 1179656 | tf_op jit(solution)/shard_map/ppermute | solution.py:31
  395.6 13.7 %collective-permute-start.49 = (bf16[128,1664]{1,0:T(8,128)(2,1)S(1)}, bf16[128,1664]{1,0:T(8,128)(2,1)S(1)}, u32[]{:S(2)}, u32[]{:S(2)}) collective-permute-start(bf16[128,1664]{1,0:T(8,128)(2,1)S(1)} %collective-permute-done.47), channel_id=1, source_target_pairs={{0,4},{4,8},{8,12},{12,0},{1,5},{5,9},{9,13},{13,1},{2,6},{6,10},{... | collective-permute-start | bytes 1277960 | tf_op jit(solution)/shard_map/ppermute | solution.py:36
  395.7 13.6 %collective-permute-start.50 = (bf16[128,1664]{1,0:T(8,128)(2,1)S(1)}, bf16[128,1664]{1,0:T(8,128)(2,1)S(1)}, u32[]{:S(2)}, u32[]{:S(2)}) collective-permute-start(bf16[128,1664]{1,0:T(8,128)(2,1)S(1)} %collective-permute-done.47), channel_id=1, source_target_pairs={{0,2},{2,0},{1,3},{3,1},{4,6},{6,4},{5,7},{7,5},{8,10},{10,8},{9,1... | collective-permute-start | bytes 1277960 | tf_op jit(solution)/shard_map/ppermute | solution.py:31
  396.1 43.7 %collective-permute-start.55 = (bf16[1024,1536]{1,0:T(8,128)(2,1)}, bf16[1024,1536]{1,0:T(8,128)(2,1)}, u32[]{:S(2)}, u32[]{:S(2)}) collective-permute-start(bf16[1024,1536]{1,0:T(8,128)(2,1)} %combine.6), channel_id=1, source_target_pairs={{0,1},{1,0},{2,3},{3,2},{4,5},{5,4},{6,7},{7,6},{8,9},{9,8},{10,11... | collective-permute-start | bytes 9437192 | tf_op jit(solution)/shard_map/ppermute | solution.py:31
  409.3 17.1 %collective-permute-start.51 = (bf16[128,1664]{1,0:T(8,128)(2,1)S(1)}, bf16[128,1664]{1,0:T(8,128)(2,1)}, u32[]{:S(2)}, u32[]{:S(2)}) collective-permute-start(bf16[128,1664]{1,0:T(8,128)(2,1)S(1)} %collective-permute-done.49), channel_id=1, source_target_pairs={{0,4},{4,8},{8,12},{12,0},{1,5},{5,9},{9,13},{13,1},{2,6},{6,10},{... | collective-permute-start | bytes 1277960 | tf_op jit(solution)/shard_map/ppermute | solution.py:36
  414.1 12.4 %collective-permute-start.52 = (bf16[128,1664]{1,0:T(8,128)(2,1)S(1)}, bf16[128,1664]{1,0:T(8,128)(2,1)S(1)}, u32[]{:S(2)}, u32[]{:S(2)}) collective-permute-start(bf16[128,1664]{1,0:T(8,128)(2,1)S(1)} %collective-permute-done.49), channel_id=1, source_target_pairs={{0,2},{2,0},{1,3},{3,1},{4,6},{6,4},{5,7},{7,5},{8,10},{10,8},{9,1... | collective-permute-start | bytes 1277960 | tf_op jit(solution)/shard_map/ppermute | solution.py:31
  426.5 11.3 %collective-permute-start.53 = (bf16[128,1664]{1,0:T(8,128)(2,1)}, bf16[128,1664]{1,0:T(8,128)(2,1)S(1)}, u32[]{:S(2)}, u32[]{:S(2)}) collective-permute-start(bf16[128,1664]{1,0:T(8,128)(2,1)} %collective-permute-done.51), channel_id=1, source_target_pairs={{0,2},{2,0},{1,3},{3,1},{4,6},{6,4},{5,7},{7,5},{8,10},{10,8},{9,1... | collective-permute-start | bytes 1277960 | tf_op jit(solution)/shard_map/ppermute | solution.py:31
  451.7 14.0 %collective-permute-start.56 = (bf16[128,1536]{1,0:T(8,128)(2,1)S(1)}, bf16[128,1536]{1,0:T(8,128)(2,1)S(1)}, u32[]{:S(2)}, u32[]{:S(2)}) collective-permute-start(bf16[128,1536]{1,0:T(8,128)(2,1)S(1)} %slice_bitcast_fusion.3), channel_id=1, source_target_pairs={{0,2},{2,0},{1,3},{3,1},{4,6},{6,4},{5,7},{7,5},{8,10},{10,8},{9,1... | collective-permute-start | bytes 1179656 | tf_op jit(solution)/shard_map/ppermute | solution.py:31
  452.1 18.9 %collective-permute-start.57 = (bf16[128,1536]{1,0:T(8,128)(2,1)S(1)}, bf16[128,1536]{1,0:T(8,128)(2,1)S(1)}, u32[]{:S(2)}, u32[]{:S(2)}) collective-permute-start(bf16[128,1536]{1,0:T(8,128)(2,1)S(1)} %slice_bitcast_fusion.2), channel_id=1, source_target_pairs={{0,2},{2,0},{1,3},{3,1},{4,6},{6,4},{5,7},{7,5},{8,10},{10,8},{9,1... | collective-permute-start | bytes 1179656 | tf_op jit(solution)/shard_map/ppermute | solution.py:31
  471.1 13.3 %collective-permute-start.58 = (bf16[128,1536]{1,0:T(8,128)(2,1)S(1)}, bf16[128,1536]{1,0:T(8,128)(2,1)S(1)}, u32[]{:S(2)}, u32[]{:S(2)}) collective-permute-start(bf16[128,1536]{1,0:T(8,128)(2,1)S(1)} %fusion.40), channel_id=1, source_target_pairs={{0,4},{4,8},{8,12},{12,0},{1,5},{5,9},{9,13},{13,1},{2,6},{6,10},{... | collective-permute-start | bytes 1179656 | tf_op jit(solution)/shard_map/ppermute | solution.py:36
  472.4 12.9 %collective-permute-start.59 = (bf16[128,1536]{1,0:T(8,128)(2,1)S(1)}, bf16[128,1536]{1,0:T(8,128)(2,1)S(1)}, u32[]{:S(2)}, u32[]{:S(2)}) collective-permute-start(bf16[128,1536]{1,0:T(8,128)(2,1)S(1)} %slice_bitcast_fusion.1), channel_id=1, source_target_pairs={{0,2},{2,0},{1,3},{3,1},{4,6},{6,4},{5,7},{7,5},{8,10},{10,8},{9,1... | collective-permute-start | bytes 1179656 | tf_op jit(solution)/shard_map/ppermute | solution.py:31
  486.0 20.0 %collective-permute-start.60 = (bf16[1024,1536]{1,0:T(8,128)(2,1)}, bf16[1024,1536]{1,0:T(8,128)(2,1)}, u32[]{:S(2)}, u32[]{:S(2)}) collective-permute-start(bf16[1024,1536]{1,0:T(8,128)(2,1)} %get-tuple-element.365), channel_id=1, source_target_pairs={{0,1},{1,0},{2,3},{3,2},{4,5},{5,4},{6,7},{7,6},{8,9},{9,8},{10,11... | collective-permute-start | bytes 9437192 | tf_op jit(solution)/shard_map/ppermute | solution.py:31
  490.7 40.5 %collective-permute-start.74 = (bf16[768,128]{1,0:T(8,128)(2,1)}, bf16[768,128]{1,0:T(8,128)(2,1)}, u32[]{:S(2)}, u32[]{:S(2)}) collective-permute-start(bf16[768,128]{1,0:T(8,128)(2,1)} %dynamic-slice_convert_fusion), channel_id=1, source_target_pairs={{0,16},{16,0},{1,17},{17,1},{2,18},{18,2},{3,19},{19,3},{4,20},{20... | collective-permute-start | bytes 589832 | tf_op jit(solution)/shard_map/ppermute | solution.py:31
  491.7 113.4 %collective-permute-start.76 = (bf16[1,32,1536]{2,1,0:T(8,128)(2,1)}, bf16[1,32,1536]{2,1,0:T(8,128)(2,1)}, u32[]{:S(2)}, u32[]{:S(2)}) collective-permute-start(bf16[1,32,1536]{2,1,0:T(8,128)(2,1)} %dynamic-slice_convert_fusion.1), channel_id=1, source_target_pairs={{0,16},{16,0},{1,17},{17,1},{2,18},{18,2},{3,19},{19,3},{4,20},{20... | collective-permute-start | bytes 294920 | tf_op jit(solution)/shard_map/ppermute | solution.py:31
  492.8 13.0 %collective-permute-start.61 = (bf16[128,1536]{1,0:T(8,128)(2,1)}, bf16[128,1536]{1,0:T(8,128)(2,1)S(1)}, u32[]{:S(2)}, u32[]{:S(2)}) collective-permute-start(bf16[128,1536]{1,0:T(8,128)(2,1)} %fusion.39), channel_id=1, source_target_pairs={{0,4},{4,8},{8,12},{12,0},{1,5},{5,9},{9,13},{13,1},{2,6},{6,10},{... | collective-permute-start | bytes 1179656 | tf_op jit(solution)/shard_map/ppermute | solution.py:36
  493.0 13.0 %collective-permute-start.62 = (bf16[128,1536]{1,0:T(8,128)(2,1)S(1)}, bf16[128,1536]{1,0:T(8,128)(2,1)S(1)}, u32[]{:S(2)}, u32[]{:S(2)}) collective-permute-start(bf16[128,1536]{1,0:T(8,128)(2,1)S(1)} %slice_bitcast_fusion), channel_id=1, source_target_pairs={{0,2},{2,0},{1,3},{3,1},{4,6},{6,4},{5,7},{7,5},{8,10},{10,8},{9,1... | collective-permute-start | bytes 1179656 | tf_op jit(solution)/shard_map/ppermute | solution.py:31
  506.0 15.2 %collective-permute-start.63 = (bf16[128,1536]{1,0:T(8,128)(2,1)S(1)}, bf16[128,1536]{1,0:T(8,128)(2,1)S(1)}, u32[]{:S(2)}, u32[]{:S(2)}) collective-permute-start(bf16[128,1536]{1,0:T(8,128)(2,1)S(1)} %fusion.37), channel_id=1, source_target_pairs={{0,4},{4,8},{8,12},{12,0},{1,5},{5,9},{9,13},{13,1},{2,6},{6,10},{... | collective-permute-start | bytes 1179656 | tf_op jit(solution)/shard_map/ppermute | solution.py:36
  506.1 32.4 %collective-permute-start.65 = (bf16[192,1536]{1,0:T(8,128)(2,1)}, bf16[192,1536]{1,0:T(8,128)(2,1)}, u32[]{:S(2)}, u32[]{:S(2)}) collective-permute-start(bf16[192,1536]{1,0:T(8,128)(2,1)} %fusion.50), channel_id=1, source_target_pairs={{16,0},{1,17},{18,2},{3,19},{20,4},{5,21},{22,6},{7,23},{24,8},{9,... | collective-permute-start | bytes 1769480 | tf_op jit(solution)/shard_map/ppermute | solution.py:82
  527.3 19.1 %collective-permute-start.67 = (bf16[128,1536]{1,0:T(8,128)(2,1)S(1)}, bf16[128,1536]{1,0:T(8,128)(2,1)S(1)}, u32[]{:S(2)}, u32[]{:S(2)}) collective-permute-start(bf16[128,1536]{1,0:T(8,128)(2,1)S(1)} %slice.580), channel_id=1, source_target_pairs={{0,2},{2,0},{1,3},{3,1},{4,6},{6,4},{5,7},{7,5},{8,10},{10,8},{9,1... | collective-permute-start | bytes 1179656 | tf_op jit(solution)/shard_map/ppermute | solution.py:31
  531.2 23.3 %collective-permute-start.69 = (bf16[128,1536]{1,0:T(8,128)(2,1)S(1)}, bf16[128,1536]{1,0:T(8,128)(2,1)}, u32[]{:S(2)}, u32[]{:S(2)}) collective-permute-start(bf16[128,1536]{1,0:T(8,128)(2,1)S(1)} %slice.582), channel_id=1, source_target_pairs={{0,2},{2,0},{1,3},{3,1},{4,6},{6,4},{5,7},{7,5},{8,10},{10,8},{9,1... | collective-permute-start | bytes 1179656 | tf_op jit(solution)/shard_map/ppermute | solution.py:31
  537.7 37.9 %collective-permute-start.71 = (bf16[128,1536]{1,0:T(8,128)(2,1)}, bf16[128,1536]{1,0:T(8,128)(2,1)}, u32[]{:S(2)}, u32[]{:S(2)}) collective-permute-start(bf16[128,1536]{1,0:T(8,128)(2,1)} %slice.587), channel_id=1, source_target_pairs={{0,2},{2,0},{1,3},{3,1},{4,6},{6,4},{5,7},{7,5},{8,10},{10,8},{9,1... | collective-permute-start | bytes 1179656 | tf_op jit(solution)/shard_map/ppermute | solution.py:31
  538.5 11.5 %collective-permute-start.66 = (bf16[128,1536]{1,0:T(8,128)(2,1)S(1)}, bf16[128,1536]{1,0:T(8,128)(2,1)S(1)}, u32[]{:S(2)}, u32[]{:S(2)}) collective-permute-start(bf16[128,1536]{1,0:T(8,128)(2,1)S(1)} %add_convert_fusion.23), channel_id=1, source_target_pairs={{0,4},{4,8},{8,12},{12,0},{1,5},{5,9},{9,13},{13,1},{2,6},{6,10},{... | collective-permute-start | bytes 1179656 | tf_op jit(solution)/shard_map/ppermute | solution.py:36
  546.3 41.0 %collective-permute-start.72 = (bf16[384,768]{1,0:T(8,128)(2,1)}, bf16[384,768]{1,0:T(8,128)(2,1)}, u32[]{:S(2)}, u32[]{:S(2)}) collective-permute-start(bf16[384,768]{1,0:T(8,128)(2,1)} %get-tuple-element.414), channel_id=1, source_target_pairs={{0,16},{16,0},{1,17},{17,1},{2,18},{18,2},{3,19},{19,3},{4,20},{20... | collective-permute-start | bytes 1769480 | tf_op jit(solution)/shard_map/ppermute | solution.py:31
  554.5 38.5 %collective-permute-start.73 = (bf16[384,768]{1,0:T(8,128)(2,1)}, bf16[384,768]{1,0:T(8,128)(2,1)}, u32[]{:S(2)}, u32[]{:S(2)}) collective-permute-start(bf16[384,768]{1,0:T(8,128)(2,1)} %get-tuple-element.415), channel_id=1, source_target_pairs={{0,16},{16,0},{1,17},{17,1},{2,18},{18,2},{3,19},{19,3},{4,20},{20... | collective-permute-start | bytes 1769480 | tf_op jit(solution)/shard_map/ppermute | solution.py:31
  563.3 12.3 %collective-permute-start.70 = (bf16[128,1536]{1,0:T(8,128)(2,1)}, bf16[128,1536]{1,0:T(8,128)(2,1)}, u32[]{:S(2)}, u32[]{:S(2)}) collective-permute-start(bf16[128,1536]{1,0:T(8,128)(2,1)} %add_convert_fusion.21), channel_id=1, source_target_pairs={{0,4},{4,8},{8,12},{12,0},{1,5},{5,9},{9,13},{13,1},{2,6},{6,10},{... | collective-permute-start | bytes 1179656 | tf_op jit(solution)/shard_map/ppermute | solution.py:36
  566.1 30.4 %all-to-all-start.2 = ((f32[32,1,712]{2,1,0:T(1,128)}), f32[32,1,712]{2,1,0:T(1,128)}, u32[]{:S(2)}, u32[]{:S(2)}) async-start(f32[32,1,712]{2,1,0:T(1,128)} %copy.204), calls=%async_computation.5 | async-start | bytes 196608 | tf_op jit(solution)/shard_map/all_to_all | solution.py:1126
  596.5 39.3 %all-to-all-start.1 = ((bf16[16,48,896]{2,1,0:T(8,128)(2,1)}), bf16[16,48,896]{2,1,0:T(8,128)(2,1)}, u32[]{:S(2)}, u32[]{:S(2)}) async-start(bf16[16,48,896]{2,1,0:T(8,128)(2,1)} %bitcast.136), calls=%async_computation.4 | async-start | bytes 2752512 | tf_op jit(solution)/shard_map/all_to_all | solution.py:1083
  (90 other events, 1094.1 us)
Sparse Core Ops, SparseCore 0:
  28.3 97.7 all-gather.3
  127.7 80.3 all-gather.5
  209.7 80.3 all-gather.7
  319.7 77.0 reduce-scatter.3
  399.6 77.0 reduce-scatter.5
  479.4 107.8 reduce-scatter.7
